TPU v7x, 32 devices: a whole 2x2x4 slice. The times are simulated.
32 devices in a mesh: blk: 8 (over z, x), group: 4 (over y, core).
Axes of the slice: x: 2, y: 2, z: 4, core: 2. Of those that a mesh axis runs over, the one named last changes fastest.
Arguments:
- queries: bfloat16 [8, 2048, 2560], P('blk', 'group'), may hold values from -6 to 6
- new_keys: bfloat16 [8, 2048, 256], P('blk', 'group'), may hold values from -15 to 15
- new_values: bfloat16 [8, 2048, 256], P('blk', 'group'), may hold values from -4 to 4
- key_cache: bfloat16 [320, 128, 256], P('blk', 'group'), may hold values from -4 to 4
- value_cache: bfloat16 [320, 128, 256], P('blk', 'group'), may hold values from -4 to 4
- out_weight: bfloat16 [2560, 2560], replicated, may hold values from -0.375 to 0.375
- lengths: int32 [8], replicated, may hold values from 0 to 30720, as said below
- page_table: int32 [8, 32], replicated, may hold values from 0 to 319, as said below
Outputs:
- hidden_states: bfloat16 [8, 2048, 2560], P('blk', 'group')
- key_cache_out: bfloat16 [320, 128, 256], P('blk', 'group')
- value_cache_out: bfloat16 [320, 128, 256], P('blk', 'group')
Inputs may be any that keep to these rules, and one draw needn't show every extreme that they name: `lengths`: multiples of 2048; some request has length 0 and some has 30720. `page_table`: all entries differ; page p lies on blk index p // 40; columns below 16 hold the request's last 16 pages before its group in order (pages that hold no part of a request where its length is short), the others the pages of its group in order; of one request's first 16 entries at most 2 lie on one blk index, of its last 16 at most 2, and both bounds are reached for every request.
All inputs are finite; a program needn't handle non-finite values.
Results may differ from a plain program's by a relative error of at most 0.009.
Values may be sent and summed in bfloat16 or wider, within the bound.
No kernel may reach another device: no remote copies, remote signals or barrier semaphores. Data moves between devices by JAX's collectives and lax.ppermute only.
A program may use at most 256 MiB of HBM per device.

v0:
```python
import jax
import jax.numpy as jnp
import numpy as np
from jax import lax
from jax.experimental import pallas as pl
from jax.experimental.pallas import tpu as pltpu
from jax.sharding import PartitionSpec as P

masked_score = -1e30
step_keys = 512
hbm_spec = pl.BlockSpec(memory_space=pltpu.HBM)
smem_spec = pl.BlockSpec(memory_space=pltpu.SMEM)
vmem_spec = pl.BlockSpec(memory_space=pltpu.VMEM)
small_limit = 8 * 1024 * 1024
large_limit = 56 * 1024 * 1024


def params(limit):
    return pltpu.CompilerParams(vmem_limit_bytes=limit)


def in_hbm(*arrays):
    return [pltpu.with_memory_space_constraint(array, pltpu.HBM) for array in arrays]


def turn(values, cosine, sine):
    front = values[:, :128].astype(jnp.float32)
    return front * cosine + pltpu.roll(front, 64, 1) * sine


def join(pieces):
    return jnp.concatenate(pieces, axis=1)


def rotate_kernel(lengths_ref, freq_ref, keys_ref, out_ref, cos_ref, sin_ref):
    rows = keys_ref.shape[0]
    start = lengths_ref[lax.axis_index("blk")] + lax.axis_index("group") * rows
    positions = start + lax.broadcasted_iota(jnp.int32, (rows, 128), 0)
    angles = positions.astype(jnp.float32) * freq_ref[...]
    lane = lax.broadcasted_iota(jnp.int32, (rows, 128), 1)
    cosine = jnp.cos(angles)
    sine = jnp.sin(angles)
    sine = jnp.where(lane < 64, -sine, sine)
    cos_ref[...] = cosine
    sin_ref[...] = sine
    keys = keys_ref[...]
    out_ref[:, :128] = turn(keys, cosine, sine).astype(jnp.bfloat16)
    out_ref[:, 128:] = keys[:, 128:]


def rotate_keys(lengths, keys):
    rows, head_dim = keys.shape
    quarter = head_dim // 4
    freq_table = np.float32(10000.0) ** (-np.arange(quarter, dtype=np.float32) / np.float32(quarter))
    freq_table = np.concatenate([freq_table, freq_table])[None].astype(np.float32)
    table = jax.ShapeDtypeStruct((rows, 128), jnp.float32)
    return pl.pallas_call(
        rotate_kernel,
        out_shape=(jax.ShapeDtypeStruct(keys.shape, jnp.bfloat16), table, table),
        in_specs=[smem_spec, vmem_spec, vmem_spec],
        out_specs=(vmem_spec,) * 3,
        compiler_params=params(small_limit),
        name="rotate_keys",
    )(lengths, jnp.asarray(freq_table), keys)


def pick_old_kernel(table_ref, key_ref, value_ref, out_ref, sem):
    requests, cap = out_ref.shape[:2]
    pages = key_ref.shape[0]
    low = lax.axis_index("blk") * pages
    window = table_ref.shape[1] // 2
    for r in range(requests):
        count = jnp.int32(0)
        chosen = [jnp.int32(0)] * cap
        for j in range(window):
            page = table_ref[r, j] - low
            inside = (page >= 0) & (page < pages)
            chosen = [jnp.where(inside & (count == c), page, chosen[c]) for c in range(cap)]
            count = count + inside.astype(jnp.int32)
        for c in range(cap):
            pltpu.make_async_copy(key_ref.at[chosen[c]], out_ref.at[r, c, 0], sem).start()
            pltpu.make_async_copy(value_ref.at[chosen[c]], out_ref.at[r, c, 1], sem).start()
    pltpu.make_async_copy(out_ref, out_ref, sem).wait()


def pick_old(page_table, cap, key_cache, value_cache):
    requests = page_table.shape[0]
    return pl.pallas_call(
        pick_old_kernel,
        out_shape=jax.ShapeDtypeStruct((requests, cap, 2) + key_cache.shape[1:], jnp.bfloat16),
        in_specs=[smem_spec, hbm_spec, hbm_spec],
        out_specs=vmem_spec,
        scratch_shapes=[pltpu.SemaphoreType.DMA],
        compiler_params=params(small_limit),
        name="pick_old",
    )(page_table, *in_hbm(key_cache, value_cache))


def owner_of(page, pages, owners):
    factor = (1 << 20) // pages + 1
    assert all((p * factor) >> 20 == p // pages for p in range(pages * owners))
    assert pages * owners * factor < 1 << 31
    return (page * factor) >> 20


def find_slots(table_ref, first, count, cap, pages, slots_ref, counts_ref):
    owners = counts_ref.shape[0]
    row = lax.axis_index("blk")
    for o in range(owners):
        counts_ref[o] = 0
    for j in range(count):
        owner = owner_of(table_ref[row, first + j], pages, owners)
        rank = counts_ref[owner]
        counts_ref[owner] = rank + 1
        slots_ref[j] = owner * cap + rank


def pick_new_kernel(
    pages, table_ref, key_0, key_1, key_2, key_3, value_0, value_1, value_2, value_3,
    out_ref, slots_ref, counts_ref, sem,
):
    sources = ((key_0, value_0), (key_1, value_1), (key_2, value_2), (key_3, value_3))
    cap = out_ref.shape[0] // counts_ref.shape[0]
    rows = out_ref.shape[2]
    page_len = rows * 4
    block_pages = key_0.shape[0] // page_len
    count = block_pages * 4
    group_index = lax.axis_index("group")
    find_slots(table_ref, table_ref.shape[1] - count, count, cap, pages, slots_ref, counts_ref)
    for number, pair in enumerate(sources):
        block = number ^ group_index

        for place in range(block_pages):
            slot = slots_ref[block * block_pages + place]
            first = pl.multiple_of(place * page_len + rows * group_index, 32)
            for kind in range(2):
                pltpu.make_async_copy(
                    pair[kind].at[pl.ds(first, rows), :], out_ref.at[slot, kind], sem
                ).start()
    sent = out_ref.at[pl.ds(0, count)]
    pltpu.make_async_copy(sent, sent, sem).wait()


def pick_new(page_table, blk_count, cap, pages, rows, keys, values):
    window = page_table.shape[1] // 2
    return pl.pallas_call(
        lambda *refs: pick_new_kernel(pages, *refs),
        out_shape=jax.ShapeDtypeStruct((blk_count * cap, 2, rows, keys[0].shape[1]), jnp.bfloat16),
        in_specs=[smem_spec] + [hbm_spec] * 8,
        out_specs=vmem_spec,
        scratch_shapes=[
            pltpu.SMEM((window,), jnp.int32),
            pltpu.SMEM((blk_count,), jnp.int32),
            pltpu.SemaphoreType.DMA,
        ],
        compiler_params=params(small_limit),
        name="pick_new",
    )(page_table, *in_hbm(*keys, *values))


def lane_fold(values, combine):
    total = values[:, :128]
    for start in range(128, values.shape[1], 128):
        total = combine(total, values[:, start : start + 128])
    return total


def old_bias(rows, pair):
    row = lax.broadcasted_iota(jnp.int32, (rows, 256), 0)
    column = lax.broadcasted_iota(jnp.int32, (rows, 256), 1)
    return jnp.where(column + (column // 64) * 64 + 64 * pair > row, 0.0, masked_score)


def fetch_page(slot, row, sources, low, kv_ref, sem):
    for number, source in enumerate(sources):
        place = pl.multiple_of(row + 32 * (low ^ number), 32)
        pltpu.make_async_copy(source.at[slot], kv_ref.at[:, pl.ds(place, 32), :], sem).start()


def wait_rows(kv_ref, steps, most, sem):
    for n in range(1, most + 1):

        @pl.when(steps == n)
        def _(n=n):
            filled = kv_ref.at[:, pl.ds(0, n * step_keys), :]
            pltpu.make_async_copy(filled, filled, sem).wait()


def attention(heads, steps, roped_ref, kv_ref, bias_ref, s_refs, most_refs, top_ref, sum_ref, acc_ref, begin, finish):
    last_bias = bias_ref.shape[0] - 1

    def scores(h, c, which):
        keys = kv_ref[0, pl.ds(pl.multiple_of(c * step_keys, step_keys), step_keys), :]
        result = lax.dot_general(
            roped_ref[h], keys, (((1,), (1,)), ((), ())), preferred_element_type=jnp.float32
        )
        result = result + bias_ref[jnp.minimum(c, last_bias)]
        s_refs[which][c] = result
        most_refs[which][...] = jnp.maximum(most_refs[which][...], lane_fold(result, jnp.maximum))

    def weigh(c, which):
        top = top_ref[...]
        weights = jnp.exp(s_refs[which][c] - join([top] * (step_keys // 128)))
        sum_ref[...] += lane_fold(weights, jnp.add)
        values = kv_ref[1, pl.ds(pl.multiple_of(c * step_keys, step_keys), step_keys), :]
        acc_ref[...] += jnp.dot(
            weights.astype(jnp.bfloat16), values, preferred_element_type=jnp.float32
        )

    def settle(which):
        top_ref[...] = jnp.broadcast_to(
            jnp.max(most_refs[which][...], axis=1, keepdims=True), top_ref.shape
        )
        sum_ref[...] = jnp.zeros_like(sum_ref)
        acc_ref[...] = jnp.zeros_like(acc_ref)

    def loop(work):
        def step(c, carry):
            work(c)
            return carry

        lax.fori_loop(0, steps, step, 0)

    begin(0, most_refs[0])
    loop(lambda c: scores(0, c, 0))

    def two(i, carry):
        h = i * 2
        begin(h + 1, most_refs[1])
        settle(0)

        def first_work(c):
            weigh(c, 0)
            scores(h + 1, c, 1)

        loop(first_work)
        finish(h)
        settle(1)

        @pl.when(h + 2 < heads)
        def _():
            begin(h + 2, most_refs[0])

            def second_work(c):
                weigh(c, 1)
                scores(h + 2, c, 0)

            loop(second_work)

        @pl.when(h + 2 >= heads)
        def _():
            loop(lambda c: weigh(c, 1))

        finish(h + 1)
        return carry

    lax.fori_loop(0, heads // 2, two, 0)


def first_kernel(
    pages, cap, table_ref, lengths_ref, query_ref, cos_ref, sin_ref,
    key_0, key_1, key_2, key_3, value_0, value_1, value_2, value_3, old_own_ref, old_core_ref,
    roped_out, acc_out, stat_out,
    q_ref, roped_ref, acc_ref, stat_ref, kv_ref, s_0, s_1, most_0, most_1, top_ref, sum_ref, head_ref,
    bias_ref, slots_ref, counts_ref, query_sem, sem, out_sem,
):
    group_index = lax.axis_index("group")
    has_old = lengths_ref[lax.axis_index("blk")] > 0
    heads, rows = roped_ref.shape[:2]
    block_pages = slots_ref.shape[0] // 4
    even = 1 - group_index % 2
    query_copy = pltpu.make_async_copy(query_ref, q_ref, query_sem)
    query_copy.start()
    steps = jnp.where(has_old, 3 + group_index // 2, group_index + 1)

    for number, refs in enumerate(((key_0, key_1, key_2, key_3), (value_0, value_1, value_2, value_3))):
        target = kv_ref.at[number]
        pltpu.make_async_copy(refs[0], target.at[pl.ds(0, rows), :], sem).start()
        for other in range(1, 4):
            block = group_index ^ other

            @pl.when(block < group_index)
            def _(block=block, other=other, refs=refs, target=target):
                start = rows + jnp.where(has_old, 256 * even, 0) + rows * block
                pltpu.make_async_copy(
                    refs[other], target.at[pl.ds(pl.multiple_of(start, 256), rows), :], sem
                ).start()

    @pl.when(has_old)
    def _():
        find_slots(table_ref, 0, 4 * block_pages, cap, pages, slots_ref, counts_ref)
        later = rows + 256 * even + rows * group_index

        def page(j, carry):
            block = j // block_pages
            row = jnp.where(block == group_index, rows, later + 256 * (block - group_index - 1))
            row = row + 64 * (j % block_pages)

            @pl.when((block > group_index) | ((block == group_index) & (even == 1)))
            def _():
                fetch_page(slots_ref[j], row, (old_own_ref, old_core_ref), group_index % 2, kv_ref, sem)

            return carry

        lax.fori_loop(0, 4 * block_pages, page, 0)

    row = lax.broadcasted_iota(jnp.int32, (rows, step_keys), 0)
    column = lax.broadcasted_iota(jnp.int32, (rows, step_keys), 1)
    bias_ref[0] = jnp.where(column <= row, 0.0, masked_score)
    bias_ref[1] = jnp.zeros((rows, step_keys), jnp.float32)
    bias_ref[2] = jnp.zeros((rows, step_keys), jnp.float32)

    @pl.when(has_old & (even == 1))
    def _():
        bias_ref[1, :, :256] = old_bias(rows, group_index // 2)

    query_copy.wait()

    def rope(h, carry):
        raw = q_ref[:, pl.ds(pl.multiple_of(h * 256, 256), 256)]
        front = turn(raw, cos_ref[...], sin_ref[...])
        roped_ref[h, :, :128] = (front * 0.0625).astype(jnp.bfloat16)
        roped_ref[h, :, 128:] = raw[:, 128:] * jnp.bfloat16(0.0625)
        return carry

    lax.fori_loop(0, heads, rope, 0)
    roped_copy = pltpu.make_async_copy(roped_ref, roped_out, query_sem)
    roped_copy.start()
    wait_rows(kv_ref, steps, 4, sem)

    def begin(h, most_ref):
        most_ref[...] = jnp.full_like(most_ref, masked_score)

    def finish(h):
        lane = lax.broadcasted_iota(jnp.int32, (rows, 128), 1)
        sums = jnp.sum(sum_ref[...], axis=1, keepdims=True)
        stat_ref[h] = jnp.where(lane < 64, top_ref[...], sums)
        acc_ref[h] = head_ref[...]
        pltpu.make_async_copy(acc_ref.at[h], acc_out.at[h], out_sem).start()
        pltpu.make_async_copy(stat_ref.at[h], stat_out.at[h], out_sem).start()

    attention(
        heads, steps, roped_ref, kv_ref, bias_ref, (s_0, s_1), (most_0, most_1), top_ref, sum_ref,
        head_ref, begin, finish,
    )
    roped_copy.wait()
    pltpu.make_async_copy(acc_ref, acc_out, out_sem).wait()
    pltpu.make_async_copy(stat_ref, stat_out, out_sem).wait()


def working(rows, steps, biases):
    return [
        pltpu.VMEM((steps, rows, step_keys), jnp.float32),
        pltpu.VMEM((steps, rows, step_keys), jnp.float32),
        pltpu.VMEM((rows, 128), jnp.float32),
        pltpu.VMEM((rows, 128), jnp.float32),
        pltpu.VMEM((rows, 128), jnp.float32),
        pltpu.VMEM((rows, 128), jnp.float32),
        pltpu.VMEM((rows, 256), jnp.float32),
        pltpu.VMEM((biases, rows, step_keys), jnp.float32),
    ]


def first_part(page_table, lengths, blk_count, cap, pages, queries, cosine, sine, keys, values, old_own, old_core):
    rows, width = queries.shape
    heads = width // 256
    return pl.pallas_call(
        lambda *refs: first_kernel(pages, cap, *refs),
        out_shape=(
            pltpu.HBM((heads, rows, 256), jnp.bfloat16),
            pltpu.HBM((heads, rows, 256), jnp.float32),
            pltpu.HBM((heads, rows, 128), jnp.float32),
        ),
        in_specs=[smem_spec, smem_spec, hbm_spec, vmem_spec, vmem_spec] + [hbm_spec] * 10,
        out_specs=(hbm_spec,) * 3,
        scratch_shapes=[
            pltpu.VMEM((rows, width), jnp.bfloat16),
            pltpu.VMEM((heads, rows, 256), jnp.bfloat16),
            pltpu.VMEM((heads, rows, 256), jnp.float32),
            pltpu.VMEM((heads, rows, 128), jnp.float32),
            pltpu.VMEM((2, 4 * step_keys, 256), jnp.bfloat16),
        ]
        + working(rows, 4, 3)
        + [
            pltpu.SMEM((page_table.shape[1] // 2,), jnp.int32),
            pltpu.SMEM((blk_count,), jnp.int32),
            pltpu.SemaphoreType.DMA,
            pltpu.SemaphoreType.DMA,
            pltpu.SemaphoreType.DMA,
        ],
        compiler_params=params(large_limit),
        name="attend_first",
    )(page_table, lengths, *in_hbm(queries), cosine, sine, *in_hbm(*keys, *values, old_own, old_core))


def second_kernel(
    cap, table_ref, lengths_ref, roped_in, acc_in, stat_in, own_ref, core_ref, far_ref, far_core_ref,
    weight_ref, arrived_ref, key_ref, value_ref, hidden_ref, key_out_ref, value_out_ref,
    roped_ref, acc_ref, stat_ref, kv_ref, s_0, s_1, most_0, most_1, top_ref, sum_ref, head_ref,
    bias_ref, attended_ref, w_ref, stage_ref, key_pool, value_pool, slots_ref, counts_ref,
    state_sems, sem, weight_sem, pool_sems, page_sem, out_sems,
):
    group_index = lax.axis_index("group")
    blk_index = lax.axis_index("blk")
    has_old = lengths_ref[blk_index] > 0
    pages = key_ref.shape[0]
    requests, slots = table_ref.shape
    heads, rows = roped_ref.shape[:2]
    block_pages = slots // 8
    chunks = stage_ref.shape[0]
    chunk = stage_ref.shape[2]
    odd = group_index % 2
    steps = jnp.where(has_old, 2 - group_index // 2, 0)

    @pl.when(has_old)
    def _():
        find_slots(table_ref, 0, slots // 2, cap, pages, slots_ref, counts_ref)

        def page(j, carry):
            block = j // block_pages
            row = jnp.where(block == group_index, 0, 256 * (odd + block - group_index))
            row = row + 64 * (j % block_pages)

            @pl.when(block >= group_index)
            def _():
                fetch_page(slots_ref[j], row, (far_ref, far_core_ref), odd, kv_ref, sem)

            @pl.when((block == group_index) & (odd == 1))
            def _():
                fetch_page(slots_ref[j], row + 256, (own_ref, core_ref), odd, kv_ref, sem)

            return carry

        lax.fori_loop(0, slots // 2, page, 0)

    def state_copies(h):
        return [
            pltpu.make_async_copy(source.at[h], target.at[h], state_sems.at[number, h])
            for number, (source, target) in enumerate(
                ((roped_in, roped_ref), (stat_in, stat_ref), (acc_in, acc_ref))
            )
        ]

    pool_loads = [
        pltpu.make_async_copy(key_ref, key_pool, pool_sems.at[0]),
        pltpu.make_async_copy(value_ref, value_pool, pool_sems.at[1]),
    ]
    pool_stores = [
        pltpu.make_async_copy(key_pool, key_out_ref, pool_sems.at[0]),
        pltpu.make_async_copy(value_pool, value_out_ref, pool_sems.at[1]),
    ]
    for h in range(2):
        for copy in state_copies(h):
            copy.start()
    for copy in pool_loads:
        copy.start()
    for h in range(2, heads):
        for copy in state_copies(h):
            copy.start()
    weight_copy = pltpu.make_async_copy(weight_ref, w_ref, weight_sem)
    weight_copy.start()

    bias_ref[...] = jnp.zeros_like(bias_ref)
    bias_ref[0, :, :256] = old_bias(rows, 1 - group_index // 2)

    @pl.when(odd == 1)
    def _():
        bias_ref[0, :, 256:] = old_bias(rows, group_index // 2)

    for copy in pool_loads:
        copy.wait()
    low = blk_index * pages

    def place(r, placed):
        rank = jnp.int32(0)
        for j in range(slots // 2, slots):
            page = table_ref[r, j] - low
            inside = (page >= 0) & (page < pages)

            @pl.when(inside)
            def _(page=page, rank=rank):
                slot = r * cap + rank
                pltpu.make_async_copy(arrived_ref.at[slot, 0], key_pool.at[page], page_sem).start()
                pltpu.make_async_copy(arrived_ref.at[slot, 1], value_pool.at[page], page_sem).start()

            rank = rank + inside.astype(jnp.int32)
        return placed + rank

    placed = lax.fori_loop(0, requests, place, jnp.int32(0))
    wait_rows(kv_ref, steps, 2, sem)
    lane = lax.broadcasted_iota(jnp.int32, (rows, 128), 1)

    def begin(h, most_ref):
        for copy in state_copies(h):
            copy.wait()
        most_ref[...] = jnp.where(lane < 64, stat_ref[h], masked_score)

    def finish(h):
        stat = stat_ref[h]
        top = top_ref[...]
        factor = jnp.exp(stat[:, :1] - top)
        sums = stat[:, 64:65] * factor + jnp.sum(sum_ref[...], axis=1, keepdims=True)
        inverse = 1.0 / sums
        old = factor * inverse
        mixed = acc_ref[h] * join([old, old]) + head_ref[...] * join([inverse, inverse])
        attended_ref[:, pl.ds(pl.multiple_of(h * 256, 256), 256)] = mixed.astype(jnp.bfloat16)

    attention(
        heads, steps, roped_ref, kv_ref, bias_ref, (s_0, s_1), (most_0, most_1), top_ref, sum_ref,
        head_ref, begin, finish,
    )

    def settle(n, carry):
        pltpu.make_async_copy(arrived_ref.at[0, 0], key_pool.at[0], page_sem).wait()
        pltpu.make_async_copy(arrived_ref.at[0, 1], value_pool.at[0], page_sem).wait()
        return carry

    lax.fori_loop(0, placed, settle, 0)
    for copy in pool_stores:
        copy.start()
    weight_copy.wait()

    def project(n, carry):
        columns = pl.ds(pl.multiple_of(n * chunk, chunk), chunk)
        stage_ref[n] = jnp.dot(
            attended_ref[...], w_ref[:, columns], preferred_element_type=jnp.float32
        ).astype(jnp.bfloat16)
        pltpu.make_async_copy(stage_ref.at[n], hidden_ref.at[:, columns], out_sems.at[n]).start()
        return carry

    lax.fori_loop(0, chunks, project, 0)
    for n in range(chunks):
        pltpu.make_async_copy(
            stage_ref.at[n], hidden_ref.at[:, pl.ds(n * chunk, chunk)], out_sems.at[n]
        ).wait()
    for copy in pool_stores:
        copy.wait()


def second_part(page_table, lengths, blk_count, cap, state, olds, weight, arrived, key_cache, value_cache):
    heads, rows, _ = state[0].shape
    width = weight.shape[1]
    chunk = 256
    return pl.pallas_call(
        lambda *refs: second_kernel(cap, *refs),
        out_shape=(
            pltpu.HBM((rows, width), jnp.bfloat16),
            pltpu.HBM(key_cache.shape, jnp.bfloat16),
            pltpu.HBM(value_cache.shape, jnp.bfloat16),
        ),
        in_specs=[smem_spec] * 2 + [hbm_spec] * 11,
        out_specs=(hbm_spec,) * 3,
        scratch_shapes=[
            pltpu.VMEM((heads, rows, 256), jnp.bfloat16),
            pltpu.VMEM((heads, rows, 256), jnp.float32),
            pltpu.VMEM((heads, rows, 128), jnp.float32),
            pltpu.VMEM((2, 2 * step_keys, 256), jnp.bfloat16),
        ]
        + working(rows, 2, 2)
        + [
            pltpu.VMEM((rows, weight.shape[0]), jnp.bfloat16),
            pltpu.VMEM(weight.shape, jnp.bfloat16),
            pltpu.VMEM((width // chunk, rows, chunk), jnp.bfloat16),
            pltpu.VMEM(key_cache.shape, jnp.bfloat16),
            pltpu.VMEM(value_cache.shape, jnp.bfloat16),
            pltpu.SMEM((page_table.shape[1] // 2,), jnp.int32),
            pltpu.SMEM((blk_count,), jnp.int32),
            pltpu.SemaphoreType.DMA((3, heads)),
            pltpu.SemaphoreType.DMA,
            pltpu.SemaphoreType.DMA,
            pltpu.SemaphoreType.DMA((2,)),
            pltpu.SemaphoreType.DMA,
            pltpu.SemaphoreType.DMA((width // chunk,)),
        ],
        compiler_params=params(large_limit),
        name="attend_second",
    )(page_table, lengths, *in_hbm(*state, *olds, weight, arrived, key_cache, value_cache))


def body(queries, new_keys, new_values, key_cache, value_cache, out_weight, lengths, page_table):
    blk_count = lax.axis_size("blk")
    pages_here, page_rows, _ = key_cache.shape
    window_pages = page_table.shape[1] // 2
    cap = (window_pages + blk_count - 1) // blk_count

    swap_core = [(0, 1), (1, 0), (2, 3), (3, 2)]
    swap_chip = [(0, 2), (2, 0), (1, 3), (3, 1)]

    def swap(value, pairs):
        return lax.ppermute(value, "group", pairs)

    value_own = new_values[0]
    value_far = swap(value_own, swap_chip)
    key_own, cosine, sine = rotate_keys(lengths, new_keys[0])
    key_far = swap(key_own, swap_chip)

    table, _ = lax.optimization_barrier((page_table, key_own))
    old_out = pick_old(table, cap, key_cache, value_cache)
    old_own = lax.all_to_all(old_out, "blk", split_axis=0, concat_axis=0, tiled=True)
    old_own = old_own.reshape((blk_count * cap,) + old_own.shape[2:])
    old_far = swap(old_own, swap_chip)
    old_core = swap(old_own, swap_core)

    value_core = swap(value_own, swap_core)
    key_core = swap(key_own, swap_core)
    value_far_core = swap(value_far, swap_core)
    key_far_core = swap(key_far, swap_core)
    keys = (key_own, key_core, key_far, key_far_core)
    values = (value_own, value_core, value_far, value_far_core)

    new_out = pick_new(page_table, blk_count, cap, pages_here, page_rows, keys, values)
    arrived = lax.all_to_all(new_out, "blk", split_axis=0, concat_axis=0, tiled=True)

    state = first_part(
        page_table, lengths, blk_count, cap, pages_here, queries[0], cosine, sine, keys, values,
        old_own, old_core,
    )
    old_far_core = swap(old_far, swap_core)
    hidden, key_out, value_out = second_part(
        page_table, lengths, blk_count, cap, state, (old_own, old_core, old_far, old_far_core),
        out_weight, arrived, key_cache, value_cache,
    )
    return (hidden[None], key_out, value_out)


def solution(mesh):
    return jax.shard_map(
        body,
        mesh=mesh,
        in_specs=(
            P("blk", "group", None),
            P("blk", "group", None),
            P("blk", "group", None),
            P("blk", "group", None),
            P("blk", "group", None),
            P(),
            P(),
            P(),
        ),
        out_specs=(P("blk", "group", None), P("blk", "group", None), P("blk", "group", None)),
        check_vma=False,
    )
```

profile of v0, /device:TPU:0, one launch (start us, length us, event | category | flops | bytes accessed | tf_op | source)
XLA Modules:
  0.0 98.9 jit_solution(3181605110440873336)
XLA Ops:
  0.6 0.0 copy-start.3
  0.6 0.9 copy-done.3
  1.6 0.0 copy-start.6
  1.6 0.7 copy-done.6
  2.2 0.7 copy-done.7
  2.9 0.0 copy-start.5
  2.9 1.7 %rotate_keys.1 = (bf16[512,256]{1,0:T(8,128)(2,1)S(1)}, f32[512,128]{1,0:T(8,128)S(1)}, f32[512,128]{1,0:T(8,128)S(1)}) custom-call(s32[8]{0:T(128)S(1)} %copy-done.6, f32[1,128]{1,0:T(1,128)S(1)} %copy-done.7, bf16[512,256]{1,0:T(8,128)(2,1)S(1)} %bitcast.5), custom_call_target="tpu_custom_call" | custom-call | tf_op jit(solution)/shard_map/rotate_keys/pallas_call | solution.py:57
  4.6 0.0 copy-start.1
  4.6 0.7 copy-done.1
  5.3 0.0 copy-start.2
  5.3 0.7 copy-done.2
  6.0 0.0 copy-start
  6.0 0.0 copy-start.4
  6.0 0.7 copy-done.4
  6.7 0.0 copy-start.11
  6.7 2.8 %pick_old.1 = bf16[8,2,2,32,256]{4,3,2,1,0:T(8,128)(2,1)} custom-call(s32[8,32]{1,0:T(8,128)S(1)} %copy-done.4, bf16[40,32,256]{2,1,0:T(8,128)(2,1)} %refs_11_.1, bf16[40,32,256]{2,1,0:T(8,128)(2,1)} %refs_12_.1), custom_call_target="tpu_custom_call" | custom-call | tf_op jit(solution)/shard_map/pick_old/pallas_call | solution.py:88
  9.4 7.3 %all-to-all-start = ((bf16[8,2,2,32,256]{4,3,2,1,0:T(8,128)(2,1)}), bf16[8,2,2,32,256]{4,3,2,1,0:T(8,128)(2,1)S(1)}, u32[]{:S(2)}, u32[]{:S(2)}) async-start(bf16[8,2,2,32,256]{4,3,2,1,0:T(8,128)(2,1)} %pick_old.1), calls=%async_computation | async-start | bytes 1048576 | tf_op jit(solution)/shard_map/all_to_all | solution.py:599
  16.7 0.0 copy-done.11
  16.7 1.6 %collective-permute-start.4 = (bf16[512,256]{1,0:T(8,128)(2,1)S(1)}, bf16[512,256]{1,0:T(8,128)(2,1)S(1)}, u32[]{:S(2)}, u32[]{:S(2)}) collective-permute-start(bf16[512,256]{1,0:T(8,128)(2,1)S(1)} %bitcast.13), channel_id=1, source_target_pairs={{0,2},{2,0},{1,3},{3,1},{4,6},{6,4},{5,7},{7,5},{8,10},{10,8},{9,1... | collective-permute-start | bytes 786440 | tf_op jit(solution)/shard_map/ppermute | solution.py:590
  18.3 0.5 collective-permute-start.1
  18.8 0.0 collective-permute-start.3
  18.8 0.5 collective-permute-start
  19.3 6.7 %collective-permute-done.4.refs_11_.refs_7_ = bf16[512,256]{1,0:T(8,128)(2,1)S(1)} collective-permute-done((bf16[512,256]{1,0:T(8,128)(2,1)S(1)}, bf16[512,256]{1,0:T(8,128)(2,1)S(1)}, u32[]{:S(2)}, u32[]{:S(2)}) %collective-permute-start.4) | collective-permute-done | bytes 262176 | tf_op jit(solution)/shard_map/ppermute | solution.py:590
  26.0 0.0 copy-start.12
  26.0 0.0 collective-permute-start.5
  26.0 4.1 %collective-permute-done.1.refs_7_.refs_3_ = bf16[512,256]{1,0:T(8,128)(2,1)S(1)} collective-permute-done((bf16[512,256]{1,0:T(8,128)(2,1)S(1)}, bf16[512,256]{1,0:T(8,128)(2,1)S(1)}, u32[]{:S(2)}, u32[]{:S(2)}) %collective-permute-start.1) | collective-permute-done | bytes 262176 | tf_op jit(solution)/shard_map/ppermute | solution.py:590
  30.1 0.0 copy-start.13
  30.1 0.0 collective-permute-start.2
  30.2 1.0 %all-to-all-done = bf16[8,2,2,32,256]{4,3,2,1,0:T(8,128)(2,1)S(1)} async-done(((bf16[8,2,2,32,256]{4,3,2,1,0:T(8,128)(2,1)}), bf16[8,2,2,32,256]{4,3,2,1,0:T(8,128)(2,1)S(1)}, u32[]{:S(2)}, u32[]{:S(2)}) %all-to-all-start) | async-done | bytes 524320 | tf_op jit(solution)/shard_map/all_to_all | solution.py:599
  31.2 0.0 copy-start.8
  31.2 1.5 %collective-permute-start.7 = (bf16[16,2,32,256]{3,2,1,0:T(8,128)(2,1)S(1)}, bf16[16,2,32,256]{3,2,1,0:T(8,128)(2,1)}, u32[]{:S(2)}, u32[]{:S(2)}) collective-permute-start(bf16[16,2,32,256]{3,2,1,0:T(8,128)(2,1)S(1)} %bitcast.6), channel_id=1, source_target_pairs={{0,2},{2,0},{1,3},{3,1},{4,6},{6,4},{5,7},{7,5},{8,10},{10,8},{9,1... | collective-permute-start | bytes 1572872 | tf_op jit(solution)/shard_map/ppermute | solution.py:590
  32.7 0.0 collective-permute-done.3.refs_10_.refs_6_
  32.7 0.0 copy-start.14
  32.7 0.0 collective-permute-done.refs_6_.refs_2_
  32.7 0.0 copy-start.15
  32.7 0.0 collective-permute-done.5.refs_12_.refs_8_
  32.7 0.0 copy-start.16
  32.7 0.0 collective-permute-done.2.refs_8_.refs_4_
  32.8 0.0 copy-done
  32.8 0.0 copy-done.12
  32.8 0.0 copy-done.13
  32.8 0.6 copy-done.14
  33.4 0.1 copy-done.15
  33.5 0.1 copy-done.16
  33.6 0.0 copy-start.17
  33.6 0.7 copy-done.17
  34.3 0.0 copy-done.5
  34.3 2.5 %pick_new.1 = bf16[16,2,32,256]{3,2,1,0:T(8,128)(2,1)} custom-call(s32[8,32]{1,0:T(8,128)S(1)} %copy-done.5, bf16[512,256]{1,0:T(8,128)(2,1)} %copy-done, bf16[512,256]{1,0:T(8,128)(2,1)} %copy-done.15, bf16[512,256]{1,0:T(8,128)(2,1)} %copy-done.13, bf16[512,256]{1,0:T(8,128)(2,1)} %copy-done.17, bf16[512,256]{1,0:T(8,128)(2,1)} %bitcast.11, ...), custom_call_target="tpu_custom_call" | custom-call | tf_op jit(solution)/shard_map/pick_new/pallas_call | solution.py:146
  36.8 4.7 %all-to-all-start.1 = ((bf16[16,2,32,256]{3,2,1,0:T(8,128)(2,1)}), bf16[16,2,32,256]{3,2,1,0:T(8,128)(2,1)S(1)}, u32[]{:S(2)}, u32[]{:S(2)}) async-start(bf16[16,2,32,256]{3,2,1,0:T(8,128)(2,1)} %pick_new.1), calls=%async_computation.1 | async-start | bytes 1048576 | tf_op jit(solution)/shard_map/all_to_all | solution.py:612
  41.5 0.0 collective-permute-start.6
  41.5 3.1 %collective-permute-done.7.refs_7_ = bf16[16,2,32,256]{3,2,1,0:T(8,128)(2,1)} collective-permute-done((bf16[16,2,32,256]{3,2,1,0:T(8,128)(2,1)S(1)}, bf16[16,2,32,256]{3,2,1,0:T(8,128)(2,1)}, u32[]{:S(2)}, u32[]{:S(2)}) %collective-permute-start.7) | collective-permute-done | bytes 524320 | tf_op jit(solution)/shard_map/ppermute | solution.py:590
  44.6 0.0 collective-permute-start.8
  44.6 0.0 collective-permute-done.6.refs_14_.refs_6_
  44.6 0.0 copy-start.9
  44.6 0.0 copy-done.8
  44.6 0.8 copy-done.9
  45.4 22.2 %attend_first.1 = (bf16[10,512,256]{2,1,0:T(8,128)(2,1)}, f32[10,512,256]{2,1,0:T(8,128)}, f32[10,512,128]{2,1,0:T(8,128)}) custom-call(s32[8,32]{1,0:T(8,128)} %refs_0_.5, s32[8]{0:T(128)} %refs_1_.3, bf16[512,2560]{1,0:T(8,128)(2,1)} %bitcast.10, f32[512,128]{1,0:T(8,128)} %copy-done.1, f32[512,128]{1,0:T(8,128)} %copy-done.2, bf16[512,256]{1,0:T(8,128)(2,1)} %copy-done, ...), custom_call_target="tpu_custom_call" | custom-call | tf_op jit(solution)/shard_map/attend_first/pallas_call | solution.py:367
  67.6 0.0 all-to-all-done.1.refs_10_
  67.6 0.0 copy-start.10
  67.6 0.0 collective-permute-done.8.refs_8_
  67.6 0.0 copy-start.18
  67.6 0.8 copy-done.10
  68.4 0.2 copy-done.18
  68.6 30.3 %attend_second.1 = (bf16[512,2560]{1,0:T(8,128)(2,1)}, bf16[40,32,256]{2,1,0:T(8,128)(2,1)}, bf16[40,32,256]{2,1,0:T(8,128)(2,1)}) custom-call(s32[8,32]{1,0:T(8,128)} %refs_0_.5, s32[8]{0:T(128)} %refs_1_.3, bf16[10,512,256]{2,1,0:T(8,128)(2,1)} %get-tuple-element.17.refs_2_, f32[10,512,256]{2,1,0:T(8,128)} %get-tuple-element.18.refs_3_, ...), custom_call_target="tpu_custom_call" | custom-call | tf_op jit(solution)/shard_map/attend_second/pallas_call | solution.py:544
  (1 shorter events, 0.0 us)
Async XLA Ops:
  0.6 1.0 copy-start.3
  1.6 0.7 copy-start.6
  2.2 0.7 copy-start.7
  2.9 31.4 %copy-start.5 = (s32[8,32]{1,0:T(8,128)S(1)}, s32[8,32]{1,0:T(8,128)}, u32[]{:S(2)}) copy-start(s32[8,32]{1,0:T(8,128)} %refs_0_.5) | copy-start | bytes 3076
  4.6 0.7 copy-start.1
  5.3 0.7 copy-start.2
  6.0 26.8 %copy-start = (bf16[512,256]{1,0:T(8,128)(2,1)}, bf16[512,256]{1,0:T(8,128)(2,1)S(1)}, u32[]{:S(2)}) copy-start(bf16[512,256]{1,0:T(8,128)(2,1)S(1)} %get-tuple-element.15.refs_5_.refs_1_) | copy-start | bytes 786436
  6.0 0.7 copy-start.4
  6.7 10.0 %copy-start.11 = (bf16[1,512,256]{2,1,0:T(8,128)(2,1)S(1)}, bf16[1,512,256]{2,1,0:T(8,128)(2,1)}, u32[]{:S(2)}) copy-start(bf16[1,512,256]{2,1,0:T(8,128)(2,1)} %param.11) | copy-start | bytes 786436
  9.4 21.8 %all-to-all-start = ((bf16[8,2,2,32,256]{4,3,2,1,0:T(8,128)(2,1)}), bf16[8,2,2,32,256]{4,3,2,1,0:T(8,128)(2,1)S(1)}, u32[]{:S(2)}, u32[]{:S(2)}) async-start(bf16[8,2,2,32,256]{4,3,2,1,0:T(8,128)(2,1)} %pick_old.1), calls=%async_computation | async-start | bytes 1048576 | tf_op jit(solution)/shard_map/all_to_all | solution.py:599
  16.7 9.3 %collective-permute-start.4 = (bf16[512,256]{1,0:T(8,128)(2,1)S(1)}, bf16[512,256]{1,0:T(8,128)(2,1)S(1)}, u32[]{:S(2)}, u32[]{:S(2)}) collective-permute-start(bf16[512,256]{1,0:T(8,128)(2,1)S(1)} %bitcast.13), channel_id=1, source_target_pairs={{0,2},{2,0},{1,3},{3,1},{4,6},{6,4},{5,7},{7,5},{8,10},{10,8},{9,1... | collective-permute-start | bytes 786440 | tf_op jit(solution)/shard_map/ppermute | solution.py:590
  18.3 11.9 %collective-permute-start.1 = (bf16[512,256]{1,0:T(8,128)(2,1)S(1)}, bf16[512,256]{1,0:T(8,128)(2,1)S(1)}, u32[]{:S(2)}, u32[]{:S(2)}) collective-permute-start(bf16[512,256]{1,0:T(8,128)(2,1)S(1)} %get-tuple-element.15.refs_5_.refs_1_), channel_id=1, source_target_pairs={{0,2},{2,0},{1,3},{3,1},{4,6},{6,4},{5,7},{7,5},{8,10},{10,8},{9,1... | collective-permute-start | bytes 786440 | tf_op jit(solution)/shard_map/ppermute | solution.py:590
  18.8 13.9 %collective-permute-start.3 = (bf16[512,256]{1,0:T(8,128)(2,1)S(1)}, bf16[512,256]{1,0:T(8,128)(2,1)S(1)}, u32[]{:S(2)}, u32[]{:S(2)}) collective-permute-start(bf16[512,256]{1,0:T(8,128)(2,1)S(1)} %bitcast.14), channel_id=1, source_target_pairs={{0,1},{1,0},{2,3},{3,2},{4,5},{5,4},{6,7},{7,6},{8,9},{9,8},{10,11... | collective-permute-start | bytes 786440 | tf_op jit(solution)/shard_map/ppermute | solution.py:590
  18.8 13.9 %collective-permute-start = (bf16[512,256]{1,0:T(8,128)(2,1)S(1)}, bf16[512,256]{1,0:T(8,128)(2,1)S(1)}, u32[]{:S(2)}, u32[]{:S(2)}) collective-permute-start(bf16[512,256]{1,0:T(8,128)(2,1)S(1)} %get-tuple-element.15.refs_5_.refs_1_), channel_id=1, source_target_pairs={{0,1},{1,0},{2,3},{3,2},{4,5},{5,4},{6,7},{7,6},{8,9},{9,8},{10,11... | collective-permute-start | bytes 786440 | tf_op jit(solution)/shard_map/ppermute | solution.py:590
  26.0 6.8 %copy-start.12 = (bf16[512,256]{1,0:T(8,128)(2,1)}, bf16[512,256]{1,0:T(8,128)(2,1)S(1)}, u32[]{:S(2)}) copy-start(bf16[512,256]{1,0:T(8,128)(2,1)S(1)} %collective-permute-done.4.refs_11_.refs_7_) | copy-start | bytes 786436
  26.0 6.7 %collective-permute-start.5 = (bf16[512,256]{1,0:T(8,128)(2,1)S(1)}, bf16[512,256]{1,0:T(8,128)(2,1)S(1)}, u32[]{:S(2)}, u32[]{:S(2)}) collective-permute-start(bf16[512,256]{1,0:T(8,128)(2,1)S(1)} %collective-permute-done.4.refs_11_.refs_7_), channel_id=1, source_target_pairs={{0,1},{1,0},{2,3},{3,2},{4,5},{5,4},{6,7},{7,6},{8,9},{9,8},{10,11... | collective-permute-start | bytes 786440 | tf_op jit(solution)/shard_map/ppermute | solution.py:590
  30.1 2.6 %copy-start.13 = (bf16[512,256]{1,0:T(8,128)(2,1)}, bf16[512,256]{1,0:T(8,128)(2,1)S(1)}, u32[]{:S(2)}) copy-start(bf16[512,256]{1,0:T(8,128)(2,1)S(1)} %collective-permute-done.1.refs_7_.refs_3_) | copy-start | bytes 786436
  30.1 2.6 %collective-permute-start.2 = (bf16[512,256]{1,0:T(8,128)(2,1)S(1)}, bf16[512,256]{1,0:T(8,128)(2,1)S(1)}, u32[]{:S(2)}, u32[]{:S(2)}) collective-permute-start(bf16[512,256]{1,0:T(8,128)(2,1)S(1)} %collective-permute-done.1.refs_7_.refs_3_), channel_id=1, source_target_pairs={{0,1},{1,0},{2,3},{3,2},{4,5},{5,4},{6,7},{7,6},{8,9},{9,8},{10,11... | collective-permute-start | bytes 786440 | tf_op jit(solution)/shard_map/ppermute | solution.py:590
  31.2 13.4 %copy-start.8 = (bf16[8,2,2,32,256]{4,3,2,1,0:T(8,128)(2,1)}, bf16[8,2,2,32,256]{4,3,2,1,0:T(8,128)(2,1)S(1)}, u32[]{:S(2)}) copy-start(bf16[8,2,2,32,256]{4,3,2,1,0:T(8,128)(2,1)S(1)} %all-to-all-done) | copy-start | bytes 1572868
  31.2 13.4 %collective-permute-start.7 = (bf16[16,2,32,256]{3,2,1,0:T(8,128)(2,1)S(1)}, bf16[16,2,32,256]{3,2,1,0:T(8,128)(2,1)}, u32[]{:S(2)}, u32[]{:S(2)}) collective-permute-start(bf16[16,2,32,256]{3,2,1,0:T(8,128)(2,1)S(1)} %bitcast.6), channel_id=1, source_target_pairs={{0,2},{2,0},{1,3},{3,1},{4,6},{6,4},{5,7},{7,5},{8,10},{10,8},{9,1... | collective-permute-start | bytes 1572872 | tf_op jit(solution)/shard_map/ppermute | solution.py:590
  32.7 0.7 copy-start.14
  32.7 0.8 copy-start.15
  32.7 0.8 copy-start.16
  33.6 0.7 copy-start.17
  36.8 30.8 %all-to-all-start.1 = ((bf16[16,2,32,256]{3,2,1,0:T(8,128)(2,1)}), bf16[16,2,32,256]{3,2,1,0:T(8,128)(2,1)S(1)}, u32[]{:S(2)}, u32[]{:S(2)}) async-start(bf16[16,2,32,256]{3,2,1,0:T(8,128)(2,1)} %pick_new.1), calls=%async_computation.1 | async-start | bytes 1048576 | tf_op jit(solution)/shard_map/all_to_all | solution.py:612
  41.5 3.1 %collective-permute-start.6 = (bf16[16,2,32,256]{3,2,1,0:T(8,128)(2,1)S(1)}, bf16[16,2,32,256]{3,2,1,0:T(8,128)(2,1)S(1)}, u32[]{:S(2)}, u32[]{:S(2)}) collective-permute-start(bf16[16,2,32,256]{3,2,1,0:T(8,128)(2,1)S(1)} %bitcast.7), channel_id=1, source_target_pairs={{0,1},{1,0},{2,3},{3,2},{4,5},{5,4},{6,7},{7,6},{8,9},{9,8},{10,11... | collective-permute-start | bytes 1572872 | tf_op jit(solution)/shard_map/ppermute | solution.py:590
  44.6 23.0 %collective-permute-start.8 = (bf16[16,2,32,256]{3,2,1,0:T(8,128)(2,1)}, bf16[16,2,32,256]{3,2,1,0:T(8,128)(2,1)S(1)}, u32[]{:S(2)}, u32[]{:S(2)}) collective-permute-start(bf16[16,2,32,256]{3,2,1,0:T(8,128)(2,1)} %collective-permute-done.7.refs_7_), channel_id=1, source_target_pairs={{0,1},{1,0},{2,3},{3,2},{4,5},{5,4},{6,7},{7,6},{8,9},{9,8},{10,11... | collective-permute-start | bytes 1572872 | tf_op jit(solution)/shard_map/ppermute | solution.py:590
  44.6 0.8 copy-start.9
  67.6 0.8 copy-start.10
  67.6 1.0 %copy-start.18 = (bf16[16,2,32,256]{3,2,1,0:T(8,128)(2,1)}, bf16[16,2,32,256]{3,2,1,0:T(8,128)(2,1)S(1)}, u32[]{:S(2)}) copy-start(bf16[16,2,32,256]{3,2,1,0:T(8,128)(2,1)S(1)} %collective-permute-done.8.refs_8_) | copy-start | bytes 1572868
where the time goes:
time: 99.7 us; the launch traced here: 98.9 us
  Pallas kernels  59.4 us (60%)
  starting transfers between devices  16.1 us (16%)
  waiting for transfers between devices  15 us (15%)
  local copies, waits for them, and re-layouts  7.66 us (8%)
    pallas_call x1, Pallas kernels, second_part(): pl.pallas_call(lambda *refs: second_kernel(cap, *refs), out_shape=(pltpu....  30.3 us
    pallas_call x1, Pallas kernels, first_part(): pl.pallas_call(lambda *refs: first_kernel(pages, cap, *refs), out_shape=(...  22.2 us
    ppermute x9, waiting for transfers between devices, swap(): return lax.ppermute(value, 'group', pairs)  14 us
    unnamed x38, local copies, waits for them, and re-layouts  7.66 us
    all_to_all x1, starting transfers between devices, body(): lax.all_to_all(old_out, 'blk', split_axis=0, concat_axis=0, tiled=True)  7.26 us
    all_to_all x1, starting transfers between devices, body(): lax.all_to_all(new_out, 'blk', split_axis=0, concat_axis=0, tiled=True)  4.71 us
    ppermute x9, starting transfers between devices, swap(): return lax.ppermute(value, 'group', pairs)  4.13 us
    pallas_call x1, Pallas kernels, pick_old(): pl.pallas_call(pick_old_kernel, out_shape=jax.ShapeDtypeStruct((requests,...  2.75 us
  transfers between devices with their start and end apart: 11, of which 4 were waited for; matrix products, arithmetic and copies ran while one was open for 0% of the time, Pallas kernels for 25%

commit v1 on v0

v1 whole, which is shorter than its diff:
```python
import jax
import jax.numpy as jnp
import numpy as np
from jax import lax
from jax.experimental import pallas as pl
from jax.experimental.pallas import tpu as pltpu
from jax.sharding import PartitionSpec as P

masked_score = -1e30
step_keys = 512
step_slots = 16
hbm_spec = pl.BlockSpec(memory_space=pltpu.HBM)
smem_spec = pl.BlockSpec(memory_space=pltpu.SMEM)
vmem_spec = pl.BlockSpec(memory_space=pltpu.VMEM)
small_limit = 16 * 1024 * 1024
large_limit = 56 * 1024 * 1024


def params(limit):
    return pltpu.CompilerParams(vmem_limit_bytes=limit)


def in_hbm(*arrays):
    return [pltpu.with_memory_space_constraint(array, pltpu.HBM) for array in arrays]


def turn(values, cosine, sine):
    front = values[:, :128].astype(jnp.float32)
    return front * cosine + pltpu.roll(front, 64, 1) * sine


def join(pieces):
    return jnp.concatenate(pieces, axis=1)


def pages_here(table_ref, r, first, count, cap, pages):
    low = lax.axis_index("blk") * pages
    found = jnp.int32(0)
    chosen = [jnp.int32(0)] * cap
    for j in range(first, first + count):
        page = table_ref[r, j] - low
        inside = (page >= 0) & (page < pages)
        chosen = [jnp.where(inside & (found == c), page, chosen[c]) for c in range(cap)]
        found = found + inside.astype(jnp.int32)
    return chosen, found


def pick_old_kernel(table_ref, key_ref, value_ref, out_ref, sem):
    requests, cap = out_ref.shape[:2]
    for r in range(requests):
        chosen, _ = pages_here(table_ref, r, 0, table_ref.shape[1] // 2, cap, key_ref.shape[0])
        for c in range(cap):
            pltpu.make_async_copy(key_ref.at[chosen[c]], out_ref.at[r, c, 0], sem).start()
            pltpu.make_async_copy(value_ref.at[chosen[c]], out_ref.at[r, c, 1], sem).start()
    pltpu.make_async_copy(out_ref, out_ref, sem).wait()


def pick_old(page_table, cap, key_cache, value_cache):
    requests = page_table.shape[0]
    return pl.pallas_call(
        pick_old_kernel,
        out_shape=jax.ShapeDtypeStruct((requests, cap, 2) + key_cache.shape[1:], jnp.bfloat16),
        in_specs=[smem_spec, hbm_spec, hbm_spec],
        out_specs=vmem_spec,
        scratch_shapes=[pltpu.SemaphoreType.DMA],
        compiler_params=params(small_limit),
        name="pick_old",
    )(page_table, *in_hbm(key_cache, value_cache))


def owner_of(page, pages, owners):
    factor = (1 << 20) // pages + 1
    assert all((p * factor) >> 20 == p // pages for p in range(pages * owners))
    assert pages * owners * factor < 1 << 31
    return (page * factor) >> 20


def find_slots(table_ref, first, count, cap, pages, counts_ref):
    owners = counts_ref.shape[0]
    row = lax.axis_index("blk")
    for o in range(owners):
        counts_ref[o] = 0
    slots = []
    for j in range(count):
        owner = owner_of(table_ref[row, first + j], pages, owners)
        rank = counts_ref[owner]
        counts_ref[owner] = rank + 1
        slots.append(owner * cap + rank)
    return slots


def pack_kernel(
    pages, cap, table_ref, lengths_ref, freq_ref, keys_ref, values_ref, old_ref,
    both_ref, one_ref, two_ref, cos_ref, sin_ref, counts_ref, sem,
):
    rows = keys_ref.shape[0]
    slots = rows // 32
    for j, slot in enumerate(find_slots(table_ref, 0, slots, cap, pages, counts_ref)):
        pltpu.make_async_copy(old_ref.at[slot], both_ref.at[slots + j], sem).start()
    group_index = lax.axis_index("group")
    start = lengths_ref[lax.axis_index("blk")] + group_index * rows
    positions = start + lax.broadcasted_iota(jnp.int32, (rows, 128), 0)
    angles = positions.astype(jnp.float32) * freq_ref[...]
    lane = lax.broadcasted_iota(jnp.int32, (rows, 128), 1)
    cosine = jnp.cos(angles)
    sine = jnp.sin(angles)
    sine = jnp.where(lane < 64, -sine, sine)
    cos_ref[...] = cosine
    sin_ref[...] = sine
    keys = keys_ref[...]
    turned = join([turn(keys, cosine, sine).astype(jnp.bfloat16), keys[:, 128:]])
    both_ref[:slots, 0] = turned.reshape(slots, 32, 256)
    both_ref[:slots, 1] = values_ref[...].reshape(slots, 32, 256)
    sorted_ref = both_ref.at[pl.ds(slots, slots)]
    pltpu.make_async_copy(sorted_ref, sorted_ref, sem).wait()

    @pl.when(group_index < 2)
    def _():
        one_ref[...] = both_ref[:slots]
        two_ref[...] = both_ref[slots + slots // 2 :]

    @pl.when(group_index >= 2)
    def _():
        one_ref[...] = both_ref[slots:]
        for page in range(slots // 4):
            two_ref[2 * page : 2 * page + 2] = both_ref[4 * page : 4 * page + 2]


def pack(page_table, lengths, blk_count, cap, pages, keys, values, old):
    rows, head_dim = keys.shape
    slots = rows // 32
    quarter = head_dim // 4
    freq_table = np.float32(10000.0) ** (-np.arange(quarter, dtype=np.float32) / np.float32(quarter))
    freq_table = np.concatenate([freq_table, freq_table])[None].astype(np.float32)
    return pl.pallas_call(
        lambda *refs: pack_kernel(pages, cap, *refs),
        out_shape=(
            jax.ShapeDtypeStruct((2 * slots, 2, 32, head_dim), jnp.bfloat16),
            jax.ShapeDtypeStruct((slots, 2, 32, head_dim), jnp.bfloat16),
            jax.ShapeDtypeStruct((slots // 2, 2, 32, head_dim), jnp.bfloat16),
            jax.ShapeDtypeStruct((rows, 128), jnp.float32),
            jax.ShapeDtypeStruct((rows, 128), jnp.float32),
        ),
        in_specs=[smem_spec, smem_spec, vmem_spec, vmem_spec, vmem_spec, hbm_spec],
        out_specs=(vmem_spec,) * 5,
        scratch_shapes=[pltpu.SMEM((blk_count,), jnp.int32), pltpu.SemaphoreType.DMA],
        compiler_params=params(small_limit),
        name="pack",
    )(page_table, lengths, jnp.asarray(freq_table), keys, values, *in_hbm(old))


def rope_kernel(query_ref, cos_ref, sin_ref, out_ref):
    raw = query_ref[...]
    front = turn(raw, cos_ref[...], sin_ref[...])
    out_ref[0, :, :128] = (front * 0.0625).astype(jnp.bfloat16)
    out_ref[0, :, 128:] = raw[:, 128:] * jnp.bfloat16(0.0625)


def rotate_queries(queries, cosine, sine):
    rows, width = queries.shape
    heads = width // 256
    return pl.pallas_call(
        rope_kernel,
        out_shape=pltpu.HBM((heads, rows, 256), jnp.bfloat16),
        grid=(heads,),
        in_specs=[
            pl.BlockSpec((rows, 256), lambda h: (0, h)),
            pl.BlockSpec((rows, 128), lambda h: (0, 0)),
            pl.BlockSpec((rows, 128), lambda h: (0, 0)),
        ],
        out_specs=pl.BlockSpec((1, rows, 256), lambda h: (h, 0, 0)),
        compiler_params=params(small_limit),
        cost_estimate=pl.CostEstimate(flops=8 * rows * width, bytes_accessed=4 * rows * width, transcendentals=0),
        name="rotate_queries",
    )(queries, cosine, sine)


def pick_new_kernel(
    pages, cap, table_ref, both_ref, core_ref, one_ref, one_core_ref, two_ref, two_core_ref,
    out_ref, slots_ref, counts_ref, sem,
):
    count = slots_ref.shape[0]
    block_pages = count // 4
    group_index = lax.axis_index("group")
    for j, slot in enumerate(find_slots(table_ref, table_ref.shape[1] - count, count, cap, pages, counts_ref)):
        slots_ref[j] = slot

    def send(ref, block, stride):
        for place in range(block_pages):
            source = ref.at[stride * place + group_index]
            target = out_ref.at[slots_ref[block * block_pages + place]]
            pltpu.make_async_copy(source, target, sem).start()

    send(both_ref, group_index, 4)
    send(core_ref, group_index ^ 1, 4)

    @pl.when(group_index < 2)
    def _():
        send(two_ref, group_index ^ 2, 2)
        send(two_core_ref, group_index ^ 3, 2)

    @pl.when(group_index >= 2)
    def _():
        send(one_ref, group_index ^ 2, 4)
        send(one_core_ref, group_index ^ 3, 4)

    sent = out_ref.at[pl.ds(0, count)]
    pltpu.make_async_copy(sent, sent, sem).wait()


def pick_new(page_table, blk_count, cap, pages, sources):
    window = page_table.shape[1] // 2
    return pl.pallas_call(
        lambda *refs: pick_new_kernel(pages, cap, *refs),
        out_shape=jax.ShapeDtypeStruct((blk_count * cap,) + sources[0].shape[1:], jnp.bfloat16),
        in_specs=[smem_spec] + [hbm_spec] * 6,
        out_specs=vmem_spec,
        scratch_shapes=[
            pltpu.SMEM((window,), jnp.int32),
            pltpu.SMEM((blk_count,), jnp.int32),
            pltpu.SemaphoreType.DMA,
        ],
        compiler_params=params(small_limit),
        name="pick_new",
    )(page_table, *in_hbm(*sources))


def lane_fold(values, combine):
    total = values[:, :128]
    for start in range(128, values.shape[1], 128):
        total = combine(total, values[:, start : start + 128])
    return total


def old_bias(rows, quarter):
    row = lax.broadcasted_iota(jnp.int32, (rows, 256), 0)
    column = lax.broadcasted_iota(jnp.int32, (rows, 256), 1)
    held = quarter ^ (column // 128)
    position = ((column % 128) // 32) * 128 + 32 * held + column % 32
    return jnp.where(position > row, 0.0, masked_score)


def fetch(source, first, kv_ref, place, count, sem):
    for kind in range(2):
        pltpu.make_async_copy(
            source.at[pl.ds(first, count), kind], kv_ref.at[kind, pl.ds(place, count)], sem
        ).start()


def fetch_pair(sources, first, kv_ref, place, sem):
    fetch(sources[0], first, kv_ref, place, 4, sem)
    fetch(sources[1], first, kv_ref, place + 4, 4, sem)


def wait_rows(kv_ref, steps, most, sem):
    for n in range(1, most + 1):

        @pl.when(steps == n)
        def _(n=n):
            filled = kv_ref.at[:, pl.ds(0, n * step_slots)]
            pltpu.make_async_copy(filled, filled, sem).wait()


def attention(heads, steps, roped_ref, kv_ref, bias_ref, s_refs, most_refs, top_ref, sum_ref, acc_of, begin, finish):
    last_bias = bias_ref.shape[0] - 1
    rows = roped_ref.shape[1]
    parts = 2
    part_rows = rows // parts

    def block(kind, c):
        return kv_ref[kind, pl.ds(c * step_slots, step_slots)].reshape(step_keys, 256)

    def scores(h, c, which, part, keys):
        some = pl.ds(part * part_rows, part_rows)
        result = lax.dot_general(
            roped_ref[h, some, :], keys, (((1,), (1,)), ((), ())), preferred_element_type=jnp.float32
        )
        result = result + bias_ref[jnp.minimum(c, last_bias), some, :]
        s_refs[which][c, some, :] = result
        most_refs[which][some, :] = jnp.maximum(most_refs[which][some, :], lane_fold(result, jnp.maximum))

    def exponentials(c, which, part):
        some = pl.ds(part * part_rows, part_rows)
        weights = jnp.exp(s_refs[which][c, some, :] - join([top_ref[some, :]] * (step_keys // 128)))
        sum_ref[some, :] += lane_fold(weights, jnp.add)
        return weights.astype(jnp.bfloat16)

    def gather(h, part, weights, values):
        some = pl.ds(part * part_rows, part_rows)
        acc_of(h)[some, :] += jnp.dot(weights, values, preferred_element_type=jnp.float32)

    def settle(h, which):
        top_ref[...] = jnp.broadcast_to(
            jnp.max(most_refs[which][...], axis=1, keepdims=True), top_ref.shape
        )
        sum_ref[...] = jnp.zeros_like(sum_ref)
        acc = acc_of(h)
        acc[...] = jnp.zeros(acc.shape, jnp.float32)

    def loop(h, which, following):
        def step(c, carry):
            keys = block(0, c)
            values = block(1, c)
            weights = None
            for part in range(parts):
                if following:
                    scores(h + 1, c, 1 - which, part, keys)
                if weights is not None:
                    gather(h, part - 1, weights, values)
                weights = exponentials(c, which, part)
            gather(h, parts - 1, weights, values)
            return carry

        lax.fori_loop(0, steps, step, 0)

    def first_scores(c, carry):
        for part in range(parts):
            scores(0, c, 0, part, block(0, c))
        return carry

    begin(0, most_refs[0])
    lax.fori_loop(0, steps, first_scores, 0)

    def two(i, carry):
        h = i * 2
        begin(h + 1, most_refs[1])
        settle(h, 0)
        loop(h, 0, True)
        finish(h)
        settle(h + 1, 1)

        @pl.when(h + 2 < heads)
        def _():
            begin(h + 2, most_refs[0])
            loop(h + 1, 1, True)

        @pl.when(h + 2 >= heads)
        def _():
            loop(h + 1, 1, False)

        finish(h + 1)
        return carry

    lax.fori_loop(0, heads // 2, two, 0)


def first_kernel(
    lengths_ref, roped_in, both_ref, core_ref, acc_out, stat_out,
    roped_ref, acc_ref, stat_ref, kv_ref, s_0, s_1, most_0, most_1, top_ref, sum_ref,
    bias_ref, roped_sem, sem, out_sem,
):
    group_index = lax.axis_index("group")
    has_old = lengths_ref[lax.axis_index("blk")] > 0
    heads, rows = roped_ref.shape[:2]
    odd = group_index % 2
    roped_copy = pltpu.make_async_copy(roped_in, roped_ref, roped_sem)
    roped_copy.start()
    steps = jnp.where(has_old, 3 - group_index // 2, 1 + odd)
    fetch(both_ref, 0, kv_ref, 0, 16, sem)

    @pl.when(odd == 1)
    def _():
        fetch(core_ref, 0, kv_ref, 16, 16, sem)

    @pl.when(has_old)
    def _():
        for block in range(4):

            @pl.when((block == group_index) & (odd == 0))
            def _(block=block):
                fetch_pair((both_ref, core_ref), 16 + 4 * block, kv_ref, 16, sem)

            @pl.when(block > group_index)
            def _(block=block):
                place = 24 + 8 * odd + 8 * (block - 1 - group_index)
                fetch_pair((both_ref, core_ref), 16 + 4 * block, kv_ref, place, sem)

    row = lax.broadcasted_iota(jnp.int32, (rows, step_keys), 0)
    column = lax.broadcasted_iota(jnp.int32, (rows, step_keys), 1)
    bias_ref[0] = jnp.where(column <= row, 0.0, masked_score)
    bias_ref[1] = jnp.zeros((rows, step_keys), jnp.float32)
    bias_ref[2] = jnp.zeros((rows, step_keys), jnp.float32)

    @pl.when(has_old & (odd == 0))
    def _():
        bias_ref[1, :, :256] = old_bias(rows, group_index)

    roped_copy.wait()
    wait_rows(kv_ref, steps, 3, sem)

    def begin(h, most_ref):
        most_ref[...] = jnp.full_like(most_ref, masked_score)

    def finish(h):
        lane = lax.broadcasted_iota(jnp.int32, (rows, 128), 1)
        sums = jnp.sum(sum_ref[...], axis=1, keepdims=True)
        stat_ref[h] = jnp.where(lane < 64, top_ref[...], sums)
        pltpu.make_async_copy(acc_ref.at[h], acc_out.at[h], out_sem).start()
        pltpu.make_async_copy(stat_ref.at[h], stat_out.at[h], out_sem).start()

    attention(
        heads, steps, roped_ref, kv_ref, bias_ref, (s_0, s_1), (most_0, most_1), top_ref, sum_ref,
        lambda h: acc_ref.at[h], begin, finish,
    )
    pltpu.make_async_copy(acc_ref, acc_out, out_sem).wait()
    pltpu.make_async_copy(stat_ref, stat_out, out_sem).wait()


def working(rows, steps, biases):
    return [
        pltpu.VMEM((2, steps * step_slots, 32, 256), jnp.bfloat16),
        pltpu.VMEM((steps, rows, step_keys), jnp.float32),
        pltpu.VMEM((steps, rows, step_keys), jnp.float32),
        pltpu.VMEM((rows, 128), jnp.float32),
        pltpu.VMEM((rows, 128), jnp.float32),
        pltpu.VMEM((rows, 128), jnp.float32),
        pltpu.VMEM((rows, 128), jnp.float32),
        pltpu.VMEM((biases, rows, step_keys), jnp.float32),
    ]


def first_part(lengths, roped, both, core):
    heads, rows, _ = roped.shape
    return pl.pallas_call(
        first_kernel,
        out_shape=(
            pltpu.HBM((heads, rows, 256), jnp.float32),
            pltpu.HBM((heads, rows, 128), jnp.float32),
        ),
        in_specs=[smem_spec] + [hbm_spec] * 3,
        out_specs=(hbm_spec,) * 2,
        scratch_shapes=[
            pltpu.VMEM((heads, rows, 256), jnp.bfloat16),
            pltpu.VMEM((heads, rows, 256), jnp.float32),
            pltpu.VMEM((heads, rows, 128), jnp.float32),
        ]
        + working(rows, 3, 3)
        + [pltpu.SemaphoreType.DMA] * 3,
        compiler_params=params(large_limit),
        cost_estimate=pl.CostEstimate(
            flops=4 * heads * rows * 1536 * 256, bytes_accessed=1 << 24, transcendentals=heads * rows * 1536
        ),
        name="attend_first",
    )(lengths, *in_hbm(roped, both, core))


def second_kernel(
    cap, table_ref, lengths_ref, roped_in, acc_in, stat_in, both_ref, core_ref, one_ref, one_core_ref,
    two_ref, two_core_ref, weight_ref, arrived_ref, key_ref, value_ref,
    hidden_ref, key_out_ref, value_out_ref,
    roped_ref, acc_ref, stat_ref, kv_ref, s_0, s_1, most_0, most_1, top_ref, sum_ref,
    bias_ref, head_ref, attended_ref, w_ref, stage_ref, key_pool, value_pool,
    state_sems, sem, weight_sem, pool_sems, page_sem, out_sems,
):
    group_index = lax.axis_index("group")
    has_old = lengths_ref[lax.axis_index("blk")] > 0
    pages = key_ref.shape[0]
    requests, slots = table_ref.shape
    heads, rows = roped_ref.shape[:2]
    chunks = stage_ref.shape[0]
    chunk = stage_ref.shape[2]
    odd = group_index % 2
    chip = group_index // 2
    steps = 2 * chip + jnp.where(has_old, 2 - chip, 0)

    def state_copies(h):
        return [
            pltpu.make_async_copy(source.at[h], target.at[h], state_sems.at[number, h])
            for number, (source, target) in enumerate(
                ((roped_in, roped_ref), (stat_in, stat_ref), (acc_in, acc_ref))
            )
        ]

    pool_loads = [
        pltpu.make_async_copy(key_ref, key_pool, pool_sems.at[0]),
        pltpu.make_async_copy(value_ref, value_pool, pool_sems.at[1]),
    ]
    pool_stores = [
        pltpu.make_async_copy(key_pool, key_out_ref, pool_sems.at[0]),
        pltpu.make_async_copy(value_pool, value_out_ref, pool_sems.at[1]),
    ]
    for copy in pool_loads:
        copy.start()

    @pl.when(has_old)
    def _():
        for block in range(4):
            if block < 2:
                fars = (one_ref, one_core_ref)

                @pl.when((chip == 0) & (block == group_index))
                def _(block=block, fars=fars):
                    fetch_pair(fars, 4 * block, kv_ref, 0, sem)

            for number, fars in enumerate(((one_ref, one_core_ref), (two_ref, two_core_ref))):
                if block < 2 and number == 1:
                    continue
                page = 4 * block - 8 * number

                @pl.when((chip == number) & (block == group_index) & (block >= 2))
                def _(fars=fars, page=page):
                    fetch_pair(fars, page, kv_ref, 0, sem)

                @pl.when((chip == number) & (block > group_index))
                def _(block=block, fars=fars, page=page):
                    fetch_pair(fars, page, kv_ref, 8 * (odd + block - group_index), sem)

            @pl.when((block == group_index) & (odd == 1))
            def _(block=block):
                fetch_pair((both_ref, core_ref), 16 + 4 * block, kv_ref, 8, sem)

    @pl.when(chip == 1)
    def _():
        place = jnp.where(has_old, 16, 0)
        fetch(one_ref, 0, kv_ref, place, 16, sem)
        fetch(one_core_ref, 0, kv_ref, place + 16, 16, sem)

    for h in range(heads):
        for copy in state_copies(h):
            copy.start()
    weight_copy = pltpu.make_async_copy(weight_ref, w_ref, weight_sem)
    weight_copy.start()

    bias_ref[...] = jnp.zeros_like(bias_ref)

    @pl.when(has_old)
    def _():
        bias_ref[0, :, :256] = old_bias(rows, group_index ^ 2)

        @pl.when(odd == 1)
        def _():
            bias_ref[0, :, 256:] = old_bias(rows, group_index)

    for copy in pool_loads:
        copy.wait()
    placed = jnp.int32(0)
    for r in range(requests):
        chosen, found = pages_here(table_ref, r, slots // 2, slots // 2, cap, pages)
        placed = placed + found
        for c in range(cap):

            @pl.when(found > c)
            def _(page=chosen[c], slot=r * cap + c):
                pltpu.make_async_copy(arrived_ref.at[slot, 0], key_pool.at[page], page_sem).start()
                pltpu.make_async_copy(arrived_ref.at[slot, 1], value_pool.at[page], page_sem).start()

    wait_rows(kv_ref, steps, 3, sem)
    lane = lax.broadcasted_iota(jnp.int32, (rows, 128), 1)

    def begin(h, most_ref):
        for copy in state_copies(h):
            copy.wait()
        most_ref[...] = jnp.where(lane < 64, stat_ref[h], masked_score)

    def finish(h):
        stat = stat_ref[h]
        top = top_ref[...]
        factor = jnp.exp(stat[:, :1] - top)
        sums = stat[:, 64:65] * factor + jnp.sum(sum_ref[...], axis=1, keepdims=True)
        inverse = 1.0 / sums
        old = factor * inverse
        mixed = acc_ref[h] * join([old, old]) + head_ref[...] * join([inverse, inverse])
        attended_ref[:, pl.ds(pl.multiple_of(h * 256, 256), 256)] = mixed.astype(jnp.bfloat16)

    attention(
        heads, steps, roped_ref, kv_ref, bias_ref, (s_0, s_1), (most_0, most_1), top_ref, sum_ref,
        lambda h: head_ref, begin, finish,
    )

    def settle(n, carry):
        pltpu.make_async_copy(arrived_ref.at[0, 0], key_pool.at[0], page_sem).wait()
        pltpu.make_async_copy(arrived_ref.at[0, 1], value_pool.at[0], page_sem).wait()
        return carry

    lax.fori_loop(0, placed, settle, 0)
    for copy in pool_stores:
        copy.start()
    weight_copy.wait()

    def project(n, carry):
        columns = pl.ds(pl.multiple_of(n * chunk, chunk), chunk)
        stage_ref[n] = jnp.dot(
            attended_ref[...], w_ref[:, columns], preferred_element_type=jnp.float32
        ).astype(jnp.bfloat16)
        pltpu.make_async_copy(stage_ref.at[n], hidden_ref.at[:, columns], out_sems.at[n]).start()
        return carry

    lax.fori_loop(0, chunks, project, 0)
    for n in range(chunks):
        pltpu.make_async_copy(
            stage_ref.at[n], hidden_ref.at[:, pl.ds(n * chunk, chunk)], out_sems.at[n]
        ).wait()
    for copy in pool_stores:
        copy.wait()


def second_part(page_table, lengths, cap, state, slots, weight, arrived, key_cache, value_cache):
    heads, rows, _ = state[0].shape
    width = weight.shape[1]
    chunk = 512
    return pl.pallas_call(
        lambda *refs: second_kernel(cap, *refs),
        out_shape=(
            pltpu.HBM((rows, width), jnp.bfloat16),
            pltpu.HBM(key_cache.shape, jnp.bfloat16),
            pltpu.HBM(value_cache.shape, jnp.bfloat16),
        ),
        in_specs=[smem_spec] * 2 + [hbm_spec] * 13,
        out_specs=(hbm_spec,) * 3,
        scratch_shapes=[
            pltpu.VMEM((heads, rows, 256), jnp.bfloat16),
            pltpu.VMEM((heads, rows, 256), jnp.float32),
            pltpu.VMEM((heads, rows, 128), jnp.float32),
        ]
        + working(rows, 3, 2)
        + [
            pltpu.VMEM((rows, 256), jnp.float32),
            pltpu.VMEM((rows, weight.shape[0]), jnp.bfloat16),
            pltpu.VMEM(weight.shape, jnp.bfloat16),
            pltpu.VMEM((width // chunk, rows, chunk), jnp.bfloat16),
            pltpu.VMEM(key_cache.shape, jnp.bfloat16),
            pltpu.VMEM(value_cache.shape, jnp.bfloat16),
            pltpu.SemaphoreType.DMA((3, heads)),
            pltpu.SemaphoreType.DMA,
            pltpu.SemaphoreType.DMA,
            pltpu.SemaphoreType.DMA((2,)),
            pltpu.SemaphoreType.DMA,
            pltpu.SemaphoreType.DMA((width // chunk,)),
        ],
        compiler_params=params(large_limit),
        name="attend_second",
    )(page_table, lengths, *in_hbm(*state, *slots, weight, arrived, key_cache, value_cache))


def body(queries, new_keys, new_values, key_cache, value_cache, out_weight, lengths, page_table):
    blk_count = lax.axis_size("blk")
    pages = key_cache.shape[0]
    window_pages = page_table.shape[1] // 2
    cap = (window_pages + blk_count - 1) // blk_count

    def other_core(value):
        return lax.ppermute(value, "group", [(0, 1), (1, 0), (2, 3), (3, 2)])

    def other_chip(value):
        return lax.ppermute(value, "group", [(0, 2), (2, 0), (1, 3), (3, 1)])

    old = pick_old(page_table, cap, key_cache, value_cache)
    old = lax.all_to_all(old, "blk", split_axis=0, concat_axis=0, tiled=True)
    old = old.reshape((blk_count * cap,) + old.shape[2:])
    both, one, two, cosine, sine = pack(
        page_table, lengths, blk_count, cap, pages, new_keys[0], new_values[0], old
    )
    one = other_chip(one)
    core = other_core(both)
    two = other_chip(two)
    roped = rotate_queries(queries[0], cosine, sine)
    acc, stat = first_part(lengths, roped, both, core)
    one_core = other_core(one)
    two_core = other_core(two)
    slots = (both, core, one, one_core, two, two_core)
    late_table, _ = lax.optimization_barrier((page_table, stat))
    new = pick_new(late_table, blk_count, cap, pages, slots)
    arrived = lax.all_to_all(new, "blk", split_axis=0, concat_axis=0, tiled=True)
    hidden, key_out, value_out = second_part(
        page_table, lengths, cap, (roped, acc, stat), slots, out_weight, arrived, key_cache, value_cache
    )
    return (hidden[None], key_out, value_out)


def solution(mesh):
    return jax.shard_map(
        body,
        mesh=mesh,
        in_specs=(
            P("blk", "group", None),
            P("blk", "group", None),
            P("blk", "group", None),
            P("blk", "group", None),
            P("blk", "group", None),
            P(),
            P(),
            P(),
        ),
        out_specs=(P("blk", "group", None), P("blk", "group", None), P("blk", "group", None)),
        check_vma=False,
    )
```

time: 99.7 us -> 123 us (1.23)
  blocking collectives: 0 us -> 40.1 us
  starting transfers between devices: 16.1 us -> 2.66 us
  local copies, waits for them, and re-layouts: 7.66 us -> 4.72 us
  waiting for transfers between devices: 15 us -> 13.4 us
    all_to_all x0 -> x2, blocking collectives: none -> 40.1 us  [the longest x1 21.7 us: body(): old = lax.all_to_all(old, 'blk', split_axis=0, concat_axis=0, tiled=True)]
    all_to_all x2 -> x0, starting transfers between devices: 12 us -> none  [the longest x1 7.26 us: body(): lax.all_to_all(old_out, 'blk', split_axis=0, concat_axis=0, tiled=True)]
    pallas_call x3 -> x4, Pallas kernels: 26.3 us -> 30.3 us  [the longest x1 22.3 us: first_part(): pl.pallas_call(first_kernel, out_shape=(pltpu.HBM((heads, rows, 256), jnp...]
    pallas_call x1, Pallas kernels: 30.3 us -> 27.2 us  [second_part(): pl.pallas_call(lambda *refs: second_kernel(cap, *refs), out_shape=(pltpu....]
    unnamed x38 -> x26, local copies, waits for them, and re-layouts: 7.66 us -> 4.72 us
    ppermute x9 -> x5, starting transfers between devices: 4.13 us -> 2.66 us  [the longest x2 2.09 us: other_chip(): return lax.ppermute(value, 'group', [(0, 2), (2, 0), (1, 3), (3, 1)])]
    ppermute x9 -> x5, waiting for transfers between devices: 14 us -> 13.4 us  [the longest x2 13.4 us: other_chip(): return lax.ppermute(value, 'group', [(0, 2), (2, 0), (1, 3), (3, 1)])]
  transfers between devices with their start and end apart: 11 -> 5, of which waited for: 4 -> 1; matrix products, arithmetic and copies ran while one was open for 0% -> 0% of each run, Pallas kernels for 25% -> 22%
where the time goes in v1:
time: 123 us; the launch traced here: 121 us
  Pallas kernels  59.5 us (48%)
  blocking collectives  40.1 us (33%)
  waiting for transfers between devices  13.4 us (11%)
  local copies, waits for them, and re-layouts  4.72 us (4%)
  starting transfers between devices  2.66 us (2%)
    pallas_call x1, Pallas kernels, second_part(): pl.pallas_call(lambda *refs: second_kernel(cap, *refs), out_shape=(pltpu....  27.2 us
    pallas_call x1, Pallas kernels, first_part(): pl.pallas_call(first_kernel, out_shape=(pltpu.HBM((heads, rows, 256), jnp...  22.3 us
    all_to_all x1, blocking collectives, body(): old = lax.all_to_all(old, 'blk', split_axis=0, concat_axis=0, tiled=True)  21.7 us
    all_to_all x1, blocking collectives, body(): lax.all_to_all(new, 'blk', split_axis=0, concat_axis=0, tiled=True)  18.4 us
    ppermute x2, waiting for transfers between devices, other_chip(): return lax.ppermute(value, 'group', [(0, 2), (2, 0), (1, 3), (3, 1)])  13.4 us
    unnamed x26, local copies, waits for them, and re-layouts  4.72 us
    pallas_call x1, Pallas kernels, rotate_queries(): pl.pallas_call(rope_kernel, out_shape=pltpu.HBM((heads, rows, 256), jnp.b...  4.42 us
  transfers between devices with their start and end apart: 5, of which 1 were waited for; matrix products, arithmetic and copies ran while one was open for 0% of the time, Pallas kernels for 22%

profile of v1, /device:TPU:0, one launch (start us, length us, event | category | flops | bytes accessed | tf_op | source)
XLA Modules:
  0.0 121.2 jit_solution(3089402032035700224)
XLA Ops:
  0.6 0.0 copy-start.3
  0.6 0.0 copy-start.2
  0.7 0.0 copy-start.1
  0.7 0.0 copy-start.4
  0.7 0.8 copy-done.4
  1.5 2.0 %pick_old.1 = bf16[8,2,2,32,256]{4,3,2,1,0:T(8,128)(2,1)S(1)} custom-call(s32[8,32]{1,0:T(8,128)S(1)} %copy-done.4, bf16[40,32,256]{2,1,0:T(8,128)(2,1)} %refs_13_.1, bf16[40,32,256]{2,1,0:T(8,128)(2,1)} %refs_14_.1), custom_call_target="tpu_custom_call" | custom-call | tf_op jit(solution)/shard_map/pick_old/pallas_call | solution.py:60
  3.5 21.7 %all_to_all.10 = bf16[8,2,2,32,256]{4,3,2,1,0:T(8,128)(2,1)} all-to-all(bf16[8,2,2,32,256]{4,3,2,1,0:T(8,128)(2,1)S(1)} %pick_old.1), channel_id=1, replica_groups=mesh['blk'=8,'group'=4] {'blk'}, dimensions={0} | all-to-all | bytes 1048576 | tf_op jit(solution)/shard_map/all_to_all | solution.py:648
  25.2 0.0 copy-done.3
  25.2 0.0 copy-done.2
  25.2 0.0 copy-start.6
  25.2 0.7 copy-done.6
  25.8 0.0 copy-start.7
  25.8 0.7 copy-done.7
  26.5 1.9 %pack.1 = (bf16[32,2,32,256]{3,2,1,0:T(8,128)(2,1)S(1)}, bf16[16,2,32,256]{3,2,1,0:T(8,128)(2,1)S(1)}, bf16[8,2,32,256]{3,2,1,0:T(8,128)(2,1)S(1)}, f32[512,128]{1,0:T(8,128)S(1)}, f32[512,128]{1,0:T(8,128)S(1)}) custom-call(s32[8,32]{1,0:T(8,128)S(1)} %copy-done.4, s32[8]{0:T(128)S(1)} %copy-done.6, f32[1,128]{1,0:T(1,128)S(1)} %copy-done.7, ...), custom_call_target="tpu_custom_call" | custom-call | tf_op jit(solution)/shard_map/pack/pallas_call | solution.py:135
  28.3 0.0 copy-start
  28.4 0.1 collective-permute-start
  28.4 1.6 %collective-permute-start.1 = (bf16[16,2,32,256]{3,2,1,0:T(8,128)(2,1)S(1)}, bf16[16,2,32,256]{3,2,1,0:T(8,128)(2,1)S(1)}, u32[]{:S(2)}, u32[]{:S(2)}) collective-permute-start(bf16[16,2,32,256]{3,2,1,0:T(8,128)(2,1)S(1)} %get-tuple-element.19), channel_id=1, source_target_pairs={{0,2},{2,0},{1,3},{3,1},{4,6},{6,4},{5,7},{7,5},{8,10},{10,8},{9,1... | collective-permute-start | bytes 1572872 | tf_op jit(solution)/shard_map/ppermute | solution.py:645
  30.0 0.5 collective-permute-start.3
  30.5 0.0 copy-done.1
  30.5 4.4 %rotate_queries.1.roped_in.refs_2_ = bf16[10,512,256]{2,1,0:T(8,128)(2,1)} custom-call(bf16[512,2560]{1,0:T(8,128)(2,1)S(1)} %bitcast.5, f32[512,128]{1,0:T(8,128)S(1)} %get-tuple-element.14.cos_ref, f32[512,128]{1,0:T(8,128)S(1)} %get-tuple-element.15.sin_ref), custom_call_target="tpu_custom_call" | custom-call | flops 10485760 | bytes 5242880 | tf_op jit(solution)/shard_map/rotate_queries/pallas_call | solution.py:162
  35.0 0.0 copy-done
  35.0 0.0 copy-start.5
  35.0 13.4 %collective-permute-done.3.refs_5_.refs_9_ = bf16[8,2,32,256]{3,2,1,0:T(8,128)(2,1)S(1)} collective-permute-done((bf16[8,2,32,256]{3,2,1,0:T(8,128)(2,1)S(1)}, bf16[8,2,32,256]{3,2,1,0:T(8,128)(2,1)S(1)}, u32[]{:S(2)}, u32[]{:S(2)}) %collective-permute-start.3) | collective-permute-done | bytes 262176 | tf_op jit(solution)/shard_map/ppermute | solution.py:645
  48.4 0.0 copy-start.11
  48.4 0.0 collective-permute-start.4
  48.4 0.0 collective-permute-done.1.refs_3_.refs_7_
  48.4 0.0 copy-start.9
  48.4 0.5 collective-permute-start.2
  48.9 0.0 collective-permute-done.core_ref.refs_2_.refs_6_
  48.9 0.0 copy-start.8
  48.9 1.0 copy-done.8
  49.9 22.3 %attend_first.1 = (f32[10,512,256]{2,1,0:T(8,128)}, f32[10,512,128]{2,1,0:T(8,128)}) custom-call(s32[8]{0:T(128)} %refs_1_.3, bf16[10,512,256]{2,1,0:T(8,128)(2,1)} %rotate_queries.1.roped_in.refs_2_, bf16[32,2,32,256]{3,2,1,0:T(8,128)(2,1)} %copy-done, bf16[32,2,32,256]{3,2,1,0:T(8,128)(2,1)} %copy-done.8), custom_call_target="tpu_custom_call" | custom-call | flops 8053063680 | bytes 16777216 | tf_op jit(solution)/shard_map/attend_first/pallas_call | solution.py:424
  72.3 0.0 copy-done.11
  72.3 0.0 copy-done.9
  72.3 0.0 collective-permute-done.4.refs_6_.refs_10_
  72.3 0.0 copy-start.12
  72.3 0.0 collective-permute-done.2.refs_4_.refs_8_
  72.3 0.7 copy-done.12
  73.0 0.0 copy-start.10
  73.0 0.8 copy-done.10
  73.9 0.0 copy-done.5
  73.9 1.7 %pick_new.1 = bf16[16,2,32,256]{3,2,1,0:T(8,128)(2,1)S(1)} custom-call(s32[8,32]{1,0:T(8,128)S(1)} %copy-done.5, bf16[32,2,32,256]{3,2,1,0:T(8,128)(2,1)} %copy-done, bf16[32,2,32,256]{3,2,1,0:T(8,128)(2,1)} %copy-done.8, bf16[16,2,32,256]{3,2,1,0:T(8,128)(2,1)} %copy-done.9, bf16[16,2,32,256]{3,2,1,0:T(8,128)(2,1)} %copy-done.10, ...), custom_call_target="tpu_custom_call" | custom-call | tf_op jit(solution)/shard_map/pick_new/pallas_call | solution.py:213
  75.6 18.4 %all_to_all.11.refs_12_ = bf16[16,2,32,256]{3,2,1,0:T(8,128)(2,1)} all-to-all(bf16[16,2,32,256]{3,2,1,0:T(8,128)(2,1)S(1)} %pick_new.1), channel_id=1, replica_groups=mesh['blk'=8,'group'=4] {'blk'}, dimensions={0} | all-to-all | bytes 1048576 | tf_op jit(solution)/shard_map/all_to_all | solution.py:663
  94.0 27.2 %attend_second.1 = (bf16[512,2560]{1,0:T(8,128)(2,1)}, bf16[40,32,256]{2,1,0:T(8,128)(2,1)}, bf16[40,32,256]{2,1,0:T(8,128)(2,1)}) custom-call(s32[8,32]{1,0:T(8,128)} %refs_0_.4, s32[8]{0:T(128)} %refs_1_.3, bf16[10,512,256]{2,1,0:T(8,128)(2,1)} %rotate_queries.1.roped_in.refs_2_, f32[10,512,256]{2,1,0:T(8,128)} %get-tuple-element.17.refs_3_, ...), custom_call_target="tpu_custom_call" | custom-call | tf_op jit(solution)/shard_map/attend_second/pallas_call | solution.py:601
Async XLA Ops:
  0.6 24.5 %copy-start.3 = (bf16[1,512,256]{2,1,0:T(8,128)(2,1)S(1)}, bf16[1,512,256]{2,1,0:T(8,128)(2,1)}, u32[]{:S(2)}) copy-start(bf16[1,512,256]{2,1,0:T(8,128)(2,1)} %param.11) | copy-start | bytes 786436
  0.6 24.5 %copy-start.2 = (bf16[1,512,256]{2,1,0:T(8,128)(2,1)S(1)}, bf16[1,512,256]{2,1,0:T(8,128)(2,1)}, u32[]{:S(2)}) copy-start(bf16[1,512,256]{2,1,0:T(8,128)(2,1)} %param.10) | copy-start | bytes 786436
  0.7 29.9 %copy-start.1 = (bf16[1,512,2560]{2,1,0:T(8,128)(2,1)S(1)}, bf16[1,512,2560]{2,1,0:T(8,128)(2,1)}, u32[]{:S(2)}) copy-start(bf16[1,512,2560]{2,1,0:T(8,128)(2,1)} %param.9) | copy-start | bytes 7864324
  0.7 0.8 copy-start.4
  25.2 0.7 copy-start.6
  25.8 0.7 copy-start.7
  28.3 6.6 %copy-start = (bf16[32,2,32,256]{3,2,1,0:T(8,128)(2,1)}, bf16[32,2,32,256]{3,2,1,0:T(8,128)(2,1)S(1)}, u32[]{:S(2)}) copy-start(bf16[32,2,32,256]{3,2,1,0:T(8,128)(2,1)S(1)} %get-tuple-element.16.both_ref.refs_1_.refs_5_) | copy-start | bytes 3145732
  28.4 20.6 %collective-permute-start = (bf16[32,2,32,256]{3,2,1,0:T(8,128)(2,1)S(1)}, bf16[32,2,32,256]{3,2,1,0:T(8,128)(2,1)S(1)}, u32[]{:S(2)}, u32[]{:S(2)}) collective-permute-start(bf16[32,2,32,256]{3,2,1,0:T(8,128)(2,1)S(1)} %get-tuple-element.16.both_ref.refs_1_.refs_5_), channel_id=1, source_target_pairs={{0,1},{1,0},{2,3},{3,2},{4,5},{5,4},{6,7},{7,6},{8,9},{9,8},{10,11... | collective-permute-start | bytes 3145736 | tf_op jit(solution)/shard_map/ppermute | solution.py:642
  28.4 20.0 %collective-permute-start.1 = (bf16[16,2,32,256]{3,2,1,0:T(8,128)(2,1)S(1)}, bf16[16,2,32,256]{3,2,1,0:T(8,128)(2,1)S(1)}, u32[]{:S(2)}, u32[]{:S(2)}) collective-permute-start(bf16[16,2,32,256]{3,2,1,0:T(8,128)(2,1)S(1)} %get-tuple-element.19), channel_id=1, source_target_pairs={{0,2},{2,0},{1,3},{3,1},{4,6},{6,4},{5,7},{7,5},{8,10},{10,8},{9,1... | collective-permute-start | bytes 1572872 | tf_op jit(solution)/shard_map/ppermute | solution.py:645
  30.0 18.4 %collective-permute-start.3 = (bf16[8,2,32,256]{3,2,1,0:T(8,128)(2,1)S(1)}, bf16[8,2,32,256]{3,2,1,0:T(8,128)(2,1)S(1)}, u32[]{:S(2)}, u32[]{:S(2)}) collective-permute-start(bf16[8,2,32,256]{3,2,1,0:T(8,128)(2,1)S(1)} %get-tuple-element.20), channel_id=1, source_target_pairs={{0,2},{2,0},{1,3},{3,1},{4,6},{6,4},{5,7},{7,5},{8,10},{10,8},{9,1... | collective-permute-start | bytes 786440 | tf_op jit(solution)/shard_map/ppermute | solution.py:645
  35.0 38.9 %copy-start.5 = (s32[8,32]{1,0:T(8,128)S(1)}, s32[8,32]{1,0:T(8,128)}, u32[]{:S(2)}) copy-start(s32[8,32]{1,0:T(8,128)} %refs_0_.4) | copy-start | bytes 3076
  48.4 23.9 %copy-start.11 = (bf16[8,2,32,256]{3,2,1,0:T(8,128)(2,1)}, bf16[8,2,32,256]{3,2,1,0:T(8,128)(2,1)S(1)}, u32[]{:S(2)}) copy-start(bf16[8,2,32,256]{3,2,1,0:T(8,128)(2,1)S(1)} %collective-permute-done.3.refs_5_.refs_9_) | copy-start | bytes 786436
  48.4 23.9 %collective-permute-start.4 = (bf16[8,2,32,256]{3,2,1,0:T(8,128)(2,1)S(1)}, bf16[8,2,32,256]{3,2,1,0:T(8,128)(2,1)S(1)}, u32[]{:S(2)}, u32[]{:S(2)}) collective-permute-start(bf16[8,2,32,256]{3,2,1,0:T(8,128)(2,1)S(1)} %collective-permute-done.3.refs_5_.refs_9_), channel_id=1, source_target_pairs={{0,1},{1,0},{2,3},{3,2},{4,5},{5,4},{6,7},{7,6},{8,9},{9,8},{10,11... | collective-permute-start | bytes 786440 | tf_op jit(solution)/shard_map/ppermute | solution.py:642
  48.4 23.9 %copy-start.9 = (bf16[16,2,32,256]{3,2,1,0:T(8,128)(2,1)}, bf16[16,2,32,256]{3,2,1,0:T(8,128)(2,1)S(1)}, u32[]{:S(2)}) copy-start(bf16[16,2,32,256]{3,2,1,0:T(8,128)(2,1)S(1)} %collective-permute-done.1.refs_3_.refs_7_) | copy-start | bytes 1572868
  48.4 23.9 %collective-permute-start.2 = (bf16[16,2,32,256]{3,2,1,0:T(8,128)(2,1)S(1)}, bf16[16,2,32,256]{3,2,1,0:T(8,128)(2,1)S(1)}, u32[]{:S(2)}, u32[]{:S(2)}) collective-permute-start(bf16[16,2,32,256]{3,2,1,0:T(8,128)(2,1)S(1)} %collective-permute-done.1.refs_3_.refs_7_), channel_id=1, source_target_pairs={{0,1},{1,0},{2,3},{3,2},{4,5},{5,4},{6,7},{7,6},{8,9},{9,8},{10,11... | collective-permute-start | bytes 1572872 | tf_op jit(solution)/shard_map/ppermute | solution.py:642
  48.9 1.0 copy-start.8
  72.3 0.7 copy-start.12
  73.0 0.8 copy-start.10

commit v2 on v1

v2 whole, which is shorter than its diff:
```python
import jax
import jax.numpy as jnp
import numpy as np
from jax import lax
from jax.experimental import pallas as pl
from jax.experimental.pallas import tpu as pltpu
from jax.sharding import PartitionSpec as P

masked_score = -1e30
step_keys = 512
step_slots = 16
hbm_spec = pl.BlockSpec(memory_space=pltpu.HBM)
smem_spec = pl.BlockSpec(memory_space=pltpu.SMEM)
vmem_spec = pl.BlockSpec(memory_space=pltpu.VMEM)
small_limit = 16 * 1024 * 1024
head_pair = 2
large_limit = 56 * 1024 * 1024


def params(limit):
    return pltpu.CompilerParams(vmem_limit_bytes=limit)


def in_hbm(*arrays):
    return [pltpu.with_memory_space_constraint(array, pltpu.HBM) for array in arrays]


def turn(values, cosine, sine):
    front = values[:, :128].astype(jnp.float32)
    return front * cosine + pltpu.roll(front, 64, 1) * sine


def join(pieces):
    return jnp.concatenate(pieces, axis=1)


def pages_here(table_ref, r, first, count, cap, pages):
    low = lax.axis_index("blk") * pages
    found = jnp.int32(0)
    chosen = [jnp.int32(0)] * cap
    for j in range(first, first + count):
        page = table_ref[r, j] - low
        inside = (page >= 0) & (page < pages)
        chosen = [jnp.where(inside & (found == c), page, chosen[c]) for c in range(cap)]
        found = found + inside.astype(jnp.int32)
    return chosen, found


def pick_old_kernel(table_ref, key_ref, value_ref, out_ref, sem):
    requests, cap = out_ref.shape[:2]
    for r in range(requests):
        chosen, _ = pages_here(table_ref, r, 0, table_ref.shape[1] // 2, cap, key_ref.shape[0])
        for c in range(cap):
            pltpu.make_async_copy(key_ref.at[chosen[c]], out_ref.at[r, c, 0], sem).start()
            pltpu.make_async_copy(value_ref.at[chosen[c]], out_ref.at[r, c, 1], sem).start()
    pltpu.make_async_copy(out_ref, out_ref, sem).wait()


def pick_old(page_table, cap, key_cache, value_cache):
    requests = page_table.shape[0]
    return pl.pallas_call(
        pick_old_kernel,
        out_shape=jax.ShapeDtypeStruct((requests, cap, 2) + key_cache.shape[1:], jnp.bfloat16),
        in_specs=[smem_spec, hbm_spec, hbm_spec],
        out_specs=vmem_spec,
        scratch_shapes=[pltpu.SemaphoreType.DMA],
        compiler_params=params(small_limit),
        name="pick_old",
    )(page_table, *in_hbm(key_cache, value_cache))


def owner_of(page, pages, owners):
    factor = (1 << 20) // pages + 1
    assert all((p * factor) >> 20 == p // pages for p in range(pages * owners))
    assert pages * owners * factor < 1 << 31
    return (page * factor) >> 20


def find_slots(table_ref, first, count, cap, pages, counts_ref):
    owners = counts_ref.shape[0]
    row = lax.axis_index("blk")
    for o in range(owners):
        counts_ref[o] = 0
    slots = []
    for j in range(count):
        owner = owner_of(table_ref[row, first + j], pages, owners)
        rank = counts_ref[owner]
        counts_ref[owner] = rank + 1
        slots.append(owner * cap + rank)
    return slots


def rotate_kernel(lengths_ref, freq_ref, keys_ref, values_ref, out_ref, cos_ref, sin_ref):
    rows = keys_ref.shape[0]
    slots = rows // 32
    start = lengths_ref[lax.axis_index("blk")] + lax.axis_index("group") * rows
    positions = start + lax.broadcasted_iota(jnp.int32, (rows, 128), 0)
    angles = positions.astype(jnp.float32) * freq_ref[...]
    lane = lax.broadcasted_iota(jnp.int32, (rows, 128), 1)
    cosine = jnp.cos(angles)
    sine = jnp.sin(angles)
    sine = jnp.where(lane < 64, -sine, sine)
    cos_ref[...] = cosine
    sin_ref[...] = sine
    keys = keys_ref[...]
    turned = join([turn(keys, cosine, sine).astype(jnp.bfloat16), keys[:, 128:]])
    out_ref[:, 0] = turned.reshape(slots, 32, 256)
    out_ref[:, 1] = values_ref[...].reshape(slots, 32, 256)


def rotate_keys(lengths, keys, values):
    rows, head_dim = keys.shape
    quarter = head_dim // 4
    freq_table = np.float32(10000.0) ** (-np.arange(quarter, dtype=np.float32) / np.float32(quarter))
    freq_table = np.concatenate([freq_table, freq_table])[None].astype(np.float32)
    return pl.pallas_call(
        rotate_kernel,
        out_shape=(
            jax.ShapeDtypeStruct((rows // 32, 2, 32, head_dim), jnp.bfloat16),
            jax.ShapeDtypeStruct((rows, 128), jnp.float32),
            jax.ShapeDtypeStruct((rows, 128), jnp.float32),
        ),
        in_specs=[smem_spec, vmem_spec, vmem_spec, vmem_spec],
        out_specs=(vmem_spec,) * 3,
        compiler_params=params(small_limit),
        name="rotate_keys",
    )(lengths, jnp.asarray(freq_table), keys, values)


def sort_kernel(pages, cap, table_ref, old_ref, out_ref, counts_ref, sem):
    count = out_ref.shape[0]
    for j, slot in enumerate(find_slots(table_ref, 0, count, cap, pages, counts_ref)):
        pltpu.make_async_copy(old_ref.at[slot], out_ref.at[j], sem).start()
    pltpu.make_async_copy(out_ref, out_ref, sem).wait()


def sort_old(page_table, blk_count, cap, pages, old):
    window = page_table.shape[1] // 2
    return pl.pallas_call(
        lambda *refs: sort_kernel(pages, cap, *refs),
        out_shape=jax.ShapeDtypeStruct((window,) + old.shape[1:], jnp.bfloat16),
        in_specs=[smem_spec, hbm_spec],
        out_specs=vmem_spec,
        scratch_shapes=[pltpu.SMEM((blk_count,), jnp.int32), pltpu.SemaphoreType.DMA],
        compiler_params=params(small_limit),
        name="sort_old",
    )(page_table, *in_hbm(old))


def pick_new_kernel(pages, cap, table_ref, own_ref, core_ref, far_ref, far_core_ref, out_ref, slots_ref, counts_ref, sem):
    count = slots_ref.shape[0]
    block_pages = count // 4
    group_index = lax.axis_index("group")
    for j, slot in enumerate(find_slots(table_ref, table_ref.shape[1] - count, count, cap, pages, counts_ref)):
        slots_ref[j] = slot
    for number, ref in enumerate((own_ref, core_ref, far_ref, far_core_ref)):
        block = group_index ^ number
        for place in range(block_pages):
            source = ref.at[4 * place + group_index]
            target = out_ref.at[slots_ref[block * block_pages + place]]
            pltpu.make_async_copy(source, target, sem).start()
    sent = out_ref.at[pl.ds(0, count)]
    pltpu.make_async_copy(sent, sent, sem).wait()


def pick_new(page_table, blk_count, cap, pages, sources):
    window = page_table.shape[1] // 2
    return pl.pallas_call(
        lambda *refs: pick_new_kernel(pages, cap, *refs),
        out_shape=jax.ShapeDtypeStruct((blk_count * cap,) + sources[0].shape[1:], jnp.bfloat16),
        in_specs=[smem_spec] + [hbm_spec] * 4,
        out_specs=vmem_spec,
        scratch_shapes=[
            pltpu.SMEM((window,), jnp.int32),
            pltpu.SMEM((blk_count,), jnp.int32),
            pltpu.SemaphoreType.DMA,
        ],
        compiler_params=params(small_limit),
        name="pick_new",
    )(page_table, *in_hbm(*sources))


def lane_fold(values, combine):
    total = values[:, :128]
    for start in range(128, values.shape[1], 128):
        total = combine(total, values[:, start : start + 128])
    return total


def old_bias(rows, quarter):
    row = lax.broadcasted_iota(jnp.int32, (rows, 256), 0)
    column = lax.broadcasted_iota(jnp.int32, (rows, 256), 1)
    held = quarter ^ (column // 128)
    position = ((column % 128) // 32) * 128 + 32 * held + column % 32
    return jnp.where(position > row, 0.0, masked_score)


def fetch(source, first, kv_ref, place, count, sem):
    for kind in range(2):
        pltpu.make_async_copy(
            source.at[pl.ds(first, count), kind], kv_ref.at[kind, pl.ds(place, count)], sem
        ).start()


def fetch_pair(sources, first, kv_ref, place, sem):
    fetch(sources[0], first, kv_ref, place, 4, sem)
    fetch(sources[1], first, kv_ref, place + 4, 4, sem)


def wait_rows(kv_ref, steps, most, sem):
    for n in range(1, most + 1):

        @pl.when(steps == n)
        def _(n=n):
            filled = kv_ref.at[:, pl.ds(0, n * step_slots)]
            pltpu.make_async_copy(filled, filled, sem).wait()


def attention(steps, roped_ref, kv_ref, bias_ref, s_refs, most_refs, top_ref, sum_ref, sum_of_values, begin, finish):
    items, rows, _ = roped_ref.shape
    last_bias = bias_ref.shape[0] - 1

    def block(kind, c):
        return kv_ref[kind, pl.ds(c * step_slots, step_slots)].reshape(step_keys, 256)

    def scores(t, c, which):
        result = lax.dot_general(
            roped_ref[t], block(0, c), (((1,), (1,)), ((), ())), preferred_element_type=jnp.float32
        )
        bias = bias_ref[jnp.minimum(c, last_bias)]
        result = (result.reshape(head_pair, rows // head_pair, step_keys) + bias).reshape(rows, step_keys)
        s_refs[which][c] = result
        most_refs[which][...] = jnp.maximum(most_refs[which][...], lane_fold(result, jnp.maximum))

    def weigh(c, which):
        weights = jnp.exp(s_refs[which][c] - join([top_ref[...]] * (step_keys // 128)))
        sum_ref[...] += lane_fold(weights, jnp.add)
        sum_of_values[...] += jnp.dot(
            weights.astype(jnp.bfloat16), block(1, c), preferred_element_type=jnp.float32
        )

    def settle(which):
        top_ref[...] = jnp.broadcast_to(
            jnp.max(most_refs[which][...], axis=1, keepdims=True), top_ref.shape
        )
        sum_ref[...] = jnp.zeros_like(sum_ref)
        sum_of_values[...] = jnp.zeros_like(sum_of_values)

    def loop(work):
        def step(c, carry):
            work(c)
            return carry

        lax.fori_loop(0, steps, step, 0)

    def one(t, which):
        begin(t + 1, most_refs[1 - which])
        settle(which)

        def work(c):
            weigh(c, which)
            scores(t + 1, c, 1 - which)

        loop(work)
        finish(t)

    def two(i, carry):
        one(2 * i, 0)
        one(2 * i + 1, 1)
        return carry

    begin(0, most_refs[0])
    loop(lambda c: scores(0, c, 0))
    pairs = (items - 1) // 2
    lax.fori_loop(0, pairs, two, 0)
    last = 2 * pairs
    if last < items - 1:
        one(last, 0)
        last += 1
    settle(last % 2)
    loop(lambda c: weigh(c, last % 2))
    finish(last)


def working(rows, steps, biases):
    return [
        pltpu.VMEM((2, steps * step_slots, 32, 256), jnp.bfloat16),
        pltpu.VMEM((steps, head_pair * rows, step_keys), jnp.float32),
        pltpu.VMEM((steps, head_pair * rows, step_keys), jnp.float32),
        pltpu.VMEM((head_pair * rows, 128), jnp.float32),
        pltpu.VMEM((head_pair * rows, 128), jnp.float32),
        pltpu.VMEM((head_pair * rows, 128), jnp.float32),
        pltpu.VMEM((head_pair * rows, 128), jnp.float32),
        pltpu.VMEM((head_pair * rows, 256), jnp.float32),
        pltpu.VMEM((biases, rows, step_keys), jnp.float32),
    ]


def state_shapes(items, rows):
    return [
        pltpu.VMEM((items, head_pair * rows, 256), jnp.bfloat16),
        pltpu.VMEM((items, head_pair * rows, 256), jnp.float32),
        pltpu.VMEM((items, head_pair * rows, 128), jnp.float32),
    ]


def state_out(items, rows):
    return (
        pltpu.HBM((items, head_pair * rows, 256), jnp.float32),
        pltpu.HBM((items, head_pair * rows, 128), jnp.float32),
    )


def cost(items, rows, keys):
    pairs = items * head_pair * rows * keys
    return pl.CostEstimate(flops=4 * pairs * 256, bytes_accessed=1 << 24, transcendentals=pairs)


def diagonal_kernel(
    query_ref, cos_ref, sin_ref, own_ref, roped_out, acc_out, stat_out,
    q_ref, roped_ref, acc_ref, stat_ref, kv_ref, s_0, s_1, most_0, most_1, top_ref, sum_ref, values_ref,
    bias_ref, query_sem, sem, out_sem,
):
    rows = q_ref.shape[0]
    items = roped_ref.shape[0]
    query_copy = pltpu.make_async_copy(query_ref, q_ref, query_sem)
    query_copy.start()
    fetch(own_ref, 0, kv_ref, 0, step_slots, sem)
    row = lax.broadcasted_iota(jnp.int32, (rows, step_keys), 0)
    column = lax.broadcasted_iota(jnp.int32, (rows, step_keys), 1)
    bias_ref[0] = jnp.where(column <= row, 0.0, masked_score)
    query_copy.wait()

    def rope(t, carry):
        for one in range(head_pair):
            raw = q_ref[:, pl.ds(pl.multiple_of((t * head_pair + one) * 256, 256), 256)]
            front = turn(raw, cos_ref[...], sin_ref[...])
            some = pl.ds(one * rows, rows)
            roped_ref[t, some, :128] = (front * 0.0625).astype(jnp.bfloat16)
            roped_ref[t, some, 128:] = raw[:, 128:] * jnp.bfloat16(0.0625)
        return carry

    lax.fori_loop(0, items, rope, 0)
    roped_copy = pltpu.make_async_copy(roped_ref, roped_out, query_sem)
    roped_copy.start()
    pltpu.make_async_copy(kv_ref, kv_ref, sem).wait()

    def begin(t, most_ref):
        most_ref[...] = jnp.full_like(most_ref, masked_score)

    def finish(t):
        lane = lax.broadcasted_iota(jnp.int32, stat_ref.shape[1:], 1)
        sums = jnp.sum(sum_ref[...], axis=1, keepdims=True)
        stat_ref[t] = jnp.where(lane < 64, top_ref[...], sums)
        acc_ref[t] = values_ref[...]
        pltpu.make_async_copy(acc_ref.at[t], acc_out.at[t], out_sem).start()
        pltpu.make_async_copy(stat_ref.at[t], stat_out.at[t], out_sem).start()

    attention(
        1, roped_ref, kv_ref, bias_ref, (s_0, s_1), (most_0, most_1), top_ref, sum_ref, values_ref,
        begin, finish,
    )
    roped_copy.wait()
    pltpu.make_async_copy(acc_ref, acc_out, out_sem).wait()
    pltpu.make_async_copy(stat_ref, stat_out, out_sem).wait()


def diagonal_part(queries, cosine, sine, own):
    rows, width = queries.shape
    items = width // (256 * head_pair)
    return pl.pallas_call(
        diagonal_kernel,
        out_shape=(pltpu.HBM((items, head_pair * rows, 256), jnp.bfloat16),) + state_out(items, rows),
        in_specs=[hbm_spec, vmem_spec, vmem_spec, hbm_spec],
        out_specs=(hbm_spec,) * 3,
        scratch_shapes=[pltpu.VMEM((rows, width), jnp.bfloat16)]
        + state_shapes(items, rows)
        + working(rows, 1, 1)
        + [pltpu.SemaphoreType.DMA] * 3,
        compiler_params=params(large_limit),
        cost_estimate=cost(items, rows, 512),
        name="attend_diagonal",
    )(*in_hbm(queries), cosine, sine, *in_hbm(own))


def state_copies(t, sources, targets, sems):
    return [
        pltpu.make_async_copy(source.at[t], target.at[t], sems.at[number, t])
        for number, (source, target) in enumerate(zip(sources, targets))
    ]


def near_kernel(
    lengths_ref, roped_in, acc_in, stat_in, core_ref, far_ref, far_core_ref, old_ref, old_core_ref,
    acc_out, stat_out,
    roped_ref, acc_ref, stat_ref, kv_ref, s_0, s_1, most_0, most_1, top_ref, sum_ref, values_ref,
    bias_ref, state_sems, sem, out_sem,
):
    group_index = lax.axis_index("group")
    has_old = lengths_ref[lax.axis_index("blk")] > 0
    items = roped_ref.shape[0]
    rows = bias_ref.shape[1]
    odd = group_index % 2
    chip = group_index // 2
    steps = jnp.where(has_old, 2 + chip, odd + 2 * chip)
    olds = (old_ref, old_core_ref)

    @pl.when(odd == 1)
    def _():
        fetch(core_ref, 0, kv_ref, 0, 16, sem)

    @pl.when(has_old)
    def _():
        for block in range(4):

            @pl.when((block == group_index) & (odd == 0))
            def _(block=block):
                fetch_pair(olds, 4 * block, kv_ref, 0, sem)

            @pl.when(block > group_index)
            def _(block=block):
                fetch_pair(olds, 4 * block, kv_ref, 8 * (odd + block - group_index), sem)

    @pl.when(chip == 1)
    def _():
        place = jnp.where(has_old, 16, 16 * odd)
        fetch(far_ref, 0, kv_ref, place, 16, sem)
        fetch(far_core_ref, 0, kv_ref, place + 16, 16, sem)

    def copies(t):
        return state_copies(t, (roped_in, stat_in, acc_in), (roped_ref, stat_ref, acc_ref), state_sems)

    for t in range(items):
        for copy in copies(t):
            copy.start()
    bias_ref[...] = jnp.zeros_like(bias_ref)

    @pl.when(has_old & (odd == 0))
    def _():
        bias_ref[0, :, :256] = old_bias(rows, group_index)

    wait_rows(kv_ref, steps, 3, sem)
    lane = lax.broadcasted_iota(jnp.int32, stat_ref.shape[1:], 1)

    def begin(t, most_ref):
        for copy in copies(t):
            copy.wait()
        most_ref[...] = jnp.where(lane < 64, stat_ref[t], masked_score)

    def finish(t):
        stat = stat_ref[t]
        top = top_ref[...]
        factor = jnp.exp(stat[:, :1] - top)
        sums = stat[:, 64:65] * factor + jnp.sum(sum_ref[...], axis=1, keepdims=True)
        stat_ref[t] = jnp.where(lane < 64, top, sums)
        acc_ref[t] = acc_ref[t] * join([factor, factor]) + values_ref[...]
        pltpu.make_async_copy(acc_ref.at[t], acc_out.at[t], out_sem).start()
        pltpu.make_async_copy(stat_ref.at[t], stat_out.at[t], out_sem).start()

    attention(
        steps, roped_ref, kv_ref, bias_ref, (s_0, s_1), (most_0, most_1), top_ref, sum_ref, values_ref,
        begin, finish,
    )
    pltpu.make_async_copy(acc_ref, acc_out, out_sem).wait()
    pltpu.make_async_copy(stat_ref, stat_out, out_sem).wait()


def near_part(lengths, state, slots):
    items, pair_rows, _ = state[0].shape
    rows = pair_rows // head_pair
    return pl.pallas_call(
        near_kernel,
        out_shape=state_out(items, rows),
        in_specs=[smem_spec] + [hbm_spec] * 8,
        out_specs=(hbm_spec,) * 2,
        scratch_shapes=state_shapes(items, rows)
        + working(rows, 3, 2)
        + [pltpu.SemaphoreType.DMA((3, items))]
        + [pltpu.SemaphoreType.DMA] * 2,
        compiler_params=params(large_limit),
        cost_estimate=cost(items, rows, 1024),
        name="attend_near",
    )(lengths, *in_hbm(*state, *slots))


def far_kernel(
    cap, table_ref, lengths_ref, roped_in, acc_in, stat_in, old_ref, old_core_ref, far_ref, far_core_ref,
    weight_ref, arrived_ref, key_ref, value_ref,
    hidden_ref, key_out_ref, value_out_ref,
    roped_ref, acc_ref, stat_ref, kv_ref, s_0, s_1, most_0, most_1, top_ref, sum_ref, values_ref,
    bias_ref, attended_ref, w_ref, stage_ref, key_pool, value_pool,
    state_sems, sem, weight_sem, pool_sems, page_sem, out_sems,
):
    group_index = lax.axis_index("group")
    has_old = lengths_ref[lax.axis_index("blk")] > 0
    pages = key_ref.shape[0]
    requests, slots = table_ref.shape
    items = roped_ref.shape[0]
    rows = bias_ref.shape[1]
    chunks = stage_ref.shape[0]
    chunk = stage_ref.shape[2]
    odd = group_index % 2
    steps = jnp.where(has_old, 2 - group_index // 2, 0)

    def copies(t):
        return state_copies(t, (roped_in, stat_in, acc_in), (roped_ref, stat_ref, acc_ref), state_sems)

    pool_loads = [
        pltpu.make_async_copy(key_ref, key_pool, pool_sems.at[0]),
        pltpu.make_async_copy(value_ref, value_pool, pool_sems.at[1]),
    ]
    pool_stores = [
        pltpu.make_async_copy(key_pool, key_out_ref, pool_sems.at[0]),
        pltpu.make_async_copy(value_pool, value_out_ref, pool_sems.at[1]),
    ]
    for copy in pool_loads:
        copy.start()

    @pl.when(has_old)
    def _():
        for block in range(4):

            @pl.when(block == group_index)
            def _(block=block):
                fetch_pair((far_ref, far_core_ref), 4 * block, kv_ref, 0, sem)

            @pl.when((block == group_index) & (odd == 1))
            def _(block=block):
                fetch_pair((old_ref, old_core_ref), 4 * block, kv_ref, 8, sem)

            @pl.when(block > group_index)
            def _(block=block):
                place = 8 * (odd + block - group_index)
                fetch_pair((far_ref, far_core_ref), 4 * block, kv_ref, place, sem)

    for t in range(items):
        for copy in copies(t):
            copy.start()
    weight_copy = pltpu.make_async_copy(weight_ref, w_ref, weight_sem)
    weight_copy.start()

    bias_ref[1] = jnp.zeros(bias_ref.shape[1:], jnp.float32)
    bias_ref[0, :, :256] = old_bias(rows, group_index ^ 2)
    bias_ref[0, :, 256:] = jnp.zeros((rows, 256), jnp.float32)

    @pl.when(odd == 1)
    def _():
        bias_ref[0, :, 256:] = old_bias(rows, group_index)

    for copy in pool_loads:
        copy.wait()
    placed = jnp.int32(0)
    for r in range(requests):
        chosen, found = pages_here(table_ref, r, slots // 2, slots // 2, cap, pages)
        placed = placed + found
        for c in range(cap):

            @pl.when(found > c)
            def _(page=chosen[c], slot=r * cap + c):
                pltpu.make_async_copy(arrived_ref.at[slot, 0], key_pool.at[page], page_sem).start()
                pltpu.make_async_copy(arrived_ref.at[slot, 1], value_pool.at[page], page_sem).start()

    wait_rows(kv_ref, steps, 2, sem)
    lane = lax.broadcasted_iota(jnp.int32, stat_ref.shape[1:], 1)

    def begin(t, most_ref):
        for copy in copies(t):
            copy.wait()
        most_ref[...] = jnp.where(lane < 64, stat_ref[t], masked_score)

    def finish(t):
        stat = stat_ref[t]
        factor = jnp.exp(stat[:, :1] - top_ref[...])
        sums = stat[:, 64:65] * factor + jnp.sum(sum_ref[...], axis=1, keepdims=True)
        inverse = 1.0 / sums
        old = factor * inverse
        mixed = acc_ref[t] * join([old, old]) + values_ref[...] * join([inverse, inverse])
        mixed = mixed.astype(jnp.bfloat16)
        for one in range(head_pair):
            column = pl.multiple_of((t * head_pair + one) * 256, 256)
            attended_ref[:, pl.ds(column, 256)] = mixed[one * rows : (one + 1) * rows]

    attention(
        steps, roped_ref, kv_ref, bias_ref, (s_0, s_1), (most_0, most_1), top_ref, sum_ref, values_ref,
        begin, finish,
    )

    def settle(n, carry):
        pltpu.make_async_copy(arrived_ref.at[0, 0], key_pool.at[0], page_sem).wait()
        pltpu.make_async_copy(arrived_ref.at[0, 1], value_pool.at[0], page_sem).wait()
        return carry

    lax.fori_loop(0, placed, settle, 0)
    for copy in pool_stores:
        copy.start()
    weight_copy.wait()

    def project(n, carry):
        columns = pl.ds(pl.multiple_of(n * chunk, chunk), chunk)
        stage_ref[n] = jnp.dot(
            attended_ref[...], w_ref[:, columns], preferred_element_type=jnp.float32
        ).astype(jnp.bfloat16)
        pltpu.make_async_copy(stage_ref.at[n], hidden_ref.at[:, columns], out_sems.at[n]).start()
        return carry

    lax.fori_loop(0, chunks, project, 0)
    for n in range(chunks):
        pltpu.make_async_copy(
            stage_ref.at[n], hidden_ref.at[:, pl.ds(n * chunk, chunk)], out_sems.at[n]
        ).wait()
    for copy in pool_stores:
        copy.wait()


def far_part(page_table, lengths, cap, state, slots, weight, arrived, key_cache, value_cache):
    items, pair_rows, _ = state[0].shape
    rows = pair_rows // head_pair
    width = weight.shape[1]
    chunk = 512
    return pl.pallas_call(
        lambda *refs: far_kernel(cap, *refs),
        out_shape=(
            pltpu.HBM((rows, width), jnp.bfloat16),
            pltpu.HBM(key_cache.shape, jnp.bfloat16),
            pltpu.HBM(value_cache.shape, jnp.bfloat16),
        ),
        in_specs=[smem_spec] * 2 + [hbm_spec] * 11,
        out_specs=(hbm_spec,) * 3,
        scratch_shapes=state_shapes(items, rows)
        + working(rows, 2, 2)
        + [
            pltpu.VMEM((rows, weight.shape[0]), jnp.bfloat16),
            pltpu.VMEM(weight.shape, jnp.bfloat16),
            pltpu.VMEM((width // chunk, rows, chunk), jnp.bfloat16),
            pltpu.VMEM(key_cache.shape, jnp.bfloat16),
            pltpu.VMEM(value_cache.shape, jnp.bfloat16),
            pltpu.SemaphoreType.DMA((3, items)),
            pltpu.SemaphoreType.DMA,
            pltpu.SemaphoreType.DMA,
            pltpu.SemaphoreType.DMA((2,)),
            pltpu.SemaphoreType.DMA,
            pltpu.SemaphoreType.DMA((width // chunk,)),
        ],
        compiler_params=params(large_limit),
        cost_estimate=cost(items, rows, 1536),
        name="attend_far",
    )(page_table, lengths, *in_hbm(*state, *slots, weight, arrived, key_cache, value_cache))


def after(value, *others):
    return lax.optimization_barrier((value,) + others)[0]


def body(queries, new_keys, new_values, key_cache, value_cache, out_weight, lengths, page_table):
    blk_count = lax.axis_size("blk")
    pages = key_cache.shape[0]
    window_pages = page_table.shape[1] // 2
    cap = (window_pages + blk_count - 1) // blk_count

    def other_core(value):
        return lax.ppermute(value, "group", [(0, 1), (1, 0), (2, 3), (3, 2)])

    def other_chip(value):
        return lax.ppermute(value, "group", [(0, 2), (2, 0), (1, 3), (3, 1)])

    picked = pick_old(page_table, cap, key_cache, value_cache)
    old = lax.all_to_all(picked, "blk", split_axis=0, concat_axis=0, tiled=True)
    old = old.reshape((blk_count * cap,) + old.shape[2:])

    fresh, cosine, sine = rotate_keys(lengths, new_keys[0], new_values[0])
    fresh_far = other_chip(fresh)
    fresh_core = other_core(fresh)
    roped, acc, stat = diagonal_part(after(queries[0], picked), cosine, sine, fresh)

    old = sort_old(after(page_table, stat), blk_count, cap, pages, old)
    old_far = other_chip(old)
    old_core = other_core(old)
    fresh_far_core = other_core(fresh_far)
    new = pick_new(page_table, blk_count, cap, pages, (fresh, fresh_core, fresh_far, fresh_far_core))
    arrived = lax.all_to_all(new, "blk", split_axis=0, concat_axis=0, tiled=True)
    acc, stat = near_part(
        after(lengths, new), (roped, acc, stat), (fresh_core, fresh_far, fresh_far_core, old, old_core)
    )
    old_far_core = other_core(old_far)
    hidden, key_out, value_out = far_part(
        page_table, lengths, cap, (roped, acc, stat), (old, old_core, old_far, old_far_core),
        out_weight, arrived, key_cache, value_cache,
    )
    return (hidden[None], key_out, value_out)


def solution(mesh):
    return jax.shard_map(
        body,
        mesh=mesh,
        in_specs=(
            P("blk", "group", None),
            P("blk", "group", None),
            P("blk", "group", None),
            P("blk", "group", None),
            P("blk", "group", None),
            P(),
            P(),
            P(),
        ),
        out_specs=(P("blk", "group", None), P("blk", "group", None), P("blk", "group", None)),
        check_vma=False,
    )
```

time: 123 us -> 98.5 us (0.80)
  the two profiles are of different devices: /device:TPU:0 before, /device:TPU:7 now
where the time goes in v2:
time: 98.5 us; the launch traced here: 97.9 us
  Pallas kernels  60.8 us (62%)
  starting transfers between devices  16.9 us (17%)
  waiting for transfers between devices  13.5 us (14%)
  local copies, waits for them, and re-layouts  5.62 us (6%)
    pallas_call x1, Pallas kernels, near_part(): pl.pallas_call(near_kernel, out_shape=state_out(items, rows), in_specs=[s...  22.4 us
    pallas_call x1, Pallas kernels, far_part(): pl.pallas_call(lambda *refs: far_kernel(cap, *refs), out_shape=(pltpu.HBM...  20.3 us
    ppermute x2, waiting for transfers between devices, other_chip(): return lax.ppermute(value, 'group', [(0, 2), (2, 0), (1, 3), (3, 1)])  13.5 us
    pallas_call x1, Pallas kernels, diagonal_part(): pl.pallas_call(diagonal_kernel, out_shape=(pltpu.HBM((items, head_pair *...  9.66 us
    all_to_all x1, starting transfers between devices, body(): old = lax.all_to_all(picked, 'blk', split_axis=0, concat_axis=0, tiled=True)  5.79 us
    unnamed x34, local copies, waits for them, and re-layouts  5.62 us
    all_to_all x1, starting transfers between devices, body(): lax.all_to_all(new, 'blk', split_axis=0, concat_axis=0, tiled=True)  5.46 us
    ppermute x4, starting transfers between devices, other_core(): return lax.ppermute(value, 'group', [(0, 1), (1, 0), (2, 3), (3, 2)])  5.15 us
  transfers between devices with their start and end apart: 8, of which 2 were waited for; matrix products, arithmetic and copies ran while one was open for 0% of the time, Pallas kernels for 39%

profile of v2, /device:TPU:7, one launch (start us, length us, event | category | flops | bytes accessed | tf_op | source)
XLA Modules:
  0.0 97.9 jit_solution(280726239176107147)
XLA Ops:
  0.6 0.0 copy-start.2
  0.6 0.0 copy-start.3
  0.7 0.0 copy-start.4
  0.7 0.7 copy-done.4
  1.4 0.0 copy-start.6
  1.4 0.0 copy-start.7
  1.4 2.8 %pick_old.1 = bf16[8,2,2,32,256]{4,3,2,1,0:T(8,128)(2,1)} custom-call(s32[8,32]{1,0:T(8,128)S(1)} %copy-done.4, bf16[40,32,256]{2,1,0:T(8,128)(2,1)} %refs_11_.1, bf16[40,32,256]{2,1,0:T(8,128)(2,1)} %refs_12_.1), custom_call_target="tpu_custom_call" | custom-call | tf_op jit(solution)/shard_map/pick_old/pallas_call | solution.py:61
  4.2 5.8 %all-to-all-start = ((bf16[8,2,2,32,256]{4,3,2,1,0:T(8,128)(2,1)}), bf16[8,2,2,32,256]{4,3,2,1,0:T(8,128)(2,1)S(1)}, u32[]{:S(2)}, u32[]{:S(2)}) async-start(bf16[8,2,2,32,256]{4,3,2,1,0:T(8,128)(2,1)} %pick_old.1), calls=%async_computation | async-start | bytes 1048576 | tf_op jit(solution)/shard_map/all_to_all | solution.py:667
  9.9 0.0 copy-done.2
  9.9 0.0 copy-done.3
  10.0 0.0 copy-done.6
  10.0 0.0 copy-done.7
  10.0 1.7 %rotate_keys.1 = (bf16[16,2,32,256]{3,2,1,0:T(8,128)(2,1)S(1)}, f32[512,128]{1,0:T(8,128)S(1)}, f32[512,128]{1,0:T(8,128)S(1)}) custom-call(s32[8]{0:T(128)S(1)} %copy-done.6, f32[1,128]{1,0:T(1,128)S(1)} %copy-done.7, bf16[512,256]{1,0:T(8,128)(2,1)S(1)} %bitcast.5, bf16[512,256]{1,0:T(8,128)(2,1)S(1)} %bitcast.6), custom_call_target="tpu_custom_call" | custom-call | tf_op jit(solution)/shard_map/rotate_keys/pallas_call | solution.py:116
  11.6 0.0 copy-start.8
  11.6 0.7 copy-done.8
  12.3 0.0 copy-start.9
  12.3 0.7 copy-done.9
  13.0 0.0 copy-start
  13.0 0.2 collective-permute-start.1
  13.3 1.5 %collective-permute-start = (bf16[16,2,32,256]{3,2,1,0:T(8,128)(2,1)S(1)}, bf16[16,2,32,256]{3,2,1,0:T(8,128)(2,1)S(1)}, u32[]{:S(2)}, u32[]{:S(2)}) collective-permute-start(bf16[16,2,32,256]{3,2,1,0:T(8,128)(2,1)S(1)} %get-tuple-element.20.own_ref.refs_1_), channel_id=1, source_target_pairs={{0,1},{1,0},{2,3},{3,2},{4,5},{5,4},{6,7},{7,6},{8,9},{9,8},{10,11... | collective-permute-start | bytes 1572872 | tf_op jit(solution)/shard_map/ppermute | solution.py:661
  14.8 10.4 %collective-permute-done.1.refs_3_.far_ref = bf16[16,2,32,256]{3,2,1,0:T(8,128)(2,1)S(1)} collective-permute-done((bf16[16,2,32,256]{3,2,1,0:T(8,128)(2,1)S(1)}, bf16[16,2,32,256]{3,2,1,0:T(8,128)(2,1)S(1)}, u32[]{:S(2)}, u32[]{:S(2)}) %collective-permute-start.1) | collective-permute-done | bytes 524320 | tf_op jit(solution)/shard_map/ppermute | solution.py:664
  25.2 0.0 copy-start.11
  25.2 2.2 %collective-permute-start.2 = (bf16[16,2,32,256]{3,2,1,0:T(8,128)(2,1)S(1)}, bf16[16,2,32,256]{3,2,1,0:T(8,128)(2,1)S(1)}, u32[]{:S(2)}, u32[]{:S(2)}) collective-permute-start(bf16[16,2,32,256]{3,2,1,0:T(8,128)(2,1)S(1)} %collective-permute-done.1.refs_3_.far_ref), channel_id=1, source_target_pairs={{0,1},{1,0},{2,3},{3,2},{4,5},{5,4},{6,7},{7,6},{8,9},{9,8},{10,11... | collective-permute-start | bytes 1572872 | tf_op jit(solution)/shard_map/ppermute | solution.py:661
  27.4 0.0 copy-done
  27.4 0.0 copy-start.5
  27.4 9.7 %attend_diagonal.1 = (bf16[5,1024,256]{2,1,0:T(8,128)(2,1)}, f32[5,1024,256]{2,1,0:T(8,128)}, f32[5,1024,128]{2,1,0:T(8,128)}) custom-call(bf16[512,2560]{1,0:T(8,128)(2,1)} %bitcast.8, f32[512,128]{1,0:T(8,128)} %copy-done.8, f32[512,128]{1,0:T(8,128)} %copy-done.9, bf16[16,2,32,256]{3,2,1,0:T(8,128)(2,1)} %copy-done), custom_call_target="tpu_custom_call" | custom-call | flops 2684354560 | bytes 16777216 | tf_op jit(solution)/shard_map/attend_diagonal/pallas_call | solution.py:371
  37.1 0.0 copy-done.11
  37.1 0.0 all-to-all-done
  37.1 0.0 copy-start.10
  37.1 0.8 copy-done.10
  37.9 0.0 copy-done.5
  37.9 1.6 %sort_old.1.old_ref.refs_5_ = bf16[16,2,32,256]{3,2,1,0:T(8,128)(2,1)S(1)} custom-call(s32[8,32]{1,0:T(8,128)S(1)} %copy-done.5, bf16[16,2,32,256]{3,2,1,0:T(8,128)(2,1)} %bitcast.7), custom_call_target="tpu_custom_call" | custom-call | tf_op jit(solution)/shard_map/sort_old/pallas_call | solution.py:139
  39.5 0.0 copy-start.1
  39.5 0.3 collective-permute-start.4
  39.8 0.5 collective-permute-start.3
  40.3 0.0 collective-permute-done.refs_2_.core_ref
  40.3 0.0 copy-start.12
  40.3 0.0 collective-permute-done.2.refs_4_.far_core_ref
  40.3 0.8 copy-done.12
  41.1 0.0 copy-start.13
  41.1 0.8 copy-done.13
  41.9 2.5 %pick_new.1 = bf16[16,2,32,256]{3,2,1,0:T(8,128)(2,1)} custom-call(s32[8,32]{1,0:T(8,128)S(1)} %copy-done.5, bf16[16,2,32,256]{3,2,1,0:T(8,128)(2,1)} %copy-done, bf16[16,2,32,256]{3,2,1,0:T(8,128)(2,1)} %copy-done.12, bf16[16,2,32,256]{3,2,1,0:T(8,128)(2,1)} %copy-done.11, bf16[16,2,32,256]{3,2,1,0:T(8,128)(2,1)} %copy-done.13), custom_call_target="tpu_custom_call" | custom-call | tf_op jit(solution)/shard_map/pick_new/pallas_call | solution.py:168
  44.4 5.5 %all-to-all-start.1 = ((bf16[16,2,32,256]{3,2,1,0:T(8,128)(2,1)}), bf16[16,2,32,256]{3,2,1,0:T(8,128)(2,1)S(1)}, u32[]{:S(2)}, u32[]{:S(2)}) async-start(bf16[16,2,32,256]{3,2,1,0:T(8,128)(2,1)} %pick_new.1), calls=%async_computation.1 | async-start | bytes 1048576 | tf_op jit(solution)/shard_map/all_to_all | solution.py:680
  49.9 3.1 %collective-permute-done.4.refs_7_ = bf16[16,2,32,256]{3,2,1,0:T(8,128)(2,1)S(1)} collective-permute-done((bf16[16,2,32,256]{3,2,1,0:T(8,128)(2,1)S(1)}, bf16[16,2,32,256]{3,2,1,0:T(8,128)(2,1)S(1)}, u32[]{:S(2)}, u32[]{:S(2)}) %collective-permute-start.4) | collective-permute-done | bytes 524320 | tf_op jit(solution)/shard_map/ppermute | solution.py:664
  52.9 0.0 copy-start.15
  52.9 1.0 %collective-permute-start.5 = (bf16[16,2,32,256]{3,2,1,0:T(8,128)(2,1)S(1)}, bf16[16,2,32,256]{3,2,1,0:T(8,128)(2,1)S(1)}, u32[]{:S(2)}, u32[]{:S(2)}) collective-permute-start(bf16[16,2,32,256]{3,2,1,0:T(8,128)(2,1)S(1)} %collective-permute-done.4.refs_7_), channel_id=1, source_target_pairs={{0,1},{1,0},{2,3},{3,2},{4,5},{5,4},{6,7},{7,6},{8,9},{9,8},{10,11... | collective-permute-start | bytes 1572872 | tf_op jit(solution)/shard_map/ppermute | solution.py:661
  53.9 0.0 collective-permute-done.3.old_core_ref.refs_6_
  53.9 0.0 copy-done.1
  53.9 22.4 %attend_near.1 = (f32[5,1024,256]{2,1,0:T(8,128)}, f32[5,1024,128]{2,1,0:T(8,128)}) custom-call(s32[8]{0:T(128)} %refs_1_.1, bf16[5,1024,256]{2,1,0:T(8,128)(2,1)} %get-tuple-element.21.roped_in.refs_2_, f32[5,1024,256]{2,1,0:T(8,128)} %get-tuple-element.23.acc_in, f32[5,1024,128]{2,1,0:T(8,128)} %get-tuple-element.24.stat_in, ...), custom_call_target="tpu_custom_call" | custom-call | flops 5368709120 | bytes 16777216 | tf_op jit(solution)/shard_map/attend_near/pallas_call | solution.py:471
  76.3 0.0 copy-done.15
  76.3 0.0 all-to-all-done.1.refs_10_
  76.4 0.0 copy-start.14
  76.4 0.0 collective-permute-done.5.refs_8_
  76.4 0.0 copy-start.16
  76.4 0.8 copy-done.14
  77.2 0.3 copy-done.16
  77.4 20.3 %attend_far.1 = (bf16[512,2560]{1,0:T(8,128)(2,1)}, bf16[40,32,256]{2,1,0:T(8,128)(2,1)}, bf16[40,32,256]{2,1,0:T(8,128)(2,1)}) custom-call(s32[8,32]{1,0:T(8,128)} %refs_0_.4, s32[8]{0:T(128)} %refs_1_.1, bf16[5,1024,256]{2,1,0:T(8,128)(2,1)} %get-tuple-element.21.roped_in.refs_2_, f32[5,1024,256]{2,1,0:T(8,128)} %get-tuple-element.26.refs_3_, ...), custom_call_target="tpu_custom_call" | custom-call | flops 8053063680 | bytes 16777216 | tf_op jit(solution)/shard_map/attend_far/pallas_call | solution.py:620
Async XLA Ops:
  0.6 9.3 %copy-start.2 = (bf16[1,512,256]{2,1,0:T(8,128)(2,1)S(1)}, bf16[1,512,256]{2,1,0:T(8,128)(2,1)}, u32[]{:S(2)}) copy-start(bf16[1,512,256]{2,1,0:T(8,128)(2,1)} %param.10) | copy-start | bytes 786436
  0.6 9.3 %copy-start.3 = (bf16[1,512,256]{2,1,0:T(8,128)(2,1)S(1)}, bf16[1,512,256]{2,1,0:T(8,128)(2,1)}, u32[]{:S(2)}) copy-start(bf16[1,512,256]{2,1,0:T(8,128)(2,1)} %param.11) | copy-start | bytes 786436
  0.7 0.7 copy-start.4
  1.4 8.6 %copy-start.6 = (s32[8]{0:T(128)S(1)}, s32[8]{0:T(128)}, u32[]{:S(2)}) copy-start(s32[8]{0:T(128)} %refs_1_.1) | copy-start | bytes 100
  1.4 8.6 %copy-start.7 = (f32[1,128]{1,0:T(1,128)S(1)}, f32[1,128]{1,0:T(1,128)}, u32[]{:S(2)}) copy-start(f32[1,128]{1,0:T(1,128)} %constant.2.clone.freq_ref) | copy-start | bytes 1540
  4.2 32.9 %all-to-all-start = ((bf16[8,2,2,32,256]{4,3,2,1,0:T(8,128)(2,1)}), bf16[8,2,2,32,256]{4,3,2,1,0:T(8,128)(2,1)S(1)}, u32[]{:S(2)}, u32[]{:S(2)}) async-start(bf16[8,2,2,32,256]{4,3,2,1,0:T(8,128)(2,1)} %pick_old.1), calls=%async_computation | async-start | bytes 1048576 | tf_op jit(solution)/shard_map/all_to_all | solution.py:667
  11.6 0.7 copy-start.8
  12.3 0.7 copy-start.9
  13.0 14.3 %copy-start = (bf16[16,2,32,256]{3,2,1,0:T(8,128)(2,1)}, bf16[16,2,32,256]{3,2,1,0:T(8,128)(2,1)S(1)}, u32[]{:S(2)}) copy-start(bf16[16,2,32,256]{3,2,1,0:T(8,128)(2,1)S(1)} %get-tuple-element.20.own_ref.refs_1_) | copy-start | bytes 1572868
  13.0 12.2 %collective-permute-start.1 = (bf16[16,2,32,256]{3,2,1,0:T(8,128)(2,1)S(1)}, bf16[16,2,32,256]{3,2,1,0:T(8,128)(2,1)S(1)}, u32[]{:S(2)}, u32[]{:S(2)}) collective-permute-start(bf16[16,2,32,256]{3,2,1,0:T(8,128)(2,1)S(1)} %get-tuple-element.20.own_ref.refs_1_), channel_id=1, source_target_pairs={{0,2},{2,0},{1,3},{3,1},{4,6},{6,4},{5,7},{7,5},{8,10},{10,8},{9,1... | collective-permute-start | bytes 1572872 | tf_op jit(solution)/shard_map/ppermute | solution.py:664
  13.3 27.0 %collective-permute-start = (bf16[16,2,32,256]{3,2,1,0:T(8,128)(2,1)S(1)}, bf16[16,2,32,256]{3,2,1,0:T(8,128)(2,1)S(1)}, u32[]{:S(2)}, u32[]{:S(2)}) collective-permute-start(bf16[16,2,32,256]{3,2,1,0:T(8,128)(2,1)S(1)} %get-tuple-element.20.own_ref.refs_1_), channel_id=1, source_target_pairs={{0,1},{1,0},{2,3},{3,2},{4,5},{5,4},{6,7},{7,6},{8,9},{9,8},{10,11... | collective-permute-start | bytes 1572872 | tf_op jit(solution)/shard_map/ppermute | solution.py:661
  25.2 11.8 %copy-start.11 = (bf16[16,2,32,256]{3,2,1,0:T(8,128)(2,1)}, bf16[16,2,32,256]{3,2,1,0:T(8,128)(2,1)S(1)}, u32[]{:S(2)}) copy-start(bf16[16,2,32,256]{3,2,1,0:T(8,128)(2,1)S(1)} %collective-permute-done.1.refs_3_.far_ref) | copy-start | bytes 1572868
  25.2 15.1 %collective-permute-start.2 = (bf16[16,2,32,256]{3,2,1,0:T(8,128)(2,1)S(1)}, bf16[16,2,32,256]{3,2,1,0:T(8,128)(2,1)S(1)}, u32[]{:S(2)}, u32[]{:S(2)}) collective-permute-start(bf16[16,2,32,256]{3,2,1,0:T(8,128)(2,1)S(1)} %collective-permute-done.1.refs_3_.far_ref), channel_id=1, source_target_pairs={{0,1},{1,0},{2,3},{3,2},{4,5},{5,4},{6,7},{7,6},{8,9},{9,8},{10,11... | collective-permute-start | bytes 1572872 | tf_op jit(solution)/shard_map/ppermute | solution.py:661
  27.4 10.5 %copy-start.5 = (s32[8,32]{1,0:T(8,128)S(1)}, s32[8,32]{1,0:T(8,128)}, u32[]{:S(2)}) copy-start(s32[8,32]{1,0:T(8,128)} %refs_0_.4) | copy-start | bytes 3076
  37.1 0.8 copy-start.10
  39.5 14.4 %copy-start.1 = (bf16[16,2,32,256]{3,2,1,0:T(8,128)(2,1)}, bf16[16,2,32,256]{3,2,1,0:T(8,128)(2,1)S(1)}, u32[]{:S(2)}) copy-start(bf16[16,2,32,256]{3,2,1,0:T(8,128)(2,1)S(1)} %sort_old.1.old_ref.refs_5_) | copy-start | bytes 1572868
  39.5 13.4 %collective-permute-start.4 = (bf16[16,2,32,256]{3,2,1,0:T(8,128)(2,1)S(1)}, bf16[16,2,32,256]{3,2,1,0:T(8,128)(2,1)S(1)}, u32[]{:S(2)}, u32[]{:S(2)}) collective-permute-start(bf16[16,2,32,256]{3,2,1,0:T(8,128)(2,1)S(1)} %sort_old.1.old_ref.refs_5_), channel_id=1, source_target_pairs={{0,2},{2,0},{1,3},{3,1},{4,6},{6,4},{5,7},{7,5},{8,10},{10,8},{9,1... | collective-permute-start | bytes 1572872 | tf_op jit(solution)/shard_map/ppermute | solution.py:664
  39.8 14.1 %collective-permute-start.3 = (bf16[16,2,32,256]{3,2,1,0:T(8,128)(2,1)S(1)}, bf16[16,2,32,256]{3,2,1,0:T(8,128)(2,1)}, u32[]{:S(2)}, u32[]{:S(2)}) collective-permute-start(bf16[16,2,32,256]{3,2,1,0:T(8,128)(2,1)S(1)} %sort_old.1.old_ref.refs_5_), channel_id=1, source_target_pairs={{0,1},{1,0},{2,3},{3,2},{4,5},{5,4},{6,7},{7,6},{8,9},{9,8},{10,11... | collective-permute-start | bytes 1572872 | tf_op jit(solution)/shard_map/ppermute | solution.py:661
  40.3 0.8 copy-start.12
  41.1 0.8 copy-start.13
  44.4 31.9 %all-to-all-start.1 = ((bf16[16,2,32,256]{3,2,1,0:T(8,128)(2,1)}), bf16[16,2,32,256]{3,2,1,0:T(8,128)(2,1)S(1)}, u32[]{:S(2)}, u32[]{:S(2)}) async-start(bf16[16,2,32,256]{3,2,1,0:T(8,128)(2,1)} %pick_new.1), calls=%async_computation.1 | async-start | bytes 1048576 | tf_op jit(solution)/shard_map/all_to_all | solution.py:680
  52.9 23.4 %copy-start.15 = (bf16[16,2,32,256]{3,2,1,0:T(8,128)(2,1)}, bf16[16,2,32,256]{3,2,1,0:T(8,128)(2,1)S(1)}, u32[]{:S(2)}) copy-start(bf16[16,2,32,256]{3,2,1,0:T(8,128)(2,1)S(1)} %collective-permute-done.4.refs_7_) | copy-start | bytes 1572868
  52.9 23.4 %collective-permute-start.5 = (bf16[16,2,32,256]{3,2,1,0:T(8,128)(2,1)S(1)}, bf16[16,2,32,256]{3,2,1,0:T(8,128)(2,1)S(1)}, u32[]{:S(2)}, u32[]{:S(2)}) collective-permute-start(bf16[16,2,32,256]{3,2,1,0:T(8,128)(2,1)S(1)} %collective-permute-done.4.refs_7_), channel_id=1, source_target_pairs={{0,1},{1,0},{2,3},{3,2},{4,5},{5,4},{6,7},{7,6},{8,9},{9,8},{10,11... | collective-permute-start | bytes 1572872 | tf_op jit(solution)/shard_map/ppermute | solution.py:661
  76.4 0.8 copy-start.14
  76.4 1.1 %copy-start.16 = (bf16[16,2,32,256]{3,2,1,0:T(8,128)(2,1)}, bf16[16,2,32,256]{3,2,1,0:T(8,128)(2,1)S(1)}, u32[]{:S(2)}) copy-start(bf16[16,2,32,256]{3,2,1,0:T(8,128)(2,1)S(1)} %collective-permute-done.5.refs_8_) | copy-start | bytes 1572868

commit v3 on v2

--- a/solution.py
+++ b/solution.py
@@ -9,12 +9,13 @@
 masked_score = -1e30
 step_keys = 512
 step_slots = 16
+any_spec = pl.BlockSpec(memory_space=pl.ANY)
 hbm_spec = pl.BlockSpec(memory_space=pltpu.HBM)
 smem_spec = pl.BlockSpec(memory_space=pltpu.SMEM)
 vmem_spec = pl.BlockSpec(memory_space=pltpu.VMEM)
 small_limit = 16 * 1024 * 1024
 head_pair = 2
-large_limit = 56 * 1024 * 1024
+large_limit = 58 * 1024 * 1024
 
 
 def params(limit):
@@ -116,9 +117,9 @@
     return pl.pallas_call(
         rotate_kernel,
         out_shape=(
-            jax.ShapeDtypeStruct((rows // 32, 2, 32, head_dim), jnp.bfloat16),
-            jax.ShapeDtypeStruct((rows, 128), jnp.float32),
-            jax.ShapeDtypeStruct((rows, 128), jnp.float32),
+            pltpu.HBM((rows // 32, 2, 32, head_dim), jnp.bfloat16),
+            pltpu.HBM((rows, 128), jnp.float32),
+            pltpu.HBM((rows, 128), jnp.float32),
         ),
         in_specs=[smem_spec, vmem_spec, vmem_spec, vmem_spec],
         out_specs=(vmem_spec,) * 3,
@@ -168,7 +169,7 @@
     return pl.pallas_call(
         lambda *refs: pick_new_kernel(pages, cap, *refs),
         out_shape=jax.ShapeDtypeStruct((blk_count * cap,) + sources[0].shape[1:], jnp.bfloat16),
-        in_specs=[smem_spec] + [hbm_spec] * 4,
+        in_specs=[smem_spec] + [any_spec] * 4,
         out_specs=vmem_spec,
         scratch_shapes=[
             pltpu.SMEM((window,), jnp.int32),
@@ -177,7 +178,7 @@
         ],
         compiler_params=params(small_limit),
         name="pick_new",
-    )(page_table, *in_hbm(*sources))
+    )(page_table, *sources)
 
 
 def lane_fold(values, combine):
@@ -383,112 +384,12 @@
     )(*in_hbm(queries), cosine, sine, *in_hbm(own))
 
 
-def state_copies(t, sources, targets, sems):
-    return [
-        pltpu.make_async_copy(source.at[t], target.at[t], sems.at[number, t])
-        for number, (source, target) in enumerate(zip(sources, targets))
-    ]
-
-
-def near_kernel(
-    lengths_ref, roped_in, acc_in, stat_in, core_ref, far_ref, far_core_ref, old_ref, old_core_ref,
-    acc_out, stat_out,
-    roped_ref, acc_ref, stat_ref, kv_ref, s_0, s_1, most_0, most_1, top_ref, sum_ref, values_ref,
-    bias_ref, state_sems, sem, out_sem,
-):
-    group_index = lax.axis_index("group")
-    has_old = lengths_ref[lax.axis_index("blk")] > 0
-    items = roped_ref.shape[0]
-    rows = bias_ref.shape[1]
-    odd = group_index % 2
-    chip = group_index // 2
-    steps = jnp.where(has_old, 2 + chip, odd + 2 * chip)
-    olds = (old_ref, old_core_ref)
-
-    @pl.when(odd == 1)
-    def _():
-        fetch(core_ref, 0, kv_ref, 0, 16, sem)
-
-    @pl.when(has_old)
-    def _():
-        for block in range(4):
-
-            @pl.when((block == group_index) & (odd == 0))
-            def _(block=block):
-                fetch_pair(olds, 4 * block, kv_ref, 0, sem)
-
-            @pl.when(block > group_index)
-            def _(block=block):
-                fetch_pair(olds, 4 * block, kv_ref, 8 * (odd + block - group_index), sem)
-
-    @pl.when(chip == 1)
-    def _():
-        place = jnp.where(has_old, 16, 16 * odd)
-        fetch(far_ref, 0, kv_ref, place, 16, sem)
-        fetch(far_core_ref, 0, kv_ref, place + 16, 16, sem)
-
-    def copies(t):
-        return state_copies(t, (roped_in, stat_in, acc_in), (roped_ref, stat_ref, acc_ref), state_sems)
-
-    for t in range(items):
-        for copy in copies(t):
-            copy.start()
-    bias_ref[...] = jnp.zeros_like(bias_ref)
-
-    @pl.when(has_old & (odd == 0))
-    def _():
-        bias_ref[0, :, :256] = old_bias(rows, group_index)
-
-    wait_rows(kv_ref, steps, 3, sem)
-    lane = lax.broadcasted_iota(jnp.int32, stat_ref.shape[1:], 1)
-
-    def begin(t, most_ref):
-        for copy in copies(t):
-            copy.wait()
-        most_ref[...] = jnp.where(lane < 64, stat_ref[t], masked_score)
-
-    def finish(t):
-        stat = stat_ref[t]
-        top = top_ref[...]
-        factor = jnp.exp(stat[:, :1] - top)
-        sums = stat[:, 64:65] * factor + jnp.sum(sum_ref[...], axis=1, keepdims=True)
-        stat_ref[t] = jnp.where(lane < 64, top, sums)
-        acc_ref[t] = acc_ref[t] * join([factor, factor]) + values_ref[...]
-        pltpu.make_async_copy(acc_ref.at[t], acc_out.at[t], out_sem).start()
-        pltpu.make_async_copy(stat_ref.at[t], stat_out.at[t], out_sem).start()
-
-    attention(
-        steps, roped_ref, kv_ref, bias_ref, (s_0, s_1), (most_0, most_1), top_ref, sum_ref, values_ref,
-        begin, finish,
-    )
-    pltpu.make_async_copy(acc_ref, acc_out, out_sem).wait()
-    pltpu.make_async_copy(stat_ref, stat_out, out_sem).wait()
-
-
-def near_part(lengths, state, slots):
-    items, pair_rows, _ = state[0].shape
-    rows = pair_rows // head_pair
-    return pl.pallas_call(
-        near_kernel,
-        out_shape=state_out(items, rows),
-        in_specs=[smem_spec] + [hbm_spec] * 8,
-        out_specs=(hbm_spec,) * 2,
-        scratch_shapes=state_shapes(items, rows)
-        + working(rows, 3, 2)
-        + [pltpu.SemaphoreType.DMA((3, items))]
-        + [pltpu.SemaphoreType.DMA] * 2,
-        compiler_params=params(large_limit),
-        cost_estimate=cost(items, rows, 1024),
-        name="attend_near",
-    )(lengths, *in_hbm(*state, *slots))
-
-
-def far_kernel(
-    cap, table_ref, lengths_ref, roped_in, acc_in, stat_in, old_ref, old_core_ref, far_ref, far_core_ref,
-    weight_ref, arrived_ref, key_ref, value_ref,
+def rest_kernel(
+    cap, table_ref, lengths_ref, roped_in, acc_in, stat_in, core_ref, far_ref, far_core_ref,
+    old_ref, old_core_ref, old_far_ref, old_far_core_ref, weight_ref, arrived_ref, key_ref, value_ref,
     hidden_ref, key_out_ref, value_out_ref,
     roped_ref, acc_ref, stat_ref, kv_ref, s_0, s_1, most_0, most_1, top_ref, sum_ref, values_ref,
-    bias_ref, attended_ref, w_ref, stage_ref, key_pool, value_pool,
+    bias_ref, w_ref, stage_ref, key_pool, value_pool,
     state_sems, sem, weight_sem, pool_sems, page_sem, out_sems,
 ):
     group_index = lax.axis_index("group")
@@ -497,13 +398,22 @@
     requests, slots = table_ref.shape
     items = roped_ref.shape[0]
     rows = bias_ref.shape[1]
-    chunks = stage_ref.shape[0]
     chunk = stage_ref.shape[2]
+    chunks = w_ref.shape[1] // chunk
     odd = group_index % 2
-    steps = jnp.where(has_old, 2 - group_index // 2, 0)
+    chip = group_index // 2
+    steps = jnp.where(has_old, 4, odd + 2 * chip)
+    base = jnp.where(has_old, 16, 0)
+    near = (old_ref, old_core_ref)
+    far = (old_far_ref, old_far_core_ref)
 
     def copies(t):
-        return state_copies(t, (roped_in, stat_in, acc_in), (roped_ref, stat_ref, acc_ref), state_sems)
+        return [
+            pltpu.make_async_copy(source.at[t], target.at[t], state_sems.at[number, t])
+            for number, (source, target) in enumerate(
+                ((roped_in, roped_ref), (stat_in, stat_ref), (acc_in, acc_ref))
+            )
+        ]
 
     pool_loads = [
         pltpu.make_async_copy(key_ref, key_pool, pool_sems.at[0]),
@@ -513,39 +423,44 @@
         pltpu.make_async_copy(key_pool, key_out_ref, pool_sems.at[0]),
         pltpu.make_async_copy(value_pool, value_out_ref, pool_sems.at[1]),
     ]
-    for copy in pool_loads:
+    for copy in copies(0):
         copy.start()
+
+    @pl.when(odd == 1)
+    def _():
+        fetch(core_ref, 0, kv_ref, base, 16, sem)
+
+    @pl.when(chip == 1)
+    def _():
+        place = base + 16 * jnp.where(has_old, 1, odd)
+        fetch(far_ref, 0, kv_ref, place, 16, sem)
+        fetch(far_core_ref, 0, kv_ref, place + 16, 16, sem)
 
     @pl.when(has_old)
     def _():
         for block in range(4):
 
-            @pl.when(block == group_index)
+            @pl.when(block >= group_index)
             def _(block=block):
-                fetch_pair((far_ref, far_core_ref), 4 * block, kv_ref, 0, sem)
-
-            @pl.when((block == group_index) & (odd == 1))
-            def _(block=block):
-                fetch_pair((old_ref, old_core_ref), 4 * block, kv_ref, 8, sem)
-
-            @pl.when(block > group_index)
-            def _(block=block):
-                place = 8 * (odd + block - group_index)
-                fetch_pair((far_ref, far_core_ref), 4 * block, kv_ref, place, sem)
-
-    for t in range(items):
+                gap = jnp.where(block == group_index, 0, odd)
+                place = 16 * (gap + block - group_index)
+                fetch_pair(near, 4 * block, kv_ref, place, sem)
+                fetch_pair(far, 4 * block, kv_ref, place + 8, sem)
+
+    for copy in pool_loads:
+        copy.start()
+    for t in range(1, items):
         for copy in copies(t):
             copy.start()
     weight_copy = pltpu.make_async_copy(weight_ref, w_ref, weight_sem)
     weight_copy.start()
 
-    bias_ref[1] = jnp.zeros(bias_ref.shape[1:], jnp.float32)
-    bias_ref[0, :, :256] = old_bias(rows, group_index ^ 2)
-    bias_ref[0, :, 256:] = jnp.zeros((rows, 256), jnp.float32)
-
-    @pl.when(odd == 1)
+    bias_ref[...] = jnp.zeros_like(bias_ref)
+
+    @pl.when(has_old)
     def _():
-        bias_ref[0, :, 256:] = old_bias(rows, group_index)
+        bias_ref[0, :, :256] = old_bias(rows, group_index)
+        bias_ref[0, :, 256:] = old_bias(rows, group_index ^ 2)
 
     for copy in pool_loads:
         copy.wait()
@@ -560,7 +475,7 @@
                 pltpu.make_async_copy(arrived_ref.at[slot, 0], key_pool.at[page], page_sem).start()
                 pltpu.make_async_copy(arrived_ref.at[slot, 1], value_pool.at[page], page_sem).start()
 
-    wait_rows(kv_ref, steps, 2, sem)
+    wait_rows(kv_ref, steps, 4, sem)
     lane = lax.broadcasted_iota(jnp.int32, stat_ref.shape[1:], 1)
 
     def begin(t, most_ref):
@@ -575,10 +490,7 @@
         inverse = 1.0 / sums
         old = factor * inverse
         mixed = acc_ref[t] * join([old, old]) + values_ref[...] * join([inverse, inverse])
-        mixed = mixed.astype(jnp.bfloat16)
-        for one in range(head_pair):
-            column = pl.multiple_of((t * head_pair + one) * 256, 256)
-            attended_ref[:, pl.ds(column, 256)] = mixed[one * rows : (one + 1) * rows]
+        roped_ref[t] = mixed.astype(jnp.bfloat16)
 
     attention(
         steps, roped_ref, kv_ref, bias_ref, (s_0, s_1), (most_0, most_1), top_ref, sum_ref, values_ref,
@@ -595,43 +507,55 @@
         copy.start()
     weight_copy.wait()
 
+    def out_copy(n, columns):
+        return pltpu.make_async_copy(stage_ref.at[n % 2], hidden_ref.at[:, columns], out_sems.at[n % 2])
+
     def project(n, carry):
         columns = pl.ds(pl.multiple_of(n * chunk, chunk), chunk)
-        stage_ref[n] = jnp.dot(
-            attended_ref[...], w_ref[:, columns], preferred_element_type=jnp.float32
+
+        @pl.when(n >= 2)
+        def _():
+            out_copy(n, columns).wait()
+
+        attended = join(
+            [
+                roped_ref[t, one * rows : (one + 1) * rows, :]
+                for t in range(items)
+                for one in range(head_pair)
+            ]
+        )
+        stage_ref[n % 2] = jnp.dot(
+            attended, w_ref[:, columns], preferred_element_type=jnp.float32
         ).astype(jnp.bfloat16)
-        pltpu.make_async_copy(stage_ref.at[n], hidden_ref.at[:, columns], out_sems.at[n]).start()
+        out_copy(n, columns).start()
         return carry
 
     lax.fori_loop(0, chunks, project, 0)
-    for n in range(chunks):
-        pltpu.make_async_copy(
-            stage_ref.at[n], hidden_ref.at[:, pl.ds(n * chunk, chunk)], out_sems.at[n]
-        ).wait()
+    for n in range(2):
+        out_copy(n, pl.ds(0, chunk)).wait()
     for copy in pool_stores:
         copy.wait()
 
 
-def far_part(page_table, lengths, cap, state, slots, weight, arrived, key_cache, value_cache):
+def rest_part(page_table, lengths, cap, state, slots, weight, arrived, key_cache, value_cache):
     items, pair_rows, _ = state[0].shape
     rows = pair_rows // head_pair
     width = weight.shape[1]
     chunk = 512
     return pl.pallas_call(
-        lambda *refs: far_kernel(cap, *refs),
+        lambda *refs: rest_kernel(cap, *refs),
         out_shape=(
             pltpu.HBM((rows, width), jnp.bfloat16),
             pltpu.HBM(key_cache.shape, jnp.bfloat16),
             pltpu.HBM(value_cache.shape, jnp.bfloat16),
         ),
-        in_specs=[smem_spec] * 2 + [hbm_spec] * 11,
+        in_specs=[smem_spec] * 2 + [hbm_spec] * 3 + [any_spec] * 7 + [hbm_spec] * 4,
         out_specs=(hbm_spec,) * 3,
         scratch_shapes=state_shapes(items, rows)
-        + working(rows, 2, 2)
+        + working(rows, 4, 2)
         + [
-            pltpu.VMEM((rows, weight.shape[0]), jnp.bfloat16),
             pltpu.VMEM(weight.shape, jnp.bfloat16),
-            pltpu.VMEM((width // chunk, rows, chunk), jnp.bfloat16),
+            pltpu.VMEM((2, rows, chunk), jnp.bfloat16),
             pltpu.VMEM(key_cache.shape, jnp.bfloat16),
             pltpu.VMEM(value_cache.shape, jnp.bfloat16),
             pltpu.SemaphoreType.DMA((3, items)),
@@ -639,12 +563,12 @@
             pltpu.SemaphoreType.DMA,
             pltpu.SemaphoreType.DMA((2,)),
             pltpu.SemaphoreType.DMA,
-            pltpu.SemaphoreType.DMA((width // chunk,)),
+            pltpu.SemaphoreType.DMA((2,)),
         ],
         compiler_params=params(large_limit),
-        cost_estimate=cost(items, rows, 1536),
-        name="attend_far",
-    )(page_table, lengths, *in_hbm(*state, *slots, weight, arrived, key_cache, value_cache))
+        cost_estimate=cost(items, rows, 2560),
+        name="attend_rest",
+    )(page_table, lengths, *in_hbm(*state), *slots, *in_hbm(weight, arrived, key_cache, value_cache))
 
 
 def after(value, *others):
@@ -675,15 +599,13 @@
     old = sort_old(after(page_table, stat), blk_count, cap, pages, old)
     old_far = other_chip(old)
     old_core = other_core(old)
-    fresh_far_core = other_core(fresh_far)
+    fresh_far_core = other_core(after(fresh_far, stat))
     new = pick_new(page_table, blk_count, cap, pages, (fresh, fresh_core, fresh_far, fresh_far_core))
     arrived = lax.all_to_all(new, "blk", split_axis=0, concat_axis=0, tiled=True)
-    acc, stat = near_part(
-        after(lengths, new), (roped, acc, stat), (fresh_core, fresh_far, fresh_far_core, old, old_core)
-    )
-    old_far_core = other_core(old_far)
-    hidden, key_out, value_out = far_part(
-        page_table, lengths, cap, (roped, acc, stat), (old, old_core, old_far, old_far_core),
+    old_far_core = other_core(after(old_far, new))
+    hidden, key_out, value_out = rest_part(
+        page_table, lengths, cap, (roped, acc, stat),
+        (fresh_core, fresh_far, fresh_far_core, old, old_core, old_far, old_far_core),
         out_weight, arrived, key_cache, value_cache,
     )
     return (hidden[None], key_out, value_out)

time: 98.5 us -> 89.4 us (0.908)
  the two profiles are of different devices: /device:TPU:7 before, /device:TPU:2 now
where the time goes in v3:
time: 89.4 us; the launch traced here: 88.9 us
  Pallas kernels  54 us (60%)
  waiting for transfers between devices  16.3 us (18%)
  starting transfers between devices  15.5 us (17%)
  local copies, waits for them, and re-layouts  2.36 us (3%)
    pallas_call x1, Pallas kernels, rest_part(): pl.pallas_call(lambda *refs: rest_kernel(cap, *refs), out_shape=(pltpu.HB...  35.1 us
    pallas_call x1, Pallas kernels, diagonal_part(): pl.pallas_call(diagonal_kernel, out_shape=(pltpu.HBM((items, head_pair *...  9.78 us
    all_to_all x1, waiting for transfers between devices, body(): lax.all_to_all(new, 'blk', split_axis=0, concat_axis=0, tiled=True)  9.78 us
    ppermute x2, waiting for transfers between devices, other_chip(): return lax.ppermute(value, 'group', [(0, 2), (2, 0), (1, 3), (3, 1)])  6.49 us
    all_to_all x1, starting transfers between devices, body(): old = lax.all_to_all(picked, 'blk', split_axis=0, concat_axis=0, tiled=True)  6.35 us
    all_to_all x1, starting transfers between devices, body(): lax.all_to_all(new, 'blk', split_axis=0, concat_axis=0, tiled=True)  6.01 us
    ppermute x2, starting transfers between devices, other_chip(): return lax.ppermute(value, 'group', [(0, 2), (2, 0), (1, 3), (3, 1)])  3.1 us
    pallas_call x1, Pallas kernels, pick_old(): pl.pallas_call(pick_old_kernel, out_shape=jax.ShapeDtypeStruct((requests,...  2.75 us
  transfers between devices with their start and end apart: 8, of which 3 were waited for; matrix products, arithmetic and copies ran while one was open for 0% of the time, Pallas kernels for 18%

profile of v3, /device:TPU:2, one launch (start us, length us, event | category | flops | bytes accessed | tf_op | source)
XLA Modules:
  0.0 88.9 jit_solution(12864184105213747036)
XLA Ops:
  0.6 0.0 copy-start.6
  0.6 0.0 copy-start.5
  0.7 0.0 copy-start.7
  0.7 0.7 copy-done.7
  1.4 0.0 copy-start.9
  1.4 0.0 copy-start.10
  1.4 2.8 %pick_old.1 = bf16[8,2,2,32,256]{4,3,2,1,0:T(8,128)(2,1)} custom-call(s32[8,32]{1,0:T(8,128)S(1)} %copy-done.7, bf16[40,32,256]{2,1,0:T(8,128)(2,1)} %refs_14_.1, bf16[40,32,256]{2,1,0:T(8,128)(2,1)} %refs_15_.1), custom_call_target="tpu_custom_call" | custom-call | tf_op jit(solution)/shard_map/pick_old/pallas_call | solution.py:62
  4.2 6.3 %all-to-all-start = ((bf16[8,2,2,32,256]{4,3,2,1,0:T(8,128)(2,1)}), bf16[8,2,2,32,256]{4,3,2,1,0:T(8,128)(2,1)S(1)}, u32[]{:S(2)}, u32[]{:S(2)}) async-start(bf16[8,2,2,32,256]{4,3,2,1,0:T(8,128)(2,1)} %pick_old.1), calls=%async_computation | async-start | bytes 1048576 | tf_op jit(solution)/shard_map/all_to_all | solution.py:591
  10.5 0.0 copy-done.6
  10.5 0.0 copy-done.5
  10.5 0.0 copy-done.9
  10.5 0.0 copy-done.10
  10.5 2.5 %rotate_keys.1 = (bf16[16,2,32,256]{3,2,1,0:T(8,128)(2,1)}, f32[512,128]{1,0:T(8,128)}, f32[512,128]{1,0:T(8,128)}) custom-call(s32[8]{0:T(128)S(1)} %copy-done.9, f32[1,128]{1,0:T(1,128)S(1)} %copy-done.10, bf16[512,256]{1,0:T(8,128)(2,1)S(1)} %bitcast.5, bf16[512,256]{1,0:T(8,128)(2,1)S(1)} %bitcast.6), custom_call_target="tpu_custom_call" | custom-call | tf_op jit(solution)/shard_map/rotate_keys/pallas_call | solution.py:117
  13.0 1.5 %collective-permute-start.1 = (bf16[16,2,32,256]{3,2,1,0:T(8,128)(2,1)}, bf16[16,2,32,256]{3,2,1,0:T(8,128)(2,1)S(1)}, u32[]{:S(2)}, u32[]{:S(2)}) collective-permute-start(bf16[16,2,32,256]{3,2,1,0:T(8,128)(2,1)} %get-tuple-element.19.own_ref.refs_1_), channel_id=1, source_target_pairs={{0,2},{2,0},{1,3},{3,1},{4,6},{6,4},{5,7},{7,5},{8,10},{10,8},{9,1... | collective-permute-start | bytes 1572872 | tf_op jit(solution)/shard_map/ppermute | solution.py:588
  14.5 0.0 collective-permute-start
  14.5 0.0 copy-start.8
  14.5 0.0 copy-start.3
  14.5 9.8 %attend_diagonal.1 = (bf16[5,1024,256]{2,1,0:T(8,128)(2,1)}, f32[5,1024,256]{2,1,0:T(8,128)}, f32[5,1024,128]{2,1,0:T(8,128)}) custom-call(bf16[512,2560]{1,0:T(8,128)(2,1)} %bitcast.8, f32[512,128]{1,0:T(8,128)} %get-tuple-element.17.cos_ref, f32[512,128]{1,0:T(8,128)} %get-tuple-element.18.sin_ref, bf16[16,2,32,256]{3,2,1,0:T(8,128)(2,1)} %get-tuple-element.19.own_ref.refs_1_), custom_call_target="tpu_custom_call" | custom-call | flops 2684354560 | bytes 16777216 | tf_op jit(solution)/shard_map/attend_diagonal/pallas_call | solution.py:372
  24.3 2.0 %collective-permute-done.1.refs_3_.refs_6_ = bf16[16,2,32,256]{3,2,1,0:T(8,128)(2,1)S(1)} collective-permute-done((bf16[16,2,32,256]{3,2,1,0:T(8,128)(2,1)}, bf16[16,2,32,256]{3,2,1,0:T(8,128)(2,1)S(1)}, u32[]{:S(2)}, u32[]{:S(2)}) %collective-permute-start.1) | collective-permute-done | bytes 524320 | tf_op jit(solution)/shard_map/ppermute | solution.py:588
  26.3 0.0 copy-start
  26.3 0.0 collective-permute-start.2
  26.3 0.0 all-to-all-done
  26.3 0.0 copy-start.11
  26.3 0.8 copy-done.11
  27.1 0.0 copy-done.8
  27.1 1.6 %sort_old.1.refs_8_ = bf16[16,2,32,256]{3,2,1,0:T(8,128)(2,1)S(1)} custom-call(s32[8,32]{1,0:T(8,128)S(1)} %copy-done.8, bf16[16,2,32,256]{3,2,1,0:T(8,128)(2,1)} %bitcast.7), custom_call_target="tpu_custom_call" | custom-call | tf_op jit(solution)/shard_map/sort_old/pallas_call | solution.py:140
  28.8 0.0 copy-start.4
  28.8 1.6 %collective-permute-start.4 = (bf16[16,2,32,256]{3,2,1,0:T(8,128)(2,1)S(1)}, bf16[16,2,32,256]{3,2,1,0:T(8,128)(2,1)S(1)}, u32[]{:S(2)}, u32[]{:S(2)}) collective-permute-start(bf16[16,2,32,256]{3,2,1,0:T(8,128)(2,1)S(1)} %sort_old.1.refs_8_), channel_id=1, source_target_pairs={{0,2},{2,0},{1,3},{3,1},{4,6},{6,4},{5,7},{7,5},{8,10},{10,8},{9,1... | collective-permute-start | bytes 1572872 | tf_op jit(solution)/shard_map/ppermute | solution.py:588
  30.4 0.0 collective-permute-done.refs_2_.refs_5_
  30.4 0.0 copy-start.1
  30.4 0.0 collective-permute-done.2.refs_4_.refs_7_
  30.4 0.0 copy-done.3
  30.4 0.0 copy-start.2
  30.4 2.2 %pick_new.1 = bf16[16,2,32,256]{3,2,1,0:T(8,128)(2,1)} custom-call(s32[8,32]{1,0:T(8,128)S(1)} %copy-done.8, bf16[16,2,32,256]{3,2,1,0:T(8,128)(2,1)S(1)} %copy-done.3, bf16[16,2,32,256]{3,2,1,0:T(8,128)(2,1)S(1)} %collective-permute-done.refs_2_.refs_5_, bf16[16,2,32,256]{3,2,1,0:T(8,128)(2,1)S(1)} %collective-permute-done.1.refs_3_.refs_6_, ...), custom_call_target="tpu_custom_call" | custom-call | tf_op jit(solution)/shard_map/pick_new/pallas_call | solution.py:169
  32.6 6.0 %all-to-all-start.1 = ((bf16[16,2,32,256]{3,2,1,0:T(8,128)(2,1)}), bf16[16,2,32,256]{3,2,1,0:T(8,128)(2,1)S(1)}, u32[]{:S(2)}, u32[]{:S(2)}) async-start(bf16[16,2,32,256]{3,2,1,0:T(8,128)(2,1)} %pick_new.1), calls=%async_computation.1 | async-start | bytes 1048576 | tf_op jit(solution)/shard_map/all_to_all | solution.py:604
  38.7 0.0 collective-permute-start.3
  38.7 4.5 %collective-permute-done.4.refs_10_ = bf16[16,2,32,256]{3,2,1,0:T(8,128)(2,1)S(1)} collective-permute-done((bf16[16,2,32,256]{3,2,1,0:T(8,128)(2,1)S(1)}, bf16[16,2,32,256]{3,2,1,0:T(8,128)(2,1)S(1)}, u32[]{:S(2)}, u32[]{:S(2)}) %collective-permute-start.4) | collective-permute-done | bytes 524320 | tf_op jit(solution)/shard_map/ppermute | solution.py:588
  43.2 0.0 copy-start.13
  43.2 0.0 collective-permute-start.5
  43.2 0.0 collective-permute-done.3.refs_9_
  43.2 9.8 %all-to-all-done.1.refs_13_ = bf16[16,2,32,256]{3,2,1,0:T(8,128)(2,1)S(1)} async-done(((bf16[16,2,32,256]{3,2,1,0:T(8,128)(2,1)}), bf16[16,2,32,256]{3,2,1,0:T(8,128)(2,1)S(1)}, u32[]{:S(2)}, u32[]{:S(2)}) %all-to-all-start.1) | async-done | bytes 524320 | tf_op jit(solution)/shard_map/all_to_all | solution.py:604
  52.9 0.0 copy-start.12
  52.9 0.0 collective-permute-done.5.refs_11_
  52.9 0.0 copy-done
  53.0 0.0 copy-done.4
  53.0 0.0 copy-done.1
  53.0 0.0 copy-done.2
  53.0 0.0 copy-done.13
  53.0 0.8 copy-done.12
  53.8 35.1 %attend_rest.1 = (bf16[512,2560]{1,0:T(8,128)(2,1)}, bf16[40,32,256]{2,1,0:T(8,128)(2,1)}, bf16[40,32,256]{2,1,0:T(8,128)(2,1)}) custom-call(s32[8,32]{1,0:T(8,128)} %refs_0_.4, s32[8]{0:T(128)} %refs_1_.1, bf16[5,1024,256]{2,1,0:T(8,128)(2,1)} %get-tuple-element.20.refs_2_, f32[5,1024,256]{2,1,0:T(8,128)} %get-tuple-element.21.refs_3_, ...), custom_call_target="tpu_custom_call" | custom-call | flops 13421772800 | bytes 16777216 | tf_op jit(solution)/shard_map/attend_rest/pallas_call | solution.py:545
Async XLA Ops:
  0.6 9.9 %copy-start.6 = (bf16[1,512,256]{2,1,0:T(8,128)(2,1)S(1)}, bf16[1,512,256]{2,1,0:T(8,128)(2,1)}, u32[]{:S(2)}) copy-start(bf16[1,512,256]{2,1,0:T(8,128)(2,1)} %param.11) | copy-start | bytes 786436
  0.6 9.9 %copy-start.5 = (bf16[1,512,256]{2,1,0:T(8,128)(2,1)S(1)}, bf16[1,512,256]{2,1,0:T(8,128)(2,1)}, u32[]{:S(2)}) copy-start(bf16[1,512,256]{2,1,0:T(8,128)(2,1)} %param.10) | copy-start | bytes 786436
  0.7 0.7 copy-start.7
  1.4 9.1 %copy-start.9 = (s32[8]{0:T(128)S(1)}, s32[8]{0:T(128)}, u32[]{:S(2)}) copy-start(s32[8]{0:T(128)} %refs_1_.1) | copy-start | bytes 100
  1.4 9.1 %copy-start.10 = (f32[1,128]{1,0:T(1,128)S(1)}, f32[1,128]{1,0:T(1,128)}, u32[]{:S(2)}) copy-start(f32[1,128]{1,0:T(1,128)} %constant.2.clone.freq_ref) | copy-start | bytes 1540
  4.2 22.1 %all-to-all-start = ((bf16[8,2,2,32,256]{4,3,2,1,0:T(8,128)(2,1)}), bf16[8,2,2,32,256]{4,3,2,1,0:T(8,128)(2,1)S(1)}, u32[]{:S(2)}, u32[]{:S(2)}) async-start(bf16[8,2,2,32,256]{4,3,2,1,0:T(8,128)(2,1)} %pick_old.1), calls=%async_computation | async-start | bytes 1048576 | tf_op jit(solution)/shard_map/all_to_all | solution.py:591
  13.0 13.3 %collective-permute-start.1 = (bf16[16,2,32,256]{3,2,1,0:T(8,128)(2,1)}, bf16[16,2,32,256]{3,2,1,0:T(8,128)(2,1)S(1)}, u32[]{:S(2)}, u32[]{:S(2)}) collective-permute-start(bf16[16,2,32,256]{3,2,1,0:T(8,128)(2,1)} %get-tuple-element.19.own_ref.refs_1_), channel_id=1, source_target_pairs={{0,2},{2,0},{1,3},{3,1},{4,6},{6,4},{5,7},{7,5},{8,10},{10,8},{9,1... | collective-permute-start | bytes 1572872 | tf_op jit(solution)/shard_map/ppermute | solution.py:588
  14.5 15.9 %collective-permute-start = (bf16[16,2,32,256]{3,2,1,0:T(8,128)(2,1)}, bf16[16,2,32,256]{3,2,1,0:T(8,128)(2,1)S(1)}, u32[]{:S(2)}, u32[]{:S(2)}) collective-permute-start(bf16[16,2,32,256]{3,2,1,0:T(8,128)(2,1)} %get-tuple-element.19.own_ref.refs_1_), channel_id=1, source_target_pairs={{0,1},{1,0},{2,3},{3,2},{4,5},{5,4},{6,7},{7,6},{8,9},{9,8},{10,11... | collective-permute-start | bytes 1572872 | tf_op jit(solution)/shard_map/ppermute | solution.py:585
  14.5 12.6 %copy-start.8 = (s32[8,32]{1,0:T(8,128)S(1)}, s32[8,32]{1,0:T(8,128)}, u32[]{:S(2)}) copy-start(s32[8,32]{1,0:T(8,128)} %refs_0_.4) | copy-start | bytes 3076
  14.5 15.9 %copy-start.3 = (bf16[16,2,32,256]{3,2,1,0:T(8,128)(2,1)S(1)}, bf16[16,2,32,256]{3,2,1,0:T(8,128)(2,1)}, u32[]{:S(2)}) copy-start(bf16[16,2,32,256]{3,2,1,0:T(8,128)(2,1)} %get-tuple-element.19.own_ref.refs_1_) | copy-start | bytes 1572868
  26.3 26.7 %copy-start = (bf16[16,2,32,256]{3,2,1,0:T(8,128)(2,1)}, bf16[16,2,32,256]{3,2,1,0:T(8,128)(2,1)S(1)}, u32[]{:S(2)}) copy-start(bf16[16,2,32,256]{3,2,1,0:T(8,128)(2,1)S(1)} %collective-permute-done.1.refs_3_.refs_6_) | copy-start | bytes 1572868
  26.3 4.1 %collective-permute-start.2 = (bf16[16,2,32,256]{3,2,1,0:T(8,128)(2,1)S(1)}, bf16[16,2,32,256]{3,2,1,0:T(8,128)(2,1)S(1)}, u32[]{:S(2)}, u32[]{:S(2)}) collective-permute-start(bf16[16,2,32,256]{3,2,1,0:T(8,128)(2,1)S(1)} %collective-permute-done.1.refs_3_.refs_6_), channel_id=1, source_target_pairs={{0,1},{1,0},{2,3},{3,2},{4,5},{5,4},{6,7},{7,6},{8,9},{9,8},{10,11... | collective-permute-start | bytes 1572872 | tf_op jit(solution)/shard_map/ppermute | solution.py:585
  26.3 0.8 copy-start.11
  28.8 24.2 %copy-start.4 = (bf16[16,2,32,256]{3,2,1,0:T(8,128)(2,1)}, bf16[16,2,32,256]{3,2,1,0:T(8,128)(2,1)S(1)}, u32[]{:S(2)}) copy-start(bf16[16,2,32,256]{3,2,1,0:T(8,128)(2,1)S(1)} %sort_old.1.refs_8_) | copy-start | bytes 1572868
  28.8 14.4 %collective-permute-start.4 = (bf16[16,2,32,256]{3,2,1,0:T(8,128)(2,1)S(1)}, bf16[16,2,32,256]{3,2,1,0:T(8,128)(2,1)S(1)}, u32[]{:S(2)}, u32[]{:S(2)}) collective-permute-start(bf16[16,2,32,256]{3,2,1,0:T(8,128)(2,1)S(1)} %sort_old.1.refs_8_), channel_id=1, source_target_pairs={{0,2},{2,0},{1,3},{3,1},{4,6},{6,4},{5,7},{7,5},{8,10},{10,8},{9,1... | collective-permute-start | bytes 1572872 | tf_op jit(solution)/shard_map/ppermute | solution.py:588
  30.4 22.6 %copy-start.1 = (bf16[16,2,32,256]{3,2,1,0:T(8,128)(2,1)}, bf16[16,2,32,256]{3,2,1,0:T(8,128)(2,1)S(1)}, u32[]{:S(2)}) copy-start(bf16[16,2,32,256]{3,2,1,0:T(8,128)(2,1)S(1)} %collective-permute-done.refs_2_.refs_5_) | copy-start | bytes 1572868
  30.4 22.6 %copy-start.2 = (bf16[16,2,32,256]{3,2,1,0:T(8,128)(2,1)}, bf16[16,2,32,256]{3,2,1,0:T(8,128)(2,1)S(1)}, u32[]{:S(2)}) copy-start(bf16[16,2,32,256]{3,2,1,0:T(8,128)(2,1)S(1)} %collective-permute-done.2.refs_4_.refs_7_) | copy-start | bytes 1572868
  32.6 20.3 %all-to-all-start.1 = ((bf16[16,2,32,256]{3,2,1,0:T(8,128)(2,1)}), bf16[16,2,32,256]{3,2,1,0:T(8,128)(2,1)S(1)}, u32[]{:S(2)}, u32[]{:S(2)}) async-start(bf16[16,2,32,256]{3,2,1,0:T(8,128)(2,1)} %pick_new.1), calls=%async_computation.1 | async-start | bytes 1048576 | tf_op jit(solution)/shard_map/all_to_all | solution.py:604
  38.7 4.5 %collective-permute-start.3 = (bf16[16,2,32,256]{3,2,1,0:T(8,128)(2,1)S(1)}, bf16[16,2,32,256]{3,2,1,0:T(8,128)(2,1)}, u32[]{:S(2)}, u32[]{:S(2)}) collective-permute-start(bf16[16,2,32,256]{3,2,1,0:T(8,128)(2,1)S(1)} %sort_old.1.refs_8_), channel_id=1, source_target_pairs={{0,1},{1,0},{2,3},{3,2},{4,5},{5,4},{6,7},{7,6},{8,9},{9,8},{10,11... | collective-permute-start | bytes 1572872 | tf_op jit(solution)/shard_map/ppermute | solution.py:585
  43.2 9.8 %copy-start.13 = (bf16[16,2,32,256]{3,2,1,0:T(8,128)(2,1)}, bf16[16,2,32,256]{3,2,1,0:T(8,128)(2,1)S(1)}, u32[]{:S(2)}) copy-start(bf16[16,2,32,256]{3,2,1,0:T(8,128)(2,1)S(1)} %collective-permute-done.4.refs_10_) | copy-start | bytes 1572868
  43.2 9.8 %collective-permute-start.5 = (bf16[16,2,32,256]{3,2,1,0:T(8,128)(2,1)S(1)}, bf16[16,2,32,256]{3,2,1,0:T(8,128)(2,1)}, u32[]{:S(2)}, u32[]{:S(2)}) collective-permute-start(bf16[16,2,32,256]{3,2,1,0:T(8,128)(2,1)S(1)} %collective-permute-done.4.refs_10_), channel_id=1, source_target_pairs={{0,1},{1,0},{2,3},{3,2},{4,5},{5,4},{6,7},{7,6},{8,9},{9,8},{10,11... | collective-permute-start | bytes 1572872 | tf_op jit(solution)/shard_map/ppermute | solution.py:585
  52.9 0.8 copy-start.12

commit v4 on v3

--- a/solution.py
+++ b/solution.py
@@ -148,7 +148,10 @@
     )(page_table, *in_hbm(old))
 
 
-def pick_new_kernel(pages, cap, table_ref, own_ref, core_ref, far_ref, far_core_ref, out_ref, slots_ref, counts_ref, sem):
+def pick_new_kernel(
+    pages, cap, table_ref, own_ref, core_ref, far_ref, far_core_ref, out_ref, targets_ref,
+    slots_ref, counts_ref, sem,
+):
     count = slots_ref.shape[0]
     block_pages = count // 4
     group_index = lax.axis_index("group")
@@ -160,6 +163,10 @@
             source = ref.at[4 * place + group_index]
             target = out_ref.at[slots_ref[block * block_pages + place]]
             pltpu.make_async_copy(source, target, sem).start()
+    for r in range(table_ref.shape[0]):
+        chosen, found = pages_here(table_ref, r, table_ref.shape[1] - count, count, cap, pages)
+        for c in range(cap):
+            targets_ref[r * cap + c] = jnp.where(found > c, chosen[c], -1)
     sent = out_ref.at[pl.ds(0, count)]
     pltpu.make_async_copy(sent, sent, sem).wait()
 
@@ -168,9 +175,12 @@
     window = page_table.shape[1] // 2
     return pl.pallas_call(
         lambda *refs: pick_new_kernel(pages, cap, *refs),
-        out_shape=jax.ShapeDtypeStruct((blk_count * cap,) + sources[0].shape[1:], jnp.bfloat16),
+        out_shape=(
+            jax.ShapeDtypeStruct((blk_count * cap,) + sources[0].shape[1:], jnp.bfloat16),
+            jax.ShapeDtypeStruct((blk_count * cap,), jnp.int32),
+        ),
         in_specs=[smem_spec] + [any_spec] * 4,
-        out_specs=vmem_spec,
+        out_specs=(vmem_spec, smem_spec),
         scratch_shapes=[
             pltpu.SMEM((window,), jnp.int32),
             pltpu.SMEM((blk_count,), jnp.int32),
@@ -219,17 +229,17 @@
 
 def attention(steps, roped_ref, kv_ref, bias_ref, s_refs, most_refs, top_ref, sum_ref, sum_of_values, begin, finish):
     items, rows, _ = roped_ref.shape
-    last_bias = bias_ref.shape[0] - 1
 
     def block(kind, c):
         return kv_ref[kind, pl.ds(c * step_slots, step_slots)].reshape(step_keys, 256)
 
-    def scores(t, c, which):
+    def scores(t, c, which, masked):
         result = lax.dot_general(
             roped_ref[t], block(0, c), (((1,), (1,)), ((), ())), preferred_element_type=jnp.float32
         )
-        bias = bias_ref[jnp.minimum(c, last_bias)]
-        result = (result.reshape(head_pair, rows // head_pair, step_keys) + bias).reshape(rows, step_keys)
+        if masked:
+            result = result.reshape(head_pair, rows // head_pair, step_keys) + bias_ref[...]
+            result = result.reshape(rows, step_keys)
         s_refs[which][c] = result
         most_refs[which][...] = jnp.maximum(most_refs[which][...], lane_fold(result, jnp.maximum))
 
@@ -249,18 +259,27 @@
 
     def loop(work):
         def step(c, carry):
-            work(c)
+            work(c, False)
             return carry
 
-        lax.fori_loop(0, steps, step, 0)
+        if isinstance(steps, int):
+            for c in range(steps):
+                work(c, c == 0)
+            return
+
+        @pl.when(steps > 0)
+        def _():
+            work(0, True)
+
+        lax.fori_loop(1, steps, step, 0)
 
     def one(t, which):
         begin(t + 1, most_refs[1 - which])
         settle(which)
 
-        def work(c):
+        def work(c, masked):
             weigh(c, which)
-            scores(t + 1, c, 1 - which)
+            scores(t + 1, c, 1 - which, masked)
 
         loop(work)
         finish(t)
@@ -271,7 +290,7 @@
         return carry
 
     begin(0, most_refs[0])
-    loop(lambda c: scores(0, c, 0))
+    loop(lambda c, masked: scores(0, c, 0, masked))
     pairs = (items - 1) // 2
     lax.fori_loop(0, pairs, two, 0)
     last = 2 * pairs
@@ -279,11 +298,11 @@
         one(last, 0)
         last += 1
     settle(last % 2)
-    loop(lambda c: weigh(c, last % 2))
+    loop(lambda c, masked: weigh(c, last % 2))
     finish(last)
 
 
-def working(rows, steps, biases):
+def working(rows, steps):
     return [
         pltpu.VMEM((2, steps * step_slots, 32, 256), jnp.bfloat16),
         pltpu.VMEM((steps, head_pair * rows, step_keys), jnp.float32),
@@ -293,7 +312,7 @@
         pltpu.VMEM((head_pair * rows, 128), jnp.float32),
         pltpu.VMEM((head_pair * rows, 128), jnp.float32),
         pltpu.VMEM((head_pair * rows, 256), jnp.float32),
-        pltpu.VMEM((biases, rows, step_keys), jnp.float32),
+        pltpu.VMEM((rows, step_keys), jnp.float32),
     ]
 
 
@@ -329,7 +348,7 @@
     fetch(own_ref, 0, kv_ref, 0, step_slots, sem)
     row = lax.broadcasted_iota(jnp.int32, (rows, step_keys), 0)
     column = lax.broadcasted_iota(jnp.int32, (rows, step_keys), 1)
-    bias_ref[0] = jnp.where(column <= row, 0.0, masked_score)
+    bias_ref[...] = jnp.where(column <= row, 0.0, masked_score)
     query_copy.wait()
 
     def rope(t, carry):
@@ -376,7 +395,7 @@
         out_specs=(hbm_spec,) * 3,
         scratch_shapes=[pltpu.VMEM((rows, width), jnp.bfloat16)]
         + state_shapes(items, rows)
-        + working(rows, 1, 1)
+        + working(rows, 1)
         + [pltpu.SemaphoreType.DMA] * 3,
         compiler_params=params(large_limit),
         cost_estimate=cost(items, rows, 512),
@@ -385,19 +404,17 @@
 
 
 def rest_kernel(
-    cap, table_ref, lengths_ref, roped_in, acc_in, stat_in, core_ref, far_ref, far_core_ref,
-    old_ref, old_core_ref, old_far_ref, old_far_core_ref, weight_ref, arrived_ref, key_ref, value_ref,
+    lengths_ref, roped_in, acc_in, stat_in, core_ref, far_ref, far_core_ref,
+    old_ref, old_core_ref, old_far_ref, old_far_core_ref, weight_ref, key_ref, value_ref,
     hidden_ref, key_out_ref, value_out_ref,
     roped_ref, acc_ref, stat_ref, kv_ref, s_0, s_1, most_0, most_1, top_ref, sum_ref, values_ref,
     bias_ref, w_ref, stage_ref, key_pool, value_pool,
-    state_sems, sem, weight_sem, pool_sems, page_sem, out_sems,
+    state_sems, sem, weight_sem, pool_sems, out_sems,
 ):
     group_index = lax.axis_index("group")
     has_old = lengths_ref[lax.axis_index("blk")] > 0
-    pages = key_ref.shape[0]
-    requests, slots = table_ref.shape
     items = roped_ref.shape[0]
-    rows = bias_ref.shape[1]
+    rows = bias_ref.shape[0]
     chunk = stage_ref.shape[2]
     chunks = w_ref.shape[1] // chunk
     odd = group_index % 2
@@ -459,21 +476,8 @@
 
     @pl.when(has_old)
     def _():
-        bias_ref[0, :, :256] = old_bias(rows, group_index)
-        bias_ref[0, :, 256:] = old_bias(rows, group_index ^ 2)
-
-    for copy in pool_loads:
-        copy.wait()
-    placed = jnp.int32(0)
-    for r in range(requests):
-        chosen, found = pages_here(table_ref, r, slots // 2, slots // 2, cap, pages)
-        placed = placed + found
-        for c in range(cap):
-
-            @pl.when(found > c)
-            def _(page=chosen[c], slot=r * cap + c):
-                pltpu.make_async_copy(arrived_ref.at[slot, 0], key_pool.at[page], page_sem).start()
-                pltpu.make_async_copy(arrived_ref.at[slot, 1], value_pool.at[page], page_sem).start()
+        bias_ref[:, :256] = old_bias(rows, group_index)
+        bias_ref[:, 256:] = old_bias(rows, group_index ^ 2)
 
     wait_rows(kv_ref, steps, 4, sem)
     lane = lax.broadcasted_iota(jnp.int32, stat_ref.shape[1:], 1)
@@ -497,12 +501,8 @@
         begin, finish,
     )
 
-    def settle(n, carry):
-        pltpu.make_async_copy(arrived_ref.at[0, 0], key_pool.at[0], page_sem).wait()
-        pltpu.make_async_copy(arrived_ref.at[0, 1], value_pool.at[0], page_sem).wait()
-        return carry
-
-    lax.fori_loop(0, placed, settle, 0)
+    for copy in pool_loads:
+        copy.wait()
     for copy in pool_stores:
         copy.start()
     weight_copy.wait()
@@ -537,22 +537,22 @@
         copy.wait()
 
 
-def rest_part(page_table, lengths, cap, state, slots, weight, arrived, key_cache, value_cache):
+def rest_part(lengths, state, slots, weight, key_cache, value_cache):
     items, pair_rows, _ = state[0].shape
     rows = pair_rows // head_pair
     width = weight.shape[1]
     chunk = 512
     return pl.pallas_call(
-        lambda *refs: rest_kernel(cap, *refs),
+        rest_kernel,
         out_shape=(
             pltpu.HBM((rows, width), jnp.bfloat16),
             pltpu.HBM(key_cache.shape, jnp.bfloat16),
             pltpu.HBM(value_cache.shape, jnp.bfloat16),
         ),
-        in_specs=[smem_spec] * 2 + [hbm_spec] * 3 + [any_spec] * 7 + [hbm_spec] * 4,
+        in_specs=[smem_spec] + [hbm_spec] * 3 + [any_spec] * 7 + [hbm_spec] * 3,
         out_specs=(hbm_spec,) * 3,
         scratch_shapes=state_shapes(items, rows)
-        + working(rows, 4, 2)
+        + working(rows, 4)
         + [
             pltpu.VMEM(weight.shape, jnp.bfloat16),
             pltpu.VMEM((2, rows, chunk), jnp.bfloat16),
@@ -562,13 +562,50 @@
             pltpu.SemaphoreType.DMA,
             pltpu.SemaphoreType.DMA,
             pltpu.SemaphoreType.DMA((2,)),
-            pltpu.SemaphoreType.DMA,
             pltpu.SemaphoreType.DMA((2,)),
         ],
         compiler_params=params(large_limit),
         cost_estimate=cost(items, rows, 2560),
         name="attend_rest",
-    )(page_table, lengths, *in_hbm(*state), *slots, *in_hbm(weight, arrived, key_cache, value_cache))
+    )(lengths, *in_hbm(*state), *slots, *in_hbm(weight, key_cache, value_cache))
+
+
+def place_kernel(targets_ref, arrived_ref, key_in, value_in, key_ref, value_ref, buffer_ref, load_sem, sem):
+    load = pltpu.make_async_copy(arrived_ref, buffer_ref, load_sem)
+    load.start()
+    load.wait()
+
+    def each(act):
+        for slot in range(targets_ref.shape[0]):
+            page = targets_ref[slot]
+
+            @pl.when(page >= 0)
+            def _(slot=slot, page=page):
+                for kind, out_ref in enumerate((key_ref, value_ref)):
+                    act(pltpu.make_async_copy(buffer_ref.at[slot, kind], out_ref.at[page], sem))
+
+    each(lambda copy: copy.start())
+    each(lambda copy: copy.wait())
+
+
+def place_new(targets, arrived, key_pool, value_pool):
+    return pl.pallas_call(
+        place_kernel,
+        out_shape=(
+            pltpu.HBM(key_pool.shape, jnp.bfloat16),
+            pltpu.HBM(value_pool.shape, jnp.bfloat16),
+        ),
+        in_specs=[smem_spec] + [hbm_spec] * 3,
+        out_specs=(hbm_spec,) * 2,
+        input_output_aliases={2: 0, 3: 1},
+        scratch_shapes=[
+            pltpu.VMEM(arrived.shape, jnp.bfloat16),
+            pltpu.SemaphoreType.DMA,
+            pltpu.SemaphoreType.DMA,
+        ],
+        compiler_params=params(small_limit),
+        name="place_new",
+    )(targets, *in_hbm(arrived, key_pool, value_pool))
 
 
 def after(value, *others):
@@ -599,15 +636,18 @@
     old = sort_old(after(page_table, stat), blk_count, cap, pages, old)
     old_far = other_chip(old)
     old_core = other_core(old)
-    fresh_far_core = other_core(after(fresh_far, stat))
-    new = pick_new(page_table, blk_count, cap, pages, (fresh, fresh_core, fresh_far, fresh_far_core))
+    fresh_far_core = other_core(after(fresh_far, old))
+    new, targets = pick_new(
+        page_table, blk_count, cap, pages, (fresh, fresh_core, fresh_far, fresh_far_core)
+    )
     arrived = lax.all_to_all(new, "blk", split_axis=0, concat_axis=0, tiled=True)
     old_far_core = other_core(after(old_far, new))
     hidden, key_out, value_out = rest_part(
-        page_table, lengths, cap, (roped, acc, stat),
+        lengths, (roped, acc, stat),
         (fresh_core, fresh_far, fresh_far_core, old, old_core, old_far, old_far_core),
-        out_weight, arrived, key_cache, value_cache,
+        out_weight, key_cache, value_cache,
     )
+    key_out, value_out = place_new(targets, arrived, key_out, value_out)
     return (hidden[None], key_out, value_out)
 
 

time: 89.4 us -> 83.4 us (0.933)
  the two profiles are of different devices: /device:TPU:2 before, /device:TPU:3 now
where the time goes in v4:
time: 83.4 us; the launch traced here: 82.8 us
  Pallas kernels  53.8 us (65%)
  starting transfers between devices  17 us (20%)
  waiting for transfers between devices  8.75 us (10%)
  local copies, waits for them, and re-layouts  2.37 us (3%)
  between operations  0.98 us (1%)
    pallas_call x1, Pallas kernels, rest_part(): pl.pallas_call(rest_kernel, out_shape=(pltpu.HBM((rows, width), jnp.bfloa...  32 us
    pallas_call x1, Pallas kernels, diagonal_part(): pl.pallas_call(diagonal_kernel, out_shape=(pltpu.HBM((items, head_pair *...  9.79 us
    ppermute x2, waiting for transfers between devices, other_chip(): return lax.ppermute(value, 'group', [(0, 2), (2, 0), (1, 3), (3, 1)])  8.54 us
    all_to_all x1, starting transfers between devices, body(): old = lax.all_to_all(picked, 'blk', split_axis=0, concat_axis=0, tiled=True)  5.79 us
    all_to_all x1, starting transfers between devices, body(): lax.all_to_all(new, 'blk', split_axis=0, concat_axis=0, tiled=True)  5.4 us
    ppermute x4, starting transfers between devices, other_core(): return lax.ppermute(value, 'group', [(0, 1), (1, 0), (2, 3), (3, 2)])  3.27 us
    pallas_call x1, Pallas kernels, pick_new(): pl.pallas_call(lambda *refs: pick_new_kernel(pages, cap, *refs), out_shap...  2.75 us
    pallas_call x1, Pallas kernels, pick_old(): pl.pallas_call(pick_old_kernel, out_shape=jax.ShapeDtypeStruct((requests,...  2.75 us
  transfers between devices with their start and end apart: 8, of which 2 were waited for; matrix products, arithmetic and copies ran while one was open for 0% of the time, Pallas kernels for 59%

profile of v4, /device:TPU:3, one launch (start us, length us, event | category | flops | bytes accessed | tf_op | source)
XLA Modules:
  0.0 82.8 jit_solution(13809728222713056514)
XLA Ops:
  0.6 0.0 copy-start.6
  0.6 0.0 copy-start.5
  0.7 0.0 copy-start.7
  0.7 0.7 copy-done.7
  1.4 0.0 copy-start.9
  1.4 0.0 copy-start.10
  1.4 2.8 %pick_old.1 = bf16[8,2,2,32,256]{4,3,2,1,0:T(8,128)(2,1)} custom-call(s32[8,32]{1,0:T(8,128)S(1)} %copy-done.7, bf16[40,32,256]{2,1,0:T(8,128)(2,1)} %key_ref.3, bf16[40,32,256]{2,1,0:T(8,128)(2,1)} %value_ref.3), custom_call_target="tpu_custom_call" | custom-call | tf_op jit(solution)/shard_map/pick_old/pallas_call | solution.py:62
  4.2 5.8 %all-to-all-start = ((bf16[8,2,2,32,256]{4,3,2,1,0:T(8,128)(2,1)}), bf16[8,2,2,32,256]{4,3,2,1,0:T(8,128)(2,1)S(1)}, u32[]{:S(2)}, u32[]{:S(2)}) async-start(bf16[8,2,2,32,256]{4,3,2,1,0:T(8,128)(2,1)} %pick_old.1), calls=%async_computation | async-start | bytes 1048576 | tf_op jit(solution)/shard_map/all_to_all | solution.py:628
  9.9 0.0 copy-done.6
  9.9 0.0 copy-done.5
  10.0 0.0 copy-done.9
  10.0 0.0 copy-done.10
  10.0 2.5 %rotate_keys.1 = (bf16[16,2,32,256]{3,2,1,0:T(8,128)(2,1)}, f32[512,128]{1,0:T(8,128)}, f32[512,128]{1,0:T(8,128)}) custom-call(s32[8]{0:T(128)S(1)} %copy-done.9, f32[1,128]{1,0:T(1,128)S(1)} %copy-done.10, bf16[512,256]{1,0:T(8,128)(2,1)S(1)} %bitcast.5, bf16[512,256]{1,0:T(8,128)(2,1)S(1)} %bitcast.6), custom_call_target="tpu_custom_call" | custom-call | tf_op jit(solution)/shard_map/rotate_keys/pallas_call | solution.py:117
  12.4 1.2 %collective-permute-start.1 = (bf16[16,2,32,256]{3,2,1,0:T(8,128)(2,1)}, bf16[16,2,32,256]{3,2,1,0:T(8,128)(2,1)S(1)}, u32[]{:S(2)}, u32[]{:S(2)}) collective-permute-start(bf16[16,2,32,256]{3,2,1,0:T(8,128)(2,1)} %get-tuple-element.23.own_ref.refs_1_), channel_id=1, source_target_pairs={{0,2},{2,0},{1,3},{3,1},{4,6},{6,4},{5,7},{7,5},{8,10},{10,8},{9,1... | collective-permute-start | bytes 1572872 | tf_op jit(solution)/shard_map/ppermute | solution.py:625
  13.7 1.5 %collective-permute-start = (bf16[16,2,32,256]{3,2,1,0:T(8,128)(2,1)}, bf16[16,2,32,256]{3,2,1,0:T(8,128)(2,1)S(1)}, u32[]{:S(2)}, u32[]{:S(2)}) collective-permute-start(bf16[16,2,32,256]{3,2,1,0:T(8,128)(2,1)} %get-tuple-element.23.own_ref.refs_1_), channel_id=1, source_target_pairs={{0,1},{1,0},{2,3},{3,2},{4,5},{5,4},{6,7},{7,6},{8,9},{9,8},{10,11... | collective-permute-start | bytes 1572872 | tf_op jit(solution)/shard_map/ppermute | solution.py:622
  15.2 0.0 copy-start.8
  15.2 0.0 copy-start.3
  15.2 9.8 %attend_diagonal.1 = (bf16[5,1024,256]{2,1,0:T(8,128)(2,1)}, f32[5,1024,256]{2,1,0:T(8,128)}, f32[5,1024,128]{2,1,0:T(8,128)}) custom-call(bf16[512,2560]{1,0:T(8,128)(2,1)} %bitcast.8, f32[512,128]{1,0:T(8,128)} %get-tuple-element.21.cos_ref, f32[512,128]{1,0:T(8,128)} %get-tuple-element.22.sin_ref, bf16[16,2,32,256]{3,2,1,0:T(8,128)(2,1)} %get-tuple-element.23.own_ref.refs_1_), custom_call_target="tpu_custom_call" | custom-call | flops 2684354560 | bytes 16777216 | tf_op jit(solution)/shard_map/attend_diagonal/pallas_call | solution.py:391
  25.0 0.0 all-to-all-done
  25.0 0.0 copy-start.11
  25.0 0.8 copy-done.11
  25.8 0.0 copy-done.8
  25.8 1.6 %sort_old.1.old_ref = bf16[16,2,32,256]{3,2,1,0:T(8,128)(2,1)S(1)} custom-call(s32[8,32]{1,0:T(8,128)S(1)} %copy-done.8, bf16[16,2,32,256]{3,2,1,0:T(8,128)(2,1)} %bitcast.7), custom_call_target="tpu_custom_call" | custom-call | tf_op jit(solution)/shard_map/sort_old/pallas_call | solution.py:140
  27.4 0.0 copy-start
  27.4 0.0 collective-permute-done.1.refs_3_.far_ref
  27.5 0.0 copy-start.1
  27.5 0.2 collective-permute-start.2
  27.6 1.3 %collective-permute-start.4 = (bf16[16,2,32,256]{3,2,1,0:T(8,128)(2,1)S(1)}, bf16[16,2,32,256]{3,2,1,0:T(8,128)(2,1)S(1)}, u32[]{:S(2)}, u32[]{:S(2)}) collective-permute-start(bf16[16,2,32,256]{3,2,1,0:T(8,128)(2,1)S(1)} %sort_old.1.old_ref), channel_id=1, source_target_pairs={{0,2},{2,0},{1,3},{3,1},{4,6},{6,4},{5,7},{7,5},{8,10},{10,8},{9,1... | collective-permute-start | bytes 1572872 | tf_op jit(solution)/shard_map/ppermute | solution.py:625
  28.9 0.3 collective-permute-start.3
  29.2 0.0 collective-permute-done.refs_2_.core_ref
  29.2 0.0 copy-start.2
  29.2 0.2 collective-permute-done.2.refs_4_.far_core_ref
  29.4 0.0 copy-done.3
  29.4 0.0 copy-start.4
  29.4 2.8 %pick_new.1 = (bf16[16,2,32,256]{3,2,1,0:T(8,128)(2,1)}, s32[16]{0:T(128)S(1)}) custom-call(s32[8,32]{1,0:T(8,128)S(1)} %copy-done.8, bf16[16,2,32,256]{3,2,1,0:T(8,128)(2,1)S(1)} %copy-done.3, bf16[16,2,32,256]{3,2,1,0:T(8,128)(2,1)S(1)} %collective-permute-done.refs_2_.core_ref, bf16[16,2,32,256]{3,2,1,0:T(8,128)(2,1)S(1)} %collective-permute-done.1.refs_3_.far_ref, ...), custom_call_target="tpu_custom_call" | custom-call | tf_op jit(solution)/shard_map/pick_new/pallas_call | solution.py:176
  32.2 8.5 %collective-permute-done.4.old_far_ref = bf16[16,2,32,256]{3,2,1,0:T(8,128)(2,1)S(1)} collective-permute-done((bf16[16,2,32,256]{3,2,1,0:T(8,128)(2,1)S(1)}, bf16[16,2,32,256]{3,2,1,0:T(8,128)(2,1)S(1)}, u32[]{:S(2)}, u32[]{:S(2)}) %collective-permute-start.4) | collective-permute-done | bytes 524320 | tf_op jit(solution)/shard_map/ppermute | solution.py:625
  40.7 0.0 copy-start.13
  40.8 1.2 %collective-permute-start.5 = (bf16[16,2,32,256]{3,2,1,0:T(8,128)(2,1)S(1)}, bf16[16,2,32,256]{3,2,1,0:T(8,128)(2,1)}, u32[]{:S(2)}, u32[]{:S(2)}) collective-permute-start(bf16[16,2,32,256]{3,2,1,0:T(8,128)(2,1)S(1)} %collective-permute-done.4.old_far_ref), channel_id=1, source_target_pairs={{0,1},{1,0},{2,3},{3,2},{4,5},{5,4},{6,7},{7,6},{8,9},{9,8},{10,11... | collective-permute-start | bytes 1572872 | tf_op jit(solution)/shard_map/ppermute | solution.py:622
  42.0 5.4 %all-to-all-start.1 = ((bf16[16,2,32,256]{3,2,1,0:T(8,128)(2,1)}), bf16[16,2,32,256]{3,2,1,0:T(8,128)(2,1)S(1)}, u32[]{:S(2)}, u32[]{:S(2)}) async-start(bf16[16,2,32,256]{3,2,1,0:T(8,128)(2,1)} %get-tuple-element.29), calls=%async_computation.1 | async-start | bytes 1048576 | tf_op jit(solution)/shard_map/all_to_all | solution.py:643
  47.4 0.0 collective-permute-done.3.old_core_ref
  47.4 0.0 collective-permute-done.5.old_far_core_ref
  47.4 0.0 copy-done
  47.4 0.0 copy-done.1
  47.4 0.0 copy-done.2
  47.4 0.0 copy-done.4
  47.4 0.0 copy-done.13
  47.4 32.0 %attend_rest.1 = (bf16[512,2560]{1,0:T(8,128)(2,1)}, bf16[40,32,256]{2,1,0:T(8,128)(2,1)}, bf16[40,32,256]{2,1,0:T(8,128)(2,1)}) custom-call(s32[8]{0:T(128)} %lengths_ref.3, bf16[5,1024,256]{2,1,0:T(8,128)(2,1)} %get-tuple-element.24.roped_in, f32[5,1024,256]{2,1,0:T(8,128)} %get-tuple-element.25.acc_in, f32[5,1024,128]{2,1,0:T(8,128)} %get-tuple-element.26.stat_in, ...), custom_call_target="tpu_custom_call" | custom-call | flops 13421772800 | bytes 16777216 | tf_op jit(solution)/shard_map/attend_rest/pallas_call | solution.py:545
  79.5 0.0 all-to-all-done.1.arrived_ref
  79.5 0.0 copy-start.12
  79.5 0.8 copy-done.12
  80.3 2.4 %place_new.1 = (bf16[40,32,256]{2,1,0:T(8,128)(2,1)}, bf16[40,32,256]{2,1,0:T(8,128)(2,1)}) custom-call(s32[16]{0:T(128)S(1)} %get-tuple-element.32.targets_ref, bf16[16,2,32,256]{3,2,1,0:T(8,128)(2,1)} %copy-done.12, bf16[40,32,256]{2,1,0:T(8,128)(2,1)} %get-tuple-element.33.key_in, ...), custom_call_target="tpu_custom_call", output_to_operand_aliasing={{0}: (2, {}), {1}: (3, {})} | custom-call | tf_op jit(solution)/shard_map/place_new/pallas_call | solution.py:592
Async XLA Ops:
  0.6 9.3 %copy-start.6 = (bf16[1,512,256]{2,1,0:T(8,128)(2,1)S(1)}, bf16[1,512,256]{2,1,0:T(8,128)(2,1)}, u32[]{:S(2)}) copy-start(bf16[1,512,256]{2,1,0:T(8,128)(2,1)} %param.11) | copy-start | bytes 786436
  0.6 9.3 %copy-start.5 = (bf16[1,512,256]{2,1,0:T(8,128)(2,1)S(1)}, bf16[1,512,256]{2,1,0:T(8,128)(2,1)}, u32[]{:S(2)}) copy-start(bf16[1,512,256]{2,1,0:T(8,128)(2,1)} %param.10) | copy-start | bytes 786436
  0.7 0.7 copy-start.7
  1.4 8.6 %copy-start.9 = (s32[8]{0:T(128)S(1)}, s32[8]{0:T(128)}, u32[]{:S(2)}) copy-start(s32[8]{0:T(128)} %lengths_ref.3) | copy-start | bytes 100
  1.4 8.6 %copy-start.10 = (f32[1,128]{1,0:T(1,128)S(1)}, f32[1,128]{1,0:T(1,128)}, u32[]{:S(2)}) copy-start(f32[1,128]{1,0:T(1,128)} %constant.2.clone.freq_ref) | copy-start | bytes 1540
  4.2 20.8 %all-to-all-start = ((bf16[8,2,2,32,256]{4,3,2,1,0:T(8,128)(2,1)}), bf16[8,2,2,32,256]{4,3,2,1,0:T(8,128)(2,1)S(1)}, u32[]{:S(2)}, u32[]{:S(2)}) async-start(bf16[8,2,2,32,256]{4,3,2,1,0:T(8,128)(2,1)} %pick_old.1), calls=%async_computation | async-start | bytes 1048576 | tf_op jit(solution)/shard_map/all_to_all | solution.py:628
  12.4 15.0 %collective-permute-start.1 = (bf16[16,2,32,256]{3,2,1,0:T(8,128)(2,1)}, bf16[16,2,32,256]{3,2,1,0:T(8,128)(2,1)S(1)}, u32[]{:S(2)}, u32[]{:S(2)}) collective-permute-start(bf16[16,2,32,256]{3,2,1,0:T(8,128)(2,1)} %get-tuple-element.23.own_ref.refs_1_), channel_id=1, source_target_pairs={{0,2},{2,0},{1,3},{3,1},{4,6},{6,4},{5,7},{7,5},{8,10},{10,8},{9,1... | collective-permute-start | bytes 1572872 | tf_op jit(solution)/shard_map/ppermute | solution.py:625
  13.7 15.6 %collective-permute-start = (bf16[16,2,32,256]{3,2,1,0:T(8,128)(2,1)}, bf16[16,2,32,256]{3,2,1,0:T(8,128)(2,1)S(1)}, u32[]{:S(2)}, u32[]{:S(2)}) collective-permute-start(bf16[16,2,32,256]{3,2,1,0:T(8,128)(2,1)} %get-tuple-element.23.own_ref.refs_1_), channel_id=1, source_target_pairs={{0,1},{1,0},{2,3},{3,2},{4,5},{5,4},{6,7},{7,6},{8,9},{9,8},{10,11... | collective-permute-start | bytes 1572872 | tf_op jit(solution)/shard_map/ppermute | solution.py:622
  15.2 10.6 %copy-start.8 = (s32[8,32]{1,0:T(8,128)S(1)}, s32[8,32]{1,0:T(8,128)}, u32[]{:S(2)}) copy-start(s32[8,32]{1,0:T(8,128)} %refs_0_.2) | copy-start | bytes 3076
  15.2 14.3 %copy-start.3 = (bf16[16,2,32,256]{3,2,1,0:T(8,128)(2,1)S(1)}, bf16[16,2,32,256]{3,2,1,0:T(8,128)(2,1)}, u32[]{:S(2)}) copy-start(bf16[16,2,32,256]{3,2,1,0:T(8,128)(2,1)} %get-tuple-element.23.own_ref.refs_1_) | copy-start | bytes 1572868
  25.0 0.8 copy-start.11
  27.4 20.0 %copy-start = (bf16[16,2,32,256]{3,2,1,0:T(8,128)(2,1)}, bf16[16,2,32,256]{3,2,1,0:T(8,128)(2,1)S(1)}, u32[]{:S(2)}) copy-start(bf16[16,2,32,256]{3,2,1,0:T(8,128)(2,1)S(1)} %sort_old.1.old_ref) | copy-start | bytes 1572868
  27.5 20.0 %copy-start.1 = (bf16[16,2,32,256]{3,2,1,0:T(8,128)(2,1)}, bf16[16,2,32,256]{3,2,1,0:T(8,128)(2,1)S(1)}, u32[]{:S(2)}) copy-start(bf16[16,2,32,256]{3,2,1,0:T(8,128)(2,1)S(1)} %collective-permute-done.1.refs_3_.far_ref) | copy-start | bytes 1572868
  27.5 2.0 %collective-permute-start.2 = (bf16[16,2,32,256]{3,2,1,0:T(8,128)(2,1)S(1)}, bf16[16,2,32,256]{3,2,1,0:T(8,128)(2,1)S(1)}, u32[]{:S(2)}, u32[]{:S(2)}) collective-permute-start(bf16[16,2,32,256]{3,2,1,0:T(8,128)(2,1)S(1)} %collective-permute-done.1.refs_3_.far_ref), channel_id=1, source_target_pairs={{0,1},{1,0},{2,3},{3,2},{4,5},{5,4},{6,7},{7,6},{8,9},{9,8},{10,11... | collective-permute-start | bytes 1572872 | tf_op jit(solution)/shard_map/ppermute | solution.py:622
  27.6 13.1 %collective-permute-start.4 = (bf16[16,2,32,256]{3,2,1,0:T(8,128)(2,1)S(1)}, bf16[16,2,32,256]{3,2,1,0:T(8,128)(2,1)S(1)}, u32[]{:S(2)}, u32[]{:S(2)}) collective-permute-start(bf16[16,2,32,256]{3,2,1,0:T(8,128)(2,1)S(1)} %sort_old.1.old_ref), channel_id=1, source_target_pairs={{0,2},{2,0},{1,3},{3,1},{4,6},{6,4},{5,7},{7,5},{8,10},{10,8},{9,1... | collective-permute-start | bytes 1572872 | tf_op jit(solution)/shard_map/ppermute | solution.py:625
  28.9 18.5 %collective-permute-start.3 = (bf16[16,2,32,256]{3,2,1,0:T(8,128)(2,1)S(1)}, bf16[16,2,32,256]{3,2,1,0:T(8,128)(2,1)}, u32[]{:S(2)}, u32[]{:S(2)}) collective-permute-start(bf16[16,2,32,256]{3,2,1,0:T(8,128)(2,1)S(1)} %sort_old.1.old_ref), channel_id=1, source_target_pairs={{0,1},{1,0},{2,3},{3,2},{4,5},{5,4},{6,7},{7,6},{8,9},{9,8},{10,11... | collective-permute-start | bytes 1572872 | tf_op jit(solution)/shard_map/ppermute | solution.py:622
  29.2 18.2 %copy-start.2 = (bf16[16,2,32,256]{3,2,1,0:T(8,128)(2,1)}, bf16[16,2,32,256]{3,2,1,0:T(8,128)(2,1)S(1)}, u32[]{:S(2)}) copy-start(bf16[16,2,32,256]{3,2,1,0:T(8,128)(2,1)S(1)} %collective-permute-done.refs_2_.core_ref) | copy-start | bytes 1572868
  29.4 18.0 %copy-start.4 = (bf16[16,2,32,256]{3,2,1,0:T(8,128)(2,1)}, bf16[16,2,32,256]{3,2,1,0:T(8,128)(2,1)S(1)}, u32[]{:S(2)}) copy-start(bf16[16,2,32,256]{3,2,1,0:T(8,128)(2,1)S(1)} %collective-permute-done.2.refs_4_.far_core_ref) | copy-start | bytes 1572868
  40.7 6.7 %copy-start.13 = (bf16[16,2,32,256]{3,2,1,0:T(8,128)(2,1)}, bf16[16,2,32,256]{3,2,1,0:T(8,128)(2,1)S(1)}, u32[]{:S(2)}) copy-start(bf16[16,2,32,256]{3,2,1,0:T(8,128)(2,1)S(1)} %collective-permute-done.4.old_far_ref) | copy-start | bytes 1572868
  40.8 6.6 %collective-permute-start.5 = (bf16[16,2,32,256]{3,2,1,0:T(8,128)(2,1)S(1)}, bf16[16,2,32,256]{3,2,1,0:T(8,128)(2,1)}, u32[]{:S(2)}, u32[]{:S(2)}) collective-permute-start(bf16[16,2,32,256]{3,2,1,0:T(8,128)(2,1)S(1)} %collective-permute-done.4.old_far_ref), channel_id=1, source_target_pairs={{0,1},{1,0},{2,3},{3,2},{4,5},{5,4},{6,7},{7,6},{8,9},{9,8},{10,11... | collective-permute-start | bytes 1572872 | tf_op jit(solution)/shard_map/ppermute | solution.py:622
  42.0 37.5 %all-to-all-start.1 = ((bf16[16,2,32,256]{3,2,1,0:T(8,128)(2,1)}), bf16[16,2,32,256]{3,2,1,0:T(8,128)(2,1)S(1)}, u32[]{:S(2)}, u32[]{:S(2)}) async-start(bf16[16,2,32,256]{3,2,1,0:T(8,128)(2,1)} %get-tuple-element.29), calls=%async_computation.1 | async-start | bytes 1048576 | tf_op jit(solution)/shard_map/all_to_all | solution.py:643
  79.5 0.8 copy-start.12

commit v5 on v4

--- a/solution.py
+++ b/solution.py
@@ -18,6 +18,9 @@
 large_limit = 58 * 1024 * 1024
 
 
+light = pl.CostEstimate(flops=1, bytes_accessed=1, transcendentals=0)
+
+
 def params(limit):
     return pltpu.CompilerParams(vmem_limit_bytes=limit)
 
@@ -65,6 +68,7 @@
         in_specs=[smem_spec, hbm_spec, hbm_spec],
         out_specs=vmem_spec,
         scratch_shapes=[pltpu.SemaphoreType.DMA],
+        cost_estimate=light,
         compiler_params=params(small_limit),
         name="pick_old",
     )(page_table, *in_hbm(key_cache, value_cache))
@@ -123,6 +127,7 @@
         ),
         in_specs=[smem_spec, vmem_spec, vmem_spec, vmem_spec],
         out_specs=(vmem_spec,) * 3,
+        cost_estimate=light,
         compiler_params=params(small_limit),
         name="rotate_keys",
     )(lengths, jnp.asarray(freq_table), keys, values)
@@ -143,6 +148,7 @@
         in_specs=[smem_spec, hbm_spec],
         out_specs=vmem_spec,
         scratch_shapes=[pltpu.SMEM((blk_count,), jnp.int32), pltpu.SemaphoreType.DMA],
+        cost_estimate=light,
         compiler_params=params(small_limit),
         name="sort_old",
     )(page_table, *in_hbm(old))
@@ -186,6 +192,7 @@
             pltpu.SMEM((blk_count,), jnp.int32),
             pltpu.SemaphoreType.DMA,
         ],
+        cost_estimate=light,
         compiler_params=params(small_limit),
         name="pick_new",
     )(page_table, *sources)
@@ -329,11 +336,6 @@
         pltpu.HBM((items, head_pair * rows, 256), jnp.float32),
         pltpu.HBM((items, head_pair * rows, 128), jnp.float32),
     )
-
-
-def cost(items, rows, keys):
-    pairs = items * head_pair * rows * keys
-    return pl.CostEstimate(flops=4 * pairs * 256, bytes_accessed=1 << 24, transcendentals=pairs)
 
 
 def diagonal_kernel(
@@ -397,8 +399,8 @@
         + state_shapes(items, rows)
         + working(rows, 1)
         + [pltpu.SemaphoreType.DMA] * 3,
+        cost_estimate=light,
         compiler_params=params(large_limit),
-        cost_estimate=cost(items, rows, 512),
         name="attend_diagonal",
     )(*in_hbm(queries), cosine, sine, *in_hbm(own))
 
@@ -564,8 +566,8 @@
             pltpu.SemaphoreType.DMA((2,)),
             pltpu.SemaphoreType.DMA((2,)),
         ],
+        cost_estimate=light,
         compiler_params=params(large_limit),
-        cost_estimate=cost(items, rows, 2560),
         name="attend_rest",
     )(lengths, *in_hbm(*state), *slots, *in_hbm(weight, key_cache, value_cache))
 
@@ -595,7 +597,7 @@
             pltpu.HBM(key_pool.shape, jnp.bfloat16),
             pltpu.HBM(value_pool.shape, jnp.bfloat16),
         ),
-        in_specs=[smem_spec] + [hbm_spec] * 3,
+        in_specs=[smem_spec, any_spec, hbm_spec, hbm_spec],
         out_specs=(hbm_spec,) * 2,
         input_output_aliases={2: 0, 3: 1},
         scratch_shapes=[
@@ -603,9 +605,10 @@
             pltpu.SemaphoreType.DMA,
             pltpu.SemaphoreType.DMA,
         ],
+        cost_estimate=light,
         compiler_params=params(small_limit),
         name="place_new",
-    )(targets, *in_hbm(arrived, key_pool, value_pool))
+    )(targets, arrived, *in_hbm(key_pool, value_pool))
 
 
 def after(value, *others):

time: 83.4 us -> 79.6 us (0.954)
  the two profiles are of different devices: /device:TPU:3 before, /device:TPU:0 now
where the time goes in v5:
time: 79.6 us; the launch traced here: 79.1 us
  Pallas kernels  52.7 us (66%)
  starting transfers between devices  15.9 us (20%)
  waiting for transfers between devices  7.13 us (9%)
  local copies, waits for them, and re-layouts  2.35 us (3%)
  between operations  0.98 us (1%)
    pallas_call x1, Pallas kernels, rest_part(): pl.pallas_call(rest_kernel, out_shape=(pltpu.HBM((rows, width), jnp.bfloa...  32 us
    pallas_call x1, Pallas kernels, diagonal_part(): pl.pallas_call(diagonal_kernel, out_shape=(pltpu.HBM((items, head_pair *...  9.72 us
    all_to_all x1, starting transfers between devices, body(): old = lax.all_to_all(picked, 'blk', split_axis=0, concat_axis=0, tiled=True)  7.26 us
    all_to_all x1, starting transfers between devices, body(): lax.all_to_all(new, 'blk', split_axis=0, concat_axis=0, tiled=True)  5.41 us
    ppermute x2, waiting for transfers between devices, other_chip(): return lax.ppermute(value, 'group', [(0, 2), (2, 0), (1, 3), (3, 1)])  4.18 us
    ppermute x2, starting transfers between devices, other_chip(): return lax.ppermute(value, 'group', [(0, 2), (2, 0), (1, 3), (3, 1)])  3.1 us
    pallas_call x1, Pallas kernels, pick_new(): pl.pallas_call(lambda *refs: pick_new_kernel(pages, cap, *refs), out_shap...  2.76 us
    pallas_call x1, Pallas kernels, pick_old(): pl.pallas_call(pick_old_kernel, out_shape=jax.ShapeDtypeStruct((requests,...  2.75 us
  transfers between devices with their start and end apart: 8, of which 4 were waited for; matrix products, arithmetic and copies ran while one was open for 0% of the time, Pallas kernels for 61%

profile of v5, /device:TPU:0, one launch (start us, length us, event | category | flops | bytes accessed | tf_op | source)
XLA Modules:
  0.0 79.1 jit_solution(11005596300016766067)
XLA Ops:
  0.6 0.0 copy-start.6
  0.6 0.0 copy-start.5
  0.7 0.0 copy-start.7
  0.7 0.7 copy-done.7
  1.4 0.0 copy-start.9
  1.4 0.0 copy-start.10
  1.4 2.8 %pick_old.1 = bf16[8,2,2,32,256]{4,3,2,1,0:T(8,128)(2,1)} custom-call(s32[8,32]{1,0:T(8,128)S(1)} %copy-done.7, bf16[40,32,256]{2,1,0:T(8,128)(2,1)} %key_ref.3, bf16[40,32,256]{2,1,0:T(8,128)(2,1)} %value_ref.3), custom_call_target="tpu_custom_call" | custom-call | flops 1 | bytes 1 | tf_op jit(solution)/shard_map/pick_old/pallas_call | solution.py:65
  4.2 0.0 copy-start.8
  4.2 7.3 %all-to-all-start = ((bf16[8,2,2,32,256]{4,3,2,1,0:T(8,128)(2,1)}), bf16[8,2,2,32,256]{4,3,2,1,0:T(8,128)(2,1)S(1)}, u32[]{:S(2)}, u32[]{:S(2)}) async-start(bf16[8,2,2,32,256]{4,3,2,1,0:T(8,128)(2,1)} %pick_old.1), calls=%async_computation | async-start | bytes 1048576 | tf_op jit(solution)/shard_map/all_to_all | solution.py:631
  11.4 0.0 copy-done.6
  11.4 0.0 copy-done.5
  11.4 0.0 copy-done.9
  11.5 0.0 copy-done.10
  11.5 2.5 %rotate_keys.1 = (bf16[16,2,32,256]{3,2,1,0:T(8,128)(2,1)}, f32[512,128]{1,0:T(8,128)}, f32[512,128]{1,0:T(8,128)}) custom-call(s32[8]{0:T(128)S(1)} %copy-done.9, f32[1,128]{1,0:T(1,128)S(1)} %copy-done.10, bf16[512,256]{1,0:T(8,128)(2,1)S(1)} %bitcast.5, bf16[512,256]{1,0:T(8,128)(2,1)S(1)} %bitcast.6), custom_call_target="tpu_custom_call" | custom-call | flops 1 | bytes 1 | tf_op jit(solution)/shard_map/rotate_keys/pallas_call | solution.py:121
  13.9 0.0 copy-start
  13.9 1.5 %collective-permute-start.1 = (bf16[16,2,32,256]{3,2,1,0:T(8,128)(2,1)}, bf16[16,2,32,256]{3,2,1,0:T(8,128)(2,1)S(1)}, u32[]{:S(2)}, u32[]{:S(2)}) collective-permute-start(bf16[16,2,32,256]{3,2,1,0:T(8,128)(2,1)} %get-tuple-element.23.own_ref.refs_1_), channel_id=1, source_target_pairs={{0,2},{2,0},{1,3},{3,1},{4,6},{6,4},{5,7},{7,5},{8,10},{10,8},{9,1... | collective-permute-start | bytes 1572872 | tf_op jit(solution)/shard_map/ppermute | solution.py:628
  15.4 0.0 collective-permute-start
  15.4 9.7 %attend_diagonal.1 = (bf16[5,1024,256]{2,1,0:T(8,128)(2,1)}, f32[5,1024,256]{2,1,0:T(8,128)}, f32[5,1024,128]{2,1,0:T(8,128)}) custom-call(bf16[512,2560]{1,0:T(8,128)(2,1)} %bitcast.7, f32[512,128]{1,0:T(8,128)} %get-tuple-element.21.cos_ref, f32[512,128]{1,0:T(8,128)} %get-tuple-element.22.sin_ref, bf16[16,2,32,256]{3,2,1,0:T(8,128)(2,1)} %get-tuple-element.23.own_ref.refs_1_), custom_call_target="tpu_custom_call" | custom-call | flops 1 | bytes 1 | tf_op jit(solution)/shard_map/attend_diagonal/pallas_call | solution.py:393
  25.2 0.7 all-to-all-done
  25.9 0.0 copy-start.11
  25.9 0.8 copy-done.11
  26.7 0.0 copy-done.8
  26.7 1.6 %sort_old.1.old_ref = bf16[16,2,32,256]{3,2,1,0:T(8,128)(2,1)S(1)} custom-call(s32[8,32]{1,0:T(8,128)S(1)} %copy-done.8, bf16[16,2,32,256]{3,2,1,0:T(8,128)(2,1)} %bitcast.8), custom_call_target="tpu_custom_call" | custom-call | flops 1 | bytes 1 | tf_op jit(solution)/shard_map/sort_old/pallas_call | solution.py:145
  28.4 0.0 copy-start.1
  28.4 0.0 collective-permute-done.1.refs_3_.far_ref
  28.4 0.0 copy-start.2
  28.4 0.1 collective-permute-start.2
  28.5 1.6 %collective-permute-start.4 = (bf16[16,2,32,256]{3,2,1,0:T(8,128)(2,1)S(1)}, bf16[16,2,32,256]{3,2,1,0:T(8,128)(2,1)S(1)}, u32[]{:S(2)}, u32[]{:S(2)}) collective-permute-start(bf16[16,2,32,256]{3,2,1,0:T(8,128)(2,1)S(1)} %sort_old.1.old_ref), channel_id=1, source_target_pairs={{0,2},{2,0},{1,3},{3,1},{4,6},{6,4},{5,7},{7,5},{8,10},{10,8},{9,1... | collective-permute-start | bytes 1572872 | tf_op jit(solution)/shard_map/ppermute | solution.py:628
  30.1 0.0 collective-permute-done.refs_2_.core_ref
  30.1 0.0 copy-start.3
  30.1 0.3 collective-permute-done.2.refs_4_.far_core_ref
  30.4 0.0 copy-done
  30.4 0.0 copy-start.4
  30.4 2.8 %pick_new.1 = (bf16[16,2,32,256]{3,2,1,0:T(8,128)(2,1)}, s32[16]{0:T(128)S(1)}) custom-call(s32[8,32]{1,0:T(8,128)S(1)} %copy-done.8, bf16[16,2,32,256]{3,2,1,0:T(8,128)(2,1)S(1)} %copy-done, bf16[16,2,32,256]{3,2,1,0:T(8,128)(2,1)S(1)} %collective-permute-done.refs_2_.core_ref, bf16[16,2,32,256]{3,2,1,0:T(8,128)(2,1)S(1)} %collective-permute-done.1.refs_3_.far_ref, ...), custom_call_target="tpu_custom_call" | custom-call | flops 1 | bytes 1 | tf_op jit(solution)/shard_map/pick_new/pallas_call | solution.py:182
  33.1 5.4 %all-to-all-start.1 = ((bf16[16,2,32,256]{3,2,1,0:T(8,128)(2,1)}), bf16[16,2,32,256]{3,2,1,0:T(8,128)(2,1)S(1)}, u32[]{:S(2)}, u32[]{:S(2)}) async-start(bf16[16,2,32,256]{3,2,1,0:T(8,128)(2,1)} %get-tuple-element.29), calls=%async_computation.1 | async-start | bytes 1048576 | tf_op jit(solution)/shard_map/all_to_all | solution.py:646
  38.6 0.1 collective-permute-start.3
  38.6 4.2 %collective-permute-done.4.old_far_ref = bf16[16,2,32,256]{3,2,1,0:T(8,128)(2,1)S(1)} collective-permute-done((bf16[16,2,32,256]{3,2,1,0:T(8,128)(2,1)S(1)}, bf16[16,2,32,256]{3,2,1,0:T(8,128)(2,1)S(1)}, u32[]{:S(2)}, u32[]{:S(2)}) %collective-permute-start.4) | collective-permute-done | bytes 524320 | tf_op jit(solution)/shard_map/ppermute | solution.py:628
  42.8 0.0 copy-start.12
  42.8 0.0 collective-permute-start.5
  42.8 0.0 collective-permute-done.3.old_core_ref
  42.8 0.0 copy-start.13
  42.8 1.9 %collective-permute-done.5.old_far_core_ref = bf16[16,2,32,256]{3,2,1,0:T(8,128)(2,1)S(1)} collective-permute-done((bf16[16,2,32,256]{3,2,1,0:T(8,128)(2,1)S(1)}, bf16[16,2,32,256]{3,2,1,0:T(8,128)(2,1)S(1)}, u32[]{:S(2)}, u32[]{:S(2)}) %collective-permute-start.5) | collective-permute-done | bytes 524320 | tf_op jit(solution)/shard_map/ppermute | solution.py:625
  44.7 0.0 copy-start.14
  44.7 0.0 copy-done.1
  44.7 0.0 copy-done.2
  44.7 0.0 copy-done.3
  44.7 0.0 copy-done.4
  44.7 0.0 copy-done.12
  44.8 0.0 copy-done.13
  44.8 0.8 copy-done.14
  45.5 32.0 %attend_rest.1 = (bf16[512,2560]{1,0:T(8,128)(2,1)}, bf16[40,32,256]{2,1,0:T(8,128)(2,1)}, bf16[40,32,256]{2,1,0:T(8,128)(2,1)}) custom-call(s32[8]{0:T(128)} %lengths_ref.3, bf16[5,1024,256]{2,1,0:T(8,128)(2,1)} %get-tuple-element.24.roped_in, f32[5,1024,256]{2,1,0:T(8,128)} %get-tuple-element.25.acc_in, f32[5,1024,128]{2,1,0:T(8,128)} %get-tuple-element.26.stat_in, ...), custom_call_target="tpu_custom_call" | custom-call | flops 1 | bytes 1 | tf_op jit(solution)/shard_map/attend_rest/pallas_call | solution.py:547
  77.6 0.0 all-to-all-done.1.arrived_ref
  77.6 1.4 %place_new.1 = (bf16[40,32,256]{2,1,0:T(8,128)(2,1)}, bf16[40,32,256]{2,1,0:T(8,128)(2,1)}) custom-call(s32[16]{0:T(128)S(1)} %get-tuple-element.32.targets_ref, bf16[16,2,32,256]{3,2,1,0:T(8,128)(2,1)S(1)} %all-to-all-done.1.arrived_ref, bf16[40,32,256]{2,1,0:T(8,128)(2,1)} %get-tuple-element.33.key_in, ...), custom_call_target="tpu_custom_call", output_to_operand_aliasing={{0}: (2, {}), {1}: (3, {})} | custom-call | flops 1 | bytes 1 | tf_op jit(solution)/shard_map/place_new/pallas_call | solution.py:594
Async XLA Ops:
  0.6 10.8 %copy-start.6 = (bf16[1,512,256]{2,1,0:T(8,128)(2,1)S(1)}, bf16[1,512,256]{2,1,0:T(8,128)(2,1)}, u32[]{:S(2)}) copy-start(bf16[1,512,256]{2,1,0:T(8,128)(2,1)} %param.11) | copy-start | bytes 786436
  0.6 10.8 %copy-start.5 = (bf16[1,512,256]{2,1,0:T(8,128)(2,1)S(1)}, bf16[1,512,256]{2,1,0:T(8,128)(2,1)}, u32[]{:S(2)}) copy-start(bf16[1,512,256]{2,1,0:T(8,128)(2,1)} %param.10) | copy-start | bytes 786436
  0.7 0.7 copy-start.7
  1.4 10.1 %copy-start.9 = (s32[8]{0:T(128)S(1)}, s32[8]{0:T(128)}, u32[]{:S(2)}) copy-start(s32[8]{0:T(128)} %lengths_ref.3) | copy-start | bytes 100
  1.4 10.1 %copy-start.10 = (f32[1,128]{1,0:T(1,128)S(1)}, f32[1,128]{1,0:T(1,128)}, u32[]{:S(2)}) copy-start(f32[1,128]{1,0:T(1,128)} %constant.2.clone.freq_ref) | copy-start | bytes 1540
  4.2 22.6 %copy-start.8 = (s32[8,32]{1,0:T(8,128)S(1)}, s32[8,32]{1,0:T(8,128)}, u32[]{:S(2)}) copy-start(s32[8,32]{1,0:T(8,128)} %refs_0_.2) | copy-start | bytes 3076
  4.2 21.8 %all-to-all-start = ((bf16[8,2,2,32,256]{4,3,2,1,0:T(8,128)(2,1)}), bf16[8,2,2,32,256]{4,3,2,1,0:T(8,128)(2,1)S(1)}, u32[]{:S(2)}, u32[]{:S(2)}) async-start(bf16[8,2,2,32,256]{4,3,2,1,0:T(8,128)(2,1)} %pick_old.1), calls=%async_computation | async-start | bytes 1048576 | tf_op jit(solution)/shard_map/all_to_all | solution.py:631
  13.9 16.4 %copy-start = (bf16[16,2,32,256]{3,2,1,0:T(8,128)(2,1)S(1)}, bf16[16,2,32,256]{3,2,1,0:T(8,128)(2,1)}, u32[]{:S(2)}) copy-start(bf16[16,2,32,256]{3,2,1,0:T(8,128)(2,1)} %get-tuple-element.23.own_ref.refs_1_) | copy-start | bytes 1572868
  13.9 14.4 %collective-permute-start.1 = (bf16[16,2,32,256]{3,2,1,0:T(8,128)(2,1)}, bf16[16,2,32,256]{3,2,1,0:T(8,128)(2,1)S(1)}, u32[]{:S(2)}, u32[]{:S(2)}) collective-permute-start(bf16[16,2,32,256]{3,2,1,0:T(8,128)(2,1)} %get-tuple-element.23.own_ref.refs_1_), channel_id=1, source_target_pairs={{0,2},{2,0},{1,3},{3,1},{4,6},{6,4},{5,7},{7,5},{8,10},{10,8},{9,1... | collective-permute-start | bytes 1572872 | tf_op jit(solution)/shard_map/ppermute | solution.py:628
  15.4 14.6 %collective-permute-start = (bf16[16,2,32,256]{3,2,1,0:T(8,128)(2,1)}, bf16[16,2,32,256]{3,2,1,0:T(8,128)(2,1)S(1)}, u32[]{:S(2)}, u32[]{:S(2)}) collective-permute-start(bf16[16,2,32,256]{3,2,1,0:T(8,128)(2,1)} %get-tuple-element.23.own_ref.refs_1_), channel_id=1, source_target_pairs={{0,1},{1,0},{2,3},{3,2},{4,5},{5,4},{6,7},{7,6},{8,9},{9,8},{10,11... | collective-permute-start | bytes 1572872 | tf_op jit(solution)/shard_map/ppermute | solution.py:625
  25.9 0.8 %copy-start.11 = (bf16[8,2,2,32,256]{4,3,2,1,0:T(8,128)(2,1)}, bf16[8,2,2,32,256]{4,3,2,1,0:T(8,128)(2,1)S(1)}, u32[]{:S(2)}) copy-start(bf16[8,2,2,32,256]{4,3,2,1,0:T(8,128)(2,1)S(1)} %all-to-all-done) | copy-start | bytes 1572868
  28.4 16.4 %copy-start.1 = (bf16[16,2,32,256]{3,2,1,0:T(8,128)(2,1)}, bf16[16,2,32,256]{3,2,1,0:T(8,128)(2,1)S(1)}, u32[]{:S(2)}) copy-start(bf16[16,2,32,256]{3,2,1,0:T(8,128)(2,1)S(1)} %sort_old.1.old_ref) | copy-start | bytes 1572868
  28.4 16.3 %copy-start.2 = (bf16[16,2,32,256]{3,2,1,0:T(8,128)(2,1)}, bf16[16,2,32,256]{3,2,1,0:T(8,128)(2,1)S(1)}, u32[]{:S(2)}) copy-start(bf16[16,2,32,256]{3,2,1,0:T(8,128)(2,1)S(1)} %collective-permute-done.1.refs_3_.far_ref) | copy-start | bytes 1572868
  28.4 2.0 %collective-permute-start.2 = (bf16[16,2,32,256]{3,2,1,0:T(8,128)(2,1)S(1)}, bf16[16,2,32,256]{3,2,1,0:T(8,128)(2,1)S(1)}, u32[]{:S(2)}, u32[]{:S(2)}) collective-permute-start(bf16[16,2,32,256]{3,2,1,0:T(8,128)(2,1)S(1)} %collective-permute-done.1.refs_3_.far_ref), channel_id=1, source_target_pairs={{0,1},{1,0},{2,3},{3,2},{4,5},{5,4},{6,7},{7,6},{8,9},{9,8},{10,11... | collective-permute-start | bytes 1572872 | tf_op jit(solution)/shard_map/ppermute | solution.py:625
  28.5 14.3 %collective-permute-start.4 = (bf16[16,2,32,256]{3,2,1,0:T(8,128)(2,1)S(1)}, bf16[16,2,32,256]{3,2,1,0:T(8,128)(2,1)S(1)}, u32[]{:S(2)}, u32[]{:S(2)}) collective-permute-start(bf16[16,2,32,256]{3,2,1,0:T(8,128)(2,1)S(1)} %sort_old.1.old_ref), channel_id=1, source_target_pairs={{0,2},{2,0},{1,3},{3,1},{4,6},{6,4},{5,7},{7,5},{8,10},{10,8},{9,1... | collective-permute-start | bytes 1572872 | tf_op jit(solution)/shard_map/ppermute | solution.py:628
  30.1 14.7 %copy-start.3 = (bf16[16,2,32,256]{3,2,1,0:T(8,128)(2,1)}, bf16[16,2,32,256]{3,2,1,0:T(8,128)(2,1)S(1)}, u32[]{:S(2)}) copy-start(bf16[16,2,32,256]{3,2,1,0:T(8,128)(2,1)S(1)} %collective-permute-done.refs_2_.core_ref) | copy-start | bytes 1572868
  30.4 14.4 %copy-start.4 = (bf16[16,2,32,256]{3,2,1,0:T(8,128)(2,1)}, bf16[16,2,32,256]{3,2,1,0:T(8,128)(2,1)S(1)}, u32[]{:S(2)}) copy-start(bf16[16,2,32,256]{3,2,1,0:T(8,128)(2,1)S(1)} %collective-permute-done.2.refs_4_.far_core_ref) | copy-start | bytes 1572868
  33.1 44.4 %all-to-all-start.1 = ((bf16[16,2,32,256]{3,2,1,0:T(8,128)(2,1)}), bf16[16,2,32,256]{3,2,1,0:T(8,128)(2,1)S(1)}, u32[]{:S(2)}, u32[]{:S(2)}) async-start(bf16[16,2,32,256]{3,2,1,0:T(8,128)(2,1)} %get-tuple-element.29), calls=%async_computation.1 | async-start | bytes 1048576 | tf_op jit(solution)/shard_map/all_to_all | solution.py:646
  38.6 4.3 %collective-permute-start.3 = (bf16[16,2,32,256]{3,2,1,0:T(8,128)(2,1)S(1)}, bf16[16,2,32,256]{3,2,1,0:T(8,128)(2,1)S(1)}, u32[]{:S(2)}, u32[]{:S(2)}) collective-permute-start(bf16[16,2,32,256]{3,2,1,0:T(8,128)(2,1)S(1)} %sort_old.1.old_ref), channel_id=1, source_target_pairs={{0,1},{1,0},{2,3},{3,2},{4,5},{5,4},{6,7},{7,6},{8,9},{9,8},{10,11... | collective-permute-start | bytes 1572872 | tf_op jit(solution)/shard_map/ppermute | solution.py:625
  42.8 1.9 %copy-start.12 = (bf16[16,2,32,256]{3,2,1,0:T(8,128)(2,1)}, bf16[16,2,32,256]{3,2,1,0:T(8,128)(2,1)S(1)}, u32[]{:S(2)}) copy-start(bf16[16,2,32,256]{3,2,1,0:T(8,128)(2,1)S(1)} %collective-permute-done.4.old_far_ref) | copy-start | bytes 1572868
  42.8 1.9 %collective-permute-start.5 = (bf16[16,2,32,256]{3,2,1,0:T(8,128)(2,1)S(1)}, bf16[16,2,32,256]{3,2,1,0:T(8,128)(2,1)S(1)}, u32[]{:S(2)}, u32[]{:S(2)}) collective-permute-start(bf16[16,2,32,256]{3,2,1,0:T(8,128)(2,1)S(1)} %collective-permute-done.4.old_far_ref), channel_id=1, source_target_pairs={{0,1},{1,0},{2,3},{3,2},{4,5},{5,4},{6,7},{7,6},{8,9},{9,8},{10,11... | collective-permute-start | bytes 1572872 | tf_op jit(solution)/shard_map/ppermute | solution.py:625
  42.8 1.9 %copy-start.13 = (bf16[16,2,32,256]{3,2,1,0:T(8,128)(2,1)}, bf16[16,2,32,256]{3,2,1,0:T(8,128)(2,1)S(1)}, u32[]{:S(2)}) copy-start(bf16[16,2,32,256]{3,2,1,0:T(8,128)(2,1)S(1)} %collective-permute-done.3.old_core_ref) | copy-start | bytes 1572868
  44.7 0.8 %copy-start.14 = (bf16[16,2,32,256]{3,2,1,0:T(8,128)(2,1)}, bf16[16,2,32,256]{3,2,1,0:T(8,128)(2,1)S(1)}, u32[]{:S(2)}) copy-start(bf16[16,2,32,256]{3,2,1,0:T(8,128)(2,1)S(1)} %collective-permute-done.5.old_far_core_ref) | copy-start | bytes 1572868

commit v6 on v5

--- a/solution.py
+++ b/solution.py
@@ -50,28 +50,32 @@
     return chosen, found
 
 
-def pick_old_kernel(table_ref, key_ref, value_ref, out_ref, sem):
-    requests, cap = out_ref.shape[:2]
-    for r in range(requests):
-        chosen, _ = pages_here(table_ref, r, 0, table_ref.shape[1] // 2, cap, key_ref.shape[0])
-        for c in range(cap):
-            pltpu.make_async_copy(key_ref.at[chosen[c]], out_ref.at[r, c, 0], sem).start()
-            pltpu.make_async_copy(value_ref.at[chosen[c]], out_ref.at[r, c, 1], sem).start()
-    pltpu.make_async_copy(out_ref, out_ref, sem).wait()
-
-
-def pick_old(page_table, cap, key_cache, value_cache):
-    requests = page_table.shape[0]
+def pick_old_kernel(cap, table_ref, key_ref, value_ref, *refs):
+    outs, sems = refs[:-1], refs[-1]
+    for number, out_ref in enumerate(outs):
+        for place in range(out_ref.shape[0] // cap):
+            r = lax.axis_index("blk") ^ number if len(outs) > 1 else place
+            chosen, _ = pages_here(table_ref, r, 0, table_ref.shape[1] // 2, cap, key_ref.shape[0])
+            for c in range(cap):
+                slot = out_ref.at[place * cap + c]
+                pltpu.make_async_copy(key_ref.at[chosen[c]], slot.at[0], sems.at[number]).start()
+                pltpu.make_async_copy(value_ref.at[chosen[c]], slot.at[1], sems.at[number]).start()
+    for number, out_ref in enumerate(outs):
+        pltpu.make_async_copy(out_ref, out_ref, sems.at[number]).wait()
+
+
+def pick_old(page_table, cap, partners, key_cache, value_cache):
+    slots = page_table.shape[0] * cap // partners
     return pl.pallas_call(
-        pick_old_kernel,
-        out_shape=jax.ShapeDtypeStruct((requests, cap, 2) + key_cache.shape[1:], jnp.bfloat16),
+        lambda *refs: pick_old_kernel(cap, *refs),
+        out_shape=[jax.ShapeDtypeStruct((slots, 2) + key_cache.shape[1:], jnp.bfloat16)] * partners,
         in_specs=[smem_spec, hbm_spec, hbm_spec],
-        out_specs=vmem_spec,
-        scratch_shapes=[pltpu.SemaphoreType.DMA],
+        out_specs=[vmem_spec] * partners,
+        scratch_shapes=[pltpu.SemaphoreType.DMA((partners,))],
         cost_estimate=light,
         compiler_params=params(small_limit),
         name="pick_old",
-    )(page_table, *in_hbm(key_cache, value_cache))
+    )(*in_hbm(page_table, key_cache, value_cache))
 
 
 def owner_of(page, pages, owners):
@@ -133,25 +137,47 @@
     )(lengths, jnp.asarray(freq_table), keys, values)
 
 
-def sort_kernel(pages, cap, table_ref, old_ref, out_ref, counts_ref, sem):
+def sort_kernel(pages, cap, table_ref, *refs):
+    olds, (out_ref, page_of_ref, counts_ref, sem) = refs[:-4], refs[-4:]
     count = out_ref.shape[0]
-    for j, slot in enumerate(find_slots(table_ref, 0, count, cap, pages, counts_ref)):
-        pltpu.make_async_copy(old_ref.at[slot], out_ref.at[j], sem).start()
+    slots = find_slots(table_ref, 0, count, cap, pages, counts_ref)
+    if len(olds) == 1:
+        for j, slot in enumerate(slots):
+            pltpu.make_async_copy(olds[0].at[slot], out_ref.at[j], sem).start()
+    else:
+        for slot in range(page_of_ref.shape[0]):
+            page_of_ref[slot] = -1
+        for j, slot in enumerate(slots):
+            page_of_ref[slot] = j
+        for number, old_ref in enumerate(olds):
+            owner = lax.axis_index("blk") ^ number
+            for c in range(cap):
+                page = page_of_ref[owner * cap + c]
+
+                @pl.when(page >= 0)
+                def _(old_ref=old_ref, c=c, page=page):
+                    pltpu.make_async_copy(old_ref.at[c], out_ref.at[page], sem).start()
+
     pltpu.make_async_copy(out_ref, out_ref, sem).wait()
 
 
-def sort_old(page_table, blk_count, cap, pages, old):
+def sort_old(page_table, blk_count, cap, pages, olds):
     window = page_table.shape[1] // 2
+    shape = olds[0].shape[1:]
     return pl.pallas_call(
         lambda *refs: sort_kernel(pages, cap, *refs),
-        out_shape=jax.ShapeDtypeStruct((window,) + old.shape[1:], jnp.bfloat16),
-        in_specs=[smem_spec, hbm_spec],
+        out_shape=jax.ShapeDtypeStruct((window,) + shape, jnp.bfloat16),
+        in_specs=[smem_spec] + [any_spec] * len(olds),
         out_specs=vmem_spec,
-        scratch_shapes=[pltpu.SMEM((blk_count,), jnp.int32), pltpu.SemaphoreType.DMA],
+        scratch_shapes=[
+            pltpu.SMEM((blk_count * cap,), jnp.int32),
+            pltpu.SMEM((blk_count,), jnp.int32),
+            pltpu.SemaphoreType.DMA,
+        ],
         cost_estimate=light,
         compiler_params=params(small_limit),
         name="sort_old",
-    )(page_table, *in_hbm(old))
+    )(page_table, *olds)
 
 
 def pick_new_kernel(
@@ -285,8 +311,8 @@
         settle(which)
 
         def work(c, masked):
+            scores(t + 1, c, 1 - which, masked)
             weigh(c, which)
-            scores(t + 1, c, 1 - which, masked)
 
         loop(work)
         finish(t)
@@ -627,16 +653,23 @@
     def other_chip(value):
         return lax.ppermute(value, "group", [(0, 2), (2, 0), (1, 3), (3, 1)])
 
-    picked = pick_old(page_table, cap, key_cache, value_cache)
-    old = lax.all_to_all(picked, "blk", split_axis=0, concat_axis=0, tiled=True)
-    old = old.reshape((blk_count * cap,) + old.shape[2:])
-
-    fresh, cosine, sine = rotate_keys(lengths, new_keys[0], new_values[0])
+    partners = blk_count if blk_count <= 8 and blk_count & (blk_count - 1) == 0 else 1
+    picked = pick_old(page_table, cap, partners, key_cache, value_cache)
+    if partners > 1:
+        olds = [picked[0]] + [None] * (partners - 1)
+        for number in reversed(range(1, partners)):
+            pairs = [(i, i ^ number) for i in range(blk_count)]
+            olds[number] = lax.ppermute(picked[number], "blk", pairs)
+    else:
+        olds = [lax.all_to_all(picked[0], "blk", split_axis=0, concat_axis=0, tiled=True)]
+
+    fresh, cosine, sine = rotate_keys(lengths, after(new_keys[0], picked[0]), new_values[0])
     fresh_far = other_chip(fresh)
     fresh_core = other_core(fresh)
-    roped, acc, stat = diagonal_part(after(queries[0], picked), cosine, sine, fresh)
-
-    old = sort_old(after(page_table, stat), blk_count, cap, pages, old)
+
+    roped, acc, stat = diagonal_part(after(queries[0], picked[0]), cosine, sine, fresh)
+
+    old = sort_old(after(page_table, stat), blk_count, cap, pages, olds)
     old_far = other_chip(old)
     old_core = other_core(old)
     fresh_far_core = other_core(after(fresh_far, old))

time: 79.6 us -> 86.2 us (1.083)
  starting transfers between devices: 15.9 us -> 21.1 us
  local copies, waits for them, and re-layouts: 2.35 us -> 4.02 us
    ppermute x0 -> x7, starting transfers between devices: none -> 11.7 us  [body(): olds[number] = lax.ppermute(picked[number], 'blk', pairs)]
    all_to_all x1 -> x0, starting transfers between devices: 7.26 us -> none  [body(): old = lax.all_to_all(picked, 'blk', split_axis=0, concat_axis=0, tiled=True)]
    unnamed x30 -> x26, local copies, waits for them, and re-layouts: 2.35 us -> 4.02 us
  transfers between devices with their start and end apart: 8 -> 14, of which waited for: 4 -> 3; matrix products, arithmetic and copies ran while one was open for 0% -> 0% of each run, Pallas kernels for 61% -> 54%
where the time goes in v6:
time: 86.2 us; the launch traced here: 85.7 us
  Pallas kernels  52.4 us (61%)
  starting transfers between devices  21.1 us (24%)
  waiting for transfers between devices  7.16 us (8%)
  local copies, waits for them, and re-layouts  4.02 us (5%)
  between operations  0.99 us (1%)
    pallas_call x1, Pallas kernels, rest_part(): pl.pallas_call(rest_kernel, out_shape=(pltpu.HBM((rows, width), jnp.bfloa...  32.3 us
    ppermute x7, starting transfers between devices, body(): olds[number] = lax.ppermute(picked[number], 'blk', pairs)  11.7 us
    pallas_call x1, Pallas kernels, diagonal_part(): pl.pallas_call(diagonal_kernel, out_shape=(pltpu.HBM((items, head_pair *...  9.65 us
    all_to_all x1, starting transfers between devices, body(): lax.all_to_all(new, 'blk', split_axis=0, concat_axis=0, tiled=True)  5.32 us
    ppermute x2, waiting for transfers between devices, other_chip(): return lax.ppermute(value, 'group', [(0, 2), (2, 0), (1, 3), (3, 1)])  4.22 us
    unnamed x26, local copies, waits for them, and re-layouts  4.02 us
    ppermute x2, starting transfers between devices, other_chip(): return lax.ppermute(value, 'group', [(0, 2), (2, 0), (1, 3), (3, 1)])  3.47 us
    ppermute x4, waiting for transfers between devices, other_core(): return lax.ppermute(value, 'group', [(0, 1), (1, 0), (2, 3), (3, 2)])  2.92 us
  transfers between devices with their start and end apart: 14, of which 3 were waited for; matrix products, arithmetic and copies ran while one was open for 0% of the time, Pallas kernels for 54%

profile of v6, /device:TPU:0, one launch (start us, length us, event | category | flops | bytes accessed | tf_op | source)
XLA Modules:
  0.0 85.7 jit_solution(2864118413180589710)
XLA Ops:
  0.6 0.0 copy-start.7
  0.6 2.3 %pick_old.1 = (bf16[2,2,32,256]{3,2,1,0:T(8,128)(2,1)S(1)}, bf16[2,2,32,256]{3,2,1,0:T(8,128)(2,1)S(1)}, bf16[2,2,32,256]{3,2,1,0:T(8,128)(2,1)S(1)}, bf16[2,2,3...) custom-call(s32[8,32]{1,0:T(8,128)} %refs_0_.4, ...), custom_call_target="tpu_custom_call" | custom-call | flops 1 | bytes 1 | tf_op jit(solution)/shard_map/pick_old/pallas_call | solution.py:69
  2.9 0.0 copy-start.5
  2.9 0.9 %copy-done.5 = bf16[1,512,256]{2,1,0:T(8,128)(2,1)S(1)} copy-done((bf16[1,512,256]{2,1,0:T(8,128)(2,1)S(1)}, bf16[1,512,256]{2,1,0:T(8,128)(2,1)}, u32[]{:S(2)}) %copy-start.5) | copy-done | bytes 262168
  3.9 0.0 copy-start.6
  3.9 0.9 %copy-done.6 = bf16[1,512,256]{2,1,0:T(8,128)(2,1)S(1)} copy-done((bf16[1,512,256]{2,1,0:T(8,128)(2,1)S(1)}, bf16[1,512,256]{2,1,0:T(8,128)(2,1)}, u32[]{:S(2)}) %copy-start.6) | copy-done | bytes 262168
  4.8 0.0 copy-start.8
  4.8 0.7 copy-done.8
  5.5 0.0 copy-start.9
  5.5 0.7 copy-done.9
  6.1 2.4 %rotate_keys.1 = (bf16[16,2,32,256]{3,2,1,0:T(8,128)(2,1)}, f32[512,128]{1,0:T(8,128)}, f32[512,128]{1,0:T(8,128)}) custom-call(s32[8]{0:T(128)S(1)} %copy-done.8, f32[1,128]{1,0:T(1,128)S(1)} %copy-done.9, bf16[512,256]{1,0:T(8,128)(2,1)S(1)} %bitcast.4, bf16[512,256]{1,0:T(8,128)(2,1)S(1)} %bitcast.5), custom_call_target="tpu_custom_call" | custom-call | flops 1 | bytes 1 | tf_op jit(solution)/shard_map/rotate_keys/pallas_call | solution.py:125
  8.6 0.0 copy-start
  8.6 3.0 %collective-permute-start.1 = (bf16[16,2,32,256]{3,2,1,0:T(8,128)(2,1)}, bf16[16,2,32,256]{3,2,1,0:T(8,128)(2,1)S(1)}, u32[]{:S(2)}, u32[]{:S(2)}) collective-permute-start(bf16[16,2,32,256]{3,2,1,0:T(8,128)(2,1)} %get-tuple-element.34.own_ref.refs_1_), channel_id=1, source_target_pairs={{0,2},{2,0},{1,3},{3,1},{4,6},{6,4},{5,7},{7,5},{8,10},{10,8},{9,1... | collective-permute-start | bytes 1572872 | tf_op jit(solution)/shard_map/ppermute | solution.py:654
  11.5 1.5 %collective-permute-start.2 = (bf16[2,2,32,256]{3,2,1,0:T(8,128)(2,1)S(1)}, bf16[2,2,32,256]{3,2,1,0:T(8,128)(2,1)S(1)}, u32[]{:S(2)}, u32[]{:S(2)}) collective-permute-start(bf16[2,2,32,256]{3,2,1,0:T(8,128)(2,1)S(1)} %get-tuple-element.39), channel_id=1, source_target_pairs={{0,4},{4,0},{8,12},{12,8},{16,20},{20,16},{24,28},{28,24},{1,5},{5... | collective-permute-start | bytes 196616 | tf_op jit(solution)/shard_map/ppermute | solution.py:662
  13.0 1.6 %collective-permute-start.3 = (bf16[2,2,32,256]{3,2,1,0:T(8,128)(2,1)S(1)}, bf16[2,2,32,256]{3,2,1,0:T(8,128)(2,1)S(1)}, u32[]{:S(2)}, u32[]{:S(2)}) collective-permute-start(bf16[2,2,32,256]{3,2,1,0:T(8,128)(2,1)S(1)} %get-tuple-element.40), channel_id=1, source_target_pairs={{0,8},{4,12},{8,0},{12,4},{16,24},{20,28},{24,16},{28,20},{1,9},{5... | collective-permute-start | bytes 196616 | tf_op jit(solution)/shard_map/ppermute | solution.py:662
  14.6 0.4 collective-permute-start.4
  15.0 2.6 %collective-permute-start.5 = (bf16[2,2,32,256]{3,2,1,0:T(8,128)(2,1)S(1)}, bf16[2,2,32,256]{3,2,1,0:T(8,128)(2,1)S(1)}, u32[]{:S(2)}, u32[]{:S(2)}) collective-permute-start(bf16[2,2,32,256]{3,2,1,0:T(8,128)(2,1)S(1)} %get-tuple-element.42), channel_id=1, source_target_pairs={{0,16},{4,20},{8,24},{12,28},{16,0},{20,4},{24,8},{28,12},{1,17},{... | collective-permute-start | bytes 196616 | tf_op jit(solution)/shard_map/ppermute | solution.py:662
  17.6 0.0 collective-permute-done.2.refs_2_
  17.6 1.7 %collective-permute-start.6 = (bf16[2,2,32,256]{3,2,1,0:T(8,128)(2,1)S(1)}, bf16[2,2,32,256]{3,2,1,0:T(8,128)(2,1)S(1)}, u32[]{:S(2)}, u32[]{:S(2)}) collective-permute-start(bf16[2,2,32,256]{3,2,1,0:T(8,128)(2,1)S(1)} %get-tuple-element.43), channel_id=1, source_target_pairs={{0,20},{4,16},{8,28},{12,24},{16,4},{20,0},{24,12},{28,8},{1,21},{... | collective-permute-start | bytes 196616 | tf_op jit(solution)/shard_map/ppermute | solution.py:662
  19.3 0.0 collective-permute-done.3.refs_3_
  19.3 3.2 %collective-permute-start.7 = (bf16[2,2,32,256]{3,2,1,0:T(8,128)(2,1)S(1)}, bf16[2,2,32,256]{3,2,1,0:T(8,128)(2,1)S(1)}, u32[]{:S(2)}, u32[]{:S(2)}) collective-permute-start(bf16[2,2,32,256]{3,2,1,0:T(8,128)(2,1)S(1)} %get-tuple-element.44), channel_id=1, source_target_pairs={{0,24},{4,28},{8,16},{12,20},{16,8},{20,12},{24,0},{28,4},{1,25},{... | collective-permute-start | bytes 196616 | tf_op jit(solution)/shard_map/ppermute | solution.py:662
  22.5 0.0 collective-permute-done.4.refs_4_
  22.5 0.7 collective-permute-start.8
  23.2 9.7 %attend_diagonal.1 = (bf16[5,1024,256]{2,1,0:T(8,128)(2,1)}, f32[5,1024,256]{2,1,0:T(8,128)}, f32[5,1024,128]{2,1,0:T(8,128)}) custom-call(bf16[512,2560]{1,0:T(8,128)(2,1)} %bitcast.6, f32[512,128]{1,0:T(8,128)} %get-tuple-element.32.cos_ref, f32[512,128]{1,0:T(8,128)} %get-tuple-element.33.sin_ref, bf16[16,2,32,256]{3,2,1,0:T(8,128)(2,1)} %get-tuple-element.34.own_ref.refs_1_), custom_call_target="tpu_custom_call" | custom-call | flops 1 | bytes 1 | tf_op jit(solution)/shard_map/attend_diagonal/pallas_call | solution.py:419
  32.9 0.0 collective-permute-done.5.refs_5_
  32.9 0.0 copy-done
  32.9 0.1 collective-permute-start
  33.0 0.0 collective-permute-done.6.refs_6_
  33.0 0.0 collective-permute-done.7.refs_7_
  33.0 0.0 collective-permute-done.8.refs_8_
  33.0 0.0 copy-done.7
  33.0 1.6 %sort_old.1.old_ref = bf16[16,2,32,256]{3,2,1,0:T(8,128)(2,1)S(1)} custom-call(s32[8,32]{1,0:T(8,128)S(1)} %copy-done.7, bf16[2,2,32,256]{3,2,1,0:T(8,128)(2,1)S(1)} %get-tuple-element.29.refs_1_, bf16[2,2,32,256]{3,2,1,0:T(8,128)(2,1)S(1)} %collective-permute-done.2.refs_2_, bf16[2,2,32,256]{3,2,1,0:T(8,128)(2,1)S(1)} %collective-permute-done.3.refs_3_, ...), custom_call_target="tpu_custom_call" | custom-call | flops 1 | bytes 1 | tf_op jit(solution)/shard_map/sort_old/pallas_call | solution.py:167
  34.6 0.0 copy-start.1
  34.6 0.0 collective-permute-done.1.refs_3_.far_ref
  34.7 0.0 copy-start.2
  34.7 0.5 collective-permute-start.9
  35.2 0.5 collective-permute-start.11
  35.7 0.0 collective-permute-done.refs_2_.core_ref
  35.7 0.0 copy-start.3
  35.7 1.0 %collective-permute-done.9.refs_4_.far_core_ref = bf16[16,2,32,256]{3,2,1,0:T(8,128)(2,1)S(1)} collective-permute-done((bf16[16,2,32,256]{3,2,1,0:T(8,128)(2,1)S(1)}, bf16[16,2,32,256]{3,2,1,0:T(8,128)(2,1)S(1)}, u32[]{:S(2)}, u32[]{:S(2)}) %collective-permute-start.9) | collective-permute-done | bytes 524320 | tf_op jit(solution)/shard_map/ppermute | solution.py:651
  36.7 0.0 copy-start.4
  36.7 2.7 %pick_new.1 = (bf16[16,2,32,256]{3,2,1,0:T(8,128)(2,1)}, s32[16]{0:T(128)S(1)}) custom-call(s32[8,32]{1,0:T(8,128)S(1)} %copy-done.7, bf16[16,2,32,256]{3,2,1,0:T(8,128)(2,1)S(1)} %copy-done, bf16[16,2,32,256]{3,2,1,0:T(8,128)(2,1)S(1)} %collective-permute-done.refs_2_.core_ref, bf16[16,2,32,256]{3,2,1,0:T(8,128)(2,1)S(1)} %collective-permute-done.1.refs_3_.far_ref, ...), custom_call_target="tpu_custom_call" | custom-call | flops 1 | bytes 1 | tf_op jit(solution)/shard_map/pick_new/pallas_call | solution.py:208
  39.5 5.3 %all-to-all-start = ((bf16[16,2,32,256]{3,2,1,0:T(8,128)(2,1)}), bf16[16,2,32,256]{3,2,1,0:T(8,128)(2,1)S(1)}, u32[]{:S(2)}, u32[]{:S(2)}) async-start(bf16[16,2,32,256]{3,2,1,0:T(8,128)(2,1)} %get-tuple-element.47), calls=%async_computation | async-start | bytes 1048576 | tf_op jit(solution)/shard_map/all_to_all | solution.py:679
  44.8 0.1 collective-permute-start.10
  44.9 4.2 %collective-permute-done.11.old_far_ref = bf16[16,2,32,256]{3,2,1,0:T(8,128)(2,1)S(1)} collective-permute-done((bf16[16,2,32,256]{3,2,1,0:T(8,128)(2,1)S(1)}, bf16[16,2,32,256]{3,2,1,0:T(8,128)(2,1)S(1)}, u32[]{:S(2)}, u32[]{:S(2)}) %collective-permute-start.11) | collective-permute-done | bytes 524320 | tf_op jit(solution)/shard_map/ppermute | solution.py:654
  49.1 0.0 copy-start.10
  49.1 0.0 collective-permute-start.12
  49.1 0.0 collective-permute-done.10.old_core_ref
  49.1 0.0 copy-start.11
  49.1 1.9 %collective-permute-done.12.old_far_core_ref = bf16[16,2,32,256]{3,2,1,0:T(8,128)(2,1)S(1)} collective-permute-done((bf16[16,2,32,256]{3,2,1,0:T(8,128)(2,1)S(1)}, bf16[16,2,32,256]{3,2,1,0:T(8,128)(2,1)S(1)}, u32[]{:S(2)}, u32[]{:S(2)}) %collective-permute-start.12) | collective-permute-done | bytes 524320 | tf_op jit(solution)/shard_map/ppermute | solution.py:651
  51.0 0.0 copy-start.12
  51.0 0.0 copy-done.1
  51.0 0.0 copy-done.2
  51.0 0.0 copy-done.3
  51.0 0.0 copy-done.4
  51.0 0.0 copy-done.10
  51.1 0.0 copy-done.11
  51.1 0.8 copy-done.12
  51.9 32.3 %attend_rest.1 = (bf16[512,2560]{1,0:T(8,128)(2,1)}, bf16[40,32,256]{2,1,0:T(8,128)(2,1)}, bf16[40,32,256]{2,1,0:T(8,128)(2,1)}) custom-call(s32[8]{0:T(128)} %lengths_ref.3, bf16[5,1024,256]{2,1,0:T(8,128)(2,1)} %get-tuple-element.35.roped_in, f32[5,1024,256]{2,1,0:T(8,128)} %get-tuple-element.36.acc_in, f32[5,1024,128]{2,1,0:T(8,128)} %get-tuple-element.37.stat_in, ...), custom_call_target="tpu_custom_call" | custom-call | flops 1 | bytes 1 | tf_op jit(solution)/shard_map/attend_rest/pallas_call | solution.py:573
  84.2 0.0 all-to-all-done.arrived_ref
  84.2 1.4 %place_new.1 = (bf16[40,32,256]{2,1,0:T(8,128)(2,1)}, bf16[40,32,256]{2,1,0:T(8,128)(2,1)}) custom-call(s32[16]{0:T(128)S(1)} %get-tuple-element.50.targets_ref, bf16[16,2,32,256]{3,2,1,0:T(8,128)(2,1)S(1)} %all-to-all-done.arrived_ref, bf16[40,32,256]{2,1,0:T(8,128)(2,1)} %get-tuple-element.51.key_in, ...), custom_call_target="tpu_custom_call", output_to_operand_aliasing={{0}: (2, {}), {1}: (3, {})} | custom-call | flops 1 | bytes 1 | tf_op jit(solution)/shard_map/place_new/pallas_call | solution.py:620
Async XLA Ops:
  0.6 32.4 %copy-start.7 = (s32[8,32]{1,0:T(8,128)S(1)}, s32[8,32]{1,0:T(8,128)}, u32[]{:S(2)}) copy-start(s32[8,32]{1,0:T(8,128)} %refs_0_.4) | copy-start | bytes 3076
  2.9 1.0 %copy-start.5 = (bf16[1,512,256]{2,1,0:T(8,128)(2,1)S(1)}, bf16[1,512,256]{2,1,0:T(8,128)(2,1)}, u32[]{:S(2)}) copy-start(bf16[1,512,256]{2,1,0:T(8,128)(2,1)} %param.10) | copy-start | bytes 786436
  3.9 0.9 %copy-start.6 = (bf16[1,512,256]{2,1,0:T(8,128)(2,1)S(1)}, bf16[1,512,256]{2,1,0:T(8,128)(2,1)}, u32[]{:S(2)}) copy-start(bf16[1,512,256]{2,1,0:T(8,128)(2,1)} %param.11) | copy-start | bytes 786436
  4.8 0.7 copy-start.8
  5.5 0.7 copy-start.9
  8.6 24.3 %copy-start = (bf16[16,2,32,256]{3,2,1,0:T(8,128)(2,1)S(1)}, bf16[16,2,32,256]{3,2,1,0:T(8,128)(2,1)}, u32[]{:S(2)}) copy-start(bf16[16,2,32,256]{3,2,1,0:T(8,128)(2,1)} %get-tuple-element.34.own_ref.refs_1_) | copy-start | bytes 1572868
  8.6 26.1 %collective-permute-start.1 = (bf16[16,2,32,256]{3,2,1,0:T(8,128)(2,1)}, bf16[16,2,32,256]{3,2,1,0:T(8,128)(2,1)S(1)}, u32[]{:S(2)}, u32[]{:S(2)}) collective-permute-start(bf16[16,2,32,256]{3,2,1,0:T(8,128)(2,1)} %get-tuple-element.34.own_ref.refs_1_), channel_id=1, source_target_pairs={{0,2},{2,0},{1,3},{3,1},{4,6},{6,4},{5,7},{7,5},{8,10},{10,8},{9,1... | collective-permute-start | bytes 1572872 | tf_op jit(solution)/shard_map/ppermute | solution.py:654
  11.5 6.1 %collective-permute-start.2 = (bf16[2,2,32,256]{3,2,1,0:T(8,128)(2,1)S(1)}, bf16[2,2,32,256]{3,2,1,0:T(8,128)(2,1)S(1)}, u32[]{:S(2)}, u32[]{:S(2)}) collective-permute-start(bf16[2,2,32,256]{3,2,1,0:T(8,128)(2,1)S(1)} %get-tuple-element.39), channel_id=1, source_target_pairs={{0,4},{4,0},{8,12},{12,8},{16,20},{20,16},{24,28},{28,24},{1,5},{5... | collective-permute-start | bytes 196616 | tf_op jit(solution)/shard_map/ppermute | solution.py:662
  13.0 6.3 %collective-permute-start.3 = (bf16[2,2,32,256]{3,2,1,0:T(8,128)(2,1)S(1)}, bf16[2,2,32,256]{3,2,1,0:T(8,128)(2,1)S(1)}, u32[]{:S(2)}, u32[]{:S(2)}) collective-permute-start(bf16[2,2,32,256]{3,2,1,0:T(8,128)(2,1)S(1)} %get-tuple-element.40), channel_id=1, source_target_pairs={{0,8},{4,12},{8,0},{12,4},{16,24},{20,28},{24,16},{28,20},{1,9},{5... | collective-permute-start | bytes 196616 | tf_op jit(solution)/shard_map/ppermute | solution.py:662
  14.6 7.9 %collective-permute-start.4 = (bf16[2,2,32,256]{3,2,1,0:T(8,128)(2,1)S(1)}, bf16[2,2,32,256]{3,2,1,0:T(8,128)(2,1)S(1)}, u32[]{:S(2)}, u32[]{:S(2)}) collective-permute-start(bf16[2,2,32,256]{3,2,1,0:T(8,128)(2,1)S(1)} %get-tuple-element.41), channel_id=1, source_target_pairs={{0,12},{4,8},{8,4},{12,0},{16,28},{20,24},{24,20},{28,16},{1,13},{... | collective-permute-start | bytes 196616 | tf_op jit(solution)/shard_map/ppermute | solution.py:662
  15.0 17.8 %collective-permute-start.5 = (bf16[2,2,32,256]{3,2,1,0:T(8,128)(2,1)S(1)}, bf16[2,2,32,256]{3,2,1,0:T(8,128)(2,1)S(1)}, u32[]{:S(2)}, u32[]{:S(2)}) collective-permute-start(bf16[2,2,32,256]{3,2,1,0:T(8,128)(2,1)S(1)} %get-tuple-element.42), channel_id=1, source_target_pairs={{0,16},{4,20},{8,24},{12,28},{16,0},{20,4},{24,8},{28,12},{1,17},{... | collective-permute-start | bytes 196616 | tf_op jit(solution)/shard_map/ppermute | solution.py:662
  17.6 15.3 %collective-permute-start.6 = (bf16[2,2,32,256]{3,2,1,0:T(8,128)(2,1)S(1)}, bf16[2,2,32,256]{3,2,1,0:T(8,128)(2,1)S(1)}, u32[]{:S(2)}, u32[]{:S(2)}) collective-permute-start(bf16[2,2,32,256]{3,2,1,0:T(8,128)(2,1)S(1)} %get-tuple-element.43), channel_id=1, source_target_pairs={{0,20},{4,16},{8,28},{12,24},{16,4},{20,0},{24,12},{28,8},{1,21},{... | collective-permute-start | bytes 196616 | tf_op jit(solution)/shard_map/ppermute | solution.py:662
  19.3 13.6 %collective-permute-start.7 = (bf16[2,2,32,256]{3,2,1,0:T(8,128)(2,1)S(1)}, bf16[2,2,32,256]{3,2,1,0:T(8,128)(2,1)S(1)}, u32[]{:S(2)}, u32[]{:S(2)}) collective-permute-start(bf16[2,2,32,256]{3,2,1,0:T(8,128)(2,1)S(1)} %get-tuple-element.44), channel_id=1, source_target_pairs={{0,24},{4,28},{8,16},{12,20},{16,8},{20,12},{24,0},{28,4},{1,25},{... | collective-permute-start | bytes 196616 | tf_op jit(solution)/shard_map/ppermute | solution.py:662
  22.5 10.5 %collective-permute-start.8 = (bf16[2,2,32,256]{3,2,1,0:T(8,128)(2,1)S(1)}, bf16[2,2,32,256]{3,2,1,0:T(8,128)(2,1)S(1)}, u32[]{:S(2)}, u32[]{:S(2)}) collective-permute-start(bf16[2,2,32,256]{3,2,1,0:T(8,128)(2,1)S(1)} %get-tuple-element.45), channel_id=1, source_target_pairs={{0,28},{4,24},{8,20},{12,16},{16,12},{20,8},{24,4},{28,0},{1,29},{... | collective-permute-start | bytes 196616 | tf_op jit(solution)/shard_map/ppermute | solution.py:662
  32.9 2.8 %collective-permute-start = (bf16[16,2,32,256]{3,2,1,0:T(8,128)(2,1)S(1)}, bf16[16,2,32,256]{3,2,1,0:T(8,128)(2,1)S(1)}, u32[]{:S(2)}, u32[]{:S(2)}) collective-permute-start(bf16[16,2,32,256]{3,2,1,0:T(8,128)(2,1)S(1)} %copy-done), channel_id=1, source_target_pairs={{0,1},{1,0},{2,3},{3,2},{4,5},{5,4},{6,7},{7,6},{8,9},{9,8},{10,11... | collective-permute-start | bytes 1572872 | tf_op jit(solution)/shard_map/ppermute | solution.py:651
  34.6 16.4 %copy-start.1 = (bf16[16,2,32,256]{3,2,1,0:T(8,128)(2,1)}, bf16[16,2,32,256]{3,2,1,0:T(8,128)(2,1)S(1)}, u32[]{:S(2)}) copy-start(bf16[16,2,32,256]{3,2,1,0:T(8,128)(2,1)S(1)} %sort_old.1.old_ref) | copy-start | bytes 1572868
  34.7 16.4 %copy-start.2 = (bf16[16,2,32,256]{3,2,1,0:T(8,128)(2,1)}, bf16[16,2,32,256]{3,2,1,0:T(8,128)(2,1)S(1)}, u32[]{:S(2)}) copy-start(bf16[16,2,32,256]{3,2,1,0:T(8,128)(2,1)S(1)} %collective-permute-done.1.refs_3_.far_ref) | copy-start | bytes 1572868
  34.7 2.1 %collective-permute-start.9 = (bf16[16,2,32,256]{3,2,1,0:T(8,128)(2,1)S(1)}, bf16[16,2,32,256]{3,2,1,0:T(8,128)(2,1)S(1)}, u32[]{:S(2)}, u32[]{:S(2)}) collective-permute-start(bf16[16,2,32,256]{3,2,1,0:T(8,128)(2,1)S(1)} %collective-permute-done.1.refs_3_.far_ref), channel_id=1, source_target_pairs={{0,1},{1,0},{2,3},{3,2},{4,5},{5,4},{6,7},{7,6},{8,9},{9,8},{10,11... | collective-permute-start | bytes 1572872 | tf_op jit(solution)/shard_map/ppermute | solution.py:651
  35.2 13.9 %collective-permute-start.11 = (bf16[16,2,32,256]{3,2,1,0:T(8,128)(2,1)S(1)}, bf16[16,2,32,256]{3,2,1,0:T(8,128)(2,1)S(1)}, u32[]{:S(2)}, u32[]{:S(2)}) collective-permute-start(bf16[16,2,32,256]{3,2,1,0:T(8,128)(2,1)S(1)} %sort_old.1.old_ref), channel_id=1, source_target_pairs={{0,2},{2,0},{1,3},{3,1},{4,6},{6,4},{5,7},{7,5},{8,10},{10,8},{9,1... | collective-permute-start | bytes 1572872 | tf_op jit(solution)/shard_map/ppermute | solution.py:654
  35.7 15.3 %copy-start.3 = (bf16[16,2,32,256]{3,2,1,0:T(8,128)(2,1)}, bf16[16,2,32,256]{3,2,1,0:T(8,128)(2,1)S(1)}, u32[]{:S(2)}) copy-start(bf16[16,2,32,256]{3,2,1,0:T(8,128)(2,1)S(1)} %collective-permute-done.refs_2_.core_ref) | copy-start | bytes 1572868
  36.7 14.3 %copy-start.4 = (bf16[16,2,32,256]{3,2,1,0:T(8,128)(2,1)}, bf16[16,2,32,256]{3,2,1,0:T(8,128)(2,1)S(1)}, u32[]{:S(2)}) copy-start(bf16[16,2,32,256]{3,2,1,0:T(8,128)(2,1)S(1)} %collective-permute-done.9.refs_4_.far_core_ref) | copy-start | bytes 1572868
  39.5 44.7 %all-to-all-start = ((bf16[16,2,32,256]{3,2,1,0:T(8,128)(2,1)}), bf16[16,2,32,256]{3,2,1,0:T(8,128)(2,1)S(1)}, u32[]{:S(2)}, u32[]{:S(2)}) async-start(bf16[16,2,32,256]{3,2,1,0:T(8,128)(2,1)} %get-tuple-element.47), calls=%async_computation | async-start | bytes 1048576 | tf_op jit(solution)/shard_map/all_to_all | solution.py:679
  44.8 4.3 %collective-permute-start.10 = (bf16[16,2,32,256]{3,2,1,0:T(8,128)(2,1)S(1)}, bf16[16,2,32,256]{3,2,1,0:T(8,128)(2,1)S(1)}, u32[]{:S(2)}, u32[]{:S(2)}) collective-permute-start(bf16[16,2,32,256]{3,2,1,0:T(8,128)(2,1)S(1)} %sort_old.1.old_ref), channel_id=1, source_target_pairs={{0,1},{1,0},{2,3},{3,2},{4,5},{5,4},{6,7},{7,6},{8,9},{9,8},{10,11... | collective-permute-start | bytes 1572872 | tf_op jit(solution)/shard_map/ppermute | solution.py:651
  49.1 1.9 %copy-start.10 = (bf16[16,2,32,256]{3,2,1,0:T(8,128)(2,1)}, bf16[16,2,32,256]{3,2,1,0:T(8,128)(2,1)S(1)}, u32[]{:S(2)}) copy-start(bf16[16,2,32,256]{3,2,1,0:T(8,128)(2,1)S(1)} %collective-permute-done.11.old_far_ref) | copy-start | bytes 1572868
  49.1 1.9 %collective-permute-start.12 = (bf16[16,2,32,256]{3,2,1,0:T(8,128)(2,1)S(1)}, bf16[16,2,32,256]{3,2,1,0:T(8,128)(2,1)S(1)}, u32[]{:S(2)}, u32[]{:S(2)}) collective-permute-start(bf16[16,2,32,256]{3,2,1,0:T(8,128)(2,1)S(1)} %collective-permute-done.11.old_far_ref), channel_id=1, source_target_pairs={{0,1},{1,0},{2,3},{3,2},{4,5},{5,4},{6,7},{7,6},{8,9},{9,8},{10,11... | collective-permute-start | bytes 1572872 | tf_op jit(solution)/shard_map/ppermute | solution.py:651
  49.1 1.9 %copy-start.11 = (bf16[16,2,32,256]{3,2,1,0:T(8,128)(2,1)}, bf16[16,2,32,256]{3,2,1,0:T(8,128)(2,1)S(1)}, u32[]{:S(2)}) copy-start(bf16[16,2,32,256]{3,2,1,0:T(8,128)(2,1)S(1)} %collective-permute-done.10.old_core_ref) | copy-start | bytes 1572868
  51.0 0.8 copy-start.12

commit v7 on v5

--- a/solution.py
+++ b/solution.py
@@ -15,6 +15,7 @@
 vmem_spec = pl.BlockSpec(memory_space=pltpu.VMEM)
 small_limit = 16 * 1024 * 1024
 head_pair = 2
+middle_limit = 32 * 1024 * 1024
 large_limit = 58 * 1024 * 1024
 
 
@@ -71,7 +72,7 @@
         cost_estimate=light,
         compiler_params=params(small_limit),
         name="pick_old",
-    )(page_table, *in_hbm(key_cache, value_cache))
+    )(*in_hbm(page_table, key_cache, value_cache))
 
 
 def owner_of(page, pages, owners):
@@ -151,7 +152,7 @@
         cost_estimate=light,
         compiler_params=params(small_limit),
         name="sort_old",
-    )(page_table, *in_hbm(old))
+    )(*in_hbm(page_table, old))
 
 
 def pick_new_kernel(
@@ -195,7 +196,7 @@
         cost_estimate=light,
         compiler_params=params(small_limit),
         name="pick_new",
-    )(page_table, *sources)
+    )(*in_hbm(page_table), *sources)
 
 
 def lane_fold(values, combine):
@@ -339,13 +340,14 @@
 
 
 def diagonal_kernel(
-    query_ref, cos_ref, sin_ref, own_ref, roped_out, acc_out, stat_out,
+    first, query_ref, cos_ref, sin_ref, own_ref, roped_out, acc_out, stat_out,
     q_ref, roped_ref, acc_ref, stat_ref, kv_ref, s_0, s_1, most_0, most_1, top_ref, sum_ref, values_ref,
     bias_ref, query_sem, sem, out_sem,
 ):
     rows = q_ref.shape[0]
     items = roped_ref.shape[0]
-    query_copy = pltpu.make_async_copy(query_ref, q_ref, query_sem)
+    columns = pl.ds(first * head_pair * 256, items * head_pair * 256)
+    query_copy = pltpu.make_async_copy(query_ref.at[:, columns], q_ref, query_sem)
     query_copy.start()
     fetch(own_ref, 0, kv_ref, 0, step_slots, sem)
     row = lax.broadcasted_iota(jnp.int32, (rows, step_keys), 0)
@@ -387,26 +389,25 @@
     pltpu.make_async_copy(stat_ref, stat_out, out_sem).wait()
 
 
-def diagonal_part(queries, cosine, sine, own):
-    rows, width = queries.shape
-    items = width // (256 * head_pair)
+def diagonal_part(first, items, queries, cosine, sine, own):
+    rows = queries.shape[0]
     return pl.pallas_call(
-        diagonal_kernel,
+        lambda *refs: diagonal_kernel(first, *refs),
         out_shape=(pltpu.HBM((items, head_pair * rows, 256), jnp.bfloat16),) + state_out(items, rows),
         in_specs=[hbm_spec, vmem_spec, vmem_spec, hbm_spec],
         out_specs=(hbm_spec,) * 3,
-        scratch_shapes=[pltpu.VMEM((rows, width), jnp.bfloat16)]
+        scratch_shapes=[pltpu.VMEM((rows, items * head_pair * 256), jnp.bfloat16)]
         + state_shapes(items, rows)
         + working(rows, 1)
         + [pltpu.SemaphoreType.DMA] * 3,
         cost_estimate=light,
-        compiler_params=params(large_limit),
+        compiler_params=params(middle_limit),
         name="attend_diagonal",
     )(*in_hbm(queries), cosine, sine, *in_hbm(own))
 
 
 def rest_kernel(
-    lengths_ref, roped_in, acc_in, stat_in, core_ref, far_ref, far_core_ref,
+    lengths_ref, roped_a, acc_a, stat_a, roped_b, acc_b, stat_b, core_ref, far_ref, far_core_ref,
     old_ref, old_core_ref, old_far_ref, old_far_core_ref, weight_ref, key_ref, value_ref,
     hidden_ref, key_out_ref, value_out_ref,
     roped_ref, acc_ref, stat_ref, kv_ref, s_0, s_1, most_0, most_1, top_ref, sum_ref, values_ref,
@@ -426,13 +427,18 @@
     near = (old_ref, old_core_ref)
     far = (old_far_ref, old_far_core_ref)
 
-    def copies(t):
-        return [
-            pltpu.make_async_copy(source.at[t], target.at[t], state_sems.at[number, t])
-            for number, (source, target) in enumerate(
-                ((roped_in, roped_ref), (stat_in, stat_ref), (acc_in, acc_ref))
-            )
-        ]
+    state = (roped_ref, stat_ref, acc_ref)
+    head_start = roped_a.shape[0]
+
+    def start_state(t):
+        sources = (roped_a, stat_a, acc_a) if t < head_start else (roped_b, stat_b, acc_b)
+        for number, (source, target) in enumerate(zip(sources, state)):
+            place = t if t < head_start else t - head_start
+            pltpu.make_async_copy(source.at[place], target.at[t], state_sems.at[number, t]).start()
+
+    def wait_state(t):
+        for number, target in enumerate(state):
+            pltpu.make_async_copy(target.at[t], target.at[t], state_sems.at[number, t]).wait()
 
     pool_loads = [
         pltpu.make_async_copy(key_ref, key_pool, pool_sems.at[0]),
@@ -442,8 +448,7 @@
         pltpu.make_async_copy(key_pool, key_out_ref, pool_sems.at[0]),
         pltpu.make_async_copy(value_pool, value_out_ref, pool_sems.at[1]),
     ]
-    for copy in copies(0):
-        copy.start()
+    start_state(0)
 
     @pl.when(odd == 1)
     def _():
@@ -469,8 +474,7 @@
     for copy in pool_loads:
         copy.start()
     for t in range(1, items):
-        for copy in copies(t):
-            copy.start()
+        start_state(t)
     weight_copy = pltpu.make_async_copy(weight_ref, w_ref, weight_sem)
     weight_copy.start()
 
@@ -485,8 +489,7 @@
     lane = lax.broadcasted_iota(jnp.int32, stat_ref.shape[1:], 1)
 
     def begin(t, most_ref):
-        for copy in copies(t):
-            copy.wait()
+        wait_state(t)
         most_ref[...] = jnp.where(lane < 64, stat_ref[t], masked_score)
 
     def finish(t):
@@ -539,11 +542,12 @@
         copy.wait()
 
 
-def rest_part(lengths, state, slots, weight, key_cache, value_cache):
-    items, pair_rows, _ = state[0].shape
+def rest_part(lengths, states, slots, weight, key_cache, value_cache):
+    items = sum(state[0].shape[0] for state in states)
+    pair_rows = states[0][0].shape[1]
     rows = pair_rows // head_pair
     width = weight.shape[1]
-    chunk = 512
+    chunk = 256
     return pl.pallas_call(
         rest_kernel,
         out_shape=(
@@ -551,7 +555,7 @@
             pltpu.HBM(key_cache.shape, jnp.bfloat16),
             pltpu.HBM(value_cache.shape, jnp.bfloat16),
         ),
-        in_specs=[smem_spec] + [hbm_spec] * 3 + [any_spec] * 7 + [hbm_spec] * 3,
+        in_specs=[smem_spec] + [hbm_spec] * 6 + [any_spec] * 7 + [hbm_spec] * 3,
         out_specs=(hbm_spec,) * 3,
         scratch_shapes=state_shapes(items, rows)
         + working(rows, 4)
@@ -569,7 +573,7 @@
         cost_estimate=light,
         compiler_params=params(large_limit),
         name="attend_rest",
-    )(lengths, *in_hbm(*state), *slots, *in_hbm(weight, key_cache, value_cache))
+    )(lengths, *in_hbm(*states[0], *states[1]), *slots, *in_hbm(weight, key_cache, value_cache))
 
 
 def place_kernel(targets_ref, arrived_ref, key_in, value_in, key_ref, value_ref, buffer_ref, load_sem, sem):
@@ -634,19 +638,22 @@
     fresh, cosine, sine = rotate_keys(lengths, new_keys[0], new_values[0])
     fresh_far = other_chip(fresh)
     fresh_core = other_core(fresh)
-    roped, acc, stat = diagonal_part(after(queries[0], picked), cosine, sine, fresh)
-
-    old = sort_old(after(page_table, stat), blk_count, cap, pages, old)
+    pairs = queries.shape[2] // (256 * head_pair)
+    front = (pairs + 1) // 2
+    state = diagonal_part(0, front, after(queries[0], picked), cosine, sine, fresh)
+
+    old = sort_old(after(page_table, state[2]), blk_count, cap, pages, old)
     old_far = other_chip(old)
     old_core = other_core(old)
+    later = diagonal_part(front, pairs - front, after(queries[0], old), cosine, sine, fresh)
     fresh_far_core = other_core(after(fresh_far, old))
     new, targets = pick_new(
-        page_table, blk_count, cap, pages, (fresh, fresh_core, fresh_far, fresh_far_core)
+        after(page_table, later[2]), blk_count, cap, pages, (fresh, fresh_core, fresh_far, fresh_far_core)
     )
     arrived = lax.all_to_all(new, "blk", split_axis=0, concat_axis=0, tiled=True)
     old_far_core = other_core(after(old_far, new))
     hidden, key_out, value_out = rest_part(
-        lengths, (roped, acc, stat),
+        lengths, (state, later),
         (fresh_core, fresh_far, fresh_far_core, old, old_core, old_far, old_far_core),
         out_weight, key_cache, value_cache,
     )

time: 79.6 us -> 80.9 us (1.016)
  Pallas kernels: 52.7 us -> 55.4 us
  waiting for transfers between devices: 7.13 us -> 4.77 us
    ppermute x2, waiting for transfers between devices: 4.18 us -> 0.01 us  [other_chip(): return lax.ppermute(value, 'group', [(0, 2), (2, 0), (1, 3), (3, 1)])]
    all_to_all x1, waiting for transfers between devices: 0.74 us -> 2.4 us  [body(): old = lax.all_to_all(picked, 'blk', split_axis=0, concat_axis=0, tiled=True)]
    pallas_call x1 -> x2, Pallas kernels: 9.72 us -> 11 us  [diagonal_part(): pl.pallas_call(lambda *refs: diagonal_kernel(first, *refs), out_shape=(pl...]
    pallas_call x1, Pallas kernels: 32 us -> 32.9 us  [rest_part(): pl.pallas_call(rest_kernel, out_shape=(pltpu.HBM((rows, width), jnp.bfloa...]
  transfers between devices with their start and end apart: 8 -> 8, of which waited for: 4 -> 3; matrix products, arithmetic and copies ran while one was open for 0% -> 0% of each run, Pallas kernels for 61% -> 64%
where the time goes in v7:
time: 80.9 us; the launch traced here: 80.2 us
  Pallas kernels  55.4 us (68%)
  starting transfers between devices  16.3 us (20%)
  waiting for transfers between devices  4.77 us (6%)
  local copies, waits for them, and re-layouts  2.76 us (3%)
  between operations  1.03 us (1%)
    pallas_call x1, Pallas kernels, rest_part(): pl.pallas_call(rest_kernel, out_shape=(pltpu.HBM((rows, width), jnp.bfloa...  32.9 us
    pallas_call x2, Pallas kernels, diagonal_part(): pl.pallas_call(lambda *refs: diagonal_kernel(first, *refs), out_shape=(pl...  11 us
    all_to_all x1, starting transfers between devices, body(): old = lax.all_to_all(picked, 'blk', split_axis=0, concat_axis=0, tiled=True)  7.26 us
    all_to_all x1, starting transfers between devices, body(): lax.all_to_all(new, 'blk', split_axis=0, concat_axis=0, tiled=True)  5.28 us
    ppermute x2, starting transfers between devices, other_chip(): return lax.ppermute(value, 'group', [(0, 2), (2, 0), (1, 3), (3, 1)])  3.1 us
    pallas_call x1, Pallas kernels, pick_old(): pl.pallas_call(pick_old_kernel, out_shape=jax.ShapeDtypeStruct((requests,...  3.01 us
    pallas_call x1, Pallas kernels, pick_new(): pl.pallas_call(lambda *refs: pick_new_kernel(pages, cap, *refs), out_shap...  2.9 us
    unnamed x30, local copies, waits for them, and re-layouts  2.76 us
  transfers between devices with their start and end apart: 8, of which 3 were waited for; matrix products, arithmetic and copies ran while one was open for 0% of the time, Pallas kernels for 64%

profile of v7, /device:TPU:0, one launch (start us, length us, event | category | flops | bytes accessed | tf_op | source)
XLA Modules:
  0.0 80.2 jit_solution(13089240401113294528)
XLA Ops:
  0.6 0.0 copy-start.12
  0.6 0.0 copy-start.11
  0.7 0.0 copy-start.10
  0.7 0.0 copy-start.9
  0.7 3.0 %pick_old.1 = bf16[8,2,2,32,256]{4,3,2,1,0:T(8,128)(2,1)} custom-call(s32[8,32]{1,0:T(8,128)} %refs_0_.1, bf16[40,32,256]{2,1,0:T(8,128)(2,1)} %key_ref.3, bf16[40,32,256]{2,1,0:T(8,128)(2,1)} %value_ref.3), custom_call_target="tpu_custom_call" | custom-call | flops 1 | bytes 1 | tf_op jit(solution)/shard_map/pick_old/pallas_call | solution.py:66
  3.7 7.3 %all-to-all-start = ((bf16[8,2,2,32,256]{4,3,2,1,0:T(8,128)(2,1)}), bf16[8,2,2,32,256]{4,3,2,1,0:T(8,128)(2,1)}, u32[]{:S(2)}, u32[]{:S(2)}) async-start(bf16[8,2,2,32,256]{4,3,2,1,0:T(8,128)(2,1)} %pick_old.1), calls=%async_computation | async-start | bytes 1048576 | tf_op jit(solution)/shard_map/all_to_all | solution.py:635
  11.0 0.0 copy-done.12
  11.0 0.0 copy-done.11
  11.0 0.0 copy-done.10
  11.0 0.0 copy-done.9
  11.0 2.5 %rotate_keys.1 = (bf16[16,2,32,256]{3,2,1,0:T(8,128)(2,1)}, f32[512,128]{1,0:T(8,128)}, f32[512,128]{1,0:T(8,128)}) custom-call(s32[8]{0:T(128)S(1)} %copy-done.11, f32[1,128]{1,0:T(1,128)S(1)} %copy-done.12, bf16[512,256]{1,0:T(8,128)(2,1)S(1)} %bitcast.5, bf16[512,256]{1,0:T(8,128)(2,1)S(1)} %bitcast.6), custom_call_target="tpu_custom_call" | custom-call | flops 1 | bytes 1 | tf_op jit(solution)/shard_map/rotate_keys/pallas_call | solution.py:122
  13.4 1.5 %collective-permute-start.1 = (bf16[16,2,32,256]{3,2,1,0:T(8,128)(2,1)}, bf16[16,2,32,256]{3,2,1,0:T(8,128)(2,1)S(1)}, u32[]{:S(2)}, u32[]{:S(2)}) collective-permute-start(bf16[16,2,32,256]{3,2,1,0:T(8,128)(2,1)} %get-tuple-element.28.refs_3_.refs_1_), channel_id=1, source_target_pairs={{0,2},{2,0},{1,3},{3,1},{4,6},{6,4},{5,7},{7,5},{8,10},{10,8},{9,1... | collective-permute-start | bytes 1572872 | tf_op jit(solution)/shard_map/ppermute | solution.py:632
  15.0 0.0 collective-permute-start
  15.0 0.0 copy-start.5
  15.0 0.9 %copy-done.5 = f32[512,128]{1,0:T(8,128)S(1)} copy-done((f32[512,128]{1,0:T(8,128)S(1)}, f32[512,128]{1,0:T(8,128)}, u32[]{:S(2)}) %copy-start.5) | copy-done | bytes 262168
  15.9 0.0 copy-start.7
  15.9 0.9 %copy-done.7 = f32[512,128]{1,0:T(8,128)S(1)} copy-done((f32[512,128]{1,0:T(8,128)S(1)}, f32[512,128]{1,0:T(8,128)}, u32[]{:S(2)}) %copy-start.7) | copy-done | bytes 262168
  16.9 0.0 copy-start.6
  16.9 0.0 copy-start.8
  16.9 6.3 %attend_diagonal.2 = (bf16[3,1024,256]{2,1,0:T(8,128)(2,1)}, f32[3,1024,256]{2,1,0:T(8,128)}, f32[3,1024,128]{2,1,0:T(8,128)}) custom-call(bf16[512,2560]{1,0:T(8,128)(2,1)} %bitcast.7, f32[512,128]{1,0:T(8,128)S(1)} %copy-done.5, f32[512,128]{1,0:T(8,128)S(1)} %copy-done.7, bf16[16,2,32,256]{3,2,1,0:T(8,128)(2,1)} %get-tuple-element.28.refs_3_.refs_1_), custom_call_target="tpu_custom_call" | custom-call | flops 1 | bytes 1 | tf_op jit(solution)/shard_map/attend_diagonal/pallas_call | solution.py:394
  23.1 0.0 copy-start
  23.1 2.4 %all-to-all-done = bf16[8,2,2,32,256]{4,3,2,1,0:T(8,128)(2,1)} async-done(((bf16[8,2,2,32,256]{4,3,2,1,0:T(8,128)(2,1)}), bf16[8,2,2,32,256]{4,3,2,1,0:T(8,128)(2,1)}, u32[]{:S(2)}, u32[]{:S(2)}) %all-to-all-start) | async-done | bytes 524320 | tf_op jit(solution)/shard_map/all_to_all | solution.py:635
  25.5 1.8 %sort_old.1.old_ref = bf16[16,2,32,256]{3,2,1,0:T(8,128)(2,1)S(1)} custom-call(s32[8,32]{1,0:T(8,128)} %refs_0_.1, bf16[16,2,32,256]{3,2,1,0:T(8,128)(2,1)} %bitcast.3.refs_1_), custom_call_target="tpu_custom_call" | custom-call | flops 1 | bytes 1 | tf_op jit(solution)/shard_map/sort_old/pallas_call | solution.py:146
  27.3 0.0 copy-start.1
  27.3 0.0 collective-permute-done.1.refs_3_.far_ref
  27.3 0.0 copy-start.2
  27.3 0.1 collective-permute-start.2
  27.4 1.6 %collective-permute-start.4 = (bf16[16,2,32,256]{3,2,1,0:T(8,128)(2,1)S(1)}, bf16[16,2,32,256]{3,2,1,0:T(8,128)(2,1)}, u32[]{:S(2)}, u32[]{:S(2)}) collective-permute-start(bf16[16,2,32,256]{3,2,1,0:T(8,128)(2,1)S(1)} %sort_old.1.old_ref), channel_id=1, source_target_pairs={{0,2},{2,0},{1,3},{3,1},{4,6},{6,4},{5,7},{7,5},{8,10},{10,8},{9,1... | collective-permute-start | bytes 1572872 | tf_op jit(solution)/shard_map/ppermute | solution.py:632
  29.0 0.0 copy-done.6
  29.0 0.0 copy-done.8
  29.0 4.8 %attend_diagonal.3 = (bf16[2,1024,256]{2,1,0:T(8,128)(2,1)}, f32[2,1024,256]{2,1,0:T(8,128)}, f32[2,1024,128]{2,1,0:T(8,128)}) custom-call(bf16[512,2560]{1,0:T(8,128)(2,1)} %bitcast.8, f32[512,128]{1,0:T(8,128)S(1)} %copy-done.6, f32[512,128]{1,0:T(8,128)S(1)} %copy-done.8, bf16[16,2,32,256]{3,2,1,0:T(8,128)(2,1)} %get-tuple-element.28.refs_3_.refs_1_), custom_call_target="tpu_custom_call" | custom-call | flops 1 | bytes 1 | tf_op jit(solution)/shard_map/attend_diagonal/pallas_call | solution.py:394
  33.8 0.0 collective-permute-done.refs_2_.core_ref
  33.8 0.0 copy-start.3
  33.8 0.0 collective-permute-done.2.refs_4_.far_core_ref
  33.8 0.0 copy-done
  33.8 0.0 copy-start.4
  33.8 2.9 %pick_new.1 = (bf16[16,2,32,256]{3,2,1,0:T(8,128)(2,1)}, s32[16]{0:T(128)S(1)}) custom-call(s32[8,32]{1,0:T(8,128)} %refs_0_.1, bf16[16,2,32,256]{3,2,1,0:T(8,128)(2,1)S(1)} %copy-done, bf16[16,2,32,256]{3,2,1,0:T(8,128)(2,1)S(1)} %collective-permute-done.refs_2_.core_ref, bf16[16,2,32,256]{3,2,1,0:T(8,128)(2,1)S(1)} %collective-permute-done.1.refs_3_.far_ref, ...), custom_call_target="tpu_custom_call" | custom-call | flops 1 | bytes 1 | tf_op jit(solution)/shard_map/pick_new/pallas_call | solution.py:183
  36.7 0.0 copy-done.2
  36.8 5.3 %all-to-all-start.1 = ((bf16[16,2,32,256]{3,2,1,0:T(8,128)(2,1)}), bf16[16,2,32,256]{3,2,1,0:T(8,128)(2,1)S(1)}, u32[]{:S(2)}, u32[]{:S(2)}) async-start(bf16[16,2,32,256]{3,2,1,0:T(8,128)(2,1)} %get-tuple-element.39), calls=%async_computation.1 | async-start | bytes 1048576 | tf_op jit(solution)/shard_map/all_to_all | solution.py:653
  42.0 0.0 copy-done.1
  42.0 0.1 collective-permute-start.3
  42.1 0.0 collective-permute-done.4.old_far_ref
  42.1 0.5 collective-permute-start.5
  42.6 1.4 %collective-permute-done.3.old_core_ref = bf16[16,2,32,256]{3,2,1,0:T(8,128)(2,1)S(1)} collective-permute-done((bf16[16,2,32,256]{3,2,1,0:T(8,128)(2,1)S(1)}, bf16[16,2,32,256]{3,2,1,0:T(8,128)(2,1)S(1)}, u32[]{:S(2)}, u32[]{:S(2)}) %collective-permute-start.3) | collective-permute-done | bytes 524320 | tf_op jit(solution)/shard_map/ppermute | solution.py:629
  44.0 0.0 copy-start.13
  44.0 1.0 %collective-permute-done.5.old_far_core_ref = bf16[16,2,32,256]{3,2,1,0:T(8,128)(2,1)S(1)} collective-permute-done((bf16[16,2,32,256]{3,2,1,0:T(8,128)(2,1)}, bf16[16,2,32,256]{3,2,1,0:T(8,128)(2,1)S(1)}, u32[]{:S(2)}, u32[]{:S(2)}) %collective-permute-start.5) | collective-permute-done | bytes 524320 | tf_op jit(solution)/shard_map/ppermute | solution.py:629
  45.0 0.0 copy-start.14
  45.0 0.0 copy-done.3
  45.0 0.0 copy-done.4
  45.0 0.0 copy-done.13
  45.0 0.8 %copy-done.14 = bf16[16,2,32,256]{3,2,1,0:T(8,128)(2,1)} copy-done((bf16[16,2,32,256]{3,2,1,0:T(8,128)(2,1)}, bf16[16,2,32,256]{3,2,1,0:T(8,128)(2,1)S(1)}, u32[]{:S(2)}) %copy-start.14) | copy-done | bytes 524312
  45.8 32.9 %attend_rest.1 = (bf16[512,2560]{1,0:T(8,128)(2,1)}, bf16[40,32,256]{2,1,0:T(8,128)(2,1)}, bf16[40,32,256]{2,1,0:T(8,128)(2,1)}) custom-call(s32[8]{0:T(128)} %lengths_ref.3, bf16[3,1024,256]{2,1,0:T(8,128)(2,1)} %get-tuple-element.29.roped_a, f32[3,1024,256]{2,1,0:T(8,128)} %get-tuple-element.30.acc_a, f32[3,1024,128]{2,1,0:T(8,128)} %get-tuple-element.31.stat_a, ...), custom_call_target="tpu_custom_call" | custom-call | flops 1 | bytes 1 | tf_op jit(solution)/shard_map/attend_rest/pallas_call | solution.py:551
  78.7 0.0 all-to-all-done.1.arrived_ref
  78.7 1.4 %place_new.1 = (bf16[40,32,256]{2,1,0:T(8,128)(2,1)}, bf16[40,32,256]{2,1,0:T(8,128)(2,1)}) custom-call(s32[16]{0:T(128)S(1)} %get-tuple-element.42.targets_ref, bf16[16,2,32,256]{3,2,1,0:T(8,128)(2,1)S(1)} %all-to-all-done.1.arrived_ref, bf16[40,32,256]{2,1,0:T(8,128)(2,1)} %get-tuple-element.43.key_in, ...), custom_call_target="tpu_custom_call", output_to_operand_aliasing={{0}: (2, {}), {1}: (3, {})} | custom-call | flops 1 | bytes 1 | tf_op jit(solution)/shard_map/place_new/pallas_call | solution.py:598
Async XLA Ops:
  0.6 10.3 %copy-start.12 = (f32[1,128]{1,0:T(1,128)S(1)}, f32[1,128]{1,0:T(1,128)}, u32[]{:S(2)}) copy-start(f32[1,128]{1,0:T(1,128)} %constant.2.clone.freq_ref) | copy-start | bytes 1540
  0.6 10.3 %copy-start.11 = (s32[8]{0:T(128)S(1)}, s32[8]{0:T(128)}, u32[]{:S(2)}) copy-start(s32[8]{0:T(128)} %lengths_ref.3) | copy-start | bytes 100
  0.7 10.3 %copy-start.10 = (bf16[1,512,256]{2,1,0:T(8,128)(2,1)S(1)}, bf16[1,512,256]{2,1,0:T(8,128)(2,1)}, u32[]{:S(2)}) copy-start(bf16[1,512,256]{2,1,0:T(8,128)(2,1)} %param.11) | copy-start | bytes 786436
  0.7 10.3 %copy-start.9 = (bf16[1,512,256]{2,1,0:T(8,128)(2,1)S(1)}, bf16[1,512,256]{2,1,0:T(8,128)(2,1)}, u32[]{:S(2)}) copy-start(bf16[1,512,256]{2,1,0:T(8,128)(2,1)} %param.10) | copy-start | bytes 786436
  3.7 21.9 %all-to-all-start = ((bf16[8,2,2,32,256]{4,3,2,1,0:T(8,128)(2,1)}), bf16[8,2,2,32,256]{4,3,2,1,0:T(8,128)(2,1)}, u32[]{:S(2)}, u32[]{:S(2)}) async-start(bf16[8,2,2,32,256]{4,3,2,1,0:T(8,128)(2,1)} %pick_old.1), calls=%async_computation | async-start | bytes 1048576 | tf_op jit(solution)/shard_map/all_to_all | solution.py:635
  13.4 13.9 %collective-permute-start.1 = (bf16[16,2,32,256]{3,2,1,0:T(8,128)(2,1)}, bf16[16,2,32,256]{3,2,1,0:T(8,128)(2,1)S(1)}, u32[]{:S(2)}, u32[]{:S(2)}) collective-permute-start(bf16[16,2,32,256]{3,2,1,0:T(8,128)(2,1)} %get-tuple-element.28.refs_3_.refs_1_), channel_id=1, source_target_pairs={{0,2},{2,0},{1,3},{3,1},{4,6},{6,4},{5,7},{7,5},{8,10},{10,8},{9,1... | collective-permute-start | bytes 1572872 | tf_op jit(solution)/shard_map/ppermute | solution.py:632
  15.0 18.8 %collective-permute-start = (bf16[16,2,32,256]{3,2,1,0:T(8,128)(2,1)}, bf16[16,2,32,256]{3,2,1,0:T(8,128)(2,1)S(1)}, u32[]{:S(2)}, u32[]{:S(2)}) collective-permute-start(bf16[16,2,32,256]{3,2,1,0:T(8,128)(2,1)} %get-tuple-element.28.refs_3_.refs_1_), channel_id=1, source_target_pairs={{0,1},{1,0},{2,3},{3,2},{4,5},{5,4},{6,7},{7,6},{8,9},{9,8},{10,11... | collective-permute-start | bytes 1572872 | tf_op jit(solution)/shard_map/ppermute | solution.py:629
  15.0 1.0 %copy-start.5 = (f32[512,128]{1,0:T(8,128)S(1)}, f32[512,128]{1,0:T(8,128)}, u32[]{:S(2)}) copy-start(f32[512,128]{1,0:T(8,128)} %get-tuple-element.26.refs_1_) | copy-start | bytes 786436
  15.9 0.9 %copy-start.7 = (f32[512,128]{1,0:T(8,128)S(1)}, f32[512,128]{1,0:T(8,128)}, u32[]{:S(2)}) copy-start(f32[512,128]{1,0:T(8,128)} %get-tuple-element.27.refs_2_) | copy-start | bytes 786436
  16.9 12.1 %copy-start.6 = (f32[512,128]{1,0:T(8,128)S(1)}, f32[512,128]{1,0:T(8,128)}, u32[]{:S(2)}) copy-start(f32[512,128]{1,0:T(8,128)} %get-tuple-element.26.refs_1_) | copy-start | bytes 786436
  16.9 12.1 %copy-start.8 = (f32[512,128]{1,0:T(8,128)S(1)}, f32[512,128]{1,0:T(8,128)}, u32[]{:S(2)}) copy-start(f32[512,128]{1,0:T(8,128)} %get-tuple-element.27.refs_2_) | copy-start | bytes 786436
  23.1 10.7 %copy-start = (bf16[16,2,32,256]{3,2,1,0:T(8,128)(2,1)S(1)}, bf16[16,2,32,256]{3,2,1,0:T(8,128)(2,1)}, u32[]{:S(2)}) copy-start(bf16[16,2,32,256]{3,2,1,0:T(8,128)(2,1)} %get-tuple-element.28.refs_3_.refs_1_) | copy-start | bytes 1572868
  27.3 14.7 %copy-start.1 = (bf16[16,2,32,256]{3,2,1,0:T(8,128)(2,1)}, bf16[16,2,32,256]{3,2,1,0:T(8,128)(2,1)S(1)}, u32[]{:S(2)}) copy-start(bf16[16,2,32,256]{3,2,1,0:T(8,128)(2,1)S(1)} %sort_old.1.old_ref) | copy-start | bytes 1572868
  27.3 9.4 %copy-start.2 = (bf16[16,2,32,256]{3,2,1,0:T(8,128)(2,1)}, bf16[16,2,32,256]{3,2,1,0:T(8,128)(2,1)S(1)}, u32[]{:S(2)}) copy-start(bf16[16,2,32,256]{3,2,1,0:T(8,128)(2,1)S(1)} %collective-permute-done.1.refs_3_.far_ref) | copy-start | bytes 1572868
  27.3 6.5 %collective-permute-start.2 = (bf16[16,2,32,256]{3,2,1,0:T(8,128)(2,1)S(1)}, bf16[16,2,32,256]{3,2,1,0:T(8,128)(2,1)S(1)}, u32[]{:S(2)}, u32[]{:S(2)}) collective-permute-start(bf16[16,2,32,256]{3,2,1,0:T(8,128)(2,1)S(1)} %collective-permute-done.1.refs_3_.far_ref), channel_id=1, source_target_pairs={{0,1},{1,0},{2,3},{3,2},{4,5},{5,4},{6,7},{7,6},{8,9},{9,8},{10,11... | collective-permute-start | bytes 1572872 | tf_op jit(solution)/shard_map/ppermute | solution.py:629
  27.4 14.7 %collective-permute-start.4 = (bf16[16,2,32,256]{3,2,1,0:T(8,128)(2,1)S(1)}, bf16[16,2,32,256]{3,2,1,0:T(8,128)(2,1)}, u32[]{:S(2)}, u32[]{:S(2)}) collective-permute-start(bf16[16,2,32,256]{3,2,1,0:T(8,128)(2,1)S(1)} %sort_old.1.old_ref), channel_id=1, source_target_pairs={{0,2},{2,0},{1,3},{3,1},{4,6},{6,4},{5,7},{7,5},{8,10},{10,8},{9,1... | collective-permute-start | bytes 1572872 | tf_op jit(solution)/shard_map/ppermute | solution.py:632
  33.8 11.2 %copy-start.3 = (bf16[16,2,32,256]{3,2,1,0:T(8,128)(2,1)}, bf16[16,2,32,256]{3,2,1,0:T(8,128)(2,1)S(1)}, u32[]{:S(2)}) copy-start(bf16[16,2,32,256]{3,2,1,0:T(8,128)(2,1)S(1)} %collective-permute-done.refs_2_.core_ref) | copy-start | bytes 1572868
  33.8 11.2 %copy-start.4 = (bf16[16,2,32,256]{3,2,1,0:T(8,128)(2,1)}, bf16[16,2,32,256]{3,2,1,0:T(8,128)(2,1)S(1)}, u32[]{:S(2)}) copy-start(bf16[16,2,32,256]{3,2,1,0:T(8,128)(2,1)S(1)} %collective-permute-done.2.refs_4_.far_core_ref) | copy-start | bytes 1572868
  36.8 41.9 %all-to-all-start.1 = ((bf16[16,2,32,256]{3,2,1,0:T(8,128)(2,1)}), bf16[16,2,32,256]{3,2,1,0:T(8,128)(2,1)S(1)}, u32[]{:S(2)}, u32[]{:S(2)}) async-start(bf16[16,2,32,256]{3,2,1,0:T(8,128)(2,1)} %get-tuple-element.39), calls=%async_computation.1 | async-start | bytes 1048576 | tf_op jit(solution)/shard_map/all_to_all | solution.py:653
  42.0 2.0 %collective-permute-start.3 = (bf16[16,2,32,256]{3,2,1,0:T(8,128)(2,1)S(1)}, bf16[16,2,32,256]{3,2,1,0:T(8,128)(2,1)S(1)}, u32[]{:S(2)}, u32[]{:S(2)}) collective-permute-start(bf16[16,2,32,256]{3,2,1,0:T(8,128)(2,1)S(1)} %sort_old.1.old_ref), channel_id=1, source_target_pairs={{0,1},{1,0},{2,3},{3,2},{4,5},{5,4},{6,7},{7,6},{8,9},{9,8},{10,11... | collective-permute-start | bytes 1572872 | tf_op jit(solution)/shard_map/ppermute | solution.py:629
  42.1 2.8 %collective-permute-start.5 = (bf16[16,2,32,256]{3,2,1,0:T(8,128)(2,1)}, bf16[16,2,32,256]{3,2,1,0:T(8,128)(2,1)S(1)}, u32[]{:S(2)}, u32[]{:S(2)}) collective-permute-start(bf16[16,2,32,256]{3,2,1,0:T(8,128)(2,1)} %collective-permute-done.4.old_far_ref), channel_id=1, source_target_pairs={{0,1},{1,0},{2,3},{3,2},{4,5},{5,4},{6,7},{7,6},{8,9},{9,8},{10,11... | collective-permute-start | bytes 1572872 | tf_op jit(solution)/shard_map/ppermute | solution.py:629
  44.0 1.0 %copy-start.13 = (bf16[16,2,32,256]{3,2,1,0:T(8,128)(2,1)}, bf16[16,2,32,256]{3,2,1,0:T(8,128)(2,1)S(1)}, u32[]{:S(2)}) copy-start(bf16[16,2,32,256]{3,2,1,0:T(8,128)(2,1)S(1)} %collective-permute-done.3.old_core_ref) | copy-start | bytes 1572868
  45.0 0.8 %copy-start.14 = (bf16[16,2,32,256]{3,2,1,0:T(8,128)(2,1)}, bf16[16,2,32,256]{3,2,1,0:T(8,128)(2,1)S(1)}, u32[]{:S(2)}) copy-start(bf16[16,2,32,256]{3,2,1,0:T(8,128)(2,1)S(1)} %collective-permute-done.5.old_far_core_ref) | copy-start | bytes 1572868

commit v8 on v5

--- a/solution.py
+++ b/solution.py
@@ -7,8 +7,8 @@
 from jax.sharding import PartitionSpec as P
 
 masked_score = -1e30
-step_keys = 512
-step_slots = 16
+block_keys = 512
+block_slots = 16
 any_spec = pl.BlockSpec(memory_space=pl.ANY)
 hbm_spec = pl.BlockSpec(memory_space=pltpu.HBM)
 smem_spec = pl.BlockSpec(memory_space=pltpu.SMEM)
@@ -71,7 +71,7 @@
         cost_estimate=light,
         compiler_params=params(small_limit),
         name="pick_old",
-    )(page_table, *in_hbm(key_cache, value_cache))
+    )(*in_hbm(page_table, key_cache, value_cache))
 
 
 def owner_of(page, pages, owners):
@@ -225,17 +225,19 @@
     fetch(sources[1], first, kv_ref, place + 4, 4, sem)
 
 
-def wait_rows(kv_ref, steps, most, sem):
+def wait_rows(kv_ref, blocks, most, sem):
     for n in range(1, most + 1):
 
-        @pl.when(steps == n)
+        @pl.when(blocks == n)
         def _(n=n):
-            filled = kv_ref.at[:, pl.ds(0, n * step_slots)]
+            filled = kv_ref.at[:, pl.ds(0, n * block_slots)]
             pltpu.make_async_copy(filled, filled, sem).wait()
 
 
-def attention(steps, roped_ref, kv_ref, bias_ref, s_refs, most_refs, top_ref, sum_ref, sum_of_values, begin, finish):
+def attention(steps, step_keys, roped_ref, kv_ref, bias_ref, s_refs, most_refs, top_ref, sum_ref, sum_of_values, begin, finish):
     items, rows, _ = roped_ref.shape
+    step_slots = step_keys // 32
+    biased = bias_ref.shape[1]
 
     def block(kind, c):
         return kv_ref[kind, pl.ds(c * step_slots, step_slots)].reshape(step_keys, 256)
@@ -245,8 +247,9 @@
             roped_ref[t], block(0, c), (((1,), (1,)), ((), ())), preferred_element_type=jnp.float32
         )
         if masked:
-            result = result.reshape(head_pair, rows // head_pair, step_keys) + bias_ref[...]
-            result = result.reshape(rows, step_keys)
+            head = result[:, :biased].reshape(head_pair, rows // head_pair, biased) + bias_ref[...]
+            head = head.reshape(rows, biased)
+            result = join([head, result[:, biased:]]) if step_keys > biased else head
         s_refs[which][c] = result
         most_refs[which][...] = jnp.maximum(most_refs[which][...], lane_fold(result, jnp.maximum))
 
@@ -309,9 +312,9 @@
     finish(last)
 
 
-def working(rows, steps):
+def working(rows, steps, step_keys):
     return [
-        pltpu.VMEM((2, steps * step_slots, 32, 256), jnp.bfloat16),
+        pltpu.VMEM((2, steps * step_keys // 32, 32, 256), jnp.bfloat16),
         pltpu.VMEM((steps, head_pair * rows, step_keys), jnp.float32),
         pltpu.VMEM((steps, head_pair * rows, step_keys), jnp.float32),
         pltpu.VMEM((head_pair * rows, 128), jnp.float32),
@@ -319,7 +322,7 @@
         pltpu.VMEM((head_pair * rows, 128), jnp.float32),
         pltpu.VMEM((head_pair * rows, 128), jnp.float32),
         pltpu.VMEM((head_pair * rows, 256), jnp.float32),
-        pltpu.VMEM((rows, step_keys), jnp.float32),
+        pltpu.VMEM((rows, block_keys), jnp.float32),
     ]
 
 
@@ -347,9 +350,9 @@
     items = roped_ref.shape[0]
     query_copy = pltpu.make_async_copy(query_ref, q_ref, query_sem)
     query_copy.start()
-    fetch(own_ref, 0, kv_ref, 0, step_slots, sem)
-    row = lax.broadcasted_iota(jnp.int32, (rows, step_keys), 0)
-    column = lax.broadcasted_iota(jnp.int32, (rows, step_keys), 1)
+    fetch(own_ref, 0, kv_ref, 0, block_slots, sem)
+    row = lax.broadcasted_iota(jnp.int32, (rows, block_keys), 0)
+    column = lax.broadcasted_iota(jnp.int32, (rows, block_keys), 1)
     bias_ref[...] = jnp.where(column <= row, 0.0, masked_score)
     query_copy.wait()
 
@@ -379,7 +382,7 @@
         pltpu.make_async_copy(stat_ref.at[t], stat_out.at[t], out_sem).start()
 
     attention(
-        1, roped_ref, kv_ref, bias_ref, (s_0, s_1), (most_0, most_1), top_ref, sum_ref, values_ref,
+        1, block_keys, roped_ref, kv_ref, bias_ref, (s_0, s_1), (most_0, most_1), top_ref, sum_ref, values_ref,
         begin, finish,
     )
     roped_copy.wait()
@@ -397,7 +400,7 @@
         out_specs=(hbm_spec,) * 3,
         scratch_shapes=[pltpu.VMEM((rows, width), jnp.bfloat16)]
         + state_shapes(items, rows)
-        + working(rows, 1)
+        + working(rows, 1, block_keys)
         + [pltpu.SemaphoreType.DMA] * 3,
         cost_estimate=light,
         compiler_params=params(large_limit),
@@ -421,8 +424,9 @@
     chunks = w_ref.shape[1] // chunk
     odd = group_index % 2
     chip = group_index // 2
-    steps = jnp.where(has_old, 4, odd + 2 * chip)
-    base = jnp.where(has_old, 16, 0)
+    blocks = jnp.where(has_old, 4, odd + 2 * chip)
+    steps = jnp.where(has_old, 2, odd + chip)
+    base = jnp.where(has_old, 16, 16 * odd)
     near = (old_ref, old_core_ref)
     far = (old_far_ref, old_far_core_ref)
 
@@ -451,7 +455,7 @@
 
     @pl.when(chip == 1)
     def _():
-        place = base + 16 * jnp.where(has_old, 1, odd)
+        place = jnp.where(has_old, 32, 32 * odd)
         fetch(far_ref, 0, kv_ref, place, 16, sem)
         fetch(far_core_ref, 0, kv_ref, place + 16, 16, sem)
 
@@ -474,14 +478,21 @@
     weight_copy = pltpu.make_async_copy(weight_ref, w_ref, weight_sem)
     weight_copy.start()
 
-    bias_ref[...] = jnp.zeros_like(bias_ref)
+    @pl.when(jnp.logical_not(has_old))
+    def _():
+        bias_ref[...] = jnp.where(odd == 1, masked_score, 0.0) + jnp.zeros_like(bias_ref)
+        empty = pl.ds(0, block_slots)
+
+        @pl.when(odd == 1)
+        def _():
+            kv_ref[:, empty] = jnp.zeros((2, block_slots, 32, 256), jnp.bfloat16)
 
     @pl.when(has_old)
     def _():
         bias_ref[:, :256] = old_bias(rows, group_index)
         bias_ref[:, 256:] = old_bias(rows, group_index ^ 2)
 
-    wait_rows(kv_ref, steps, 4, sem)
+    wait_rows(kv_ref, blocks, 4, sem)
     lane = lax.broadcasted_iota(jnp.int32, stat_ref.shape[1:], 1)
 
     def begin(t, most_ref):
@@ -499,7 +510,7 @@
         roped_ref[t] = mixed.astype(jnp.bfloat16)
 
     attention(
-        steps, roped_ref, kv_ref, bias_ref, (s_0, s_1), (most_0, most_1), top_ref, sum_ref, values_ref,
+        steps, 2 * block_keys, roped_ref, kv_ref, bias_ref, (s_0, s_1), (most_0, most_1), top_ref, sum_ref, values_ref,
         begin, finish,
     )
 
@@ -554,7 +565,7 @@
         in_specs=[smem_spec] + [hbm_spec] * 3 + [any_spec] * 7 + [hbm_spec] * 3,
         out_specs=(hbm_spec,) * 3,
         scratch_shapes=state_shapes(items, rows)
-        + working(rows, 4)
+        + working(rows, 2, 2 * block_keys)
         + [
             pltpu.VMEM(weight.shape, jnp.bfloat16),
             pltpu.VMEM((2, rows, chunk), jnp.bfloat16),

time: 79.6 us -> 77.4 us (0.972)
  Pallas kernels: 52.7 us -> 51.2 us
    pallas_call x1, Pallas kernels: 32 us -> 30.3 us  [rest_part(): pl.pallas_call(rest_kernel, out_shape=(pltpu.HBM((rows, width), jnp.bfloa...]
    unnamed x30 -> x28, local copies, waits for them, and re-layouts: 2.35 us -> 1.62 us
where the time goes in v8:
time: 77.4 us; the launch traced here: 76.9 us
  Pallas kernels  51.2 us (66%)
  starting transfers between devices  15.9 us (21%)
  waiting for transfers between devices  7.13 us (9%)
  local copies, waits for them, and re-layouts  1.62 us (2%)
  between operations  0.99 us (1%)
    pallas_call x1, Pallas kernels, rest_part(): pl.pallas_call(rest_kernel, out_shape=(pltpu.HBM((rows, width), jnp.bfloa...  30.3 us
    pallas_call x1, Pallas kernels, diagonal_part(): pl.pallas_call(diagonal_kernel, out_shape=(pltpu.HBM((items, head_pair *...  9.72 us
    all_to_all x1, starting transfers between devices, body(): old = lax.all_to_all(picked, 'blk', split_axis=0, concat_axis=0, tiled=True)  7.26 us
    all_to_all x1, starting transfers between devices, body(): lax.all_to_all(new, 'blk', split_axis=0, concat_axis=0, tiled=True)  5.42 us
    ppermute x2, waiting for transfers between devices, other_chip(): return lax.ppermute(value, 'group', [(0, 2), (2, 0), (1, 3), (3, 1)])  4.17 us
    ppermute x2, starting transfers between devices, other_chip(): return lax.ppermute(value, 'group', [(0, 2), (2, 0), (1, 3), (3, 1)])  3.1 us
    pallas_call x1, Pallas kernels, pick_old(): pl.pallas_call(pick_old_kernel, out_shape=jax.ShapeDtypeStruct((requests,...  3.01 us
    pallas_call x1, Pallas kernels, pick_new(): pl.pallas_call(lambda *refs: pick_new_kernel(pages, cap, *refs), out_shap...  2.75 us
  transfers between devices with their start and end apart: 8, of which 4 were waited for; matrix products, arithmetic and copies ran while one was open for 0% of the time, Pallas kernels for 61%

profile of v8, /device:TPU:0, one launch (start us, length us, event | category | flops | bytes accessed | tf_op | source)
XLA Modules:
  0.0 76.9 jit_solution(6329849978834710557)
XLA Ops:
  0.6 0.0 copy-start.9
  0.6 0.0 copy-start.8
  0.7 0.0 copy-start.6
  0.7 0.0 copy-start.5
  0.7 3.0 %pick_old.1 = bf16[8,2,2,32,256]{4,3,2,1,0:T(8,128)(2,1)} custom-call(s32[8,32]{1,0:T(8,128)} %refs_0_.2, bf16[40,32,256]{2,1,0:T(8,128)(2,1)} %key_ref.3, bf16[40,32,256]{2,1,0:T(8,128)(2,1)} %value_ref.3), custom_call_target="tpu_custom_call" | custom-call | flops 1 | bytes 1 | tf_op jit(solution)/shard_map/pick_old/pallas_call | solution.py:65
  3.7 0.0 copy-start.7
  3.7 7.3 %all-to-all-start = ((bf16[8,2,2,32,256]{4,3,2,1,0:T(8,128)(2,1)}), bf16[8,2,2,32,256]{4,3,2,1,0:T(8,128)(2,1)S(1)}, u32[]{:S(2)}, u32[]{:S(2)}) async-start(bf16[8,2,2,32,256]{4,3,2,1,0:T(8,128)(2,1)} %pick_old.1), calls=%async_computation | async-start | bytes 1048576 | tf_op jit(solution)/shard_map/all_to_all | solution.py:642
  11.0 0.0 copy-done.9
  11.0 0.0 copy-done.8
  11.0 0.0 copy-done.6
  11.0 0.0 copy-done.5
  11.0 2.5 %rotate_keys.1 = (bf16[16,2,32,256]{3,2,1,0:T(8,128)(2,1)}, f32[512,128]{1,0:T(8,128)}, f32[512,128]{1,0:T(8,128)}) custom-call(s32[8]{0:T(128)S(1)} %copy-done.8, f32[1,128]{1,0:T(1,128)S(1)} %copy-done.9, bf16[512,256]{1,0:T(8,128)(2,1)S(1)} %bitcast.5, bf16[512,256]{1,0:T(8,128)(2,1)S(1)} %bitcast.6), custom_call_target="tpu_custom_call" | custom-call | flops 1 | bytes 1 | tf_op jit(solution)/shard_map/rotate_keys/pallas_call | solution.py:121
  13.5 0.0 copy-start
  13.5 1.5 %collective-permute-start.1 = (bf16[16,2,32,256]{3,2,1,0:T(8,128)(2,1)}, bf16[16,2,32,256]{3,2,1,0:T(8,128)(2,1)S(1)}, u32[]{:S(2)}, u32[]{:S(2)}) collective-permute-start(bf16[16,2,32,256]{3,2,1,0:T(8,128)(2,1)} %get-tuple-element.23.own_ref.refs_1_), channel_id=1, source_target_pairs={{0,2},{2,0},{1,3},{3,1},{4,6},{6,4},{5,7},{7,5},{8,10},{10,8},{9,1... | collective-permute-start | bytes 1572872 | tf_op jit(solution)/shard_map/ppermute | solution.py:639
  15.0 0.0 collective-permute-start
  15.0 9.7 %attend_diagonal.1 = (bf16[5,1024,256]{2,1,0:T(8,128)(2,1)}, f32[5,1024,256]{2,1,0:T(8,128)}, f32[5,1024,128]{2,1,0:T(8,128)}) custom-call(bf16[512,2560]{1,0:T(8,128)(2,1)} %bitcast.7, f32[512,128]{1,0:T(8,128)} %get-tuple-element.21.cos_ref, f32[512,128]{1,0:T(8,128)} %get-tuple-element.22.sin_ref, bf16[16,2,32,256]{3,2,1,0:T(8,128)(2,1)} %get-tuple-element.23.own_ref.refs_1_), custom_call_target="tpu_custom_call" | custom-call | flops 1 | bytes 1 | tf_op jit(solution)/shard_map/attend_diagonal/pallas_call | solution.py:396
  24.7 0.7 all-to-all-done
  25.5 0.0 copy-start.10
  25.5 0.8 %copy-done.10 = bf16[8,2,2,32,256]{4,3,2,1,0:T(8,128)(2,1)} copy-done((bf16[8,2,2,32,256]{4,3,2,1,0:T(8,128)(2,1)}, bf16[8,2,2,32,256]{4,3,2,1,0:T(8,128)(2,1)S(1)}, u32[]{:S(2)}) %copy-start.10) | copy-done | bytes 524312
  26.2 0.0 copy-done.7
  26.3 1.6 %sort_old.1.old_ref = bf16[16,2,32,256]{3,2,1,0:T(8,128)(2,1)S(1)} custom-call(s32[8,32]{1,0:T(8,128)S(1)} %copy-done.7, bf16[16,2,32,256]{3,2,1,0:T(8,128)(2,1)} %bitcast.8), custom_call_target="tpu_custom_call" | custom-call | flops 1 | bytes 1 | tf_op jit(solution)/shard_map/sort_old/pallas_call | solution.py:145
  27.9 0.0 copy-start.1
  27.9 0.0 collective-permute-done.1.refs_3_.far_ref
  27.9 0.0 copy-start.2
  27.9 0.1 collective-permute-start.2
  28.0 1.6 %collective-permute-start.4 = (bf16[16,2,32,256]{3,2,1,0:T(8,128)(2,1)S(1)}, bf16[16,2,32,256]{3,2,1,0:T(8,128)(2,1)S(1)}, u32[]{:S(2)}, u32[]{:S(2)}) collective-permute-start(bf16[16,2,32,256]{3,2,1,0:T(8,128)(2,1)S(1)} %sort_old.1.old_ref), channel_id=1, source_target_pairs={{0,2},{2,0},{1,3},{3,1},{4,6},{6,4},{5,7},{7,5},{8,10},{10,8},{9,1... | collective-permute-start | bytes 1572872 | tf_op jit(solution)/shard_map/ppermute | solution.py:639
  29.6 0.0 collective-permute-done.refs_2_.core_ref
  29.6 0.0 copy-start.3
  29.6 0.3 collective-permute-done.2.refs_4_.far_core_ref
  29.9 0.0 copy-done
  29.9 0.0 copy-start.4
  29.9 2.8 %pick_new.1 = (bf16[16,2,32,256]{3,2,1,0:T(8,128)(2,1)}, s32[16]{0:T(128)S(1)}) custom-call(s32[8,32]{1,0:T(8,128)S(1)} %copy-done.7, bf16[16,2,32,256]{3,2,1,0:T(8,128)(2,1)S(1)} %copy-done, bf16[16,2,32,256]{3,2,1,0:T(8,128)(2,1)S(1)} %collective-permute-done.refs_2_.core_ref, bf16[16,2,32,256]{3,2,1,0:T(8,128)(2,1)S(1)} %collective-permute-done.1.refs_3_.far_ref, ...), custom_call_target="tpu_custom_call" | custom-call | flops 1 | bytes 1 | tf_op jit(solution)/shard_map/pick_new/pallas_call | solution.py:182
  32.7 5.4 %all-to-all-start.1 = ((bf16[16,2,32,256]{3,2,1,0:T(8,128)(2,1)}), bf16[16,2,32,256]{3,2,1,0:T(8,128)(2,1)S(1)}, u32[]{:S(2)}, u32[]{:S(2)}) async-start(bf16[16,2,32,256]{3,2,1,0:T(8,128)(2,1)} %get-tuple-element.29), calls=%async_computation.1 | async-start | bytes 1048576 | tf_op jit(solution)/shard_map/all_to_all | solution.py:657
  38.1 0.1 collective-permute-start.3
  38.2 4.2 %collective-permute-done.4.old_far_ref = bf16[16,2,32,256]{3,2,1,0:T(8,128)(2,1)S(1)} collective-permute-done((bf16[16,2,32,256]{3,2,1,0:T(8,128)(2,1)S(1)}, bf16[16,2,32,256]{3,2,1,0:T(8,128)(2,1)S(1)}, u32[]{:S(2)}, u32[]{:S(2)}) %collective-permute-start.4) | collective-permute-done | bytes 524320 | tf_op jit(solution)/shard_map/ppermute | solution.py:639
  42.3 0.0 copy-start.11
  42.3 0.0 collective-permute-start.5
  42.3 0.0 collective-permute-done.3.old_core_ref
  42.4 0.0 copy-start.12
  42.4 1.9 %collective-permute-done.5.old_far_core_ref = bf16[16,2,32,256]{3,2,1,0:T(8,128)(2,1)S(1)} collective-permute-done((bf16[16,2,32,256]{3,2,1,0:T(8,128)(2,1)S(1)}, bf16[16,2,32,256]{3,2,1,0:T(8,128)(2,1)S(1)}, u32[]{:S(2)}, u32[]{:S(2)}) %collective-permute-start.5) | collective-permute-done | bytes 524320 | tf_op jit(solution)/shard_map/ppermute | solution.py:636
  44.3 0.0 copy-start.13
  44.3 0.0 copy-done.1
  44.3 0.0 copy-done.2
  44.3 0.0 copy-done.3
  44.3 0.0 copy-done.4
  44.3 0.0 copy-done.11
  44.3 0.0 copy-done.12
  44.3 0.8 %copy-done.13 = bf16[16,2,32,256]{3,2,1,0:T(8,128)(2,1)} copy-done((bf16[16,2,32,256]{3,2,1,0:T(8,128)(2,1)}, bf16[16,2,32,256]{3,2,1,0:T(8,128)(2,1)S(1)}, u32[]{:S(2)}) %copy-start.13) | copy-done | bytes 524312
  45.1 30.3 %attend_rest.1 = (bf16[512,2560]{1,0:T(8,128)(2,1)}, bf16[40,32,256]{2,1,0:T(8,128)(2,1)}, bf16[40,32,256]{2,1,0:T(8,128)(2,1)}) custom-call(s32[8]{0:T(128)} %lengths_ref.3, bf16[5,1024,256]{2,1,0:T(8,128)(2,1)} %get-tuple-element.24.roped_in, f32[5,1024,256]{2,1,0:T(8,128)} %get-tuple-element.25.acc_in, f32[5,1024,128]{2,1,0:T(8,128)} %get-tuple-element.26.stat_in, ...), custom_call_target="tpu_custom_call" | custom-call | flops 1 | bytes 1 | tf_op jit(solution)/shard_map/attend_rest/pallas_call | solution.py:558
  75.4 0.0 all-to-all-done.1.arrived_ref
  75.4 1.4 %place_new.1 = (bf16[40,32,256]{2,1,0:T(8,128)(2,1)}, bf16[40,32,256]{2,1,0:T(8,128)(2,1)}) custom-call(s32[16]{0:T(128)S(1)} %get-tuple-element.32.targets_ref, bf16[16,2,32,256]{3,2,1,0:T(8,128)(2,1)S(1)} %all-to-all-done.1.arrived_ref, bf16[40,32,256]{2,1,0:T(8,128)(2,1)} %get-tuple-element.33.key_in, ...), custom_call_target="tpu_custom_call", output_to_operand_aliasing={{0}: (2, {}), {1}: (3, {})} | custom-call | flops 1 | bytes 1 | tf_op jit(solution)/shard_map/place_new/pallas_call | solution.py:605
Async XLA Ops:
  0.6 10.3 %copy-start.9 = (f32[1,128]{1,0:T(1,128)S(1)}, f32[1,128]{1,0:T(1,128)}, u32[]{:S(2)}) copy-start(f32[1,128]{1,0:T(1,128)} %constant.2.clone.freq_ref) | copy-start | bytes 1540
  0.6 10.3 %copy-start.8 = (s32[8]{0:T(128)S(1)}, s32[8]{0:T(128)}, u32[]{:S(2)}) copy-start(s32[8]{0:T(128)} %lengths_ref.3) | copy-start | bytes 100
  0.7 10.3 %copy-start.6 = (bf16[1,512,256]{2,1,0:T(8,128)(2,1)S(1)}, bf16[1,512,256]{2,1,0:T(8,128)(2,1)}, u32[]{:S(2)}) copy-start(bf16[1,512,256]{2,1,0:T(8,128)(2,1)} %param.11) | copy-start | bytes 786436
  0.7 10.3 %copy-start.5 = (bf16[1,512,256]{2,1,0:T(8,128)(2,1)S(1)}, bf16[1,512,256]{2,1,0:T(8,128)(2,1)}, u32[]{:S(2)}) copy-start(bf16[1,512,256]{2,1,0:T(8,128)(2,1)} %param.10) | copy-start | bytes 786436
  3.7 22.6 %copy-start.7 = (s32[8,32]{1,0:T(8,128)S(1)}, s32[8,32]{1,0:T(8,128)}, u32[]{:S(2)}) copy-start(s32[8,32]{1,0:T(8,128)} %refs_0_.2) | copy-start | bytes 3076
  3.7 21.8 %all-to-all-start = ((bf16[8,2,2,32,256]{4,3,2,1,0:T(8,128)(2,1)}), bf16[8,2,2,32,256]{4,3,2,1,0:T(8,128)(2,1)S(1)}, u32[]{:S(2)}, u32[]{:S(2)}) async-start(bf16[8,2,2,32,256]{4,3,2,1,0:T(8,128)(2,1)} %pick_old.1), calls=%async_computation | async-start | bytes 1048576 | tf_op jit(solution)/shard_map/all_to_all | solution.py:642
  13.5 16.4 %copy-start = (bf16[16,2,32,256]{3,2,1,0:T(8,128)(2,1)S(1)}, bf16[16,2,32,256]{3,2,1,0:T(8,128)(2,1)}, u32[]{:S(2)}) copy-start(bf16[16,2,32,256]{3,2,1,0:T(8,128)(2,1)} %get-tuple-element.23.own_ref.refs_1_) | copy-start | bytes 1572868
  13.5 14.4 %collective-permute-start.1 = (bf16[16,2,32,256]{3,2,1,0:T(8,128)(2,1)}, bf16[16,2,32,256]{3,2,1,0:T(8,128)(2,1)S(1)}, u32[]{:S(2)}, u32[]{:S(2)}) collective-permute-start(bf16[16,2,32,256]{3,2,1,0:T(8,128)(2,1)} %get-tuple-element.23.own_ref.refs_1_), channel_id=1, source_target_pairs={{0,2},{2,0},{1,3},{3,1},{4,6},{6,4},{5,7},{7,5},{8,10},{10,8},{9,1... | collective-permute-start | bytes 1572872 | tf_op jit(solution)/shard_map/ppermute | solution.py:639
  15.0 14.6 %collective-permute-start = (bf16[16,2,32,256]{3,2,1,0:T(8,128)(2,1)}, bf16[16,2,32,256]{3,2,1,0:T(8,128)(2,1)S(1)}, u32[]{:S(2)}, u32[]{:S(2)}) collective-permute-start(bf16[16,2,32,256]{3,2,1,0:T(8,128)(2,1)} %get-tuple-element.23.own_ref.refs_1_), channel_id=1, source_target_pairs={{0,1},{1,0},{2,3},{3,2},{4,5},{5,4},{6,7},{7,6},{8,9},{9,8},{10,11... | collective-permute-start | bytes 1572872 | tf_op jit(solution)/shard_map/ppermute | solution.py:636
  25.5 0.8 %copy-start.10 = (bf16[8,2,2,32,256]{4,3,2,1,0:T(8,128)(2,1)}, bf16[8,2,2,32,256]{4,3,2,1,0:T(8,128)(2,1)S(1)}, u32[]{:S(2)}) copy-start(bf16[8,2,2,32,256]{4,3,2,1,0:T(8,128)(2,1)S(1)} %all-to-all-done) | copy-start | bytes 1572868
  27.9 16.4 %copy-start.1 = (bf16[16,2,32,256]{3,2,1,0:T(8,128)(2,1)}, bf16[16,2,32,256]{3,2,1,0:T(8,128)(2,1)S(1)}, u32[]{:S(2)}) copy-start(bf16[16,2,32,256]{3,2,1,0:T(8,128)(2,1)S(1)} %sort_old.1.old_ref) | copy-start | bytes 1572868
  27.9 16.3 %copy-start.2 = (bf16[16,2,32,256]{3,2,1,0:T(8,128)(2,1)}, bf16[16,2,32,256]{3,2,1,0:T(8,128)(2,1)S(1)}, u32[]{:S(2)}) copy-start(bf16[16,2,32,256]{3,2,1,0:T(8,128)(2,1)S(1)} %collective-permute-done.1.refs_3_.far_ref) | copy-start | bytes 1572868
  27.9 2.0 %collective-permute-start.2 = (bf16[16,2,32,256]{3,2,1,0:T(8,128)(2,1)S(1)}, bf16[16,2,32,256]{3,2,1,0:T(8,128)(2,1)S(1)}, u32[]{:S(2)}, u32[]{:S(2)}) collective-permute-start(bf16[16,2,32,256]{3,2,1,0:T(8,128)(2,1)S(1)} %collective-permute-done.1.refs_3_.far_ref), channel_id=1, source_target_pairs={{0,1},{1,0},{2,3},{3,2},{4,5},{5,4},{6,7},{7,6},{8,9},{9,8},{10,11... | collective-permute-start | bytes 1572872 | tf_op jit(solution)/shard_map/ppermute | solution.py:636
  28.0 14.3 %collective-permute-start.4 = (bf16[16,2,32,256]{3,2,1,0:T(8,128)(2,1)S(1)}, bf16[16,2,32,256]{3,2,1,0:T(8,128)(2,1)S(1)}, u32[]{:S(2)}, u32[]{:S(2)}) collective-permute-start(bf16[16,2,32,256]{3,2,1,0:T(8,128)(2,1)S(1)} %sort_old.1.old_ref), channel_id=1, source_target_pairs={{0,2},{2,0},{1,3},{3,1},{4,6},{6,4},{5,7},{7,5},{8,10},{10,8},{9,1... | collective-permute-start | bytes 1572872 | tf_op jit(solution)/shard_map/ppermute | solution.py:639
  29.6 14.7 %copy-start.3 = (bf16[16,2,32,256]{3,2,1,0:T(8,128)(2,1)}, bf16[16,2,32,256]{3,2,1,0:T(8,128)(2,1)S(1)}, u32[]{:S(2)}) copy-start(bf16[16,2,32,256]{3,2,1,0:T(8,128)(2,1)S(1)} %collective-permute-done.refs_2_.core_ref) | copy-start | bytes 1572868
  29.9 14.4 %copy-start.4 = (bf16[16,2,32,256]{3,2,1,0:T(8,128)(2,1)}, bf16[16,2,32,256]{3,2,1,0:T(8,128)(2,1)S(1)}, u32[]{:S(2)}) copy-start(bf16[16,2,32,256]{3,2,1,0:T(8,128)(2,1)S(1)} %collective-permute-done.2.refs_4_.far_core_ref) | copy-start | bytes 1572868
  32.7 42.7 %all-to-all-start.1 = ((bf16[16,2,32,256]{3,2,1,0:T(8,128)(2,1)}), bf16[16,2,32,256]{3,2,1,0:T(8,128)(2,1)S(1)}, u32[]{:S(2)}, u32[]{:S(2)}) async-start(bf16[16,2,32,256]{3,2,1,0:T(8,128)(2,1)} %get-tuple-element.29), calls=%async_computation.1 | async-start | bytes 1048576 | tf_op jit(solution)/shard_map/all_to_all | solution.py:657
  38.1 4.3 %collective-permute-start.3 = (bf16[16,2,32,256]{3,2,1,0:T(8,128)(2,1)S(1)}, bf16[16,2,32,256]{3,2,1,0:T(8,128)(2,1)S(1)}, u32[]{:S(2)}, u32[]{:S(2)}) collective-permute-start(bf16[16,2,32,256]{3,2,1,0:T(8,128)(2,1)S(1)} %sort_old.1.old_ref), channel_id=1, source_target_pairs={{0,1},{1,0},{2,3},{3,2},{4,5},{5,4},{6,7},{7,6},{8,9},{9,8},{10,11... | collective-permute-start | bytes 1572872 | tf_op jit(solution)/shard_map/ppermute | solution.py:636
  42.3 1.9 %copy-start.11 = (bf16[16,2,32,256]{3,2,1,0:T(8,128)(2,1)}, bf16[16,2,32,256]{3,2,1,0:T(8,128)(2,1)S(1)}, u32[]{:S(2)}) copy-start(bf16[16,2,32,256]{3,2,1,0:T(8,128)(2,1)S(1)} %collective-permute-done.4.old_far_ref) | copy-start | bytes 1572868
  42.3 1.9 %collective-permute-start.5 = (bf16[16,2,32,256]{3,2,1,0:T(8,128)(2,1)S(1)}, bf16[16,2,32,256]{3,2,1,0:T(8,128)(2,1)S(1)}, u32[]{:S(2)}, u32[]{:S(2)}) collective-permute-start(bf16[16,2,32,256]{3,2,1,0:T(8,128)(2,1)S(1)} %collective-permute-done.4.old_far_ref), channel_id=1, source_target_pairs={{0,1},{1,0},{2,3},{3,2},{4,5},{5,4},{6,7},{7,6},{8,9},{9,8},{10,11... | collective-permute-start | bytes 1572872 | tf_op jit(solution)/shard_map/ppermute | solution.py:636
  42.4 1.9 %copy-start.12 = (bf16[16,2,32,256]{3,2,1,0:T(8,128)(2,1)}, bf16[16,2,32,256]{3,2,1,0:T(8,128)(2,1)S(1)}, u32[]{:S(2)}) copy-start(bf16[16,2,32,256]{3,2,1,0:T(8,128)(2,1)S(1)} %collective-permute-done.3.old_core_ref) | copy-start | bytes 1572868
  44.3 0.8 %copy-start.13 = (bf16[16,2,32,256]{3,2,1,0:T(8,128)(2,1)}, bf16[16,2,32,256]{3,2,1,0:T(8,128)(2,1)S(1)}, u32[]{:S(2)}) copy-start(bf16[16,2,32,256]{3,2,1,0:T(8,128)(2,1)S(1)} %collective-permute-done.5.old_far_core_ref) | copy-start | bytes 1572868

commit v9 on v8

--- a/solution.py
+++ b/solution.py
@@ -15,7 +15,8 @@
 vmem_spec = pl.BlockSpec(memory_space=pltpu.VMEM)
 small_limit = 16 * 1024 * 1024
 head_pair = 2
-large_limit = 58 * 1024 * 1024
+middle_limit = 40 * 1024 * 1024
+large_limit = 60 * 1024 * 1024
 
 
 light = pl.CostEstimate(flops=1, bytes_accessed=1, transcendentals=0)
@@ -214,10 +215,7 @@
 
 
 def fetch(source, first, kv_ref, place, count, sem):
-    for kind in range(2):
-        pltpu.make_async_copy(
-            source.at[pl.ds(first, count), kind], kv_ref.at[kind, pl.ds(place, count)], sem
-        ).start()
+    pltpu.make_async_copy(source.at[pl.ds(first, count)], kv_ref.at[pl.ds(place, count)], sem).start()
 
 
 def fetch_pair(sources, first, kv_ref, place, sem):
@@ -230,7 +228,7 @@
 
         @pl.when(blocks == n)
         def _(n=n):
-            filled = kv_ref.at[:, pl.ds(0, n * block_slots)]
+            filled = kv_ref.at[pl.ds(0, n * block_slots)]
             pltpu.make_async_copy(filled, filled, sem).wait()
 
 
@@ -240,7 +238,7 @@
     biased = bias_ref.shape[1]
 
     def block(kind, c):
-        return kv_ref[kind, pl.ds(c * step_slots, step_slots)].reshape(step_keys, 256)
+        return kv_ref[pl.ds(c * step_slots, step_slots), kind].reshape(step_keys, 256)
 
     def scores(t, c, which, masked):
         result = lax.dot_general(
@@ -272,26 +270,80 @@
             work(c, False)
             return carry
 
-        if isinstance(steps, int):
-            for c in range(steps):
-                work(c, c == 0)
-            return
-
         @pl.when(steps > 0)
         def _():
             work(0, True)
 
         lax.fori_loop(1, steps, step, 0)
 
+    def both(t, which):
+        def work(c, masked):
+            weigh(c, which)
+            scores(t + 1, c, 1 - which, masked)
+
+        loop(work)
+
+    drive(
+        items, most_refs, begin, settle, finish,
+        lambda: loop(lambda c, masked: scores(0, c, 0, masked)),
+        both,
+        lambda which: loop(lambda c, masked: weigh(c, which)),
+    )
+
+
+def attention_at_once(roped_ref, kv_ref, bias_ref, s_refs, most_refs, top_ref, sum_ref, sum_of_values, begin, finish):
+    items, rows, _ = roped_ref.shape
+    blocks, _, width = s_refs[0].shape
+    biased = bias_ref.shape[1]
+    slots = width // 32
+
+    def scores(t, which):
+        most = most_refs[which][...]
+        query = roped_ref[t]
+        for c in range(blocks):
+            keys = kv_ref[c * slots : (c + 1) * slots, 0].reshape(width, 256)
+            result = lax.dot_general(
+                query, keys, (((1,), (1,)), ((), ())), preferred_element_type=jnp.float32
+            )
+            if c == 0:
+                head = result[:, :biased].reshape(head_pair, rows // head_pair, biased) + bias_ref[...]
+                head = head.reshape(rows, biased)
+                result = join([head, result[:, biased:]]) if width > biased else head
+            s_refs[which][c] = result
+            most = jnp.maximum(most, lane_fold(result, jnp.maximum))
+        most_refs[which][...] = most
+
+    def weigh(which):
+        top = join([top_ref[...]] * (width // 128))
+        sums = None
+        total = None
+        for c in range(blocks):
+            weights = jnp.exp(s_refs[which][c] - top)
+            folded = lane_fold(weights, jnp.add)
+            sums = folded if sums is None else sums + folded
+            values = kv_ref[c * slots : (c + 1) * slots, 1].reshape(width, 256)
+            part = jnp.dot(weights.astype(jnp.bfloat16), values, preferred_element_type=jnp.float32)
+            total = part if total is None else total + part
+        sum_ref[...] = sums
+        sum_of_values[...] = total
+
+    def settle(which):
+        top_ref[...] = jnp.broadcast_to(
+            jnp.max(most_refs[which][...], axis=1, keepdims=True), top_ref.shape
+        )
+
+    def both(t, which):
+        weigh(which)
+        scores(t + 1, 1 - which)
+
+    drive(items, most_refs, begin, settle, finish, lambda: scores(0, 0), both, weigh)
+
+
+def drive(items, most_refs, begin, settle, finish, only_scores, both, only_weigh):
     def one(t, which):
         begin(t + 1, most_refs[1 - which])
         settle(which)
-
-        def work(c, masked):
-            weigh(c, which)
-            scores(t + 1, c, 1 - which, masked)
-
-        loop(work)
+        both(t, which)
         finish(t)
 
     def two(i, carry):
@@ -300,7 +352,7 @@
         return carry
 
     begin(0, most_refs[0])
-    loop(lambda c, masked: scores(0, c, 0, masked))
+    only_scores()
     pairs = (items - 1) // 2
     lax.fori_loop(0, pairs, two, 0)
     last = 2 * pairs
@@ -308,13 +360,13 @@
         one(last, 0)
         last += 1
     settle(last % 2)
-    loop(lambda c, masked: weigh(c, last % 2))
+    only_weigh(last % 2)
     finish(last)
 
 
 def working(rows, steps, step_keys):
     return [
-        pltpu.VMEM((2, steps * step_keys // 32, 32, 256), jnp.bfloat16),
+        pltpu.VMEM((steps * step_keys // 32, 2, 32, 256), jnp.bfloat16),
         pltpu.VMEM((steps, head_pair * rows, step_keys), jnp.float32),
         pltpu.VMEM((steps, head_pair * rows, step_keys), jnp.float32),
         pltpu.VMEM((head_pair * rows, 128), jnp.float32),
@@ -342,15 +394,25 @@
 
 
 def diagonal_kernel(
-    query_ref, cos_ref, sin_ref, own_ref, roped_out, acc_out, stat_out,
-    q_ref, roped_ref, acc_ref, stat_ref, kv_ref, s_0, s_1, most_0, most_1, top_ref, sum_ref, values_ref,
-    bias_ref, query_sem, sem, out_sem,
+    query_ref, cos_ref, sin_ref, own_ref, key_ref, value_ref, roped_out, acc_out, stat_out,
+    key_out_ref, value_out_ref, key_pool, value_pool, q_ref, roped_ref, acc_ref, stat_ref, kv_ref, s_0, s_1, most_0, most_1, top_ref, sum_ref, values_ref,
+    bias_ref, query_sem, sem, out_sem, pool_sems,
 ):
     rows = q_ref.shape[0]
     items = roped_ref.shape[0]
+    loads = [
+        pltpu.make_async_copy(key_ref, key_pool, pool_sems.at[0]),
+        pltpu.make_async_copy(value_ref, value_pool, pool_sems.at[1]),
+    ]
+    stores = [
+        pltpu.make_async_copy(key_pool, key_out_ref, pool_sems.at[0]),
+        pltpu.make_async_copy(value_pool, value_out_ref, pool_sems.at[1]),
+    ]
     query_copy = pltpu.make_async_copy(query_ref, q_ref, query_sem)
     query_copy.start()
     fetch(own_ref, 0, kv_ref, 0, block_slots, sem)
+    for copy in loads:
+        copy.start()
     row = lax.broadcasted_iota(jnp.int32, (rows, block_keys), 0)
     column = lax.broadcasted_iota(jnp.int32, (rows, block_keys), 1)
     bias_ref[...] = jnp.where(column <= row, 0.0, masked_score)
@@ -369,6 +431,9 @@
     roped_copy = pltpu.make_async_copy(roped_ref, roped_out, query_sem)
     roped_copy.start()
     pltpu.make_async_copy(kv_ref, kv_ref, sem).wait()
+    for load, store in zip(loads, stores):
+        load.wait()
+        store.start()
 
     def begin(t, most_ref):
         most_ref[...] = jnp.full_like(most_ref, masked_score)
@@ -381,40 +446,47 @@
         pltpu.make_async_copy(acc_ref.at[t], acc_out.at[t], out_sem).start()
         pltpu.make_async_copy(stat_ref.at[t], stat_out.at[t], out_sem).start()
 
-    attention(
-        1, block_keys, roped_ref, kv_ref, bias_ref, (s_0, s_1), (most_0, most_1), top_ref, sum_ref, values_ref,
+    attention_at_once(
+        roped_ref, kv_ref, bias_ref, (s_0, s_1), (most_0, most_1), top_ref, sum_ref, values_ref,
         begin, finish,
     )
     roped_copy.wait()
+    for copy in stores:
+        copy.wait()
     pltpu.make_async_copy(acc_ref, acc_out, out_sem).wait()
     pltpu.make_async_copy(stat_ref, stat_out, out_sem).wait()
 
 
-def diagonal_part(queries, cosine, sine, own):
+def diagonal_part(queries, cosine, sine, own, key_cache, value_cache):
     rows, width = queries.shape
     items = width // (256 * head_pair)
     return pl.pallas_call(
         diagonal_kernel,
-        out_shape=(pltpu.HBM((items, head_pair * rows, 256), jnp.bfloat16),) + state_out(items, rows),
-        in_specs=[hbm_spec, vmem_spec, vmem_spec, hbm_spec],
-        out_specs=(hbm_spec,) * 3,
-        scratch_shapes=[pltpu.VMEM((rows, width), jnp.bfloat16)]
+        out_shape=(pltpu.HBM((items, head_pair * rows, 256), jnp.bfloat16),)
+        + state_out(items, rows)
+        + (pltpu.HBM(key_cache.shape, jnp.bfloat16), pltpu.HBM(value_cache.shape, jnp.bfloat16)),
+        in_specs=[hbm_spec, vmem_spec, vmem_spec, hbm_spec, hbm_spec, hbm_spec],
+        out_specs=(hbm_spec,) * 5,
+        scratch_shapes=[
+            pltpu.VMEM(key_cache.shape, jnp.bfloat16),
+            pltpu.VMEM(value_cache.shape, jnp.bfloat16),
+            pltpu.VMEM((rows, width), jnp.bfloat16),
+        ]
         + state_shapes(items, rows)
         + working(rows, 1, block_keys)
-        + [pltpu.SemaphoreType.DMA] * 3,
+        + [pltpu.SemaphoreType.DMA] * 3
+        + [pltpu.SemaphoreType.DMA((2,))],
         cost_estimate=light,
-        compiler_params=params(large_limit),
+        compiler_params=params(middle_limit),
         name="attend_diagonal",
-    )(*in_hbm(queries), cosine, sine, *in_hbm(own))
+    )(*in_hbm(queries), cosine, sine, *in_hbm(own, key_cache, value_cache))
 
 
 def rest_kernel(
     lengths_ref, roped_in, acc_in, stat_in, core_ref, far_ref, far_core_ref,
-    old_ref, old_core_ref, old_far_ref, old_far_core_ref, weight_ref, key_ref, value_ref,
-    hidden_ref, key_out_ref, value_out_ref,
+    old_ref, old_core_ref, old_far_ref, old_far_core_ref, weight_ref, hidden_ref,
     roped_ref, acc_ref, stat_ref, kv_ref, s_0, s_1, most_0, most_1, top_ref, sum_ref, values_ref,
-    bias_ref, w_ref, stage_ref, key_pool, value_pool,
-    state_sems, sem, weight_sem, pool_sems, out_sems,
+    bias_ref, w_ref, stage_ref, roped_sem, state_sems, sem, weight_sem, out_sems,
 ):
     group_index = lax.axis_index("group")
     has_old = lengths_ref[lax.axis_index("blk")] > 0
@@ -425,29 +497,23 @@
     odd = group_index % 2
     chip = group_index // 2
     blocks = jnp.where(has_old, 4, odd + 2 * chip)
-    steps = jnp.where(has_old, 2, odd + chip)
+    steps = odd + chip
     base = jnp.where(has_old, 16, 16 * odd)
     near = (old_ref, old_core_ref)
     far = (old_far_ref, old_far_core_ref)
 
     def copies(t):
+        place = t % 2
         return [
-            pltpu.make_async_copy(source.at[t], target.at[t], state_sems.at[number, t])
-            for number, (source, target) in enumerate(
-                ((roped_in, roped_ref), (stat_in, stat_ref), (acc_in, acc_ref))
-            )
+            pltpu.make_async_copy(source.at[t], target.at[place], state_sems.at[number, place])
+            for number, (source, target) in enumerate(((stat_in, stat_ref), (acc_in, acc_ref)))
         ]
 
-    pool_loads = [
-        pltpu.make_async_copy(key_ref, key_pool, pool_sems.at[0]),
-        pltpu.make_async_copy(value_ref, value_pool, pool_sems.at[1]),
-    ]
-    pool_stores = [
-        pltpu.make_async_copy(key_pool, key_out_ref, pool_sems.at[0]),
-        pltpu.make_async_copy(value_pool, value_out_ref, pool_sems.at[1]),
-    ]
-    for copy in copies(0):
-        copy.start()
+    roped_copy = pltpu.make_async_copy(roped_in, roped_ref, roped_sem)
+    roped_copy.start()
+    for t in range(2):
+        for copy in copies(t):
+            copy.start()
 
     @pl.when(odd == 1)
     def _():
@@ -470,11 +536,6 @@
                 fetch_pair(near, 4 * block, kv_ref, place, sem)
                 fetch_pair(far, 4 * block, kv_ref, place + 8, sem)
 
-    for copy in pool_loads:
-        copy.start()
-    for t in range(1, items):
-        for copy in copies(t):
-            copy.start()
     weight_copy = pltpu.make_async_copy(weight_ref, w_ref, weight_sem)
     weight_copy.start()
 
@@ -485,39 +546,47 @@
 
         @pl.when(odd == 1)
         def _():
-            kv_ref[:, empty] = jnp.zeros((2, block_slots, 32, 256), jnp.bfloat16)
+            kv_ref[empty] = jnp.zeros((block_slots, 2, 32, 256), jnp.bfloat16)
 
     @pl.when(has_old)
     def _():
         bias_ref[:, :256] = old_bias(rows, group_index)
         bias_ref[:, 256:] = old_bias(rows, group_index ^ 2)
 
+    roped_copy.wait()
     wait_rows(kv_ref, blocks, 4, sem)
     lane = lax.broadcasted_iota(jnp.int32, stat_ref.shape[1:], 1)
 
     def begin(t, most_ref):
         for copy in copies(t):
             copy.wait()
-        most_ref[...] = jnp.where(lane < 64, stat_ref[t], masked_score)
+        most_ref[...] = jnp.where(lane < 64, stat_ref[t % 2], masked_score)
 
     def finish(t):
-        stat = stat_ref[t]
+        stat = stat_ref[t % 2]
         factor = jnp.exp(stat[:, :1] - top_ref[...])
         sums = stat[:, 64:65] * factor + jnp.sum(sum_ref[...], axis=1, keepdims=True)
         inverse = 1.0 / sums
         old = factor * inverse
-        mixed = acc_ref[t] * join([old, old]) + values_ref[...] * join([inverse, inverse])
+        mixed = acc_ref[t % 2] * join([old, old]) + values_ref[...] * join([inverse, inverse])
         roped_ref[t] = mixed.astype(jnp.bfloat16)
 
-    attention(
-        steps, 2 * block_keys, roped_ref, kv_ref, bias_ref, (s_0, s_1), (most_0, most_1), top_ref, sum_ref, values_ref,
-        begin, finish,
-    )
-
-    for copy in pool_loads:
-        copy.wait()
-    for copy in pool_stores:
-        copy.start()
+        @pl.when(t + 2 < items)
+        def _():
+            for copy in copies(t + 2):
+                copy.start()
+
+    scratch = (roped_ref, kv_ref, bias_ref, (s_0, s_1), (most_0, most_1), top_ref, sum_ref, values_ref)
+
+    @pl.when(has_old)
+    def _():
+        attention_at_once(*scratch, begin, finish)
+
+    @pl.when(jnp.logical_not(has_old))
+    def _():
+        attention(steps, 2 * block_keys, *scratch, begin, finish)
+
+
     weight_copy.wait()
 
     def out_copy(n, columns):
@@ -546,41 +615,34 @@
     lax.fori_loop(0, chunks, project, 0)
     for n in range(2):
         out_copy(n, pl.ds(0, chunk)).wait()
-    for copy in pool_stores:
-        copy.wait()
-
-
-def rest_part(lengths, state, slots, weight, key_cache, value_cache):
+
+
+def rest_part(lengths, state, slots, weight):
     items, pair_rows, _ = state[0].shape
     rows = pair_rows // head_pair
     width = weight.shape[1]
     chunk = 512
     return pl.pallas_call(
         rest_kernel,
-        out_shape=(
-            pltpu.HBM((rows, width), jnp.bfloat16),
-            pltpu.HBM(key_cache.shape, jnp.bfloat16),
-            pltpu.HBM(value_cache.shape, jnp.bfloat16),
-        ),
-        in_specs=[smem_spec] + [hbm_spec] * 3 + [any_spec] * 7 + [hbm_spec] * 3,
-        out_specs=(hbm_spec,) * 3,
-        scratch_shapes=state_shapes(items, rows)
+        out_shape=pltpu.HBM((rows, width), jnp.bfloat16),
+        in_specs=[smem_spec] + [hbm_spec] * 3 + [any_spec] * 7 + [hbm_spec],
+        out_specs=hbm_spec,
+        scratch_shapes=[pltpu.VMEM((items, pair_rows, 256), jnp.bfloat16)]
+        + state_shapes(2, rows)[1:]
         + working(rows, 2, 2 * block_keys)
         + [
             pltpu.VMEM(weight.shape, jnp.bfloat16),
             pltpu.VMEM((2, rows, chunk), jnp.bfloat16),
-            pltpu.VMEM(key_cache.shape, jnp.bfloat16),
-            pltpu.VMEM(value_cache.shape, jnp.bfloat16),
-            pltpu.SemaphoreType.DMA((3, items)),
+            pltpu.SemaphoreType.DMA,
+            pltpu.SemaphoreType.DMA((2, 2)),
             pltpu.SemaphoreType.DMA,
             pltpu.SemaphoreType.DMA,
-            pltpu.SemaphoreType.DMA((2,)),
             pltpu.SemaphoreType.DMA((2,)),
         ],
         cost_estimate=light,
         compiler_params=params(large_limit),
         name="attend_rest",
-    )(lengths, *in_hbm(*state), *slots, *in_hbm(weight, key_cache, value_cache))
+    )(lengths, *in_hbm(*state), *slots, *in_hbm(weight))
 
 
 def place_kernel(targets_ref, arrived_ref, key_in, value_in, key_ref, value_ref, buffer_ref, load_sem, sem):
@@ -645,7 +707,9 @@
     fresh, cosine, sine = rotate_keys(lengths, new_keys[0], new_values[0])
     fresh_far = other_chip(fresh)
     fresh_core = other_core(fresh)
-    roped, acc, stat = diagonal_part(after(queries[0], picked), cosine, sine, fresh)
+    roped, acc, stat, key_out, value_out = diagonal_part(
+        after(queries[0], picked), cosine, sine, fresh, key_cache, value_cache
+    )
 
     old = sort_old(after(page_table, stat), blk_count, cap, pages, old)
     old_far = other_chip(old)
@@ -656,10 +720,10 @@
     )
     arrived = lax.all_to_all(new, "blk", split_axis=0, concat_axis=0, tiled=True)
     old_far_core = other_core(after(old_far, new))
-    hidden, key_out, value_out = rest_part(
+    hidden = rest_part(
         lengths, (roped, acc, stat),
         (fresh_core, fresh_far, fresh_far_core, old, old_core, old_far, old_far_core),
-        out_weight, key_cache, value_cache,
+        out_weight,
     )
     key_out, value_out = place_new(targets, arrived, key_out, value_out)
     return (hidden[None], key_out, value_out)

time: 77.4 us -> 80.9 us (1.045)
  the two profiles are of different devices: /device:TPU:0 before, /device:TPU:3 now
where the time goes in v9:
time: 80.9 us; the launch traced here: 80 us
  Pallas kernels  53.6 us (66%)
  starting transfers between devices  16.4 us (20%)
  waiting for transfers between devices  5.38 us (7%)
  local copies, waits for them, and re-layouts  3.57 us (4%)
  between operations  0.97 us (1%)
    pallas_call x1, Pallas kernels, rest_part(): pl.pallas_call(rest_kernel, out_shape=pltpu.HBM((rows, width), jnp.bfloat...  33.5 us
    pallas_call x1, Pallas kernels, diagonal_part(): pl.pallas_call(diagonal_kernel, out_shape=(pltpu.HBM((items, head_pair *...  8.87 us
    all_to_all x1, starting transfers between devices, body(): old = lax.all_to_all(picked, 'blk', split_axis=0, concat_axis=0, tiled=True)  5.79 us
    all_to_all x1, starting transfers between devices, body(): lax.all_to_all(new, 'blk', split_axis=0, concat_axis=0, tiled=True)  5.44 us
    unnamed x32, local copies, waits for them, and re-layouts  3.57 us
    ppermute x4, starting transfers between devices, other_core(): return lax.ppermute(value, 'group', [(0, 1), (1, 0), (2, 3), (3, 2)])  3.57 us
    ppermute x4, waiting for transfers between devices, other_core(): return lax.ppermute(value, 'group', [(0, 1), (1, 0), (2, 3), (3, 2)])  3.07 us
    pallas_call x1, Pallas kernels, pick_old(): pl.pallas_call(pick_old_kernel, out_shape=jax.ShapeDtypeStruct((requests,...  3.03 us
  transfers between devices with their start and end apart: 8, of which 3 were waited for; matrix products, arithmetic and copies ran while one was open for 0% of the time, Pallas kernels for 62%

profile of v9, /device:TPU:3, one launch (start us, length us, event | category | flops | bytes accessed | tf_op | source)
XLA Modules:
  0.0 80.0 jit_solution(12693265816093994701)
XLA Ops:
  0.6 0.0 copy-start.11
  0.6 0.0 copy-start.10
  0.7 0.0 copy-start.8
  0.7 0.0 copy-start.7
  0.7 3.0 %pick_old.1 = bf16[8,2,2,32,256]{4,3,2,1,0:T(8,128)(2,1)} custom-call(s32[8,32]{1,0:T(8,128)} %refs_0_.2, bf16[40,32,256]{2,1,0:T(8,128)(2,1)} %key_ref.3, bf16[40,32,256]{2,1,0:T(8,128)(2,1)} %value_ref.3), custom_call_target="tpu_custom_call" | custom-call | flops 1 | bytes 1 | tf_op jit(solution)/shard_map/pick_old/pallas_call | solution.py:66
  3.7 5.8 %all-to-all-start = ((bf16[8,2,2,32,256]{4,3,2,1,0:T(8,128)(2,1)}), bf16[8,2,2,32,256]{4,3,2,1,0:T(8,128)(2,1)S(1)}, u32[]{:S(2)}, u32[]{:S(2)}) async-start(bf16[8,2,2,32,256]{4,3,2,1,0:T(8,128)(2,1)} %pick_old.1), calls=%async_computation | async-start | bytes 1048576 | tf_op jit(solution)/shard_map/all_to_all | solution.py:704
  9.5 0.0 copy-done.11
  9.5 0.0 copy-done.10
  9.5 0.0 copy-done.8
  9.5 0.0 copy-done.7
  9.5 2.5 %rotate_keys.1 = (bf16[16,2,32,256]{3,2,1,0:T(8,128)(2,1)}, f32[512,128]{1,0:T(8,128)}, f32[512,128]{1,0:T(8,128)}) custom-call(s32[8]{0:T(128)S(1)} %copy-done.10, f32[1,128]{1,0:T(1,128)S(1)} %copy-done.11, bf16[512,256]{1,0:T(8,128)(2,1)S(1)} %bitcast.5, bf16[512,256]{1,0:T(8,128)(2,1)S(1)} %bitcast.6), custom_call_target="tpu_custom_call" | custom-call | flops 1 | bytes 1 | tf_op jit(solution)/shard_map/rotate_keys/pallas_call | solution.py:122
  12.0 0.0 copy-start.9
  12.0 1.2 %collective-permute-start.1 = (bf16[16,2,32,256]{3,2,1,0:T(8,128)(2,1)}, bf16[16,2,32,256]{3,2,1,0:T(8,128)(2,1)S(1)}, u32[]{:S(2)}, u32[]{:S(2)}) collective-permute-start(bf16[16,2,32,256]{3,2,1,0:T(8,128)(2,1)} %get-tuple-element.22.own_ref.refs_1_), channel_id=1, source_target_pairs={{0,2},{2,0},{1,3},{3,1},{4,6},{6,4},{5,7},{7,5},{8,10},{10,8},{9,1... | collective-permute-start | bytes 1572872 | tf_op jit(solution)/shard_map/ppermute | solution.py:701
  13.2 1.5 %collective-permute-start = (bf16[16,2,32,256]{3,2,1,0:T(8,128)(2,1)}, bf16[16,2,32,256]{3,2,1,0:T(8,128)(2,1)S(1)}, u32[]{:S(2)}, u32[]{:S(2)}) collective-permute-start(bf16[16,2,32,256]{3,2,1,0:T(8,128)(2,1)} %get-tuple-element.22.own_ref.refs_1_), channel_id=1, source_target_pairs={{0,1},{1,0},{2,3},{3,2},{4,5},{5,4},{6,7},{7,6},{8,9},{9,8},{10,11... | collective-permute-start | bytes 1572872 | tf_op jit(solution)/shard_map/ppermute | solution.py:698
  14.7 0.0 copy-start.5
  14.7 0.9 %copy-done.5 = f32[512,128]{1,0:T(8,128)S(1)} copy-done((f32[512,128]{1,0:T(8,128)S(1)}, f32[512,128]{1,0:T(8,128)}, u32[]{:S(2)}) %copy-start.5) | copy-done | bytes 262168
  15.7 0.0 copy-start.6
  15.7 0.9 %copy-done.6 = f32[512,128]{1,0:T(8,128)S(1)} copy-done((f32[512,128]{1,0:T(8,128)S(1)}, f32[512,128]{1,0:T(8,128)}, u32[]{:S(2)}) %copy-start.6) | copy-done | bytes 262168
  16.6 0.0 copy-start.4
  16.6 8.9 %attend_diagonal.1 = (bf16[5,1024,256]{2,1,0:T(8,128)(2,1)}, f32[5,1024,256]{2,1,0:T(8,128)}, f32[5,1024,128]{2,1,0:T(8,128)}, bf16[40,32,256]{2,1,0:T(8,128)(2,1)}, bf16[40,32,256]{2,1,0:T(8,128)(2,1)}) custom-call(bf16[512,2560]{1,0:T(8,128)(2,1)} %bitcast.7, f32[512,128]{1,0:T(8,128)S(1)} %copy-done.5, f32[512,128]{1,0:T(8,128)S(1)} %copy-done.6, ...), custom_call_target="tpu_custom_call" | custom-call | flops 1 | bytes 1 | tf_op jit(solution)/shard_map/attend_diagonal/pallas_call | solution.py:463
  25.5 0.0 all-to-all-done
  25.5 0.0 copy-start.12
  25.5 0.8 %copy-done.12 = bf16[8,2,2,32,256]{4,3,2,1,0:T(8,128)(2,1)} copy-done((bf16[8,2,2,32,256]{4,3,2,1,0:T(8,128)(2,1)}, bf16[8,2,2,32,256]{4,3,2,1,0:T(8,128)(2,1)S(1)}, u32[]{:S(2)}) %copy-start.12) | copy-done | bytes 524312
  26.3 0.0 copy-done.9
  26.3 1.6 %sort_old.1.old_ref = bf16[16,2,32,256]{3,2,1,0:T(8,128)(2,1)S(1)} custom-call(s32[8,32]{1,0:T(8,128)S(1)} %copy-done.9, bf16[16,2,32,256]{3,2,1,0:T(8,128)(2,1)} %bitcast.9), custom_call_target="tpu_custom_call" | custom-call | flops 1 | bytes 1 | tf_op jit(solution)/shard_map/sort_old/pallas_call | solution.py:146
  28.0 0.0 copy-start
  28.0 0.0 collective-permute-done.1.refs_3_.far_ref
  28.0 0.0 copy-start.1
  28.0 0.1 collective-permute-start.2
  28.1 0.4 collective-permute-start.4
  28.5 0.0 collective-permute-done.refs_2_.core_ref
  28.5 0.0 copy-start.2
  28.5 1.5 %collective-permute-done.2.refs_4_.far_core_ref = bf16[16,2,32,256]{3,2,1,0:T(8,128)(2,1)S(1)} collective-permute-done((bf16[16,2,32,256]{3,2,1,0:T(8,128)(2,1)S(1)}, bf16[16,2,32,256]{3,2,1,0:T(8,128)(2,1)S(1)}, u32[]{:S(2)}, u32[]{:S(2)}) %collective-permute-start.2) | collective-permute-done | bytes 524320 | tf_op jit(solution)/shard_map/ppermute | solution.py:698
  30.0 0.0 copy-done.4
  30.0 0.0 copy-start.3
  30.0 2.8 %pick_new.1 = (bf16[16,2,32,256]{3,2,1,0:T(8,128)(2,1)}, s32[16]{0:T(128)S(1)}) custom-call(s32[8,32]{1,0:T(8,128)S(1)} %copy-done.9, bf16[16,2,32,256]{3,2,1,0:T(8,128)(2,1)S(1)} %copy-done.4, bf16[16,2,32,256]{3,2,1,0:T(8,128)(2,1)S(1)} %collective-permute-done.refs_2_.core_ref, bf16[16,2,32,256]{3,2,1,0:T(8,128)(2,1)S(1)} %collective-permute-done.1.refs_3_.far_ref, ...), custom_call_target="tpu_custom_call" | custom-call | flops 1 | bytes 1 | tf_op jit(solution)/shard_map/pick_new/pallas_call | solution.py:183
  32.8 5.4 %all-to-all-start.1 = ((bf16[16,2,32,256]{3,2,1,0:T(8,128)(2,1)}), bf16[16,2,32,256]{3,2,1,0:T(8,128)(2,1)S(1)}, u32[]{:S(2)}, u32[]{:S(2)}) async-start(bf16[16,2,32,256]{3,2,1,0:T(8,128)(2,1)} %get-tuple-element.28), calls=%async_computation.1 | async-start | bytes 1048576 | tf_op jit(solution)/shard_map/all_to_all | solution.py:721
  38.2 0.7 collective-permute-start.3
  38.9 2.3 %collective-permute-done.4.old_far_ref = bf16[16,2,32,256]{3,2,1,0:T(8,128)(2,1)S(1)} collective-permute-done((bf16[16,2,32,256]{3,2,1,0:T(8,128)(2,1)S(1)}, bf16[16,2,32,256]{3,2,1,0:T(8,128)(2,1)S(1)}, u32[]{:S(2)}, u32[]{:S(2)}) %collective-permute-start.4) | collective-permute-done | bytes 524320 | tf_op jit(solution)/shard_map/ppermute | solution.py:701
  41.2 0.0 copy-start.13
  41.2 1.3 %collective-permute-start.5 = (bf16[16,2,32,256]{3,2,1,0:T(8,128)(2,1)S(1)}, bf16[16,2,32,256]{3,2,1,0:T(8,128)(2,1)S(1)}, u32[]{:S(2)}, u32[]{:S(2)}) collective-permute-start(bf16[16,2,32,256]{3,2,1,0:T(8,128)(2,1)S(1)} %collective-permute-done.4.old_far_ref), channel_id=1, source_target_pairs={{0,1},{1,0},{2,3},{3,2},{4,5},{5,4},{6,7},{7,6},{8,9},{9,8},{10,11... | collective-permute-start | bytes 1572872 | tf_op jit(solution)/shard_map/ppermute | solution.py:698
  42.5 0.0 collective-permute-done.3.old_core_ref
  42.5 0.0 copy-start.14
  42.5 1.5 %collective-permute-done.5.old_far_core_ref = bf16[16,2,32,256]{3,2,1,0:T(8,128)(2,1)S(1)} collective-permute-done((bf16[16,2,32,256]{3,2,1,0:T(8,128)(2,1)S(1)}, bf16[16,2,32,256]{3,2,1,0:T(8,128)(2,1)S(1)}, u32[]{:S(2)}, u32[]{:S(2)}) %collective-permute-start.5) | collective-permute-done | bytes 524320 | tf_op jit(solution)/shard_map/ppermute | solution.py:698
  44.0 0.0 copy-start.15
  44.0 0.8 %copy-done.15 = bf16[16,2,32,256]{3,2,1,0:T(8,128)(2,1)} copy-done((bf16[16,2,32,256]{3,2,1,0:T(8,128)(2,1)}, bf16[16,2,32,256]{3,2,1,0:T(8,128)(2,1)S(1)}, u32[]{:S(2)}) %copy-start.15) | copy-done | bytes 524312
  44.9 0.0 copy-done
  44.9 0.0 copy-done.1
  44.9 0.0 copy-done.2
  44.9 0.0 copy-done.3
  44.9 0.0 copy-done.13
  44.9 0.0 copy-done.14
  44.9 33.5 %attend_rest.1 = bf16[512,2560]{1,0:T(8,128)(2,1)} custom-call(s32[8]{0:T(128)} %lengths_ref.3, bf16[5,1024,256]{2,1,0:T(8,128)(2,1)} %get-tuple-element.23.roped_in, f32[5,1024,256]{2,1,0:T(8,128)} %get-tuple-element.24.acc_in, f32[5,1024,128]{2,1,0:T(8,128)} %get-tuple-element.25.stat_in, bf16[16,2,32,256]{3,2,1,0:T(8,128)(2,1)} %copy-done.2, ...), custom_call_target="tpu_custom_call" | custom-call | flops 1 | bytes 1 | tf_op jit(solution)/shard_map/attend_rest/pallas_call | solution.py:625
  78.4 0.0 all-to-all-done.1.arrived_ref
  78.4 1.4 %place_new.1 = (bf16[40,32,256]{2,1,0:T(8,128)(2,1)}, bf16[40,32,256]{2,1,0:T(8,128)(2,1)}) custom-call(s32[16]{0:T(128)S(1)} %get-tuple-element.30.targets_ref, bf16[16,2,32,256]{3,2,1,0:T(8,128)(2,1)S(1)} %all-to-all-done.1.arrived_ref, bf16[40,32,256]{2,1,0:T(8,128)(2,1)} %get-tuple-element.31.key_in, ...), custom_call_target="tpu_custom_call", output_to_operand_aliasing={{0}: (2, {}), {1}: (3, {})} | custom-call | flops 1 | bytes 1 | tf_op jit(solution)/shard_map/place_new/pallas_call | solution.py:667
Async XLA Ops:
  0.6 8.9 %copy-start.11 = (f32[1,128]{1,0:T(1,128)S(1)}, f32[1,128]{1,0:T(1,128)}, u32[]{:S(2)}) copy-start(f32[1,128]{1,0:T(1,128)} %constant.2.clone.freq_ref) | copy-start | bytes 1540
  0.6 8.9 %copy-start.10 = (s32[8]{0:T(128)S(1)}, s32[8]{0:T(128)}, u32[]{:S(2)}) copy-start(s32[8]{0:T(128)} %lengths_ref.3) | copy-start | bytes 100
  0.7 8.9 %copy-start.8 = (bf16[1,512,256]{2,1,0:T(8,128)(2,1)S(1)}, bf16[1,512,256]{2,1,0:T(8,128)(2,1)}, u32[]{:S(2)}) copy-start(bf16[1,512,256]{2,1,0:T(8,128)(2,1)} %param.11) | copy-start | bytes 786436
  0.7 8.9 %copy-start.7 = (bf16[1,512,256]{2,1,0:T(8,128)(2,1)S(1)}, bf16[1,512,256]{2,1,0:T(8,128)(2,1)}, u32[]{:S(2)}) copy-start(bf16[1,512,256]{2,1,0:T(8,128)(2,1)} %param.10) | copy-start | bytes 786436
  3.7 21.8 %all-to-all-start = ((bf16[8,2,2,32,256]{4,3,2,1,0:T(8,128)(2,1)}), bf16[8,2,2,32,256]{4,3,2,1,0:T(8,128)(2,1)S(1)}, u32[]{:S(2)}, u32[]{:S(2)}) async-start(bf16[8,2,2,32,256]{4,3,2,1,0:T(8,128)(2,1)} %pick_old.1), calls=%async_computation | async-start | bytes 1048576 | tf_op jit(solution)/shard_map/all_to_all | solution.py:704
  12.0 14.4 %copy-start.9 = (s32[8,32]{1,0:T(8,128)S(1)}, s32[8,32]{1,0:T(8,128)}, u32[]{:S(2)}) copy-start(s32[8,32]{1,0:T(8,128)} %refs_0_.2) | copy-start | bytes 3076
  12.0 16.0 %collective-permute-start.1 = (bf16[16,2,32,256]{3,2,1,0:T(8,128)(2,1)}, bf16[16,2,32,256]{3,2,1,0:T(8,128)(2,1)S(1)}, u32[]{:S(2)}, u32[]{:S(2)}) collective-permute-start(bf16[16,2,32,256]{3,2,1,0:T(8,128)(2,1)} %get-tuple-element.22.own_ref.refs_1_), channel_id=1, source_target_pairs={{0,2},{2,0},{1,3},{3,1},{4,6},{6,4},{5,7},{7,5},{8,10},{10,8},{9,1... | collective-permute-start | bytes 1572872 | tf_op jit(solution)/shard_map/ppermute | solution.py:701
  13.2 15.2 %collective-permute-start = (bf16[16,2,32,256]{3,2,1,0:T(8,128)(2,1)}, bf16[16,2,32,256]{3,2,1,0:T(8,128)(2,1)S(1)}, u32[]{:S(2)}, u32[]{:S(2)}) collective-permute-start(bf16[16,2,32,256]{3,2,1,0:T(8,128)(2,1)} %get-tuple-element.22.own_ref.refs_1_), channel_id=1, source_target_pairs={{0,1},{1,0},{2,3},{3,2},{4,5},{5,4},{6,7},{7,6},{8,9},{9,8},{10,11... | collective-permute-start | bytes 1572872 | tf_op jit(solution)/shard_map/ppermute | solution.py:698
  14.7 0.9 %copy-start.5 = (f32[512,128]{1,0:T(8,128)S(1)}, f32[512,128]{1,0:T(8,128)}, u32[]{:S(2)}) copy-start(f32[512,128]{1,0:T(8,128)} %get-tuple-element.20.cos_ref) | copy-start | bytes 786436
  15.7 0.9 %copy-start.6 = (f32[512,128]{1,0:T(8,128)S(1)}, f32[512,128]{1,0:T(8,128)}, u32[]{:S(2)}) copy-start(f32[512,128]{1,0:T(8,128)} %get-tuple-element.21.sin_ref) | copy-start | bytes 786436
  16.6 13.4 %copy-start.4 = (bf16[16,2,32,256]{3,2,1,0:T(8,128)(2,1)S(1)}, bf16[16,2,32,256]{3,2,1,0:T(8,128)(2,1)}, u32[]{:S(2)}) copy-start(bf16[16,2,32,256]{3,2,1,0:T(8,128)(2,1)} %get-tuple-element.22.own_ref.refs_1_) | copy-start | bytes 1572868
  25.5 0.8 %copy-start.12 = (bf16[8,2,2,32,256]{4,3,2,1,0:T(8,128)(2,1)}, bf16[8,2,2,32,256]{4,3,2,1,0:T(8,128)(2,1)S(1)}, u32[]{:S(2)}) copy-start(bf16[8,2,2,32,256]{4,3,2,1,0:T(8,128)(2,1)S(1)} %all-to-all-done) | copy-start | bytes 1572868
  28.0 16.9 %copy-start = (bf16[16,2,32,256]{3,2,1,0:T(8,128)(2,1)}, bf16[16,2,32,256]{3,2,1,0:T(8,128)(2,1)S(1)}, u32[]{:S(2)}) copy-start(bf16[16,2,32,256]{3,2,1,0:T(8,128)(2,1)S(1)} %sort_old.1.old_ref) | copy-start | bytes 1572868
  28.0 16.9 %copy-start.1 = (bf16[16,2,32,256]{3,2,1,0:T(8,128)(2,1)}, bf16[16,2,32,256]{3,2,1,0:T(8,128)(2,1)S(1)}, u32[]{:S(2)}) copy-start(bf16[16,2,32,256]{3,2,1,0:T(8,128)(2,1)S(1)} %collective-permute-done.1.refs_3_.far_ref) | copy-start | bytes 1572868
  28.0 2.0 %collective-permute-start.2 = (bf16[16,2,32,256]{3,2,1,0:T(8,128)(2,1)S(1)}, bf16[16,2,32,256]{3,2,1,0:T(8,128)(2,1)S(1)}, u32[]{:S(2)}, u32[]{:S(2)}) collective-permute-start(bf16[16,2,32,256]{3,2,1,0:T(8,128)(2,1)S(1)} %collective-permute-done.1.refs_3_.far_ref), channel_id=1, source_target_pairs={{0,1},{1,0},{2,3},{3,2},{4,5},{5,4},{6,7},{7,6},{8,9},{9,8},{10,11... | collective-permute-start | bytes 1572872 | tf_op jit(solution)/shard_map/ppermute | solution.py:698
  28.1 13.1 %collective-permute-start.4 = (bf16[16,2,32,256]{3,2,1,0:T(8,128)(2,1)S(1)}, bf16[16,2,32,256]{3,2,1,0:T(8,128)(2,1)S(1)}, u32[]{:S(2)}, u32[]{:S(2)}) collective-permute-start(bf16[16,2,32,256]{3,2,1,0:T(8,128)(2,1)S(1)} %sort_old.1.old_ref), channel_id=1, source_target_pairs={{0,2},{2,0},{1,3},{3,1},{4,6},{6,4},{5,7},{7,5},{8,10},{10,8},{9,1... | collective-permute-start | bytes 1572872 | tf_op jit(solution)/shard_map/ppermute | solution.py:701
  28.5 16.4 %copy-start.2 = (bf16[16,2,32,256]{3,2,1,0:T(8,128)(2,1)}, bf16[16,2,32,256]{3,2,1,0:T(8,128)(2,1)S(1)}, u32[]{:S(2)}) copy-start(bf16[16,2,32,256]{3,2,1,0:T(8,128)(2,1)S(1)} %collective-permute-done.refs_2_.core_ref) | copy-start | bytes 1572868
  30.0 14.9 %copy-start.3 = (bf16[16,2,32,256]{3,2,1,0:T(8,128)(2,1)}, bf16[16,2,32,256]{3,2,1,0:T(8,128)(2,1)S(1)}, u32[]{:S(2)}) copy-start(bf16[16,2,32,256]{3,2,1,0:T(8,128)(2,1)S(1)} %collective-permute-done.2.refs_4_.far_core_ref) | copy-start | bytes 1572868
  32.8 45.7 %all-to-all-start.1 = ((bf16[16,2,32,256]{3,2,1,0:T(8,128)(2,1)}), bf16[16,2,32,256]{3,2,1,0:T(8,128)(2,1)S(1)}, u32[]{:S(2)}, u32[]{:S(2)}) async-start(bf16[16,2,32,256]{3,2,1,0:T(8,128)(2,1)} %get-tuple-element.28), calls=%async_computation.1 | async-start | bytes 1048576 | tf_op jit(solution)/shard_map/all_to_all | solution.py:721
  38.2 4.3 %collective-permute-start.3 = (bf16[16,2,32,256]{3,2,1,0:T(8,128)(2,1)S(1)}, bf16[16,2,32,256]{3,2,1,0:T(8,128)(2,1)S(1)}, u32[]{:S(2)}, u32[]{:S(2)}) collective-permute-start(bf16[16,2,32,256]{3,2,1,0:T(8,128)(2,1)S(1)} %sort_old.1.old_ref), channel_id=1, source_target_pairs={{0,1},{1,0},{2,3},{3,2},{4,5},{5,4},{6,7},{7,6},{8,9},{9,8},{10,11... | collective-permute-start | bytes 1572872 | tf_op jit(solution)/shard_map/ppermute | solution.py:698
  41.2 3.6 %copy-start.13 = (bf16[16,2,32,256]{3,2,1,0:T(8,128)(2,1)}, bf16[16,2,32,256]{3,2,1,0:T(8,128)(2,1)S(1)}, u32[]{:S(2)}) copy-start(bf16[16,2,32,256]{3,2,1,0:T(8,128)(2,1)S(1)} %collective-permute-done.4.old_far_ref) | copy-start | bytes 1572868
  41.2 2.8 %collective-permute-start.5 = (bf16[16,2,32,256]{3,2,1,0:T(8,128)(2,1)S(1)}, bf16[16,2,32,256]{3,2,1,0:T(8,128)(2,1)S(1)}, u32[]{:S(2)}, u32[]{:S(2)}) collective-permute-start(bf16[16,2,32,256]{3,2,1,0:T(8,128)(2,1)S(1)} %collective-permute-done.4.old_far_ref), channel_id=1, source_target_pairs={{0,1},{1,0},{2,3},{3,2},{4,5},{5,4},{6,7},{7,6},{8,9},{9,8},{10,11... | collective-permute-start | bytes 1572872 | tf_op jit(solution)/shard_map/ppermute | solution.py:698
  42.5 2.4 %copy-start.14 = (bf16[16,2,32,256]{3,2,1,0:T(8,128)(2,1)}, bf16[16,2,32,256]{3,2,1,0:T(8,128)(2,1)S(1)}, u32[]{:S(2)}) copy-start(bf16[16,2,32,256]{3,2,1,0:T(8,128)(2,1)S(1)} %collective-permute-done.3.old_core_ref) | copy-start | bytes 1572868
  44.0 0.8 %copy-start.15 = (bf16[16,2,32,256]{3,2,1,0:T(8,128)(2,1)}, bf16[16,2,32,256]{3,2,1,0:T(8,128)(2,1)S(1)}, u32[]{:S(2)}) copy-start(bf16[16,2,32,256]{3,2,1,0:T(8,128)(2,1)S(1)} %collective-permute-done.5.old_far_core_ref) | copy-start | bytes 1572868

commit v10 on v9

--- a/solution.py
+++ b/solution.py
@@ -15,7 +15,6 @@
 vmem_spec = pl.BlockSpec(memory_space=pltpu.VMEM)
 small_limit = 16 * 1024 * 1024
 head_pair = 2
-middle_limit = 40 * 1024 * 1024
 large_limit = 60 * 1024 * 1024
 
 
@@ -477,7 +476,7 @@
         + [pltpu.SemaphoreType.DMA] * 3
         + [pltpu.SemaphoreType.DMA((2,))],
         cost_estimate=light,
-        compiler_params=params(middle_limit),
+        compiler_params=params(large_limit),
         name="attend_diagonal",
     )(*in_hbm(queries), cosine, sine, *in_hbm(own, key_cache, value_cache))
 
@@ -537,7 +536,6 @@
                 fetch_pair(far, 4 * block, kv_ref, place + 8, sem)
 
     weight_copy = pltpu.make_async_copy(weight_ref, w_ref, weight_sem)
-    weight_copy.start()
 
     @pl.when(jnp.logical_not(has_old))
     def _():
@@ -575,6 +573,10 @@
         def _():
             for copy in copies(t + 2):
                 copy.start()
+
+        @pl.when(t + 3 == items)
+        def _():
+            weight_copy.start()
 
     scratch = (roped_ref, kv_ref, bias_ref, (s_0, s_1), (most_0, most_1), top_ref, sum_ref, values_ref)
 

time: 80.9 us -> 81.4 us (level)
  the two profiles are of different devices: /device:TPU:3 before, /device:TPU:0 now
where the time goes in v10:
time: 81.4 us; the launch traced here: 80.9 us
  Pallas kernels  55.4 us (68%)
  starting transfers between devices  16.1 us (20%)
  waiting for transfers between devices  6.75 us (8%)
  local copies, waits for them, and re-layouts  1.67 us (2%)
  between operations  0.97 us (1%)
    pallas_call x1, Pallas kernels, rest_part(): pl.pallas_call(rest_kernel, out_shape=pltpu.HBM((rows, width), jnp.bfloat...  34.2 us
    pallas_call x1, Pallas kernels, diagonal_part(): pl.pallas_call(diagonal_kernel, out_shape=(pltpu.HBM((items, head_pair *...  9.91 us
    all_to_all x1, starting transfers between devices, body(): old = lax.all_to_all(picked, 'blk', split_axis=0, concat_axis=0, tiled=True)  7.26 us
    all_to_all x1, starting transfers between devices, body(): lax.all_to_all(new, 'blk', split_axis=0, concat_axis=0, tiled=True)  5.6 us
    ppermute x2, waiting for transfers between devices, other_chip(): return lax.ppermute(value, 'group', [(0, 2), (2, 0), (1, 3), (3, 1)])  3.99 us
    ppermute x2, starting transfers between devices, other_chip(): return lax.ppermute(value, 'group', [(0, 2), (2, 0), (1, 3), (3, 1)])  3.1 us
    pallas_call x1, Pallas kernels, pick_old(): pl.pallas_call(pick_old_kernel, out_shape=jax.ShapeDtypeStruct((requests,...  3.02 us
    pallas_call x1, Pallas kernels, pick_new(): pl.pallas_call(lambda *refs: pick_new_kernel(pages, cap, *refs), out_shap...  2.76 us
  transfers between devices with their start and end apart: 8, of which 4 were waited for; matrix products, arithmetic and copies ran while one was open for 0% of the time, Pallas kernels for 63%

profile of v10, /device:TPU:0, one launch (start us, length us, event | category | flops | bytes accessed | tf_op | source)
XLA Modules:
  0.0 80.9 jit_solution(7424684964326960479)
XLA Ops:
  0.6 0.0 copy-start.9
  0.6 0.0 copy-start.8
  0.7 0.0 copy-start.6
  0.7 0.0 copy-start.5
  0.7 3.0 %pick_old.1 = bf16[8,2,2,32,256]{4,3,2,1,0:T(8,128)(2,1)} custom-call(s32[8,32]{1,0:T(8,128)} %refs_0_.2, bf16[40,32,256]{2,1,0:T(8,128)(2,1)} %key_ref.3, bf16[40,32,256]{2,1,0:T(8,128)(2,1)} %value_ref.3), custom_call_target="tpu_custom_call" | custom-call | flops 1 | bytes 1 | tf_op jit(solution)/shard_map/pick_old/pallas_call | solution.py:65
  3.7 7.3 %all-to-all-start = ((bf16[8,2,2,32,256]{4,3,2,1,0:T(8,128)(2,1)}), bf16[8,2,2,32,256]{4,3,2,1,0:T(8,128)(2,1)S(1)}, u32[]{:S(2)}, u32[]{:S(2)}) async-start(bf16[8,2,2,32,256]{4,3,2,1,0:T(8,128)(2,1)} %pick_old.1), calls=%async_computation | async-start | bytes 1048576 | tf_op jit(solution)/shard_map/all_to_all | solution.py:706
  11.0 0.0 copy-done.9
  11.0 0.0 copy-done.8
  11.0 0.0 copy-done.6
  11.0 0.0 copy-done.5
  11.0 2.5 %rotate_keys.1 = (bf16[16,2,32,256]{3,2,1,0:T(8,128)(2,1)}, f32[512,128]{1,0:T(8,128)}, f32[512,128]{1,0:T(8,128)}) custom-call(s32[8]{0:T(128)S(1)} %copy-done.8, f32[1,128]{1,0:T(1,128)S(1)} %copy-done.9, bf16[512,256]{1,0:T(8,128)(2,1)S(1)} %bitcast.5, bf16[512,256]{1,0:T(8,128)(2,1)S(1)} %bitcast.6), custom_call_target="tpu_custom_call" | custom-call | flops 1 | bytes 1 | tf_op jit(solution)/shard_map/rotate_keys/pallas_call | solution.py:121
  13.5 0.0 copy-start.7
  13.5 1.5 %collective-permute-start.1 = (bf16[16,2,32,256]{3,2,1,0:T(8,128)(2,1)}, bf16[16,2,32,256]{3,2,1,0:T(8,128)(2,1)S(1)}, u32[]{:S(2)}, u32[]{:S(2)}) collective-permute-start(bf16[16,2,32,256]{3,2,1,0:T(8,128)(2,1)} %get-tuple-element.22.own_ref.refs_1_), channel_id=1, source_target_pairs={{0,2},{2,0},{1,3},{3,1},{4,6},{6,4},{5,7},{7,5},{8,10},{10,8},{9,1... | collective-permute-start | bytes 1572872 | tf_op jit(solution)/shard_map/ppermute | solution.py:703
  15.0 0.0 collective-permute-start
  15.0 0.0 copy-start.4
  15.0 9.9 %attend_diagonal.1 = (bf16[5,1024,256]{2,1,0:T(8,128)(2,1)}, f32[5,1024,256]{2,1,0:T(8,128)}, f32[5,1024,128]{2,1,0:T(8,128)}, bf16[40,32,256]{2,1,0:T(8,128)(2,1)}, bf16[40,32,256]{2,1,0:T(8,128)(2,1)}) custom-call(bf16[512,2560]{1,0:T(8,128)(2,1)} %bitcast.7, f32[512,128]{1,0:T(8,128)} %get-tuple-element.20.cos_ref, f32[512,128]{1,0:T(8,128)} %get-tuple-element.21.sin_ref, ...), custom_call_target="tpu_custom_call" | custom-call | flops 1 | bytes 1 | tf_op jit(solution)/shard_map/attend_diagonal/pallas_call | solution.py:462
  24.9 0.6 all-to-all-done
  25.5 0.0 copy-start.10
  25.5 0.8 copy-done.10
  26.3 0.0 copy-done.7
  26.3 1.6 %sort_old.1.old_ref = bf16[16,2,32,256]{3,2,1,0:T(8,128)(2,1)S(1)} custom-call(s32[8,32]{1,0:T(8,128)S(1)} %copy-done.7, bf16[16,2,32,256]{3,2,1,0:T(8,128)(2,1)} %bitcast.9), custom_call_target="tpu_custom_call" | custom-call | flops 1 | bytes 1 | tf_op jit(solution)/shard_map/sort_old/pallas_call | solution.py:145
  27.9 0.0 copy-start
  27.9 0.0 collective-permute-done.1.refs_3_.far_ref
  27.9 0.0 copy-start.1
  27.9 0.1 collective-permute-start.2
  28.0 1.6 %collective-permute-start.4 = (bf16[16,2,32,256]{3,2,1,0:T(8,128)(2,1)S(1)}, bf16[16,2,32,256]{3,2,1,0:T(8,128)(2,1)S(1)}, u32[]{:S(2)}, u32[]{:S(2)}) collective-permute-start(bf16[16,2,32,256]{3,2,1,0:T(8,128)(2,1)S(1)} %sort_old.1.old_ref), channel_id=1, source_target_pairs={{0,2},{2,0},{1,3},{3,1},{4,6},{6,4},{5,7},{7,5},{8,10},{10,8},{9,1... | collective-permute-start | bytes 1572872 | tf_op jit(solution)/shard_map/ppermute | solution.py:703
  29.6 0.0 collective-permute-done.refs_2_.core_ref
  29.6 0.0 copy-start.2
  29.6 0.3 collective-permute-done.2.refs_4_.far_core_ref
  29.9 0.0 copy-done.4
  29.9 0.0 copy-start.3
  29.9 2.8 %pick_new.1 = (bf16[16,2,32,256]{3,2,1,0:T(8,128)(2,1)}, s32[16]{0:T(128)S(1)}) custom-call(s32[8,32]{1,0:T(8,128)S(1)} %copy-done.7, bf16[16,2,32,256]{3,2,1,0:T(8,128)(2,1)S(1)} %copy-done.4, bf16[16,2,32,256]{3,2,1,0:T(8,128)(2,1)S(1)} %collective-permute-done.refs_2_.core_ref, bf16[16,2,32,256]{3,2,1,0:T(8,128)(2,1)S(1)} %collective-permute-done.1.refs_3_.far_ref, ...), custom_call_target="tpu_custom_call" | custom-call | flops 1 | bytes 1 | tf_op jit(solution)/shard_map/pick_new/pallas_call | solution.py:182
  32.7 5.6 %all-to-all-start.1 = ((bf16[16,2,32,256]{3,2,1,0:T(8,128)(2,1)}), bf16[16,2,32,256]{3,2,1,0:T(8,128)(2,1)S(1)}, u32[]{:S(2)}, u32[]{:S(2)}) async-start(bf16[16,2,32,256]{3,2,1,0:T(8,128)(2,1)} %get-tuple-element.28), calls=%async_computation.1 | async-start | bytes 1048576 | tf_op jit(solution)/shard_map/all_to_all | solution.py:723
  38.3 0.1 collective-permute-start.3
  38.4 4.0 %collective-permute-done.4.old_far_ref = bf16[16,2,32,256]{3,2,1,0:T(8,128)(2,1)S(1)} collective-permute-done((bf16[16,2,32,256]{3,2,1,0:T(8,128)(2,1)S(1)}, bf16[16,2,32,256]{3,2,1,0:T(8,128)(2,1)S(1)}, u32[]{:S(2)}, u32[]{:S(2)}) %collective-permute-start.4) | collective-permute-done | bytes 524320 | tf_op jit(solution)/shard_map/ppermute | solution.py:703
  42.4 0.0 copy-start.11
  42.4 0.0 collective-permute-start.5
  42.4 0.0 collective-permute-done.3.old_core_ref
  42.4 0.0 copy-start.12
  42.4 1.9 %collective-permute-done.5.old_far_core_ref = bf16[16,2,32,256]{3,2,1,0:T(8,128)(2,1)S(1)} collective-permute-done((bf16[16,2,32,256]{3,2,1,0:T(8,128)(2,1)S(1)}, bf16[16,2,32,256]{3,2,1,0:T(8,128)(2,1)S(1)}, u32[]{:S(2)}, u32[]{:S(2)}) %collective-permute-start.5) | collective-permute-done | bytes 524320 | tf_op jit(solution)/shard_map/ppermute | solution.py:700
  44.3 0.0 copy-start.13
  44.3 0.8 copy-done.13
  45.1 0.0 copy-done
  45.1 0.0 copy-done.1
  45.1 0.0 copy-done.2
  45.1 0.0 copy-done.3
  45.1 0.0 copy-done.11
  45.1 0.0 copy-done.12
  45.1 34.2 %attend_rest.1 = bf16[512,2560]{1,0:T(8,128)(2,1)} custom-call(s32[8]{0:T(128)} %lengths_ref.3, bf16[5,1024,256]{2,1,0:T(8,128)(2,1)} %get-tuple-element.23.roped_in, f32[5,1024,256]{2,1,0:T(8,128)} %get-tuple-element.24.acc_in, f32[5,1024,128]{2,1,0:T(8,128)} %get-tuple-element.25.stat_in, bf16[16,2,32,256]{3,2,1,0:T(8,128)(2,1)} %copy-done.2, ...), custom_call_target="tpu_custom_call" | custom-call | flops 1 | bytes 1 | tf_op jit(solution)/shard_map/attend_rest/pallas_call | solution.py:627
  79.3 0.0 all-to-all-done.1.arrived_ref
  79.4 1.4 %place_new.1 = (bf16[40,32,256]{2,1,0:T(8,128)(2,1)}, bf16[40,32,256]{2,1,0:T(8,128)(2,1)}) custom-call(s32[16]{0:T(128)S(1)} %get-tuple-element.30.targets_ref, bf16[16,2,32,256]{3,2,1,0:T(8,128)(2,1)S(1)} %all-to-all-done.1.arrived_ref, bf16[40,32,256]{2,1,0:T(8,128)(2,1)} %get-tuple-element.31.key_in, ...), custom_call_target="tpu_custom_call", output_to_operand_aliasing={{0}: (2, {}), {1}: (3, {})} | custom-call | flops 1 | bytes 1 | tf_op jit(solution)/shard_map/place_new/pallas_call | solution.py:669
Async XLA Ops:
  0.6 10.3 %copy-start.9 = (f32[1,128]{1,0:T(1,128)S(1)}, f32[1,128]{1,0:T(1,128)}, u32[]{:S(2)}) copy-start(f32[1,128]{1,0:T(1,128)} %constant.2.clone.freq_ref) | copy-start | bytes 1540
  0.6 10.3 %copy-start.8 = (s32[8]{0:T(128)S(1)}, s32[8]{0:T(128)}, u32[]{:S(2)}) copy-start(s32[8]{0:T(128)} %lengths_ref.3) | copy-start | bytes 100
  0.7 10.3 %copy-start.6 = (bf16[1,512,256]{2,1,0:T(8,128)(2,1)S(1)}, bf16[1,512,256]{2,1,0:T(8,128)(2,1)}, u32[]{:S(2)}) copy-start(bf16[1,512,256]{2,1,0:T(8,128)(2,1)} %param.11) | copy-start | bytes 786436
  0.7 10.3 %copy-start.5 = (bf16[1,512,256]{2,1,0:T(8,128)(2,1)S(1)}, bf16[1,512,256]{2,1,0:T(8,128)(2,1)}, u32[]{:S(2)}) copy-start(bf16[1,512,256]{2,1,0:T(8,128)(2,1)} %param.10) | copy-start | bytes 786436
  3.7 21.8 %all-to-all-start = ((bf16[8,2,2,32,256]{4,3,2,1,0:T(8,128)(2,1)}), bf16[8,2,2,32,256]{4,3,2,1,0:T(8,128)(2,1)S(1)}, u32[]{:S(2)}, u32[]{:S(2)}) async-start(bf16[8,2,2,32,256]{4,3,2,1,0:T(8,128)(2,1)} %pick_old.1), calls=%async_computation | async-start | bytes 1048576 | tf_op jit(solution)/shard_map/all_to_all | solution.py:706
  13.5 12.8 %copy-start.7 = (s32[8,32]{1,0:T(8,128)S(1)}, s32[8,32]{1,0:T(8,128)}, u32[]{:S(2)}) copy-start(s32[8,32]{1,0:T(8,128)} %refs_0_.2) | copy-start | bytes 3076
  13.5 14.5 %collective-permute-start.1 = (bf16[16,2,32,256]{3,2,1,0:T(8,128)(2,1)}, bf16[16,2,32,256]{3,2,1,0:T(8,128)(2,1)S(1)}, u32[]{:S(2)}, u32[]{:S(2)}) collective-permute-start(bf16[16,2,32,256]{3,2,1,0:T(8,128)(2,1)} %get-tuple-element.22.own_ref.refs_1_), channel_id=1, source_target_pairs={{0,2},{2,0},{1,3},{3,1},{4,6},{6,4},{5,7},{7,5},{8,10},{10,8},{9,1... | collective-permute-start | bytes 1572872 | tf_op jit(solution)/shard_map/ppermute | solution.py:703
  15.0 14.6 %collective-permute-start = (bf16[16,2,32,256]{3,2,1,0:T(8,128)(2,1)}, bf16[16,2,32,256]{3,2,1,0:T(8,128)(2,1)S(1)}, u32[]{:S(2)}, u32[]{:S(2)}) collective-permute-start(bf16[16,2,32,256]{3,2,1,0:T(8,128)(2,1)} %get-tuple-element.22.own_ref.refs_1_), channel_id=1, source_target_pairs={{0,1},{1,0},{2,3},{3,2},{4,5},{5,4},{6,7},{7,6},{8,9},{9,8},{10,11... | collective-permute-start | bytes 1572872 | tf_op jit(solution)/shard_map/ppermute | solution.py:700
  15.0 14.9 %copy-start.4 = (bf16[16,2,32,256]{3,2,1,0:T(8,128)(2,1)S(1)}, bf16[16,2,32,256]{3,2,1,0:T(8,128)(2,1)}, u32[]{:S(2)}) copy-start(bf16[16,2,32,256]{3,2,1,0:T(8,128)(2,1)} %get-tuple-element.22.own_ref.refs_1_) | copy-start | bytes 1572868
  25.5 0.8 copy-start.10
  27.9 17.2 %copy-start = (bf16[16,2,32,256]{3,2,1,0:T(8,128)(2,1)}, bf16[16,2,32,256]{3,2,1,0:T(8,128)(2,1)S(1)}, u32[]{:S(2)}) copy-start(bf16[16,2,32,256]{3,2,1,0:T(8,128)(2,1)S(1)} %sort_old.1.old_ref) | copy-start | bytes 1572868
  27.9 17.2 %copy-start.1 = (bf16[16,2,32,256]{3,2,1,0:T(8,128)(2,1)}, bf16[16,2,32,256]{3,2,1,0:T(8,128)(2,1)S(1)}, u32[]{:S(2)}) copy-start(bf16[16,2,32,256]{3,2,1,0:T(8,128)(2,1)S(1)} %collective-permute-done.1.refs_3_.far_ref) | copy-start | bytes 1572868
  27.9 2.0 %collective-permute-start.2 = (bf16[16,2,32,256]{3,2,1,0:T(8,128)(2,1)S(1)}, bf16[16,2,32,256]{3,2,1,0:T(8,128)(2,1)S(1)}, u32[]{:S(2)}, u32[]{:S(2)}) collective-permute-start(bf16[16,2,32,256]{3,2,1,0:T(8,128)(2,1)S(1)} %collective-permute-done.1.refs_3_.far_ref), channel_id=1, source_target_pairs={{0,1},{1,0},{2,3},{3,2},{4,5},{5,4},{6,7},{7,6},{8,9},{9,8},{10,11... | collective-permute-start | bytes 1572872 | tf_op jit(solution)/shard_map/ppermute | solution.py:700
  28.0 14.3 %collective-permute-start.4 = (bf16[16,2,32,256]{3,2,1,0:T(8,128)(2,1)S(1)}, bf16[16,2,32,256]{3,2,1,0:T(8,128)(2,1)S(1)}, u32[]{:S(2)}, u32[]{:S(2)}) collective-permute-start(bf16[16,2,32,256]{3,2,1,0:T(8,128)(2,1)S(1)} %sort_old.1.old_ref), channel_id=1, source_target_pairs={{0,2},{2,0},{1,3},{3,1},{4,6},{6,4},{5,7},{7,5},{8,10},{10,8},{9,1... | collective-permute-start | bytes 1572872 | tf_op jit(solution)/shard_map/ppermute | solution.py:703
  29.6 15.5 %copy-start.2 = (bf16[16,2,32,256]{3,2,1,0:T(8,128)(2,1)}, bf16[16,2,32,256]{3,2,1,0:T(8,128)(2,1)S(1)}, u32[]{:S(2)}) copy-start(bf16[16,2,32,256]{3,2,1,0:T(8,128)(2,1)S(1)} %collective-permute-done.refs_2_.core_ref) | copy-start | bytes 1572868
  29.9 15.2 %copy-start.3 = (bf16[16,2,32,256]{3,2,1,0:T(8,128)(2,1)}, bf16[16,2,32,256]{3,2,1,0:T(8,128)(2,1)S(1)}, u32[]{:S(2)}) copy-start(bf16[16,2,32,256]{3,2,1,0:T(8,128)(2,1)S(1)} %collective-permute-done.2.refs_4_.far_core_ref) | copy-start | bytes 1572868
  32.7 46.7 %all-to-all-start.1 = ((bf16[16,2,32,256]{3,2,1,0:T(8,128)(2,1)}), bf16[16,2,32,256]{3,2,1,0:T(8,128)(2,1)S(1)}, u32[]{:S(2)}, u32[]{:S(2)}) async-start(bf16[16,2,32,256]{3,2,1,0:T(8,128)(2,1)} %get-tuple-element.28), calls=%async_computation.1 | async-start | bytes 1048576 | tf_op jit(solution)/shard_map/all_to_all | solution.py:723
  38.3 4.1 %collective-permute-start.3 = (bf16[16,2,32,256]{3,2,1,0:T(8,128)(2,1)S(1)}, bf16[16,2,32,256]{3,2,1,0:T(8,128)(2,1)S(1)}, u32[]{:S(2)}, u32[]{:S(2)}) collective-permute-start(bf16[16,2,32,256]{3,2,1,0:T(8,128)(2,1)S(1)} %sort_old.1.old_ref), channel_id=1, source_target_pairs={{0,1},{1,0},{2,3},{3,2},{4,5},{5,4},{6,7},{7,6},{8,9},{9,8},{10,11... | collective-permute-start | bytes 1572872 | tf_op jit(solution)/shard_map/ppermute | solution.py:700
  42.4 2.7 %copy-start.11 = (bf16[16,2,32,256]{3,2,1,0:T(8,128)(2,1)}, bf16[16,2,32,256]{3,2,1,0:T(8,128)(2,1)S(1)}, u32[]{:S(2)}) copy-start(bf16[16,2,32,256]{3,2,1,0:T(8,128)(2,1)S(1)} %collective-permute-done.4.old_far_ref) | copy-start | bytes 1572868
  42.4 1.9 %collective-permute-start.5 = (bf16[16,2,32,256]{3,2,1,0:T(8,128)(2,1)S(1)}, bf16[16,2,32,256]{3,2,1,0:T(8,128)(2,1)S(1)}, u32[]{:S(2)}, u32[]{:S(2)}) collective-permute-start(bf16[16,2,32,256]{3,2,1,0:T(8,128)(2,1)S(1)} %collective-permute-done.4.old_far_ref), channel_id=1, source_target_pairs={{0,1},{1,0},{2,3},{3,2},{4,5},{5,4},{6,7},{7,6},{8,9},{9,8},{10,11... | collective-permute-start | bytes 1572872 | tf_op jit(solution)/shard_map/ppermute | solution.py:700
  42.4 2.7 %copy-start.12 = (bf16[16,2,32,256]{3,2,1,0:T(8,128)(2,1)}, bf16[16,2,32,256]{3,2,1,0:T(8,128)(2,1)S(1)}, u32[]{:S(2)}) copy-start(bf16[16,2,32,256]{3,2,1,0:T(8,128)(2,1)S(1)} %collective-permute-done.3.old_core_ref) | copy-start | bytes 1572868
  44.3 0.8 copy-start.13

commit v11 on v9

--- a/solution.py
+++ b/solution.py
@@ -15,7 +15,6 @@
 vmem_spec = pl.BlockSpec(memory_space=pltpu.VMEM)
 small_limit = 16 * 1024 * 1024
 head_pair = 2
-middle_limit = 40 * 1024 * 1024
 large_limit = 60 * 1024 * 1024
 
 
@@ -235,19 +234,19 @@
 def attention(steps, step_keys, roped_ref, kv_ref, bias_ref, s_refs, most_refs, top_ref, sum_ref, sum_of_values, begin, finish):
     items, rows, _ = roped_ref.shape
     step_slots = step_keys // 32
-    biased = bias_ref.shape[1]
+    tables, _, biased = bias_ref.shape
 
     def block(kind, c):
         return kv_ref[pl.ds(c * step_slots, step_slots), kind].reshape(step_keys, 256)
 
-    def scores(t, c, which, masked):
+    def scores(t, c, which):
         result = lax.dot_general(
             roped_ref[t], block(0, c), (((1,), (1,)), ((), ())), preferred_element_type=jnp.float32
         )
-        if masked:
-            head = result[:, :biased].reshape(head_pair, rows // head_pair, biased) + bias_ref[...]
-            head = head.reshape(rows, biased)
-            result = join([head, result[:, biased:]]) if step_keys > biased else head
+        bias = bias_ref[jnp.minimum(c, tables - 1)]
+        head = result[:, :biased].reshape(head_pair, rows // head_pair, biased) + bias
+        head = head.reshape(rows, biased)
+        result = join([head, result[:, biased:]]) if step_keys > biased else head
         s_refs[which][c] = result
         most_refs[which][...] = jnp.maximum(most_refs[which][...], lane_fold(result, jnp.maximum))
 
@@ -267,34 +266,30 @@
 
     def loop(work):
         def step(c, carry):
-            work(c, False)
+            work(c)
             return carry
 
-        @pl.when(steps > 0)
-        def _():
-            work(0, True)
-
-        lax.fori_loop(1, steps, step, 0)
+        lax.fori_loop(0, steps, step, 0)
 
     def both(t, which):
-        def work(c, masked):
+        def work(c):
             weigh(c, which)
-            scores(t + 1, c, 1 - which, masked)
+            scores(t + 1, c, 1 - which)
 
         loop(work)
 
     drive(
         items, most_refs, begin, settle, finish,
-        lambda: loop(lambda c, masked: scores(0, c, 0, masked)),
+        lambda: loop(lambda c: scores(0, c, 0)),
         both,
-        lambda which: loop(lambda c, masked: weigh(c, which)),
+        lambda which: loop(lambda c: weigh(c, which)),
     )
 
 
 def attention_at_once(roped_ref, kv_ref, bias_ref, s_refs, most_refs, top_ref, sum_ref, sum_of_values, begin, finish):
     items, rows, _ = roped_ref.shape
     blocks, _, width = s_refs[0].shape
-    biased = bias_ref.shape[1]
+    biased = bias_ref.shape[2]
     slots = width // 32
 
     def scores(t, which):
@@ -306,7 +301,7 @@
                 query, keys, (((1,), (1,)), ((), ())), preferred_element_type=jnp.float32
             )
             if c == 0:
-                head = result[:, :biased].reshape(head_pair, rows // head_pair, biased) + bias_ref[...]
+                head = result[:, :biased].reshape(head_pair, rows // head_pair, biased) + bias_ref[0]
                 head = head.reshape(rows, biased)
                 result = join([head, result[:, biased:]]) if width > biased else head
             s_refs[which][c] = result
@@ -364,7 +359,7 @@
     finish(last)
 
 
-def working(rows, steps, step_keys):
+def working(rows, steps, step_keys, tables):
     return [
         pltpu.VMEM((steps * step_keys // 32, 2, 32, 256), jnp.bfloat16),
         pltpu.VMEM((steps, head_pair * rows, step_keys), jnp.float32),
@@ -374,7 +369,7 @@
         pltpu.VMEM((head_pair * rows, 128), jnp.float32),
         pltpu.VMEM((head_pair * rows, 128), jnp.float32),
         pltpu.VMEM((head_pair * rows, 256), jnp.float32),
-        pltpu.VMEM((rows, block_keys), jnp.float32),
+        pltpu.VMEM((tables, rows, block_keys), jnp.float32),
     ]
 
 
@@ -394,9 +389,9 @@
 
 
 def diagonal_kernel(
-    query_ref, cos_ref, sin_ref, own_ref, key_ref, value_ref, roped_out, acc_out, stat_out,
-    key_out_ref, value_out_ref, key_pool, value_pool, q_ref, roped_ref, acc_ref, stat_ref, kv_ref, s_0, s_1, most_0, most_1, top_ref, sum_ref, values_ref,
-    bias_ref, query_sem, sem, out_sem, pool_sems,
+    query_ref, cos_in, sin_in, own_ref, key_ref, value_ref, roped_out, acc_out, stat_out,
+    key_out_ref, value_out_ref, cos_ref, sin_ref, key_pool, value_pool, q_ref, roped_ref, acc_ref, stat_ref, kv_ref, s_0, s_1, most_0, most_1, top_ref, sum_ref, values_ref,
+    bias_ref, query_sem, sem, out_sem, pool_sems, angle_sems,
 ):
     rows = q_ref.shape[0]
     items = roped_ref.shape[0]
@@ -410,13 +405,21 @@
     ]
     query_copy = pltpu.make_async_copy(query_ref, q_ref, query_sem)
     query_copy.start()
+    angle_copies = [
+        pltpu.make_async_copy(cos_in, cos_ref, angle_sems.at[0]),
+        pltpu.make_async_copy(sin_in, sin_ref, angle_sems.at[1]),
+    ]
+    for copy in angle_copies:
+        copy.start()
     fetch(own_ref, 0, kv_ref, 0, block_slots, sem)
     for copy in loads:
         copy.start()
     row = lax.broadcasted_iota(jnp.int32, (rows, block_keys), 0)
     column = lax.broadcasted_iota(jnp.int32, (rows, block_keys), 1)
-    bias_ref[...] = jnp.where(column <= row, 0.0, masked_score)
+    bias_ref[0] = jnp.where(column <= row, 0.0, masked_score)
     query_copy.wait()
+    for copy in angle_copies:
+        copy.wait()
 
     def rope(t, carry):
         for one in range(head_pair):
@@ -465,21 +468,23 @@
         out_shape=(pltpu.HBM((items, head_pair * rows, 256), jnp.bfloat16),)
         + state_out(items, rows)
         + (pltpu.HBM(key_cache.shape, jnp.bfloat16), pltpu.HBM(value_cache.shape, jnp.bfloat16)),
-        in_specs=[hbm_spec, vmem_spec, vmem_spec, hbm_spec, hbm_spec, hbm_spec],
+        in_specs=[hbm_spec] * 6,
         out_specs=(hbm_spec,) * 5,
         scratch_shapes=[
+            pltpu.VMEM(cosine.shape, jnp.float32),
+            pltpu.VMEM(sine.shape, jnp.float32),
             pltpu.VMEM(key_cache.shape, jnp.bfloat16),
             pltpu.VMEM(value_cache.shape, jnp.bfloat16),
             pltpu.VMEM((rows, width), jnp.bfloat16),
         ]
         + state_shapes(items, rows)
-        + working(rows, 1, block_keys)
+        + working(rows, 1, block_keys, 1)
         + [pltpu.SemaphoreType.DMA] * 3
-        + [pltpu.SemaphoreType.DMA((2,))],
+        + [pltpu.SemaphoreType.DMA((2,))] * 2,
         cost_estimate=light,
-        compiler_params=params(middle_limit),
+        compiler_params=params(large_limit),
         name="attend_diagonal",
-    )(*in_hbm(queries), cosine, sine, *in_hbm(own, key_cache, value_cache))
+    )(*in_hbm(queries, cosine, sine, own, key_cache, value_cache))
 
 
 def rest_kernel(
@@ -491,30 +496,25 @@
     group_index = lax.axis_index("group")
     has_old = lengths_ref[lax.axis_index("blk")] > 0
     items = roped_ref.shape[0]
-    rows = bias_ref.shape[0]
+    rows = bias_ref.shape[1]
     chunk = stage_ref.shape[2]
     chunks = w_ref.shape[1] // chunk
     odd = group_index % 2
     chip = group_index // 2
     blocks = jnp.where(has_old, 4, odd + 2 * chip)
-    steps = odd + chip
+    steps = jnp.where(has_old, 2, odd + chip)
     base = jnp.where(has_old, 16, 16 * odd)
     near = (old_ref, old_core_ref)
     far = (old_far_ref, old_far_core_ref)
 
     def copies(t):
-        place = t % 2
         return [
-            pltpu.make_async_copy(source.at[t], target.at[place], state_sems.at[number, place])
+            pltpu.make_async_copy(source.at[t], target.at[t], state_sems.at[number, t])
             for number, (source, target) in enumerate(((stat_in, stat_ref), (acc_in, acc_ref)))
         ]
 
     roped_copy = pltpu.make_async_copy(roped_in, roped_ref, roped_sem)
     roped_copy.start()
-    for t in range(2):
-        for copy in copies(t):
-            copy.start()
-
     @pl.when(odd == 1)
     def _():
         fetch(core_ref, 0, kv_ref, base, 16, sem)
@@ -536,12 +536,17 @@
                 fetch_pair(near, 4 * block, kv_ref, place, sem)
                 fetch_pair(far, 4 * block, kv_ref, place + 8, sem)
 
+    for t in range(items):
+        for copy in copies(t):
+            copy.start()
     weight_copy = pltpu.make_async_copy(weight_ref, w_ref, weight_sem)
     weight_copy.start()
 
+    bias_ref[1] = jnp.zeros(bias_ref.shape[1:], jnp.float32)
+
     @pl.when(jnp.logical_not(has_old))
     def _():
-        bias_ref[...] = jnp.where(odd == 1, masked_score, 0.0) + jnp.zeros_like(bias_ref)
+        bias_ref[0] = jnp.where(odd == 1, masked_score, 0.0) + jnp.zeros(bias_ref.shape[1:], jnp.float32)
         empty = pl.ds(0, block_slots)
 
         @pl.when(odd == 1)
@@ -550,8 +555,8 @@
 
     @pl.when(has_old)
     def _():
-        bias_ref[:, :256] = old_bias(rows, group_index)
-        bias_ref[:, 256:] = old_bias(rows, group_index ^ 2)
+        bias_ref[0, :, :256] = old_bias(rows, group_index)
+        bias_ref[0, :, 256:] = old_bias(rows, group_index ^ 2)
 
     roped_copy.wait()
     wait_rows(kv_ref, blocks, 4, sem)
@@ -560,33 +565,20 @@
     def begin(t, most_ref):
         for copy in copies(t):
             copy.wait()
-        most_ref[...] = jnp.where(lane < 64, stat_ref[t % 2], masked_score)
+        most_ref[...] = jnp.where(lane < 64, stat_ref[t], masked_score)
 
     def finish(t):
-        stat = stat_ref[t % 2]
+        stat = stat_ref[t]
         factor = jnp.exp(stat[:, :1] - top_ref[...])
         sums = stat[:, 64:65] * factor + jnp.sum(sum_ref[...], axis=1, keepdims=True)
         inverse = 1.0 / sums
         old = factor * inverse
-        mixed = acc_ref[t % 2] * join([old, old]) + values_ref[...] * join([inverse, inverse])
+        mixed = acc_ref[t] * join([old, old]) + values_ref[...] * join([inverse, inverse])
         roped_ref[t] = mixed.astype(jnp.bfloat16)
 
-        @pl.when(t + 2 < items)
-        def _():
-            for copy in copies(t + 2):
-                copy.start()
-
     scratch = (roped_ref, kv_ref, bias_ref, (s_0, s_1), (most_0, most_1), top_ref, sum_ref, values_ref)
 
-    @pl.when(has_old)
-    def _():
-        attention_at_once(*scratch, begin, finish)
-
-    @pl.when(jnp.logical_not(has_old))
-    def _():
-        attention(steps, 2 * block_keys, *scratch, begin, finish)
-
-
+    attention(steps, 2 * block_keys, *scratch, begin, finish)
     weight_copy.wait()
 
     def out_copy(n, columns):
@@ -627,14 +619,13 @@
         out_shape=pltpu.HBM((rows, width), jnp.bfloat16),
         in_specs=[smem_spec] + [hbm_spec] * 3 + [any_spec] * 7 + [hbm_spec],
         out_specs=hbm_spec,
-        scratch_shapes=[pltpu.VMEM((items, pair_rows, 256), jnp.bfloat16)]
-        + state_shapes(2, rows)[1:]
-        + working(rows, 2, 2 * block_keys)
+        scratch_shapes=state_shapes(items, rows)
+        + working(rows, 2, 2 * block_keys, 2)
         + [
             pltpu.VMEM(weight.shape, jnp.bfloat16),
             pltpu.VMEM((2, rows, chunk), jnp.bfloat16),
             pltpu.SemaphoreType.DMA,
-            pltpu.SemaphoreType.DMA((2, 2)),
+            pltpu.SemaphoreType.DMA((2, items)),
             pltpu.SemaphoreType.DMA,
             pltpu.SemaphoreType.DMA,
             pltpu.SemaphoreType.DMA((2,)),

time: 80.9 us -> 79.3 us (0.980)
  the two profiles are of different devices: /device:TPU:3 before, /device:TPU:7 now
where the time goes in v11:
time: 79.3 us; the launch traced here: 78.2 us
  Pallas kernels  52.9 us (67%)
  starting transfers between devices  15.8 us (20%)
  waiting for transfers between devices  6.83 us (9%)
  local copies, waits for them, and re-layouts  1.66 us (2%)
  between operations  0.95 us (1%)
    pallas_call x1, Pallas kernels, rest_part(): pl.pallas_call(rest_kernel, out_shape=pltpu.HBM((rows, width), jnp.bfloat...  32.7 us
    pallas_call x1, Pallas kernels, diagonal_part(): pl.pallas_call(diagonal_kernel, out_shape=(pltpu.HBM((items, head_pair *...  8.97 us
    all_to_all x1, starting transfers between devices, body(): old = lax.all_to_all(picked, 'blk', split_axis=0, concat_axis=0, tiled=True)  5.79 us
    ppermute x4, starting transfers between devices, other_core(): return lax.ppermute(value, 'group', [(0, 1), (1, 0), (2, 3), (3, 2)])  4.82 us
    all_to_all x1, starting transfers between devices, body(): lax.all_to_all(new, 'blk', split_axis=0, concat_axis=0, tiled=True)  4.77 us
    ppermute x2, waiting for transfers between devices, other_chip(): return lax.ppermute(value, 'group', [(0, 2), (2, 0), (1, 3), (3, 1)])  3.49 us
    pallas_call x1, Pallas kernels, pick_old(): pl.pallas_call(pick_old_kernel, out_shape=jax.ShapeDtypeStruct((requests,...  3.02 us
    ppermute x4, waiting for transfers between devices, other_core(): return lax.ppermute(value, 'group', [(0, 1), (1, 0), (2, 3), (3, 2)])  2.83 us
  transfers between devices with their start and end apart: 8, of which 4 were waited for; matrix products, arithmetic and copies ran while one was open for 0% of the time, Pallas kernels for 62%

profile of v11, /device:TPU:7, one launch (start us, length us, event | category | flops | bytes accessed | tf_op | source)
XLA Modules:
  0.0 78.2 jit_solution(6835023627970377408)
XLA Ops:
  0.6 0.0 copy-start.9
  0.6 0.0 copy-start.8
  0.7 0.0 copy-start.6
  0.7 0.0 copy-start.5
  0.7 3.0 %pick_old.1 = bf16[8,2,2,32,256]{4,3,2,1,0:T(8,128)(2,1)} custom-call(s32[8,32]{1,0:T(8,128)} %refs_0_.2, bf16[40,32,256]{2,1,0:T(8,128)(2,1)} %key_ref.3, bf16[40,32,256]{2,1,0:T(8,128)(2,1)} %value_ref.3), custom_call_target="tpu_custom_call" | custom-call | flops 1 | bytes 1 | tf_op jit(solution)/shard_map/pick_old/pallas_call | solution.py:65
  3.7 5.8 %all-to-all-start = ((bf16[8,2,2,32,256]{4,3,2,1,0:T(8,128)(2,1)}), bf16[8,2,2,32,256]{4,3,2,1,0:T(8,128)(2,1)S(1)}, u32[]{:S(2)}, u32[]{:S(2)}) async-start(bf16[8,2,2,32,256]{4,3,2,1,0:T(8,128)(2,1)} %pick_old.1), calls=%async_computation | async-start | bytes 1048576 | tf_op jit(solution)/shard_map/all_to_all | solution.py:695
  9.5 0.0 copy-done.9
  9.5 0.0 copy-done.8
  9.5 0.0 copy-done.6
  9.5 0.0 copy-done.5
  9.5 2.5 %rotate_keys.1 = (bf16[16,2,32,256]{3,2,1,0:T(8,128)(2,1)}, f32[512,128]{1,0:T(8,128)}, f32[512,128]{1,0:T(8,128)}) custom-call(s32[8]{0:T(128)S(1)} %copy-done.8, f32[1,128]{1,0:T(1,128)S(1)} %copy-done.9, bf16[512,256]{1,0:T(8,128)(2,1)S(1)} %bitcast.5, bf16[512,256]{1,0:T(8,128)(2,1)S(1)} %bitcast.6), custom_call_target="tpu_custom_call" | custom-call | flops 1 | bytes 1 | tf_op jit(solution)/shard_map/rotate_keys/pallas_call | solution.py:121
  12.0 0.0 copy-start.7
  12.0 0.2 collective-permute-start.1
  12.2 1.5 %collective-permute-start = (bf16[16,2,32,256]{3,2,1,0:T(8,128)(2,1)}, bf16[16,2,32,256]{3,2,1,0:T(8,128)(2,1)S(1)}, u32[]{:S(2)}, u32[]{:S(2)}) collective-permute-start(bf16[16,2,32,256]{3,2,1,0:T(8,128)(2,1)} %get-tuple-element.22.own_ref.refs_1_), channel_id=1, source_target_pairs={{0,1},{1,0},{2,3},{3,2},{4,5},{5,4},{6,7},{7,6},{8,9},{9,8},{10,11... | collective-permute-start | bytes 1572872 | tf_op jit(solution)/shard_map/ppermute | solution.py:689
  13.7 0.0 copy-start.4
  13.7 9.0 %attend_diagonal.1 = (bf16[5,1024,256]{2,1,0:T(8,128)(2,1)}, f32[5,1024,256]{2,1,0:T(8,128)}, f32[5,1024,128]{2,1,0:T(8,128)}, bf16[40,32,256]{2,1,0:T(8,128)(2,1)}, bf16[40,32,256]{2,1,0:T(8,128)(2,1)}) custom-call(bf16[512,2560]{1,0:T(8,128)(2,1)} %bitcast.7, f32[512,128]{1,0:T(8,128)} %get-tuple-element.20.cos_in, f32[512,128]{1,0:T(8,128)} %get-tuple-element.21.sin_in, ...), custom_call_target="tpu_custom_call" | custom-call | flops 1 | bytes 1 | tf_op jit(solution)/shard_map/attend_diagonal/pallas_call | solution.py:466
  22.7 0.5 all-to-all-done
  23.2 0.0 copy-start.10
  23.2 0.8 %copy-done.10 = bf16[8,2,2,32,256]{4,3,2,1,0:T(8,128)(2,1)} copy-done((bf16[8,2,2,32,256]{4,3,2,1,0:T(8,128)(2,1)}, bf16[8,2,2,32,256]{4,3,2,1,0:T(8,128)(2,1)S(1)}, u32[]{:S(2)}) %copy-start.10) | copy-done | bytes 524312
  24.0 0.0 copy-done.7
  24.0 1.6 %sort_old.1.old_ref = bf16[16,2,32,256]{3,2,1,0:T(8,128)(2,1)S(1)} custom-call(s32[8,32]{1,0:T(8,128)S(1)} %copy-done.7, bf16[16,2,32,256]{3,2,1,0:T(8,128)(2,1)} %bitcast.9), custom_call_target="tpu_custom_call" | custom-call | flops 1 | bytes 1 | tf_op jit(solution)/shard_map/sort_old/pallas_call | solution.py:145
  25.7 0.0 copy-start
  25.7 0.0 collective-permute-done.1.refs_3_.far_ref
  25.7 0.0 copy-start.1
  25.7 1.5 %collective-permute-start.2 = (bf16[16,2,32,256]{3,2,1,0:T(8,128)(2,1)S(1)}, bf16[16,2,32,256]{3,2,1,0:T(8,128)(2,1)S(1)}, u32[]{:S(2)}, u32[]{:S(2)}) collective-permute-start(bf16[16,2,32,256]{3,2,1,0:T(8,128)(2,1)S(1)} %collective-permute-done.1.refs_3_.far_ref), channel_id=1, source_target_pairs={{0,1},{1,0},{2,3},{3,2},{4,5},{5,4},{6,7},{7,6},{8,9},{9,8},{10,11... | collective-permute-start | bytes 1572872 | tf_op jit(solution)/shard_map/ppermute | solution.py:689
  27.2 0.2 collective-permute-start.4
  27.4 0.0 collective-permute-done.refs_2_.core_ref
  27.4 0.0 copy-start.2
  27.5 1.3 %collective-permute-done.2.refs_4_.far_core_ref = bf16[16,2,32,256]{3,2,1,0:T(8,128)(2,1)S(1)} collective-permute-done((bf16[16,2,32,256]{3,2,1,0:T(8,128)(2,1)S(1)}, bf16[16,2,32,256]{3,2,1,0:T(8,128)(2,1)S(1)}, u32[]{:S(2)}, u32[]{:S(2)}) %collective-permute-start.2) | collective-permute-done | bytes 524320 | tf_op jit(solution)/shard_map/ppermute | solution.py:689
  28.7 0.0 copy-done.4
  28.7 0.0 copy-start.3
  28.7 2.8 %pick_new.1 = (bf16[16,2,32,256]{3,2,1,0:T(8,128)(2,1)}, s32[16]{0:T(128)S(1)}) custom-call(s32[8,32]{1,0:T(8,128)S(1)} %copy-done.7, bf16[16,2,32,256]{3,2,1,0:T(8,128)(2,1)S(1)} %copy-done.4, bf16[16,2,32,256]{3,2,1,0:T(8,128)(2,1)S(1)} %collective-permute-done.refs_2_.core_ref, bf16[16,2,32,256]{3,2,1,0:T(8,128)(2,1)S(1)} %collective-permute-done.1.refs_3_.far_ref, ...), custom_call_target="tpu_custom_call" | custom-call | flops 1 | bytes 1 | tf_op jit(solution)/shard_map/pick_new/pallas_call | solution.py:182
  31.5 4.8 %all-to-all-start.1 = ((bf16[16,2,32,256]{3,2,1,0:T(8,128)(2,1)}), bf16[16,2,32,256]{3,2,1,0:T(8,128)(2,1)S(1)}, u32[]{:S(2)}, u32[]{:S(2)}) async-start(bf16[16,2,32,256]{3,2,1,0:T(8,128)(2,1)} %get-tuple-element.28), calls=%async_computation.1 | async-start | bytes 1048576 | tf_op jit(solution)/shard_map/all_to_all | solution.py:712
  36.3 0.9 %collective-permute-start.3 = (bf16[16,2,32,256]{3,2,1,0:T(8,128)(2,1)S(1)}, bf16[16,2,32,256]{3,2,1,0:T(8,128)(2,1)S(1)}, u32[]{:S(2)}, u32[]{:S(2)}) collective-permute-start(bf16[16,2,32,256]{3,2,1,0:T(8,128)(2,1)S(1)} %sort_old.1.old_ref), channel_id=1, source_target_pairs={{0,1},{1,0},{2,3},{3,2},{4,5},{5,4},{6,7},{7,6},{8,9},{9,8},{10,11... | collective-permute-start | bytes 1572872 | tf_op jit(solution)/shard_map/ppermute | solution.py:689
  37.2 3.5 %collective-permute-done.4.old_far_ref = bf16[16,2,32,256]{3,2,1,0:T(8,128)(2,1)S(1)} collective-permute-done((bf16[16,2,32,256]{3,2,1,0:T(8,128)(2,1)S(1)}, bf16[16,2,32,256]{3,2,1,0:T(8,128)(2,1)S(1)}, u32[]{:S(2)}, u32[]{:S(2)}) %collective-permute-start.4) | collective-permute-done | bytes 524320 | tf_op jit(solution)/shard_map/ppermute | solution.py:692
  40.7 0.0 copy-start.11
  40.7 0.8 %collective-permute-start.5 = (bf16[16,2,32,256]{3,2,1,0:T(8,128)(2,1)S(1)}, bf16[16,2,32,256]{3,2,1,0:T(8,128)(2,1)S(1)}, u32[]{:S(2)}, u32[]{:S(2)}) collective-permute-start(bf16[16,2,32,256]{3,2,1,0:T(8,128)(2,1)S(1)} %collective-permute-done.4.old_far_ref), channel_id=1, source_target_pairs={{0,1},{1,0},{2,3},{3,2},{4,5},{5,4},{6,7},{7,6},{8,9},{9,8},{10,11... | collective-permute-start | bytes 1572872 | tf_op jit(solution)/shard_map/ppermute | solution.py:689
  41.6 0.0 collective-permute-done.3.old_core_ref
  41.6 0.0 copy-start.12
  41.6 1.5 %collective-permute-done.5.old_far_core_ref = bf16[16,2,32,256]{3,2,1,0:T(8,128)(2,1)S(1)} collective-permute-done((bf16[16,2,32,256]{3,2,1,0:T(8,128)(2,1)S(1)}, bf16[16,2,32,256]{3,2,1,0:T(8,128)(2,1)S(1)}, u32[]{:S(2)}, u32[]{:S(2)}) %collective-permute-start.5) | collective-permute-done | bytes 524320 | tf_op jit(solution)/shard_map/ppermute | solution.py:689
  43.1 0.0 copy-start.13
  43.1 0.8 %copy-done.13 = bf16[16,2,32,256]{3,2,1,0:T(8,128)(2,1)} copy-done((bf16[16,2,32,256]{3,2,1,0:T(8,128)(2,1)}, bf16[16,2,32,256]{3,2,1,0:T(8,128)(2,1)S(1)}, u32[]{:S(2)}) %copy-start.13) | copy-done | bytes 524312
  43.9 0.0 copy-done
  43.9 0.0 copy-done.1
  43.9 0.0 copy-done.2
  43.9 0.0 copy-done.3
  43.9 0.0 copy-done.11
  43.9 0.0 copy-done.12
  43.9 32.7 %attend_rest.1 = bf16[512,2560]{1,0:T(8,128)(2,1)} custom-call(s32[8]{0:T(128)} %lengths_ref.3, bf16[5,1024,256]{2,1,0:T(8,128)(2,1)} %get-tuple-element.23.roped_in, f32[5,1024,256]{2,1,0:T(8,128)} %get-tuple-element.24.acc_in, f32[5,1024,128]{2,1,0:T(8,128)} %get-tuple-element.25.stat_in, bf16[16,2,32,256]{3,2,1,0:T(8,128)(2,1)} %copy-done.2, ...), custom_call_target="tpu_custom_call" | custom-call | flops 1 | bytes 1 | tf_op jit(solution)/shard_map/attend_rest/pallas_call | solution.py:617
  76.7 0.0 all-to-all-done.1.arrived_ref
  76.7 1.4 %place_new.1 = (bf16[40,32,256]{2,1,0:T(8,128)(2,1)}, bf16[40,32,256]{2,1,0:T(8,128)(2,1)}) custom-call(s32[16]{0:T(128)S(1)} %get-tuple-element.30.targets_ref, bf16[16,2,32,256]{3,2,1,0:T(8,128)(2,1)S(1)} %all-to-all-done.1.arrived_ref, bf16[40,32,256]{2,1,0:T(8,128)(2,1)} %get-tuple-element.31.key_in, ...), custom_call_target="tpu_custom_call", output_to_operand_aliasing={{0}: (2, {}), {1}: (3, {})} | custom-call | flops 1 | bytes 1 | tf_op jit(solution)/shard_map/place_new/pallas_call | solution.py:658
Async XLA Ops:
  0.6 8.9 %copy-start.9 = (f32[1,128]{1,0:T(1,128)S(1)}, f32[1,128]{1,0:T(1,128)}, u32[]{:S(2)}) copy-start(f32[1,128]{1,0:T(1,128)} %constant.2.clone.freq_ref) | copy-start | bytes 1540
  0.6 8.9 %copy-start.8 = (s32[8]{0:T(128)S(1)}, s32[8]{0:T(128)}, u32[]{:S(2)}) copy-start(s32[8]{0:T(128)} %lengths_ref.3) | copy-start | bytes 100
  0.7 8.8 %copy-start.6 = (bf16[1,512,256]{2,1,0:T(8,128)(2,1)S(1)}, bf16[1,512,256]{2,1,0:T(8,128)(2,1)}, u32[]{:S(2)}) copy-start(bf16[1,512,256]{2,1,0:T(8,128)(2,1)} %param.11) | copy-start | bytes 786436
  0.7 8.8 %copy-start.5 = (bf16[1,512,256]{2,1,0:T(8,128)(2,1)S(1)}, bf16[1,512,256]{2,1,0:T(8,128)(2,1)}, u32[]{:S(2)}) copy-start(bf16[1,512,256]{2,1,0:T(8,128)(2,1)} %param.10) | copy-start | bytes 786436
  3.7 19.5 %all-to-all-start = ((bf16[8,2,2,32,256]{4,3,2,1,0:T(8,128)(2,1)}), bf16[8,2,2,32,256]{4,3,2,1,0:T(8,128)(2,1)S(1)}, u32[]{:S(2)}, u32[]{:S(2)}) async-start(bf16[8,2,2,32,256]{4,3,2,1,0:T(8,128)(2,1)} %pick_old.1), calls=%async_computation | async-start | bytes 1048576 | tf_op jit(solution)/shard_map/all_to_all | solution.py:695
  12.0 12.0 %copy-start.7 = (s32[8,32]{1,0:T(8,128)S(1)}, s32[8,32]{1,0:T(8,128)}, u32[]{:S(2)}) copy-start(s32[8,32]{1,0:T(8,128)} %refs_0_.2) | copy-start | bytes 3076
  12.0 13.7 %collective-permute-start.1 = (bf16[16,2,32,256]{3,2,1,0:T(8,128)(2,1)}, bf16[16,2,32,256]{3,2,1,0:T(8,128)(2,1)S(1)}, u32[]{:S(2)}, u32[]{:S(2)}) collective-permute-start(bf16[16,2,32,256]{3,2,1,0:T(8,128)(2,1)} %get-tuple-element.22.own_ref.refs_1_), channel_id=1, source_target_pairs={{0,2},{2,0},{1,3},{3,1},{4,6},{6,4},{5,7},{7,5},{8,10},{10,8},{9,1... | collective-permute-start | bytes 1572872 | tf_op jit(solution)/shard_map/ppermute | solution.py:692
  12.2 15.2 %collective-permute-start = (bf16[16,2,32,256]{3,2,1,0:T(8,128)(2,1)}, bf16[16,2,32,256]{3,2,1,0:T(8,128)(2,1)S(1)}, u32[]{:S(2)}, u32[]{:S(2)}) collective-permute-start(bf16[16,2,32,256]{3,2,1,0:T(8,128)(2,1)} %get-tuple-element.22.own_ref.refs_1_), channel_id=1, source_target_pairs={{0,1},{1,0},{2,3},{3,2},{4,5},{5,4},{6,7},{7,6},{8,9},{9,8},{10,11... | collective-permute-start | bytes 1572872 | tf_op jit(solution)/shard_map/ppermute | solution.py:689
  13.7 15.0 %copy-start.4 = (bf16[16,2,32,256]{3,2,1,0:T(8,128)(2,1)S(1)}, bf16[16,2,32,256]{3,2,1,0:T(8,128)(2,1)}, u32[]{:S(2)}) copy-start(bf16[16,2,32,256]{3,2,1,0:T(8,128)(2,1)} %get-tuple-element.22.own_ref.refs_1_) | copy-start | bytes 1572868
  23.2 0.8 %copy-start.10 = (bf16[8,2,2,32,256]{4,3,2,1,0:T(8,128)(2,1)}, bf16[8,2,2,32,256]{4,3,2,1,0:T(8,128)(2,1)S(1)}, u32[]{:S(2)}) copy-start(bf16[8,2,2,32,256]{4,3,2,1,0:T(8,128)(2,1)S(1)} %all-to-all-done) | copy-start | bytes 1572868
  25.7 18.3 %copy-start = (bf16[16,2,32,256]{3,2,1,0:T(8,128)(2,1)}, bf16[16,2,32,256]{3,2,1,0:T(8,128)(2,1)S(1)}, u32[]{:S(2)}) copy-start(bf16[16,2,32,256]{3,2,1,0:T(8,128)(2,1)S(1)} %sort_old.1.old_ref) | copy-start | bytes 1572868
  25.7 18.2 %copy-start.1 = (bf16[16,2,32,256]{3,2,1,0:T(8,128)(2,1)}, bf16[16,2,32,256]{3,2,1,0:T(8,128)(2,1)S(1)}, u32[]{:S(2)}) copy-start(bf16[16,2,32,256]{3,2,1,0:T(8,128)(2,1)S(1)} %collective-permute-done.1.refs_3_.far_ref) | copy-start | bytes 1572868
  25.7 3.1 %collective-permute-start.2 = (bf16[16,2,32,256]{3,2,1,0:T(8,128)(2,1)S(1)}, bf16[16,2,32,256]{3,2,1,0:T(8,128)(2,1)S(1)}, u32[]{:S(2)}, u32[]{:S(2)}) collective-permute-start(bf16[16,2,32,256]{3,2,1,0:T(8,128)(2,1)S(1)} %collective-permute-done.1.refs_3_.far_ref), channel_id=1, source_target_pairs={{0,1},{1,0},{2,3},{3,2},{4,5},{5,4},{6,7},{7,6},{8,9},{9,8},{10,11... | collective-permute-start | bytes 1572872 | tf_op jit(solution)/shard_map/ppermute | solution.py:689
  27.2 13.5 %collective-permute-start.4 = (bf16[16,2,32,256]{3,2,1,0:T(8,128)(2,1)S(1)}, bf16[16,2,32,256]{3,2,1,0:T(8,128)(2,1)S(1)}, u32[]{:S(2)}, u32[]{:S(2)}) collective-permute-start(bf16[16,2,32,256]{3,2,1,0:T(8,128)(2,1)S(1)} %sort_old.1.old_ref), channel_id=1, source_target_pairs={{0,2},{2,0},{1,3},{3,1},{4,6},{6,4},{5,7},{7,5},{8,10},{10,8},{9,1... | collective-permute-start | bytes 1572872 | tf_op jit(solution)/shard_map/ppermute | solution.py:692
  27.4 16.5 %copy-start.2 = (bf16[16,2,32,256]{3,2,1,0:T(8,128)(2,1)}, bf16[16,2,32,256]{3,2,1,0:T(8,128)(2,1)S(1)}, u32[]{:S(2)}) copy-start(bf16[16,2,32,256]{3,2,1,0:T(8,128)(2,1)S(1)} %collective-permute-done.refs_2_.core_ref) | copy-start | bytes 1572868
  28.7 15.2 %copy-start.3 = (bf16[16,2,32,256]{3,2,1,0:T(8,128)(2,1)}, bf16[16,2,32,256]{3,2,1,0:T(8,128)(2,1)S(1)}, u32[]{:S(2)}) copy-start(bf16[16,2,32,256]{3,2,1,0:T(8,128)(2,1)S(1)} %collective-permute-done.2.refs_4_.far_core_ref) | copy-start | bytes 1572868
  31.5 45.2 %all-to-all-start.1 = ((bf16[16,2,32,256]{3,2,1,0:T(8,128)(2,1)}), bf16[16,2,32,256]{3,2,1,0:T(8,128)(2,1)S(1)}, u32[]{:S(2)}, u32[]{:S(2)}) async-start(bf16[16,2,32,256]{3,2,1,0:T(8,128)(2,1)} %get-tuple-element.28), calls=%async_computation.1 | async-start | bytes 1048576 | tf_op jit(solution)/shard_map/all_to_all | solution.py:712
  36.3 5.3 %collective-permute-start.3 = (bf16[16,2,32,256]{3,2,1,0:T(8,128)(2,1)S(1)}, bf16[16,2,32,256]{3,2,1,0:T(8,128)(2,1)S(1)}, u32[]{:S(2)}, u32[]{:S(2)}) collective-permute-start(bf16[16,2,32,256]{3,2,1,0:T(8,128)(2,1)S(1)} %sort_old.1.old_ref), channel_id=1, source_target_pairs={{0,1},{1,0},{2,3},{3,2},{4,5},{5,4},{6,7},{7,6},{8,9},{9,8},{10,11... | collective-permute-start | bytes 1572872 | tf_op jit(solution)/shard_map/ppermute | solution.py:689
  40.7 3.2 %copy-start.11 = (bf16[16,2,32,256]{3,2,1,0:T(8,128)(2,1)}, bf16[16,2,32,256]{3,2,1,0:T(8,128)(2,1)S(1)}, u32[]{:S(2)}) copy-start(bf16[16,2,32,256]{3,2,1,0:T(8,128)(2,1)S(1)} %collective-permute-done.4.old_far_ref) | copy-start | bytes 1572868
  40.7 2.4 %collective-permute-start.5 = (bf16[16,2,32,256]{3,2,1,0:T(8,128)(2,1)S(1)}, bf16[16,2,32,256]{3,2,1,0:T(8,128)(2,1)S(1)}, u32[]{:S(2)}, u32[]{:S(2)}) collective-permute-start(bf16[16,2,32,256]{3,2,1,0:T(8,128)(2,1)S(1)} %collective-permute-done.4.old_far_ref), channel_id=1, source_target_pairs={{0,1},{1,0},{2,3},{3,2},{4,5},{5,4},{6,7},{7,6},{8,9},{9,8},{10,11... | collective-permute-start | bytes 1572872 | tf_op jit(solution)/shard_map/ppermute | solution.py:689
  41.6 2.4 %copy-start.12 = (bf16[16,2,32,256]{3,2,1,0:T(8,128)(2,1)}, bf16[16,2,32,256]{3,2,1,0:T(8,128)(2,1)S(1)}, u32[]{:S(2)}) copy-start(bf16[16,2,32,256]{3,2,1,0:T(8,128)(2,1)S(1)} %collective-permute-done.3.old_core_ref) | copy-start | bytes 1572868
  43.1 0.8 %copy-start.13 = (bf16[16,2,32,256]{3,2,1,0:T(8,128)(2,1)}, bf16[16,2,32,256]{3,2,1,0:T(8,128)(2,1)S(1)}, u32[]{:S(2)}) copy-start(bf16[16,2,32,256]{3,2,1,0:T(8,128)(2,1)S(1)} %collective-permute-done.5.old_far_core_ref) | copy-start | bytes 1572868

commit v12 on v11

--- a/solution.py
+++ b/solution.py
@@ -231,22 +231,22 @@
             pltpu.make_async_copy(filled, filled, sem).wait()
 
 
-def attention(steps, step_keys, roped_ref, kv_ref, bias_ref, s_refs, most_refs, top_ref, sum_ref, sum_of_values, begin, finish):
+def attention(steps, most_steps, step_keys, roped_ref, kv_ref, bias_ref, s_refs, most_refs, top_ref, sum_ref, sum_of_values, begin, finish):
     items, rows, _ = roped_ref.shape
     step_slots = step_keys // 32
-    tables, _, biased = bias_ref.shape
+    biased = bias_ref.shape[2]
 
     def block(kind, c):
-        return kv_ref[pl.ds(c * step_slots, step_slots), kind].reshape(step_keys, 256)
+        return kv_ref[c * step_slots : (c + 1) * step_slots, kind].reshape(step_keys, 256)
 
     def scores(t, c, which):
         result = lax.dot_general(
             roped_ref[t], block(0, c), (((1,), (1,)), ((), ())), preferred_element_type=jnp.float32
         )
-        bias = bias_ref[jnp.minimum(c, tables - 1)]
-        head = result[:, :biased].reshape(head_pair, rows // head_pair, biased) + bias
-        head = head.reshape(rows, biased)
-        result = join([head, result[:, biased:]]) if step_keys > biased else head
+        if c == 0:
+            head = result[:, :biased].reshape(head_pair, rows // head_pair, biased) + bias_ref[0]
+            head = head.reshape(rows, biased)
+            result = join([head, result[:, biased:]]) if step_keys > biased else head
         s_refs[which][c] = result
         most_refs[which][...] = jnp.maximum(most_refs[which][...], lane_fold(result, jnp.maximum))
 
@@ -265,11 +265,11 @@
         sum_of_values[...] = jnp.zeros_like(sum_of_values)
 
     def loop(work):
-        def step(c, carry):
-            work(c)
-            return carry
-
-        lax.fori_loop(0, steps, step, 0)
+        for c in range(most_steps):
+
+            @pl.when(steps > c)
+            def _(c=c):
+                work(c)
 
     def both(t, which):
         def work(c):
@@ -542,8 +542,6 @@
     weight_copy = pltpu.make_async_copy(weight_ref, w_ref, weight_sem)
     weight_copy.start()
 
-    bias_ref[1] = jnp.zeros(bias_ref.shape[1:], jnp.float32)
-
     @pl.when(jnp.logical_not(has_old))
     def _():
         bias_ref[0] = jnp.where(odd == 1, masked_score, 0.0) + jnp.zeros(bias_ref.shape[1:], jnp.float32)
@@ -578,7 +576,7 @@
 
     scratch = (roped_ref, kv_ref, bias_ref, (s_0, s_1), (most_0, most_1), top_ref, sum_ref, values_ref)
 
-    attention(steps, 2 * block_keys, *scratch, begin, finish)
+    attention(steps, 2, 2 * block_keys, *scratch, begin, finish)
     weight_copy.wait()
 
     def out_copy(n, columns):
@@ -620,7 +618,7 @@
         in_specs=[smem_spec] + [hbm_spec] * 3 + [any_spec] * 7 + [hbm_spec],
         out_specs=hbm_spec,
         scratch_shapes=state_shapes(items, rows)
-        + working(rows, 2, 2 * block_keys, 2)
+        + working(rows, 2, 2 * block_keys, 1)
         + [
             pltpu.VMEM(weight.shape, jnp.bfloat16),
             pltpu.VMEM((2, rows, chunk), jnp.bfloat16),

time: 79.3 us -> 79 us (level)
  no operation moved by 1% of the time
where the time goes in v12:
time: 79 us; the launch traced here: 78 us
  Pallas kernels  52.7 us (67%)
  starting transfers between devices  15.8 us (20%)
  waiting for transfers between devices  6.83 us (9%)
  local copies, waits for them, and re-layouts  1.66 us (2%)
  between operations  0.95 us (1%)
    pallas_call x1, Pallas kernels, rest_part(): pl.pallas_call(rest_kernel, out_shape=pltpu.HBM((rows, width), jnp.bfloat...  32.5 us
    pallas_call x1, Pallas kernels, diagonal_part(): pl.pallas_call(diagonal_kernel, out_shape=(pltpu.HBM((items, head_pair *...  8.97 us
    all_to_all x1, starting transfers between devices, body(): old = lax.all_to_all(picked, 'blk', split_axis=0, concat_axis=0, tiled=True)  5.79 us
    ppermute x4, starting transfers between devices, other_core(): return lax.ppermute(value, 'group', [(0, 1), (1, 0), (2, 3), (3, 2)])  4.82 us
    all_to_all x1, starting transfers between devices, body(): lax.all_to_all(new, 'blk', split_axis=0, concat_axis=0, tiled=True)  4.77 us
    ppermute x2, waiting for transfers between devices, other_chip(): return lax.ppermute(value, 'group', [(0, 2), (2, 0), (1, 3), (3, 1)])  3.49 us
    pallas_call x1, Pallas kernels, pick_old(): pl.pallas_call(pick_old_kernel, out_shape=jax.ShapeDtypeStruct((requests,...  3.02 us
    ppermute x4, waiting for transfers between devices, other_core(): return lax.ppermute(value, 'group', [(0, 1), (1, 0), (2, 3), (3, 2)])  2.83 us
  transfers between devices with their start and end apart: 8, of which 4 were waited for; matrix products, arithmetic and copies ran while one was open for 0% of the time, Pallas kernels for 62%

profile of v12, /device:TPU:7, one launch (start us, length us, event | category | flops | bytes accessed | tf_op | source)
XLA Modules:
  0.0 78.0 jit_solution(7720539955504258437)
XLA Ops:
  0.6 0.0 copy-start.9
  0.6 0.0 copy-start.8
  0.7 0.0 copy-start.6
  0.7 0.0 copy-start.5
  0.7 3.0 %pick_old.1 = bf16[8,2,2,32,256]{4,3,2,1,0:T(8,128)(2,1)} custom-call(s32[8,32]{1,0:T(8,128)} %refs_0_.2, bf16[40,32,256]{2,1,0:T(8,128)(2,1)} %key_ref.3, bf16[40,32,256]{2,1,0:T(8,128)(2,1)} %value_ref.3), custom_call_target="tpu_custom_call" | custom-call | flops 1 | bytes 1 | tf_op jit(solution)/shard_map/pick_old/pallas_call | solution.py:65
  3.7 5.8 %all-to-all-start = ((bf16[8,2,2,32,256]{4,3,2,1,0:T(8,128)(2,1)}), bf16[8,2,2,32,256]{4,3,2,1,0:T(8,128)(2,1)S(1)}, u32[]{:S(2)}, u32[]{:S(2)}) async-start(bf16[8,2,2,32,256]{4,3,2,1,0:T(8,128)(2,1)} %pick_old.1), calls=%async_computation | async-start | bytes 1048576 | tf_op jit(solution)/shard_map/all_to_all | solution.py:693
  9.5 0.0 copy-done.9
  9.5 0.0 copy-done.8
  9.5 0.0 copy-done.6
  9.5 0.0 copy-done.5
  9.5 2.5 %rotate_keys.1 = (bf16[16,2,32,256]{3,2,1,0:T(8,128)(2,1)}, f32[512,128]{1,0:T(8,128)}, f32[512,128]{1,0:T(8,128)}) custom-call(s32[8]{0:T(128)S(1)} %copy-done.8, f32[1,128]{1,0:T(1,128)S(1)} %copy-done.9, bf16[512,256]{1,0:T(8,128)(2,1)S(1)} %bitcast.5, bf16[512,256]{1,0:T(8,128)(2,1)S(1)} %bitcast.6), custom_call_target="tpu_custom_call" | custom-call | flops 1 | bytes 1 | tf_op jit(solution)/shard_map/rotate_keys/pallas_call | solution.py:121
  12.0 0.0 copy-start.7
  12.0 0.2 collective-permute-start.1
  12.2 1.5 %collective-permute-start = (bf16[16,2,32,256]{3,2,1,0:T(8,128)(2,1)}, bf16[16,2,32,256]{3,2,1,0:T(8,128)(2,1)S(1)}, u32[]{:S(2)}, u32[]{:S(2)}) collective-permute-start(bf16[16,2,32,256]{3,2,1,0:T(8,128)(2,1)} %get-tuple-element.22.own_ref.refs_1_), channel_id=1, source_target_pairs={{0,1},{1,0},{2,3},{3,2},{4,5},{5,4},{6,7},{7,6},{8,9},{9,8},{10,11... | collective-permute-start | bytes 1572872 | tf_op jit(solution)/shard_map/ppermute | solution.py:687
  13.7 0.0 copy-start.4
  13.7 9.0 %attend_diagonal.1 = (bf16[5,1024,256]{2,1,0:T(8,128)(2,1)}, f32[5,1024,256]{2,1,0:T(8,128)}, f32[5,1024,128]{2,1,0:T(8,128)}, bf16[40,32,256]{2,1,0:T(8,128)(2,1)}, bf16[40,32,256]{2,1,0:T(8,128)(2,1)}) custom-call(bf16[512,2560]{1,0:T(8,128)(2,1)} %bitcast.7, f32[512,128]{1,0:T(8,128)} %get-tuple-element.20.cos_in, f32[512,128]{1,0:T(8,128)} %get-tuple-element.21.sin_in, ...), custom_call_target="tpu_custom_call" | custom-call | flops 1 | bytes 1 | tf_op jit(solution)/shard_map/attend_diagonal/pallas_call | solution.py:466
  22.7 0.5 all-to-all-done
  23.2 0.0 copy-start.10
  23.2 0.8 %copy-done.10 = bf16[8,2,2,32,256]{4,3,2,1,0:T(8,128)(2,1)} copy-done((bf16[8,2,2,32,256]{4,3,2,1,0:T(8,128)(2,1)}, bf16[8,2,2,32,256]{4,3,2,1,0:T(8,128)(2,1)S(1)}, u32[]{:S(2)}) %copy-start.10) | copy-done | bytes 524312
  24.0 0.0 copy-done.7
  24.0 1.6 %sort_old.1.old_ref = bf16[16,2,32,256]{3,2,1,0:T(8,128)(2,1)S(1)} custom-call(s32[8,32]{1,0:T(8,128)S(1)} %copy-done.7, bf16[16,2,32,256]{3,2,1,0:T(8,128)(2,1)} %bitcast.9), custom_call_target="tpu_custom_call" | custom-call | flops 1 | bytes 1 | tf_op jit(solution)/shard_map/sort_old/pallas_call | solution.py:145
  25.7 0.0 copy-start
  25.7 0.0 collective-permute-done.1.refs_3_.far_ref
  25.7 0.0 copy-start.1
  25.7 1.5 %collective-permute-start.2 = (bf16[16,2,32,256]{3,2,1,0:T(8,128)(2,1)S(1)}, bf16[16,2,32,256]{3,2,1,0:T(8,128)(2,1)S(1)}, u32[]{:S(2)}, u32[]{:S(2)}) collective-permute-start(bf16[16,2,32,256]{3,2,1,0:T(8,128)(2,1)S(1)} %collective-permute-done.1.refs_3_.far_ref), channel_id=1, source_target_pairs={{0,1},{1,0},{2,3},{3,2},{4,5},{5,4},{6,7},{7,6},{8,9},{9,8},{10,11... | collective-permute-start | bytes 1572872 | tf_op jit(solution)/shard_map/ppermute | solution.py:687
  27.2 0.2 collective-permute-start.4
  27.4 0.0 collective-permute-done.refs_2_.core_ref
  27.4 0.0 copy-start.2
  27.5 1.3 %collective-permute-done.2.refs_4_.far_core_ref = bf16[16,2,32,256]{3,2,1,0:T(8,128)(2,1)S(1)} collective-permute-done((bf16[16,2,32,256]{3,2,1,0:T(8,128)(2,1)S(1)}, bf16[16,2,32,256]{3,2,1,0:T(8,128)(2,1)S(1)}, u32[]{:S(2)}, u32[]{:S(2)}) %collective-permute-start.2) | collective-permute-done | bytes 524320 | tf_op jit(solution)/shard_map/ppermute | solution.py:687
  28.7 0.0 copy-done.4
  28.7 0.0 copy-start.3
  28.7 2.8 %pick_new.1 = (bf16[16,2,32,256]{3,2,1,0:T(8,128)(2,1)}, s32[16]{0:T(128)S(1)}) custom-call(s32[8,32]{1,0:T(8,128)S(1)} %copy-done.7, bf16[16,2,32,256]{3,2,1,0:T(8,128)(2,1)S(1)} %copy-done.4, bf16[16,2,32,256]{3,2,1,0:T(8,128)(2,1)S(1)} %collective-permute-done.refs_2_.core_ref, bf16[16,2,32,256]{3,2,1,0:T(8,128)(2,1)S(1)} %collective-permute-done.1.refs_3_.far_ref, ...), custom_call_target="tpu_custom_call" | custom-call | flops 1 | bytes 1 | tf_op jit(solution)/shard_map/pick_new/pallas_call | solution.py:182
  31.5 4.8 %all-to-all-start.1 = ((bf16[16,2,32,256]{3,2,1,0:T(8,128)(2,1)}), bf16[16,2,32,256]{3,2,1,0:T(8,128)(2,1)S(1)}, u32[]{:S(2)}, u32[]{:S(2)}) async-start(bf16[16,2,32,256]{3,2,1,0:T(8,128)(2,1)} %get-tuple-element.28), calls=%async_computation.1 | async-start | bytes 1048576 | tf_op jit(solution)/shard_map/all_to_all | solution.py:710
  36.3 0.9 %collective-permute-start.3 = (bf16[16,2,32,256]{3,2,1,0:T(8,128)(2,1)S(1)}, bf16[16,2,32,256]{3,2,1,0:T(8,128)(2,1)S(1)}, u32[]{:S(2)}, u32[]{:S(2)}) collective-permute-start(bf16[16,2,32,256]{3,2,1,0:T(8,128)(2,1)S(1)} %sort_old.1.old_ref), channel_id=1, source_target_pairs={{0,1},{1,0},{2,3},{3,2},{4,5},{5,4},{6,7},{7,6},{8,9},{9,8},{10,11... | collective-permute-start | bytes 1572872 | tf_op jit(solution)/shard_map/ppermute | solution.py:687
  37.2 3.5 %collective-permute-done.4.old_far_ref = bf16[16,2,32,256]{3,2,1,0:T(8,128)(2,1)S(1)} collective-permute-done((bf16[16,2,32,256]{3,2,1,0:T(8,128)(2,1)S(1)}, bf16[16,2,32,256]{3,2,1,0:T(8,128)(2,1)S(1)}, u32[]{:S(2)}, u32[]{:S(2)}) %collective-permute-start.4) | collective-permute-done | bytes 524320 | tf_op jit(solution)/shard_map/ppermute | solution.py:690
  40.7 0.0 copy-start.11
  40.7 0.8 %collective-permute-start.5 = (bf16[16,2,32,256]{3,2,1,0:T(8,128)(2,1)S(1)}, bf16[16,2,32,256]{3,2,1,0:T(8,128)(2,1)S(1)}, u32[]{:S(2)}, u32[]{:S(2)}) collective-permute-start(bf16[16,2,32,256]{3,2,1,0:T(8,128)(2,1)S(1)} %collective-permute-done.4.old_far_ref), channel_id=1, source_target_pairs={{0,1},{1,0},{2,3},{3,2},{4,5},{5,4},{6,7},{7,6},{8,9},{9,8},{10,11... | collective-permute-start | bytes 1572872 | tf_op jit(solution)/shard_map/ppermute | solution.py:687
  41.6 0.0 collective-permute-done.3.old_core_ref
  41.6 0.0 copy-start.12
  41.6 1.5 %collective-permute-done.5.old_far_core_ref = bf16[16,2,32,256]{3,2,1,0:T(8,128)(2,1)S(1)} collective-permute-done((bf16[16,2,32,256]{3,2,1,0:T(8,128)(2,1)S(1)}, bf16[16,2,32,256]{3,2,1,0:T(8,128)(2,1)S(1)}, u32[]{:S(2)}, u32[]{:S(2)}) %collective-permute-start.5) | collective-permute-done | bytes 524320 | tf_op jit(solution)/shard_map/ppermute | solution.py:687
  43.1 0.0 copy-start.13
  43.1 0.8 %copy-done.13 = bf16[16,2,32,256]{3,2,1,0:T(8,128)(2,1)} copy-done((bf16[16,2,32,256]{3,2,1,0:T(8,128)(2,1)}, bf16[16,2,32,256]{3,2,1,0:T(8,128)(2,1)S(1)}, u32[]{:S(2)}) %copy-start.13) | copy-done | bytes 524312
  43.9 0.0 copy-done
  43.9 0.0 copy-done.1
  43.9 0.0 copy-done.2
  43.9 0.0 copy-done.3
  43.9 0.0 copy-done.11
  43.9 0.0 copy-done.12
  43.9 32.5 %attend_rest.1 = bf16[512,2560]{1,0:T(8,128)(2,1)} custom-call(s32[8]{0:T(128)} %lengths_ref.3, bf16[5,1024,256]{2,1,0:T(8,128)(2,1)} %get-tuple-element.23.roped_in, f32[5,1024,256]{2,1,0:T(8,128)} %get-tuple-element.24.acc_in, f32[5,1024,128]{2,1,0:T(8,128)} %get-tuple-element.25.stat_in, bf16[16,2,32,256]{3,2,1,0:T(8,128)(2,1)} %copy-done.2, ...), custom_call_target="tpu_custom_call" | custom-call | flops 1 | bytes 1 | tf_op jit(solution)/shard_map/attend_rest/pallas_call | solution.py:615
  76.5 0.0 all-to-all-done.1.arrived_ref
  76.5 1.4 %place_new.1 = (bf16[40,32,256]{2,1,0:T(8,128)(2,1)}, bf16[40,32,256]{2,1,0:T(8,128)(2,1)}) custom-call(s32[16]{0:T(128)S(1)} %get-tuple-element.30.targets_ref, bf16[16,2,32,256]{3,2,1,0:T(8,128)(2,1)S(1)} %all-to-all-done.1.arrived_ref, bf16[40,32,256]{2,1,0:T(8,128)(2,1)} %get-tuple-element.31.key_in, ...), custom_call_target="tpu_custom_call", output_to_operand_aliasing={{0}: (2, {}), {1}: (3, {})} | custom-call | flops 1 | bytes 1 | tf_op jit(solution)/shard_map/place_new/pallas_call | solution.py:656
Async XLA Ops:
  0.6 8.9 %copy-start.9 = (f32[1,128]{1,0:T(1,128)S(1)}, f32[1,128]{1,0:T(1,128)}, u32[]{:S(2)}) copy-start(f32[1,128]{1,0:T(1,128)} %constant.2.clone.freq_ref) | copy-start | bytes 1540
  0.6 8.9 %copy-start.8 = (s32[8]{0:T(128)S(1)}, s32[8]{0:T(128)}, u32[]{:S(2)}) copy-start(s32[8]{0:T(128)} %lengths_ref.3) | copy-start | bytes 100
  0.7 8.8 %copy-start.6 = (bf16[1,512,256]{2,1,0:T(8,128)(2,1)S(1)}, bf16[1,512,256]{2,1,0:T(8,128)(2,1)}, u32[]{:S(2)}) copy-start(bf16[1,512,256]{2,1,0:T(8,128)(2,1)} %param.11) | copy-start | bytes 786436
  0.7 8.8 %copy-start.5 = (bf16[1,512,256]{2,1,0:T(8,128)(2,1)S(1)}, bf16[1,512,256]{2,1,0:T(8,128)(2,1)}, u32[]{:S(2)}) copy-start(bf16[1,512,256]{2,1,0:T(8,128)(2,1)} %param.10) | copy-start | bytes 786436
  3.7 19.5 %all-to-all-start = ((bf16[8,2,2,32,256]{4,3,2,1,0:T(8,128)(2,1)}), bf16[8,2,2,32,256]{4,3,2,1,0:T(8,128)(2,1)S(1)}, u32[]{:S(2)}, u32[]{:S(2)}) async-start(bf16[8,2,2,32,256]{4,3,2,1,0:T(8,128)(2,1)} %pick_old.1), calls=%async_computation | async-start | bytes 1048576 | tf_op jit(solution)/shard_map/all_to_all | solution.py:693
  12.0 12.0 %copy-start.7 = (s32[8,32]{1,0:T(8,128)S(1)}, s32[8,32]{1,0:T(8,128)}, u32[]{:S(2)}) copy-start(s32[8,32]{1,0:T(8,128)} %refs_0_.2) | copy-start | bytes 3076
  12.0 13.7 %collective-permute-start.1 = (bf16[16,2,32,256]{3,2,1,0:T(8,128)(2,1)}, bf16[16,2,32,256]{3,2,1,0:T(8,128)(2,1)S(1)}, u32[]{:S(2)}, u32[]{:S(2)}) collective-permute-start(bf16[16,2,32,256]{3,2,1,0:T(8,128)(2,1)} %get-tuple-element.22.own_ref.refs_1_), channel_id=1, source_target_pairs={{0,2},{2,0},{1,3},{3,1},{4,6},{6,4},{5,7},{7,5},{8,10},{10,8},{9,1... | collective-permute-start | bytes 1572872 | tf_op jit(solution)/shard_map/ppermute | solution.py:690
  12.2 15.2 %collective-permute-start = (bf16[16,2,32,256]{3,2,1,0:T(8,128)(2,1)}, bf16[16,2,32,256]{3,2,1,0:T(8,128)(2,1)S(1)}, u32[]{:S(2)}, u32[]{:S(2)}) collective-permute-start(bf16[16,2,32,256]{3,2,1,0:T(8,128)(2,1)} %get-tuple-element.22.own_ref.refs_1_), channel_id=1, source_target_pairs={{0,1},{1,0},{2,3},{3,2},{4,5},{5,4},{6,7},{7,6},{8,9},{9,8},{10,11... | collective-permute-start | bytes 1572872 | tf_op jit(solution)/shard_map/ppermute | solution.py:687
  13.7 15.0 %copy-start.4 = (bf16[16,2,32,256]{3,2,1,0:T(8,128)(2,1)S(1)}, bf16[16,2,32,256]{3,2,1,0:T(8,128)(2,1)}, u32[]{:S(2)}) copy-start(bf16[16,2,32,256]{3,2,1,0:T(8,128)(2,1)} %get-tuple-element.22.own_ref.refs_1_) | copy-start | bytes 1572868
  23.2 0.8 %copy-start.10 = (bf16[8,2,2,32,256]{4,3,2,1,0:T(8,128)(2,1)}, bf16[8,2,2,32,256]{4,3,2,1,0:T(8,128)(2,1)S(1)}, u32[]{:S(2)}) copy-start(bf16[8,2,2,32,256]{4,3,2,1,0:T(8,128)(2,1)S(1)} %all-to-all-done) | copy-start | bytes 1572868
  25.7 18.3 %copy-start = (bf16[16,2,32,256]{3,2,1,0:T(8,128)(2,1)}, bf16[16,2,32,256]{3,2,1,0:T(8,128)(2,1)S(1)}, u32[]{:S(2)}) copy-start(bf16[16,2,32,256]{3,2,1,0:T(8,128)(2,1)S(1)} %sort_old.1.old_ref) | copy-start | bytes 1572868
  25.7 18.2 %copy-start.1 = (bf16[16,2,32,256]{3,2,1,0:T(8,128)(2,1)}, bf16[16,2,32,256]{3,2,1,0:T(8,128)(2,1)S(1)}, u32[]{:S(2)}) copy-start(bf16[16,2,32,256]{3,2,1,0:T(8,128)(2,1)S(1)} %collective-permute-done.1.refs_3_.far_ref) | copy-start | bytes 1572868
  25.7 3.1 %collective-permute-start.2 = (bf16[16,2,32,256]{3,2,1,0:T(8,128)(2,1)S(1)}, bf16[16,2,32,256]{3,2,1,0:T(8,128)(2,1)S(1)}, u32[]{:S(2)}, u32[]{:S(2)}) collective-permute-start(bf16[16,2,32,256]{3,2,1,0:T(8,128)(2,1)S(1)} %collective-permute-done.1.refs_3_.far_ref), channel_id=1, source_target_pairs={{0,1},{1,0},{2,3},{3,2},{4,5},{5,4},{6,7},{7,6},{8,9},{9,8},{10,11... | collective-permute-start | bytes 1572872 | tf_op jit(solution)/shard_map/ppermute | solution.py:687
  27.2 13.5 %collective-permute-start.4 = (bf16[16,2,32,256]{3,2,1,0:T(8,128)(2,1)S(1)}, bf16[16,2,32,256]{3,2,1,0:T(8,128)(2,1)S(1)}, u32[]{:S(2)}, u32[]{:S(2)}) collective-permute-start(bf16[16,2,32,256]{3,2,1,0:T(8,128)(2,1)S(1)} %sort_old.1.old_ref), channel_id=1, source_target_pairs={{0,2},{2,0},{1,3},{3,1},{4,6},{6,4},{5,7},{7,5},{8,10},{10,8},{9,1... | collective-permute-start | bytes 1572872 | tf_op jit(solution)/shard_map/ppermute | solution.py:690
  27.4 16.5 %copy-start.2 = (bf16[16,2,32,256]{3,2,1,0:T(8,128)(2,1)}, bf16[16,2,32,256]{3,2,1,0:T(8,128)(2,1)S(1)}, u32[]{:S(2)}) copy-start(bf16[16,2,32,256]{3,2,1,0:T(8,128)(2,1)S(1)} %collective-permute-done.refs_2_.core_ref) | copy-start | bytes 1572868
  28.7 15.2 %copy-start.3 = (bf16[16,2,32,256]{3,2,1,0:T(8,128)(2,1)}, bf16[16,2,32,256]{3,2,1,0:T(8,128)(2,1)S(1)}, u32[]{:S(2)}) copy-start(bf16[16,2,32,256]{3,2,1,0:T(8,128)(2,1)S(1)} %collective-permute-done.2.refs_4_.far_core_ref) | copy-start | bytes 1572868
  31.5 44.9 %all-to-all-start.1 = ((bf16[16,2,32,256]{3,2,1,0:T(8,128)(2,1)}), bf16[16,2,32,256]{3,2,1,0:T(8,128)(2,1)S(1)}, u32[]{:S(2)}, u32[]{:S(2)}) async-start(bf16[16,2,32,256]{3,2,1,0:T(8,128)(2,1)} %get-tuple-element.28), calls=%async_computation.1 | async-start | bytes 1048576 | tf_op jit(solution)/shard_map/all_to_all | solution.py:710
  36.3 5.3 %collective-permute-start.3 = (bf16[16,2,32,256]{3,2,1,0:T(8,128)(2,1)S(1)}, bf16[16,2,32,256]{3,2,1,0:T(8,128)(2,1)S(1)}, u32[]{:S(2)}, u32[]{:S(2)}) collective-permute-start(bf16[16,2,32,256]{3,2,1,0:T(8,128)(2,1)S(1)} %sort_old.1.old_ref), channel_id=1, source_target_pairs={{0,1},{1,0},{2,3},{3,2},{4,5},{5,4},{6,7},{7,6},{8,9},{9,8},{10,11... | collective-permute-start | bytes 1572872 | tf_op jit(solution)/shard_map/ppermute | solution.py:687
  40.7 3.2 %copy-start.11 = (bf16[16,2,32,256]{3,2,1,0:T(8,128)(2,1)}, bf16[16,2,32,256]{3,2,1,0:T(8,128)(2,1)S(1)}, u32[]{:S(2)}) copy-start(bf16[16,2,32,256]{3,2,1,0:T(8,128)(2,1)S(1)} %collective-permute-done.4.old_far_ref) | copy-start | bytes 1572868
  40.7 2.4 %collective-permute-start.5 = (bf16[16,2,32,256]{3,2,1,0:T(8,128)(2,1)S(1)}, bf16[16,2,32,256]{3,2,1,0:T(8,128)(2,1)S(1)}, u32[]{:S(2)}, u32[]{:S(2)}) collective-permute-start(bf16[16,2,32,256]{3,2,1,0:T(8,128)(2,1)S(1)} %collective-permute-done.4.old_far_ref), channel_id=1, source_target_pairs={{0,1},{1,0},{2,3},{3,2},{4,5},{5,4},{6,7},{7,6},{8,9},{9,8},{10,11... | collective-permute-start | bytes 1572872 | tf_op jit(solution)/shard_map/ppermute | solution.py:687
  41.6 2.4 %copy-start.12 = (bf16[16,2,32,256]{3,2,1,0:T(8,128)(2,1)}, bf16[16,2,32,256]{3,2,1,0:T(8,128)(2,1)S(1)}, u32[]{:S(2)}) copy-start(bf16[16,2,32,256]{3,2,1,0:T(8,128)(2,1)S(1)} %collective-permute-done.3.old_core_ref) | copy-start | bytes 1572868
  43.1 0.8 %copy-start.13 = (bf16[16,2,32,256]{3,2,1,0:T(8,128)(2,1)}, bf16[16,2,32,256]{3,2,1,0:T(8,128)(2,1)S(1)}, u32[]{:S(2)}) copy-start(bf16[16,2,32,256]{3,2,1,0:T(8,128)(2,1)S(1)} %collective-permute-done.5.old_far_core_ref) | copy-start | bytes 1572868

commit v13 on v12

--- a/solution.py
+++ b/solution.py
@@ -214,7 +214,10 @@
 
 
 def fetch(source, first, kv_ref, place, count, sem):
-    pltpu.make_async_copy(source.at[pl.ds(first, count)], kv_ref.at[pl.ds(place, count)], sem).start()
+    for kind in range(2):
+        pltpu.make_async_copy(
+            source.at[pl.ds(first, count), kind], kv_ref.at[kind, pl.ds(place, count)], sem
+        ).start()
 
 
 def fetch_pair(sources, first, kv_ref, place, sem):
@@ -227,7 +230,7 @@
 
         @pl.when(blocks == n)
         def _(n=n):
-            filled = kv_ref.at[pl.ds(0, n * block_slots)]
+            filled = kv_ref.at[:, pl.ds(0, n * block_slots)]
             pltpu.make_async_copy(filled, filled, sem).wait()
 
 
@@ -237,7 +240,7 @@
     biased = bias_ref.shape[2]
 
     def block(kind, c):
-        return kv_ref[c * step_slots : (c + 1) * step_slots, kind].reshape(step_keys, 256)
+        return kv_ref[kind, c * step_slots : (c + 1) * step_slots].reshape(step_keys, 256)
 
     def scores(t, c, which):
         result = lax.dot_general(
@@ -296,7 +299,7 @@
         most = most_refs[which][...]
         query = roped_ref[t]
         for c in range(blocks):
-            keys = kv_ref[c * slots : (c + 1) * slots, 0].reshape(width, 256)
+            keys = kv_ref[0, c * slots : (c + 1) * slots].reshape(width, 256)
             result = lax.dot_general(
                 query, keys, (((1,), (1,)), ((), ())), preferred_element_type=jnp.float32
             )
@@ -316,7 +319,7 @@
             weights = jnp.exp(s_refs[which][c] - top)
             folded = lane_fold(weights, jnp.add)
             sums = folded if sums is None else sums + folded
-            values = kv_ref[c * slots : (c + 1) * slots, 1].reshape(width, 256)
+            values = kv_ref[1, c * slots : (c + 1) * slots].reshape(width, 256)
             part = jnp.dot(weights.astype(jnp.bfloat16), values, preferred_element_type=jnp.float32)
             total = part if total is None else total + part
         sum_ref[...] = sums
@@ -361,7 +364,7 @@
 
 def working(rows, steps, step_keys, tables):
     return [
-        pltpu.VMEM((steps * step_keys // 32, 2, 32, 256), jnp.bfloat16),
+        pltpu.VMEM((2, steps * step_keys // 32, 32, 256), jnp.bfloat16),
         pltpu.VMEM((steps, head_pair * rows, step_keys), jnp.float32),
         pltpu.VMEM((steps, head_pair * rows, step_keys), jnp.float32),
         pltpu.VMEM((head_pair * rows, 128), jnp.float32),
@@ -549,7 +552,7 @@
 
         @pl.when(odd == 1)
         def _():
-            kv_ref[empty] = jnp.zeros((block_slots, 2, 32, 256), jnp.bfloat16)
+            kv_ref[:, empty] = jnp.zeros((2, block_slots, 32, 256), jnp.bfloat16)
 
     @pl.when(has_old)
     def _():

time: 79 us -> 77.5 us (0.981)
  Pallas kernels: 52.7 us -> 51.3 us
    pallas_call x1, Pallas kernels: 32.5 us -> 31 us  [rest_part(): pl.pallas_call(rest_kernel, out_shape=pltpu.HBM((rows, width), jnp.bfloat...]
  transfers between devices with their start and end apart: 8 -> 8, of which waited for: 4 -> 4; matrix products, arithmetic and copies ran while one was open for 0% -> 0% of each run, Pallas kernels for 62% -> 61%
where the time goes in v13:
time: 77.5 us; the launch traced here: 76.5 us
  Pallas kernels  51.3 us (66%)
  starting transfers between devices  15.8 us (20%)
  waiting for transfers between devices  6.75 us (9%)
  local copies, waits for them, and re-layouts  1.66 us (2%)
  between operations  0.95 us (1%)
    pallas_call x1, Pallas kernels, rest_part(): pl.pallas_call(rest_kernel, out_shape=pltpu.HBM((rows, width), jnp.bfloat...  31 us
    pallas_call x1, Pallas kernels, diagonal_part(): pl.pallas_call(diagonal_kernel, out_shape=(pltpu.HBM((items, head_pair *...  9.06 us
    all_to_all x1, starting transfers between devices, body(): old = lax.all_to_all(picked, 'blk', split_axis=0, concat_axis=0, tiled=True)  5.79 us
    ppermute x4, starting transfers between devices, other_core(): return lax.ppermute(value, 'group', [(0, 1), (1, 0), (2, 3), (3, 2)])  4.82 us
    all_to_all x1, starting transfers between devices, body(): lax.all_to_all(new, 'blk', split_axis=0, concat_axis=0, tiled=True)  4.77 us
    ppermute x2, waiting for transfers between devices, other_chip(): return lax.ppermute(value, 'group', [(0, 2), (2, 0), (1, 3), (3, 1)])  3.49 us
    pallas_call x1, Pallas kernels, pick_old(): pl.pallas_call(pick_old_kernel, out_shape=jax.ShapeDtypeStruct((requests,...  3.02 us
    ppermute x4, waiting for transfers between devices, other_core(): return lax.ppermute(value, 'group', [(0, 1), (1, 0), (2, 3), (3, 2)])  2.83 us
  transfers between devices with their start and end apart: 8, of which 4 were waited for; matrix products, arithmetic and copies ran while one was open for 0% of the time, Pallas kernels for 61%

profile of v13, /device:TPU:7, one launch (start us, length us, event | category | flops | bytes accessed | tf_op | source)
XLA Modules:
  0.0 76.5 jit_solution(11472632356516682445)
XLA Ops:
  0.6 0.0 copy-start.9
  0.6 0.0 copy-start.8
  0.7 0.0 copy-start.6
  0.7 0.0 copy-start.5
  0.7 3.0 %pick_old.1 = bf16[8,2,2,32,256]{4,3,2,1,0:T(8,128)(2,1)} custom-call(s32[8,32]{1,0:T(8,128)} %refs_0_.2, bf16[40,32,256]{2,1,0:T(8,128)(2,1)} %key_ref.3, bf16[40,32,256]{2,1,0:T(8,128)(2,1)} %value_ref.3), custom_call_target="tpu_custom_call" | custom-call | flops 1 | bytes 1 | tf_op jit(solution)/shard_map/pick_old/pallas_call | solution.py:65
  3.7 5.8 %all-to-all-start = ((bf16[8,2,2,32,256]{4,3,2,1,0:T(8,128)(2,1)}), bf16[8,2,2,32,256]{4,3,2,1,0:T(8,128)(2,1)S(1)}, u32[]{:S(2)}, u32[]{:S(2)}) async-start(bf16[8,2,2,32,256]{4,3,2,1,0:T(8,128)(2,1)} %pick_old.1), calls=%async_computation | async-start | bytes 1048576 | tf_op jit(solution)/shard_map/all_to_all | solution.py:696
  9.5 0.0 copy-done.9
  9.5 0.0 copy-done.8
  9.5 0.0 copy-done.6
  9.5 0.0 copy-done.5
  9.5 2.5 %rotate_keys.1 = (bf16[16,2,32,256]{3,2,1,0:T(8,128)(2,1)}, f32[512,128]{1,0:T(8,128)}, f32[512,128]{1,0:T(8,128)}) custom-call(s32[8]{0:T(128)S(1)} %copy-done.8, f32[1,128]{1,0:T(1,128)S(1)} %copy-done.9, bf16[512,256]{1,0:T(8,128)(2,1)S(1)} %bitcast.5, bf16[512,256]{1,0:T(8,128)(2,1)S(1)} %bitcast.6), custom_call_target="tpu_custom_call" | custom-call | flops 1 | bytes 1 | tf_op jit(solution)/shard_map/rotate_keys/pallas_call | solution.py:121
  12.0 0.0 copy-start.7
  12.0 0.2 collective-permute-start.1
  12.2 1.5 %collective-permute-start = (bf16[16,2,32,256]{3,2,1,0:T(8,128)(2,1)}, bf16[16,2,32,256]{3,2,1,0:T(8,128)(2,1)S(1)}, u32[]{:S(2)}, u32[]{:S(2)}) collective-permute-start(bf16[16,2,32,256]{3,2,1,0:T(8,128)(2,1)} %get-tuple-element.22.own_ref.refs_1_), channel_id=1, source_target_pairs={{0,1},{1,0},{2,3},{3,2},{4,5},{5,4},{6,7},{7,6},{8,9},{9,8},{10,11... | collective-permute-start | bytes 1572872 | tf_op jit(solution)/shard_map/ppermute | solution.py:690
  13.7 0.0 copy-start.4
  13.7 9.1 %attend_diagonal.1 = (bf16[5,1024,256]{2,1,0:T(8,128)(2,1)}, f32[5,1024,256]{2,1,0:T(8,128)}, f32[5,1024,128]{2,1,0:T(8,128)}, bf16[40,32,256]{2,1,0:T(8,128)(2,1)}, bf16[40,32,256]{2,1,0:T(8,128)(2,1)}) custom-call(bf16[512,2560]{1,0:T(8,128)(2,1)} %bitcast.7, f32[512,128]{1,0:T(8,128)} %get-tuple-element.20.cos_in, f32[512,128]{1,0:T(8,128)} %get-tuple-element.21.sin_in, ...), custom_call_target="tpu_custom_call" | custom-call | flops 1 | bytes 1 | tf_op jit(solution)/shard_map/attend_diagonal/pallas_call | solution.py:469
  22.8 0.4 all-to-all-done
  23.2 0.0 copy-start.10
  23.2 0.8 %copy-done.10 = bf16[8,2,2,32,256]{4,3,2,1,0:T(8,128)(2,1)} copy-done((bf16[8,2,2,32,256]{4,3,2,1,0:T(8,128)(2,1)}, bf16[8,2,2,32,256]{4,3,2,1,0:T(8,128)(2,1)S(1)}, u32[]{:S(2)}) %copy-start.10) | copy-done | bytes 524312
  24.0 0.0 copy-done.7
  24.0 1.6 %sort_old.1.old_ref = bf16[16,2,32,256]{3,2,1,0:T(8,128)(2,1)S(1)} custom-call(s32[8,32]{1,0:T(8,128)S(1)} %copy-done.7, bf16[16,2,32,256]{3,2,1,0:T(8,128)(2,1)} %bitcast.9), custom_call_target="tpu_custom_call" | custom-call | flops 1 | bytes 1 | tf_op jit(solution)/shard_map/sort_old/pallas_call | solution.py:145
  25.7 0.0 copy-start
  25.7 0.0 collective-permute-done.1.refs_3_.far_ref
  25.7 0.0 copy-start.1
  25.7 1.5 %collective-permute-start.2 = (bf16[16,2,32,256]{3,2,1,0:T(8,128)(2,1)S(1)}, bf16[16,2,32,256]{3,2,1,0:T(8,128)(2,1)S(1)}, u32[]{:S(2)}, u32[]{:S(2)}) collective-permute-start(bf16[16,2,32,256]{3,2,1,0:T(8,128)(2,1)S(1)} %collective-permute-done.1.refs_3_.far_ref), channel_id=1, source_target_pairs={{0,1},{1,0},{2,3},{3,2},{4,5},{5,4},{6,7},{7,6},{8,9},{9,8},{10,11... | collective-permute-start | bytes 1572872 | tf_op jit(solution)/shard_map/ppermute | solution.py:690
  27.2 0.2 collective-permute-start.4
  27.4 0.0 collective-permute-done.refs_2_.core_ref
  27.4 0.0 copy-start.2
  27.5 1.3 %collective-permute-done.2.refs_4_.far_core_ref = bf16[16,2,32,256]{3,2,1,0:T(8,128)(2,1)S(1)} collective-permute-done((bf16[16,2,32,256]{3,2,1,0:T(8,128)(2,1)S(1)}, bf16[16,2,32,256]{3,2,1,0:T(8,128)(2,1)S(1)}, u32[]{:S(2)}, u32[]{:S(2)}) %collective-permute-start.2) | collective-permute-done | bytes 524320 | tf_op jit(solution)/shard_map/ppermute | solution.py:690
  28.7 0.0 copy-done.4
  28.7 0.0 copy-start.3
  28.7 2.8 %pick_new.1 = (bf16[16,2,32,256]{3,2,1,0:T(8,128)(2,1)}, s32[16]{0:T(128)S(1)}) custom-call(s32[8,32]{1,0:T(8,128)S(1)} %copy-done.7, bf16[16,2,32,256]{3,2,1,0:T(8,128)(2,1)S(1)} %copy-done.4, bf16[16,2,32,256]{3,2,1,0:T(8,128)(2,1)S(1)} %collective-permute-done.refs_2_.core_ref, bf16[16,2,32,256]{3,2,1,0:T(8,128)(2,1)S(1)} %collective-permute-done.1.refs_3_.far_ref, ...), custom_call_target="tpu_custom_call" | custom-call | flops 1 | bytes 1 | tf_op jit(solution)/shard_map/pick_new/pallas_call | solution.py:182
  31.5 4.8 %all-to-all-start.1 = ((bf16[16,2,32,256]{3,2,1,0:T(8,128)(2,1)}), bf16[16,2,32,256]{3,2,1,0:T(8,128)(2,1)S(1)}, u32[]{:S(2)}, u32[]{:S(2)}) async-start(bf16[16,2,32,256]{3,2,1,0:T(8,128)(2,1)} %get-tuple-element.28), calls=%async_computation.1 | async-start | bytes 1048576 | tf_op jit(solution)/shard_map/all_to_all | solution.py:713
  36.3 0.9 %collective-permute-start.3 = (bf16[16,2,32,256]{3,2,1,0:T(8,128)(2,1)S(1)}, bf16[16,2,32,256]{3,2,1,0:T(8,128)(2,1)S(1)}, u32[]{:S(2)}, u32[]{:S(2)}) collective-permute-start(bf16[16,2,32,256]{3,2,1,0:T(8,128)(2,1)S(1)} %sort_old.1.old_ref), channel_id=1, source_target_pairs={{0,1},{1,0},{2,3},{3,2},{4,5},{5,4},{6,7},{7,6},{8,9},{9,8},{10,11... | collective-permute-start | bytes 1572872 | tf_op jit(solution)/shard_map/ppermute | solution.py:690
  37.2 3.5 %collective-permute-done.4.old_far_ref = bf16[16,2,32,256]{3,2,1,0:T(8,128)(2,1)S(1)} collective-permute-done((bf16[16,2,32,256]{3,2,1,0:T(8,128)(2,1)S(1)}, bf16[16,2,32,256]{3,2,1,0:T(8,128)(2,1)S(1)}, u32[]{:S(2)}, u32[]{:S(2)}) %collective-permute-start.4) | collective-permute-done | bytes 524320 | tf_op jit(solution)/shard_map/ppermute | solution.py:693
  40.7 0.0 copy-start.11
  40.7 0.8 %collective-permute-start.5 = (bf16[16,2,32,256]{3,2,1,0:T(8,128)(2,1)S(1)}, bf16[16,2,32,256]{3,2,1,0:T(8,128)(2,1)S(1)}, u32[]{:S(2)}, u32[]{:S(2)}) collective-permute-start(bf16[16,2,32,256]{3,2,1,0:T(8,128)(2,1)S(1)} %collective-permute-done.4.old_far_ref), channel_id=1, source_target_pairs={{0,1},{1,0},{2,3},{3,2},{4,5},{5,4},{6,7},{7,6},{8,9},{9,8},{10,11... | collective-permute-start | bytes 1572872 | tf_op jit(solution)/shard_map/ppermute | solution.py:690
  41.6 0.0 collective-permute-done.3.old_core_ref
  41.6 0.0 copy-start.12
  41.6 1.5 %collective-permute-done.5.old_far_core_ref = bf16[16,2,32,256]{3,2,1,0:T(8,128)(2,1)S(1)} collective-permute-done((bf16[16,2,32,256]{3,2,1,0:T(8,128)(2,1)S(1)}, bf16[16,2,32,256]{3,2,1,0:T(8,128)(2,1)S(1)}, u32[]{:S(2)}, u32[]{:S(2)}) %collective-permute-start.5) | collective-permute-done | bytes 524320 | tf_op jit(solution)/shard_map/ppermute | solution.py:690
  43.1 0.0 copy-start.13
  43.1 0.8 %copy-done.13 = bf16[16,2,32,256]{3,2,1,0:T(8,128)(2,1)} copy-done((bf16[16,2,32,256]{3,2,1,0:T(8,128)(2,1)}, bf16[16,2,32,256]{3,2,1,0:T(8,128)(2,1)S(1)}, u32[]{:S(2)}) %copy-start.13) | copy-done | bytes 524312
  43.9 0.0 copy-done
  43.9 0.0 copy-done.1
  43.9 0.0 copy-done.2
  43.9 0.0 copy-done.3
  43.9 0.0 copy-done.11
  43.9 0.0 copy-done.12
  43.9 31.0 %attend_rest.1 = bf16[512,2560]{1,0:T(8,128)(2,1)} custom-call(s32[8]{0:T(128)} %lengths_ref.3, bf16[5,1024,256]{2,1,0:T(8,128)(2,1)} %get-tuple-element.23.roped_in, f32[5,1024,256]{2,1,0:T(8,128)} %get-tuple-element.24.acc_in, f32[5,1024,128]{2,1,0:T(8,128)} %get-tuple-element.25.stat_in, bf16[16,2,32,256]{3,2,1,0:T(8,128)(2,1)} %copy-done.2, ...), custom_call_target="tpu_custom_call" | custom-call | flops 1 | bytes 1 | tf_op jit(solution)/shard_map/attend_rest/pallas_call | solution.py:618
  74.9 0.0 all-to-all-done.1.arrived_ref
  74.9 1.4 %place_new.1 = (bf16[40,32,256]{2,1,0:T(8,128)(2,1)}, bf16[40,32,256]{2,1,0:T(8,128)(2,1)}) custom-call(s32[16]{0:T(128)S(1)} %get-tuple-element.30.targets_ref, bf16[16,2,32,256]{3,2,1,0:T(8,128)(2,1)S(1)} %all-to-all-done.1.arrived_ref, bf16[40,32,256]{2,1,0:T(8,128)(2,1)} %get-tuple-element.31.key_in, ...), custom_call_target="tpu_custom_call", output_to_operand_aliasing={{0}: (2, {}), {1}: (3, {})} | custom-call | flops 1 | bytes 1 | tf_op jit(solution)/shard_map/place_new/pallas_call | solution.py:659
Async XLA Ops:
  0.6 8.9 %copy-start.9 = (f32[1,128]{1,0:T(1,128)S(1)}, f32[1,128]{1,0:T(1,128)}, u32[]{:S(2)}) copy-start(f32[1,128]{1,0:T(1,128)} %constant.2.clone.freq_ref) | copy-start | bytes 1540
  0.6 8.9 %copy-start.8 = (s32[8]{0:T(128)S(1)}, s32[8]{0:T(128)}, u32[]{:S(2)}) copy-start(s32[8]{0:T(128)} %lengths_ref.3) | copy-start | bytes 100
  0.7 8.8 %copy-start.6 = (bf16[1,512,256]{2,1,0:T(8,128)(2,1)S(1)}, bf16[1,512,256]{2,1,0:T(8,128)(2,1)}, u32[]{:S(2)}) copy-start(bf16[1,512,256]{2,1,0:T(8,128)(2,1)} %param.11) | copy-start | bytes 786436
  0.7 8.8 %copy-start.5 = (bf16[1,512,256]{2,1,0:T(8,128)(2,1)S(1)}, bf16[1,512,256]{2,1,0:T(8,128)(2,1)}, u32[]{:S(2)}) copy-start(bf16[1,512,256]{2,1,0:T(8,128)(2,1)} %param.10) | copy-start | bytes 786436
  3.7 19.5 %all-to-all-start = ((bf16[8,2,2,32,256]{4,3,2,1,0:T(8,128)(2,1)}), bf16[8,2,2,32,256]{4,3,2,1,0:T(8,128)(2,1)S(1)}, u32[]{:S(2)}, u32[]{:S(2)}) async-start(bf16[8,2,2,32,256]{4,3,2,1,0:T(8,128)(2,1)} %pick_old.1), calls=%async_computation | async-start | bytes 1048576 | tf_op jit(solution)/shard_map/all_to_all | solution.py:696
  12.0 12.0 %copy-start.7 = (s32[8,32]{1,0:T(8,128)S(1)}, s32[8,32]{1,0:T(8,128)}, u32[]{:S(2)}) copy-start(s32[8,32]{1,0:T(8,128)} %refs_0_.2) | copy-start | bytes 3076
  12.0 13.7 %collective-permute-start.1 = (bf16[16,2,32,256]{3,2,1,0:T(8,128)(2,1)}, bf16[16,2,32,256]{3,2,1,0:T(8,128)(2,1)S(1)}, u32[]{:S(2)}, u32[]{:S(2)}) collective-permute-start(bf16[16,2,32,256]{3,2,1,0:T(8,128)(2,1)} %get-tuple-element.22.own_ref.refs_1_), channel_id=1, source_target_pairs={{0,2},{2,0},{1,3},{3,1},{4,6},{6,4},{5,7},{7,5},{8,10},{10,8},{9,1... | collective-permute-start | bytes 1572872 | tf_op jit(solution)/shard_map/ppermute | solution.py:693
  12.2 15.2 %collective-permute-start = (bf16[16,2,32,256]{3,2,1,0:T(8,128)(2,1)}, bf16[16,2,32,256]{3,2,1,0:T(8,128)(2,1)S(1)}, u32[]{:S(2)}, u32[]{:S(2)}) collective-permute-start(bf16[16,2,32,256]{3,2,1,0:T(8,128)(2,1)} %get-tuple-element.22.own_ref.refs_1_), channel_id=1, source_target_pairs={{0,1},{1,0},{2,3},{3,2},{4,5},{5,4},{6,7},{7,6},{8,9},{9,8},{10,11... | collective-permute-start | bytes 1572872 | tf_op jit(solution)/shard_map/ppermute | solution.py:690
  13.7 15.0 %copy-start.4 = (bf16[16,2,32,256]{3,2,1,0:T(8,128)(2,1)S(1)}, bf16[16,2,32,256]{3,2,1,0:T(8,128)(2,1)}, u32[]{:S(2)}) copy-start(bf16[16,2,32,256]{3,2,1,0:T(8,128)(2,1)} %get-tuple-element.22.own_ref.refs_1_) | copy-start | bytes 1572868
  23.2 0.8 %copy-start.10 = (bf16[8,2,2,32,256]{4,3,2,1,0:T(8,128)(2,1)}, bf16[8,2,2,32,256]{4,3,2,1,0:T(8,128)(2,1)S(1)}, u32[]{:S(2)}) copy-start(bf16[8,2,2,32,256]{4,3,2,1,0:T(8,128)(2,1)S(1)} %all-to-all-done) | copy-start | bytes 1572868
  25.7 18.3 %copy-start = (bf16[16,2,32,256]{3,2,1,0:T(8,128)(2,1)}, bf16[16,2,32,256]{3,2,1,0:T(8,128)(2,1)S(1)}, u32[]{:S(2)}) copy-start(bf16[16,2,32,256]{3,2,1,0:T(8,128)(2,1)S(1)} %sort_old.1.old_ref) | copy-start | bytes 1572868
  25.7 18.2 %copy-start.1 = (bf16[16,2,32,256]{3,2,1,0:T(8,128)(2,1)}, bf16[16,2,32,256]{3,2,1,0:T(8,128)(2,1)S(1)}, u32[]{:S(2)}) copy-start(bf16[16,2,32,256]{3,2,1,0:T(8,128)(2,1)S(1)} %collective-permute-done.1.refs_3_.far_ref) | copy-start | bytes 1572868
  25.7 3.1 %collective-permute-start.2 = (bf16[16,2,32,256]{3,2,1,0:T(8,128)(2,1)S(1)}, bf16[16,2,32,256]{3,2,1,0:T(8,128)(2,1)S(1)}, u32[]{:S(2)}, u32[]{:S(2)}) collective-permute-start(bf16[16,2,32,256]{3,2,1,0:T(8,128)(2,1)S(1)} %collective-permute-done.1.refs_3_.far_ref), channel_id=1, source_target_pairs={{0,1},{1,0},{2,3},{3,2},{4,5},{5,4},{6,7},{7,6},{8,9},{9,8},{10,11... | collective-permute-start | bytes 1572872 | tf_op jit(solution)/shard_map/ppermute | solution.py:690
  27.2 13.5 %collective-permute-start.4 = (bf16[16,2,32,256]{3,2,1,0:T(8,128)(2,1)S(1)}, bf16[16,2,32,256]{3,2,1,0:T(8,128)(2,1)S(1)}, u32[]{:S(2)}, u32[]{:S(2)}) collective-permute-start(bf16[16,2,32,256]{3,2,1,0:T(8,128)(2,1)S(1)} %sort_old.1.old_ref), channel_id=1, source_target_pairs={{0,2},{2,0},{1,3},{3,1},{4,6},{6,4},{5,7},{7,5},{8,10},{10,8},{9,1... | collective-permute-start | bytes 1572872 | tf_op jit(solution)/shard_map/ppermute | solution.py:693
  27.4 16.5 %copy-start.2 = (bf16[16,2,32,256]{3,2,1,0:T(8,128)(2,1)}, bf16[16,2,32,256]{3,2,1,0:T(8,128)(2,1)S(1)}, u32[]{:S(2)}) copy-start(bf16[16,2,32,256]{3,2,1,0:T(8,128)(2,1)S(1)} %collective-permute-done.refs_2_.core_ref) | copy-start | bytes 1572868
  28.7 15.2 %copy-start.3 = (bf16[16,2,32,256]{3,2,1,0:T(8,128)(2,1)}, bf16[16,2,32,256]{3,2,1,0:T(8,128)(2,1)S(1)}, u32[]{:S(2)}) copy-start(bf16[16,2,32,256]{3,2,1,0:T(8,128)(2,1)S(1)} %collective-permute-done.2.refs_4_.far_core_ref) | copy-start | bytes 1572868
  31.5 43.4 %all-to-all-start.1 = ((bf16[16,2,32,256]{3,2,1,0:T(8,128)(2,1)}), bf16[16,2,32,256]{3,2,1,0:T(8,128)(2,1)S(1)}, u32[]{:S(2)}, u32[]{:S(2)}) async-start(bf16[16,2,32,256]{3,2,1,0:T(8,128)(2,1)} %get-tuple-element.28), calls=%async_computation.1 | async-start | bytes 1048576 | tf_op jit(solution)/shard_map/all_to_all | solution.py:713
  36.3 5.3 %collective-permute-start.3 = (bf16[16,2,32,256]{3,2,1,0:T(8,128)(2,1)S(1)}, bf16[16,2,32,256]{3,2,1,0:T(8,128)(2,1)S(1)}, u32[]{:S(2)}, u32[]{:S(2)}) collective-permute-start(bf16[16,2,32,256]{3,2,1,0:T(8,128)(2,1)S(1)} %sort_old.1.old_ref), channel_id=1, source_target_pairs={{0,1},{1,0},{2,3},{3,2},{4,5},{5,4},{6,7},{7,6},{8,9},{9,8},{10,11... | collective-permute-start | bytes 1572872 | tf_op jit(solution)/shard_map/ppermute | solution.py:690
  40.7 3.2 %copy-start.11 = (bf16[16,2,32,256]{3,2,1,0:T(8,128)(2,1)}, bf16[16,2,32,256]{3,2,1,0:T(8,128)(2,1)S(1)}, u32[]{:S(2)}) copy-start(bf16[16,2,32,256]{3,2,1,0:T(8,128)(2,1)S(1)} %collective-permute-done.4.old_far_ref) | copy-start | bytes 1572868
  40.7 2.4 %collective-permute-start.5 = (bf16[16,2,32,256]{3,2,1,0:T(8,128)(2,1)S(1)}, bf16[16,2,32,256]{3,2,1,0:T(8,128)(2,1)S(1)}, u32[]{:S(2)}, u32[]{:S(2)}) collective-permute-start(bf16[16,2,32,256]{3,2,1,0:T(8,128)(2,1)S(1)} %collective-permute-done.4.old_far_ref), channel_id=1, source_target_pairs={{0,1},{1,0},{2,3},{3,2},{4,5},{5,4},{6,7},{7,6},{8,9},{9,8},{10,11... | collective-permute-start | bytes 1572872 | tf_op jit(solution)/shard_map/ppermute | solution.py:690
  41.6 2.4 %copy-start.12 = (bf16[16,2,32,256]{3,2,1,0:T(8,128)(2,1)}, bf16[16,2,32,256]{3,2,1,0:T(8,128)(2,1)S(1)}, u32[]{:S(2)}) copy-start(bf16[16,2,32,256]{3,2,1,0:T(8,128)(2,1)S(1)} %collective-permute-done.3.old_core_ref) | copy-start | bytes 1572868
  43.1 0.8 %copy-start.13 = (bf16[16,2,32,256]{3,2,1,0:T(8,128)(2,1)}, bf16[16,2,32,256]{3,2,1,0:T(8,128)(2,1)S(1)}, u32[]{:S(2)}) copy-start(bf16[16,2,32,256]{3,2,1,0:T(8,128)(2,1)S(1)} %collective-permute-done.5.old_far_core_ref) | copy-start | bytes 1572868

commit v14 on v13

--- a/solution.py
+++ b/solution.py
@@ -234,19 +234,19 @@
             pltpu.make_async_copy(filled, filled, sem).wait()
 
 
-def attention(steps, most_steps, step_keys, roped_ref, kv_ref, bias_ref, s_refs, most_refs, top_ref, sum_ref, sum_of_values, begin, finish):
+def attention(steps, step_keys, roped_ref, kv_ref, bias_ref, s_refs, most_refs, top_ref, sum_ref, sum_of_values, begin, finish):
     items, rows, _ = roped_ref.shape
     step_slots = step_keys // 32
     biased = bias_ref.shape[2]
 
     def block(kind, c):
-        return kv_ref[kind, c * step_slots : (c + 1) * step_slots].reshape(step_keys, 256)
-
-    def scores(t, c, which):
+        return kv_ref[kind, pl.ds(c * step_slots, step_slots)].reshape(step_keys, 256)
+
+    def scores(t, c, which, masked):
         result = lax.dot_general(
             roped_ref[t], block(0, c), (((1,), (1,)), ((), ())), preferred_element_type=jnp.float32
         )
-        if c == 0:
+        if masked:
             head = result[:, :biased].reshape(head_pair, rows // head_pair, biased) + bias_ref[0]
             head = head.reshape(rows, biased)
             result = join([head, result[:, biased:]]) if step_keys > biased else head
@@ -268,24 +268,28 @@
         sum_of_values[...] = jnp.zeros_like(sum_of_values)
 
     def loop(work):
-        for c in range(most_steps):
-
-            @pl.when(steps > c)
-            def _(c=c):
-                work(c)
+        def step(c, carry):
+            work(c, False)
+            return carry
+
+        @pl.when(steps > 0)
+        def _():
+            work(0, True)
+
+        lax.fori_loop(1, steps, step, 0)
 
     def both(t, which):
-        def work(c):
+        def work(c, masked):
             weigh(c, which)
-            scores(t + 1, c, 1 - which)
+            scores(t + 1, c, 1 - which, masked)
 
         loop(work)
 
     drive(
         items, most_refs, begin, settle, finish,
-        lambda: loop(lambda c: scores(0, c, 0)),
+        lambda: loop(lambda c, masked: scores(0, c, 0, masked)),
         both,
-        lambda which: loop(lambda c: weigh(c, which)),
+        lambda which: loop(lambda c, masked: weigh(c, which)),
     )
 
 
@@ -579,7 +583,7 @@
 
     scratch = (roped_ref, kv_ref, bias_ref, (s_0, s_1), (most_0, most_1), top_ref, sum_ref, values_ref)
 
-    attention(steps, 2, 2 * block_keys, *scratch, begin, finish)
+    attention(steps, 2 * block_keys, *scratch, begin, finish)
     weight_copy.wait()
 
     def out_copy(n, columns):
@@ -706,7 +710,8 @@
     old = sort_old(after(page_table, stat), blk_count, cap, pages, old)
     old_far = other_chip(old)
     old_core = other_core(old)
-    fresh_far_core = other_core(after(fresh_far, old))
+    fresh_far = after(fresh_far, old)
+    fresh_far_core = other_core(fresh_far)
     new, targets = pick_new(
         page_table, blk_count, cap, pages, (fresh, fresh_core, fresh_far, fresh_far_core)
     )

time: 77.5 us -> 78.1 us (level)
  the two profiles are of different devices: /device:TPU:7 before, /device:TPU:0 now
where the time goes in v14:
time: 78.1 us; the launch traced here: 77.6 us
  Pallas kernels  51.2 us (66%)
  starting transfers between devices  15.3 us (20%)
  waiting for transfers between devices  8.47 us (11%)
  local copies, waits for them, and re-layouts  1.67 us (2%)
  between operations  0.97 us (1%)
    pallas_call x1, Pallas kernels, rest_part(): pl.pallas_call(rest_kernel, out_shape=pltpu.HBM((rows, width), jnp.bfloat...  30.9 us
    pallas_call x1, Pallas kernels, diagonal_part(): pl.pallas_call(diagonal_kernel, out_shape=(pltpu.HBM((items, head_pair *...  9.05 us
    all_to_all x1, starting transfers between devices, body(): old = lax.all_to_all(picked, 'blk', split_axis=0, concat_axis=0, tiled=True)  7.26 us
    ppermute x2, waiting for transfers between devices, other_chip(): return lax.ppermute(value, 'group', [(0, 2), (2, 0), (1, 3), (3, 1)])  4.85 us
    all_to_all x1, starting transfers between devices, body(): lax.all_to_all(new, 'blk', split_axis=0, concat_axis=0, tiled=True)  4.77 us
    ppermute x2, starting transfers between devices, other_chip(): return lax.ppermute(value, 'group', [(0, 2), (2, 0), (1, 3), (3, 1)])  3.1 us
    pallas_call x1, Pallas kernels, pick_old(): pl.pallas_call(pick_old_kernel, out_shape=jax.ShapeDtypeStruct((requests,...  3.02 us
    pallas_call x1, Pallas kernels, pick_new(): pl.pallas_call(lambda *refs: pick_new_kernel(pages, cap, *refs), out_shap...  2.76 us
  transfers between devices with their start and end apart: 8, of which 4 were waited for; matrix products, arithmetic and copies ran while one was open for 0% of the time, Pallas kernels for 60%

profile of v14, /device:TPU:0, one launch (start us, length us, event | category | flops | bytes accessed | tf_op | source)
XLA Modules:
  0.0 77.6 jit_solution(16585990158323630280)
XLA Ops:
  0.6 0.0 copy-start.9
  0.6 0.0 copy-start.8
  0.7 0.0 copy-start.6
  0.7 0.0 copy-start.5
  0.7 3.0 %pick_old.1 = bf16[8,2,2,32,256]{4,3,2,1,0:T(8,128)(2,1)} custom-call(s32[8,32]{1,0:T(8,128)} %refs_0_.2, bf16[40,32,256]{2,1,0:T(8,128)(2,1)} %key_ref.3, bf16[40,32,256]{2,1,0:T(8,128)(2,1)} %value_ref.3), custom_call_target="tpu_custom_call" | custom-call | flops 1 | bytes 1 | tf_op jit(solution)/shard_map/pick_old/pallas_call | solution.py:65
  3.7 7.3 %all-to-all-start = ((bf16[8,2,2,32,256]{4,3,2,1,0:T(8,128)(2,1)}), bf16[8,2,2,32,256]{4,3,2,1,0:T(8,128)(2,1)S(1)}, u32[]{:S(2)}, u32[]{:S(2)}) async-start(bf16[8,2,2,32,256]{4,3,2,1,0:T(8,128)(2,1)} %pick_old.1), calls=%async_computation | async-start | bytes 1048576 | tf_op jit(solution)/shard_map/all_to_all | solution.py:700
  11.0 0.0 copy-done.9
  11.0 0.0 copy-done.8
  11.0 0.0 copy-done.6
  11.0 0.0 copy-done.5
  11.0 2.5 %rotate_keys.1 = (bf16[16,2,32,256]{3,2,1,0:T(8,128)(2,1)}, f32[512,128]{1,0:T(8,128)}, f32[512,128]{1,0:T(8,128)}) custom-call(s32[8]{0:T(128)S(1)} %copy-done.8, f32[1,128]{1,0:T(1,128)S(1)} %copy-done.9, bf16[512,256]{1,0:T(8,128)(2,1)S(1)} %bitcast.5, bf16[512,256]{1,0:T(8,128)(2,1)S(1)} %bitcast.6), custom_call_target="tpu_custom_call" | custom-call | flops 1 | bytes 1 | tf_op jit(solution)/shard_map/rotate_keys/pallas_call | solution.py:121
  13.5 0.0 copy-start.7
  13.5 1.5 %collective-permute-start.1 = (bf16[16,2,32,256]{3,2,1,0:T(8,128)(2,1)}, bf16[16,2,32,256]{3,2,1,0:T(8,128)(2,1)S(1)}, u32[]{:S(2)}, u32[]{:S(2)}) collective-permute-start(bf16[16,2,32,256]{3,2,1,0:T(8,128)(2,1)} %get-tuple-element.22.own_ref.refs_1_), channel_id=1, source_target_pairs={{0,2},{2,0},{1,3},{3,1},{4,6},{6,4},{5,7},{7,5},{8,10},{10,8},{9,1... | collective-permute-start | bytes 1572872 | tf_op jit(solution)/shard_map/ppermute | solution.py:697
  15.0 0.0 collective-permute-start
  15.0 0.0 copy-start.4
  15.0 9.1 %attend_diagonal.1 = (bf16[5,1024,256]{2,1,0:T(8,128)(2,1)}, f32[5,1024,256]{2,1,0:T(8,128)}, f32[5,1024,128]{2,1,0:T(8,128)}, bf16[40,32,256]{2,1,0:T(8,128)(2,1)}, bf16[40,32,256]{2,1,0:T(8,128)(2,1)}) custom-call(bf16[512,2560]{1,0:T(8,128)(2,1)} %bitcast.7, f32[512,128]{1,0:T(8,128)} %get-tuple-element.20.cos_in, f32[512,128]{1,0:T(8,128)} %get-tuple-element.21.sin_in, ...), custom_call_target="tpu_custom_call" | custom-call | flops 1 | bytes 1 | tf_op jit(solution)/shard_map/attend_diagonal/pallas_call | solution.py:473
  24.0 1.4 %all-to-all-done = bf16[8,2,2,32,256]{4,3,2,1,0:T(8,128)(2,1)S(1)} async-done(((bf16[8,2,2,32,256]{4,3,2,1,0:T(8,128)(2,1)}), bf16[8,2,2,32,256]{4,3,2,1,0:T(8,128)(2,1)S(1)}, u32[]{:S(2)}, u32[]{:S(2)}) %all-to-all-start) | async-done | bytes 524320 | tf_op jit(solution)/shard_map/all_to_all | solution.py:700
  25.5 0.0 copy-start.10
  25.5 0.8 %copy-done.10 = bf16[8,2,2,32,256]{4,3,2,1,0:T(8,128)(2,1)} copy-done((bf16[8,2,2,32,256]{4,3,2,1,0:T(8,128)(2,1)}, bf16[8,2,2,32,256]{4,3,2,1,0:T(8,128)(2,1)S(1)}, u32[]{:S(2)}) %copy-start.10) | copy-done | bytes 524312
  26.3 0.0 copy-done.7
  26.3 1.6 %sort_old.1.old_ref = bf16[16,2,32,256]{3,2,1,0:T(8,128)(2,1)S(1)} custom-call(s32[8,32]{1,0:T(8,128)S(1)} %copy-done.7, bf16[16,2,32,256]{3,2,1,0:T(8,128)(2,1)} %bitcast.9), custom_call_target="tpu_custom_call" | custom-call | flops 1 | bytes 1 | tf_op jit(solution)/shard_map/sort_old/pallas_call | solution.py:145
  27.9 0.0 copy-start
  27.9 0.0 collective-permute-done.1.refs_3_.far_ref
  27.9 0.0 copy-start.1
  27.9 0.1 collective-permute-start.2
  28.0 1.6 %collective-permute-start.4 = (bf16[16,2,32,256]{3,2,1,0:T(8,128)(2,1)S(1)}, bf16[16,2,32,256]{3,2,1,0:T(8,128)(2,1)S(1)}, u32[]{:S(2)}, u32[]{:S(2)}) collective-permute-start(bf16[16,2,32,256]{3,2,1,0:T(8,128)(2,1)S(1)} %sort_old.1.old_ref), channel_id=1, source_target_pairs={{0,2},{2,0},{1,3},{3,1},{4,6},{6,4},{5,7},{7,5},{8,10},{10,8},{9,1... | collective-permute-start | bytes 1572872 | tf_op jit(solution)/shard_map/ppermute | solution.py:697
  29.6 0.0 collective-permute-done.refs_2_.core_ref
  29.6 0.0 copy-start.2
  29.6 0.3 collective-permute-done.2.refs_4_.far_core_ref
  29.9 0.0 copy-done.4
  29.9 0.0 copy-start.3
  29.9 2.8 %pick_new.1 = (bf16[16,2,32,256]{3,2,1,0:T(8,128)(2,1)}, s32[16]{0:T(128)S(1)}) custom-call(s32[8,32]{1,0:T(8,128)S(1)} %copy-done.7, bf16[16,2,32,256]{3,2,1,0:T(8,128)(2,1)S(1)} %copy-done.4, bf16[16,2,32,256]{3,2,1,0:T(8,128)(2,1)S(1)} %collective-permute-done.refs_2_.core_ref, bf16[16,2,32,256]{3,2,1,0:T(8,128)(2,1)S(1)} %collective-permute-done.1.refs_3_.far_ref, ...), custom_call_target="tpu_custom_call" | custom-call | flops 1 | bytes 1 | tf_op jit(solution)/shard_map/pick_new/pallas_call | solution.py:182
  32.7 4.8 %all-to-all-start.1 = ((bf16[16,2,32,256]{3,2,1,0:T(8,128)(2,1)}), bf16[16,2,32,256]{3,2,1,0:T(8,128)(2,1)S(1)}, u32[]{:S(2)}, u32[]{:S(2)}) async-start(bf16[16,2,32,256]{3,2,1,0:T(8,128)(2,1)} %get-tuple-element.28), calls=%async_computation.1 | async-start | bytes 1048576 | tf_op jit(solution)/shard_map/all_to_all | solution.py:718
  37.5 0.1 collective-permute-start.3
  37.5 4.8 %collective-permute-done.4.old_far_ref = bf16[16,2,32,256]{3,2,1,0:T(8,128)(2,1)S(1)} collective-permute-done((bf16[16,2,32,256]{3,2,1,0:T(8,128)(2,1)S(1)}, bf16[16,2,32,256]{3,2,1,0:T(8,128)(2,1)S(1)}, u32[]{:S(2)}, u32[]{:S(2)}) %collective-permute-start.4) | collective-permute-done | bytes 524320 | tf_op jit(solution)/shard_map/ppermute | solution.py:697
  42.4 0.0 copy-start.11
  42.4 0.0 collective-permute-start.5
  42.4 0.0 collective-permute-done.3.old_core_ref
  42.4 0.0 copy-start.12
  42.4 1.9 %collective-permute-done.5.old_far_core_ref = bf16[16,2,32,256]{3,2,1,0:T(8,128)(2,1)S(1)} collective-permute-done((bf16[16,2,32,256]{3,2,1,0:T(8,128)(2,1)S(1)}, bf16[16,2,32,256]{3,2,1,0:T(8,128)(2,1)S(1)}, u32[]{:S(2)}, u32[]{:S(2)}) %collective-permute-start.5) | collective-permute-done | bytes 524320 | tf_op jit(solution)/shard_map/ppermute | solution.py:694
  44.3 0.0 copy-start.13
  44.3 0.8 %copy-done.13 = bf16[16,2,32,256]{3,2,1,0:T(8,128)(2,1)} copy-done((bf16[16,2,32,256]{3,2,1,0:T(8,128)(2,1)}, bf16[16,2,32,256]{3,2,1,0:T(8,128)(2,1)S(1)}, u32[]{:S(2)}) %copy-start.13) | copy-done | bytes 524312
  45.1 0.0 copy-done
  45.1 0.0 copy-done.1
  45.1 0.0 copy-done.2
  45.1 0.0 copy-done.3
  45.1 0.0 copy-done.11
  45.1 0.0 copy-done.12
  45.1 30.9 %attend_rest.1 = bf16[512,2560]{1,0:T(8,128)(2,1)} custom-call(s32[8]{0:T(128)} %lengths_ref.3, bf16[5,1024,256]{2,1,0:T(8,128)(2,1)} %get-tuple-element.23.roped_in, f32[5,1024,256]{2,1,0:T(8,128)} %get-tuple-element.24.acc_in, f32[5,1024,128]{2,1,0:T(8,128)} %get-tuple-element.25.stat_in, bf16[16,2,32,256]{3,2,1,0:T(8,128)(2,1)} %copy-done.2, ...), custom_call_target="tpu_custom_call" | custom-call | flops 1 | bytes 1 | tf_op jit(solution)/shard_map/attend_rest/pallas_call | solution.py:622
  76.1 0.0 all-to-all-done.1.arrived_ref
  76.1 1.4 %place_new.1 = (bf16[40,32,256]{2,1,0:T(8,128)(2,1)}, bf16[40,32,256]{2,1,0:T(8,128)(2,1)}) custom-call(s32[16]{0:T(128)S(1)} %get-tuple-element.30.targets_ref, bf16[16,2,32,256]{3,2,1,0:T(8,128)(2,1)S(1)} %all-to-all-done.1.arrived_ref, bf16[40,32,256]{2,1,0:T(8,128)(2,1)} %get-tuple-element.31.key_in, ...), custom_call_target="tpu_custom_call", output_to_operand_aliasing={{0}: (2, {}), {1}: (3, {})} | custom-call | flops 1 | bytes 1 | tf_op jit(solution)/shard_map/place_new/pallas_call | solution.py:663
Async XLA Ops:
  0.6 10.3 %copy-start.9 = (f32[1,128]{1,0:T(1,128)S(1)}, f32[1,128]{1,0:T(1,128)}, u32[]{:S(2)}) copy-start(f32[1,128]{1,0:T(1,128)} %constant.2.clone.freq_ref) | copy-start | bytes 1540
  0.6 10.3 %copy-start.8 = (s32[8]{0:T(128)S(1)}, s32[8]{0:T(128)}, u32[]{:S(2)}) copy-start(s32[8]{0:T(128)} %lengths_ref.3) | copy-start | bytes 100
  0.7 10.3 %copy-start.6 = (bf16[1,512,256]{2,1,0:T(8,128)(2,1)S(1)}, bf16[1,512,256]{2,1,0:T(8,128)(2,1)}, u32[]{:S(2)}) copy-start(bf16[1,512,256]{2,1,0:T(8,128)(2,1)} %param.11) | copy-start | bytes 786436
  0.7 10.3 %copy-start.5 = (bf16[1,512,256]{2,1,0:T(8,128)(2,1)S(1)}, bf16[1,512,256]{2,1,0:T(8,128)(2,1)}, u32[]{:S(2)}) copy-start(bf16[1,512,256]{2,1,0:T(8,128)(2,1)} %param.10) | copy-start | bytes 786436
  3.7 21.8 %all-to-all-start = ((bf16[8,2,2,32,256]{4,3,2,1,0:T(8,128)(2,1)}), bf16[8,2,2,32,256]{4,3,2,1,0:T(8,128)(2,1)S(1)}, u32[]{:S(2)}, u32[]{:S(2)}) async-start(bf16[8,2,2,32,256]{4,3,2,1,0:T(8,128)(2,1)} %pick_old.1), calls=%async_computation | async-start | bytes 1048576 | tf_op jit(solution)/shard_map/all_to_all | solution.py:700
  13.5 12.8 %copy-start.7 = (s32[8,32]{1,0:T(8,128)S(1)}, s32[8,32]{1,0:T(8,128)}, u32[]{:S(2)}) copy-start(s32[8,32]{1,0:T(8,128)} %refs_0_.2) | copy-start | bytes 3076
  13.5 14.5 %collective-permute-start.1 = (bf16[16,2,32,256]{3,2,1,0:T(8,128)(2,1)}, bf16[16,2,32,256]{3,2,1,0:T(8,128)(2,1)S(1)}, u32[]{:S(2)}, u32[]{:S(2)}) collective-permute-start(bf16[16,2,32,256]{3,2,1,0:T(8,128)(2,1)} %get-tuple-element.22.own_ref.refs_1_), channel_id=1, source_target_pairs={{0,2},{2,0},{1,3},{3,1},{4,6},{6,4},{5,7},{7,5},{8,10},{10,8},{9,1... | collective-permute-start | bytes 1572872 | tf_op jit(solution)/shard_map/ppermute | solution.py:697
  15.0 14.6 %collective-permute-start = (bf16[16,2,32,256]{3,2,1,0:T(8,128)(2,1)}, bf16[16,2,32,256]{3,2,1,0:T(8,128)(2,1)S(1)}, u32[]{:S(2)}, u32[]{:S(2)}) collective-permute-start(bf16[16,2,32,256]{3,2,1,0:T(8,128)(2,1)} %get-tuple-element.22.own_ref.refs_1_), channel_id=1, source_target_pairs={{0,1},{1,0},{2,3},{3,2},{4,5},{5,4},{6,7},{7,6},{8,9},{9,8},{10,11... | collective-permute-start | bytes 1572872 | tf_op jit(solution)/shard_map/ppermute | solution.py:694
  15.0 14.9 %copy-start.4 = (bf16[16,2,32,256]{3,2,1,0:T(8,128)(2,1)S(1)}, bf16[16,2,32,256]{3,2,1,0:T(8,128)(2,1)}, u32[]{:S(2)}) copy-start(bf16[16,2,32,256]{3,2,1,0:T(8,128)(2,1)} %get-tuple-element.22.own_ref.refs_1_) | copy-start | bytes 1572868
  25.5 0.8 %copy-start.10 = (bf16[8,2,2,32,256]{4,3,2,1,0:T(8,128)(2,1)}, bf16[8,2,2,32,256]{4,3,2,1,0:T(8,128)(2,1)S(1)}, u32[]{:S(2)}) copy-start(bf16[8,2,2,32,256]{4,3,2,1,0:T(8,128)(2,1)S(1)} %all-to-all-done) | copy-start | bytes 1572868
  27.9 17.2 %copy-start = (bf16[16,2,32,256]{3,2,1,0:T(8,128)(2,1)}, bf16[16,2,32,256]{3,2,1,0:T(8,128)(2,1)S(1)}, u32[]{:S(2)}) copy-start(bf16[16,2,32,256]{3,2,1,0:T(8,128)(2,1)S(1)} %sort_old.1.old_ref) | copy-start | bytes 1572868
  27.9 17.2 %copy-start.1 = (bf16[16,2,32,256]{3,2,1,0:T(8,128)(2,1)}, bf16[16,2,32,256]{3,2,1,0:T(8,128)(2,1)S(1)}, u32[]{:S(2)}) copy-start(bf16[16,2,32,256]{3,2,1,0:T(8,128)(2,1)S(1)} %collective-permute-done.1.refs_3_.far_ref) | copy-start | bytes 1572868
  27.9 2.0 %collective-permute-start.2 = (bf16[16,2,32,256]{3,2,1,0:T(8,128)(2,1)S(1)}, bf16[16,2,32,256]{3,2,1,0:T(8,128)(2,1)S(1)}, u32[]{:S(2)}, u32[]{:S(2)}) collective-permute-start(bf16[16,2,32,256]{3,2,1,0:T(8,128)(2,1)S(1)} %collective-permute-done.1.refs_3_.far_ref), channel_id=1, source_target_pairs={{0,1},{1,0},{2,3},{3,2},{4,5},{5,4},{6,7},{7,6},{8,9},{9,8},{10,11... | collective-permute-start | bytes 1572872 | tf_op jit(solution)/shard_map/ppermute | solution.py:694
  28.0 14.3 %collective-permute-start.4 = (bf16[16,2,32,256]{3,2,1,0:T(8,128)(2,1)S(1)}, bf16[16,2,32,256]{3,2,1,0:T(8,128)(2,1)S(1)}, u32[]{:S(2)}, u32[]{:S(2)}) collective-permute-start(bf16[16,2,32,256]{3,2,1,0:T(8,128)(2,1)S(1)} %sort_old.1.old_ref), channel_id=1, source_target_pairs={{0,2},{2,0},{1,3},{3,1},{4,6},{6,4},{5,7},{7,5},{8,10},{10,8},{9,1... | collective-permute-start | bytes 1572872 | tf_op jit(solution)/shard_map/ppermute | solution.py:697
  29.6 15.5 %copy-start.2 = (bf16[16,2,32,256]{3,2,1,0:T(8,128)(2,1)}, bf16[16,2,32,256]{3,2,1,0:T(8,128)(2,1)S(1)}, u32[]{:S(2)}) copy-start(bf16[16,2,32,256]{3,2,1,0:T(8,128)(2,1)S(1)} %collective-permute-done.refs_2_.core_ref) | copy-start | bytes 1572868
  29.9 15.2 %copy-start.3 = (bf16[16,2,32,256]{3,2,1,0:T(8,128)(2,1)}, bf16[16,2,32,256]{3,2,1,0:T(8,128)(2,1)S(1)}, u32[]{:S(2)}) copy-start(bf16[16,2,32,256]{3,2,1,0:T(8,128)(2,1)S(1)} %collective-permute-done.2.refs_4_.far_core_ref) | copy-start | bytes 1572868
  32.7 43.4 %all-to-all-start.1 = ((bf16[16,2,32,256]{3,2,1,0:T(8,128)(2,1)}), bf16[16,2,32,256]{3,2,1,0:T(8,128)(2,1)S(1)}, u32[]{:S(2)}, u32[]{:S(2)}) async-start(bf16[16,2,32,256]{3,2,1,0:T(8,128)(2,1)} %get-tuple-element.28), calls=%async_computation.1 | async-start | bytes 1048576 | tf_op jit(solution)/shard_map/all_to_all | solution.py:718
  37.5 4.9 %collective-permute-start.3 = (bf16[16,2,32,256]{3,2,1,0:T(8,128)(2,1)S(1)}, bf16[16,2,32,256]{3,2,1,0:T(8,128)(2,1)S(1)}, u32[]{:S(2)}, u32[]{:S(2)}) collective-permute-start(bf16[16,2,32,256]{3,2,1,0:T(8,128)(2,1)S(1)} %sort_old.1.old_ref), channel_id=1, source_target_pairs={{0,1},{1,0},{2,3},{3,2},{4,5},{5,4},{6,7},{7,6},{8,9},{9,8},{10,11... | collective-permute-start | bytes 1572872 | tf_op jit(solution)/shard_map/ppermute | solution.py:694
  42.4 2.7 %copy-start.11 = (bf16[16,2,32,256]{3,2,1,0:T(8,128)(2,1)}, bf16[16,2,32,256]{3,2,1,0:T(8,128)(2,1)S(1)}, u32[]{:S(2)}) copy-start(bf16[16,2,32,256]{3,2,1,0:T(8,128)(2,1)S(1)} %collective-permute-done.4.old_far_ref) | copy-start | bytes 1572868
  42.4 1.9 %collective-permute-start.5 = (bf16[16,2,32,256]{3,2,1,0:T(8,128)(2,1)S(1)}, bf16[16,2,32,256]{3,2,1,0:T(8,128)(2,1)S(1)}, u32[]{:S(2)}, u32[]{:S(2)}) collective-permute-start(bf16[16,2,32,256]{3,2,1,0:T(8,128)(2,1)S(1)} %collective-permute-done.4.old_far_ref), channel_id=1, source_target_pairs={{0,1},{1,0},{2,3},{3,2},{4,5},{5,4},{6,7},{7,6},{8,9},{9,8},{10,11... | collective-permute-start | bytes 1572872 | tf_op jit(solution)/shard_map/ppermute | solution.py:694
  42.4 2.7 %copy-start.12 = (bf16[16,2,32,256]{3,2,1,0:T(8,128)(2,1)}, bf16[16,2,32,256]{3,2,1,0:T(8,128)(2,1)S(1)}, u32[]{:S(2)}) copy-start(bf16[16,2,32,256]{3,2,1,0:T(8,128)(2,1)S(1)} %collective-permute-done.3.old_core_ref) | copy-start | bytes 1572868
  44.3 0.8 %copy-start.13 = (bf16[16,2,32,256]{3,2,1,0:T(8,128)(2,1)}, bf16[16,2,32,256]{3,2,1,0:T(8,128)(2,1)S(1)}, u32[]{:S(2)}) copy-start(bf16[16,2,32,256]{3,2,1,0:T(8,128)(2,1)S(1)} %collective-permute-done.5.old_far_core_ref) | copy-start | bytes 1572868

commit v15 on v13

--- a/solution.py
+++ b/solution.py
@@ -50,13 +50,20 @@
     return chosen, found
 
 
-def pick_old_kernel(table_ref, key_ref, value_ref, out_ref, sem):
+def pick_old_kernel(table_ref, key_ref, value_ref, out_ref, found_ref, sem):
     requests, cap = out_ref.shape[:2]
+    pages = key_ref.shape[0]
+    low = lax.axis_index("blk") * pages
     for r in range(requests):
-        chosen, _ = pages_here(table_ref, r, 0, table_ref.shape[1] // 2, cap, key_ref.shape[0])
+        count = jnp.int32(0)
+        for j in range(table_ref.shape[1] // 2):
+            page = table_ref[r, j] - low
+            found_ref[jnp.minimum(count, cap)] = page
+            count = count + ((page >= 0) & (page < pages)).astype(jnp.int32)
         for c in range(cap):
-            pltpu.make_async_copy(key_ref.at[chosen[c]], out_ref.at[r, c, 0], sem).start()
-            pltpu.make_async_copy(value_ref.at[chosen[c]], out_ref.at[r, c, 1], sem).start()
+            page = jnp.where(count > c, found_ref[c], 0)
+            pltpu.make_async_copy(key_ref.at[page], out_ref.at[r, c, 0], sem).start()
+            pltpu.make_async_copy(value_ref.at[page], out_ref.at[r, c, 1], sem).start()
     pltpu.make_async_copy(out_ref, out_ref, sem).wait()
 
 
@@ -67,7 +74,7 @@
         out_shape=jax.ShapeDtypeStruct((requests, cap, 2) + key_cache.shape[1:], jnp.bfloat16),
         in_specs=[smem_spec, hbm_spec, hbm_spec],
         out_specs=vmem_spec,
-        scratch_shapes=[pltpu.SemaphoreType.DMA],
+        scratch_shapes=[pltpu.SMEM((cap + 1,), jnp.int32), pltpu.SemaphoreType.DMA],
         cost_estimate=light,
         compiler_params=params(small_limit),
         name="pick_old",
@@ -494,7 +501,7 @@
     lengths_ref, roped_in, acc_in, stat_in, core_ref, far_ref, far_core_ref,
     old_ref, old_core_ref, old_far_ref, old_far_core_ref, weight_ref, hidden_ref,
     roped_ref, acc_ref, stat_ref, kv_ref, s_0, s_1, most_0, most_1, top_ref, sum_ref, values_ref,
-    bias_ref, w_ref, stage_ref, roped_sem, state_sems, sem, weight_sem, out_sems,
+    bias_ref, w_ref, stage_ref, state_sems, sem, weight_sem, out_sems,
 ):
     group_index = lax.axis_index("group")
     has_old = lengths_ref[lax.axis_index("blk")] > 0
@@ -513,11 +520,14 @@
     def copies(t):
         return [
             pltpu.make_async_copy(source.at[t], target.at[t], state_sems.at[number, t])
-            for number, (source, target) in enumerate(((stat_in, stat_ref), (acc_in, acc_ref)))
+            for number, (source, target) in enumerate(
+                ((roped_in, roped_ref), (stat_in, stat_ref), (acc_in, acc_ref))
+            )
         ]
 
-    roped_copy = pltpu.make_async_copy(roped_in, roped_ref, roped_sem)
-    roped_copy.start()
+    for copy in copies(0):
+        copy.start()
+
     @pl.when(odd == 1)
     def _():
         fetch(core_ref, 0, kv_ref, base, 16, sem)
@@ -539,7 +549,7 @@
                 fetch_pair(near, 4 * block, kv_ref, place, sem)
                 fetch_pair(far, 4 * block, kv_ref, place + 8, sem)
 
-    for t in range(items):
+    for t in range(1, items):
         for copy in copies(t):
             copy.start()
     weight_copy = pltpu.make_async_copy(weight_ref, w_ref, weight_sem)
@@ -559,7 +569,6 @@
         bias_ref[0, :, :256] = old_bias(rows, group_index)
         bias_ref[0, :, 256:] = old_bias(rows, group_index ^ 2)
 
-    roped_copy.wait()
     wait_rows(kv_ref, blocks, 4, sem)
     lane = lax.broadcasted_iota(jnp.int32, stat_ref.shape[1:], 1)
 
@@ -625,8 +634,7 @@
         + [
             pltpu.VMEM(weight.shape, jnp.bfloat16),
             pltpu.VMEM((2, rows, chunk), jnp.bfloat16),
-            pltpu.SemaphoreType.DMA,
-            pltpu.SemaphoreType.DMA((2, items)),
+            pltpu.SemaphoreType.DMA((3, items)),
             pltpu.SemaphoreType.DMA,
             pltpu.SemaphoreType.DMA,
             pltpu.SemaphoreType.DMA((2,)),

time: 77.5 us -> 77.3 us (level)
  the two profiles are of different devices: /device:TPU:7 before, /device:TPU:0 now
where the time goes in v15:
time: 77.3 us; the launch traced here: 76.9 us
  Pallas kernels  50.5 us (65%)
  starting transfers between devices  15.3 us (20%)
  waiting for transfers between devices  8.46 us (11%)
  local copies, waits for them, and re-layouts  1.67 us (2%)
  between operations  0.97 us (1%)
    pallas_call x1, Pallas kernels, rest_part(): pl.pallas_call(rest_kernel, out_shape=pltpu.HBM((rows, width), jnp.bfloat...  30.3 us
    pallas_call x1, Pallas kernels, diagonal_part(): pl.pallas_call(diagonal_kernel, out_shape=(pltpu.HBM((items, head_pair *...  9.05 us
    all_to_all x1, starting transfers between devices, body(): old = lax.all_to_all(picked, 'blk', split_axis=0, concat_axis=0, tiled=True)  7.26 us
    ppermute x2, waiting for transfers between devices, other_chip(): return lax.ppermute(value, 'group', [(0, 2), (2, 0), (1, 3), (3, 1)])  4.84 us
    all_to_all x1, starting transfers between devices, body(): lax.all_to_all(new, 'blk', split_axis=0, concat_axis=0, tiled=True)  4.77 us
    ppermute x2, starting transfers between devices, other_chip(): return lax.ppermute(value, 'group', [(0, 2), (2, 0), (1, 3), (3, 1)])  3.1 us
    pallas_call x1, Pallas kernels, pick_old(): pl.pallas_call(pick_old_kernel, out_shape=jax.ShapeDtypeStruct((requests,...  2.98 us
    pallas_call x1, Pallas kernels, pick_new(): pl.pallas_call(lambda *refs: pick_new_kernel(pages, cap, *refs), out_shap...  2.76 us
  transfers between devices with their start and end apart: 8, of which 4 were waited for; matrix products, arithmetic and copies ran while one was open for 0% of the time, Pallas kernels for 60%

profile of v15, /device:TPU:0, one launch (start us, length us, event | category | flops | bytes accessed | tf_op | source)
XLA Modules:
  0.0 76.9 jit_solution(487133274889526170)
XLA Ops:
  0.6 0.0 copy-start.9
  0.6 0.0 copy-start.8
  0.7 0.0 copy-start.6
  0.7 0.0 copy-start.5
  0.7 3.0 %pick_old.1 = bf16[8,2,2,32,256]{4,3,2,1,0:T(8,128)(2,1)} custom-call(s32[8,32]{1,0:T(8,128)} %refs_0_.2, bf16[40,32,256]{2,1,0:T(8,128)(2,1)} %key_ref.3, bf16[40,32,256]{2,1,0:T(8,128)(2,1)} %value_ref.3), custom_call_target="tpu_custom_call" | custom-call | flops 1 | bytes 1 | tf_op jit(solution)/shard_map/pick_old/pallas_call | solution.py:72
  3.7 7.3 %all-to-all-start = ((bf16[8,2,2,32,256]{4,3,2,1,0:T(8,128)(2,1)}), bf16[8,2,2,32,256]{4,3,2,1,0:T(8,128)(2,1)S(1)}, u32[]{:S(2)}, u32[]{:S(2)}) async-start(bf16[8,2,2,32,256]{4,3,2,1,0:T(8,128)(2,1)} %pick_old.1), calls=%async_computation | async-start | bytes 1048576 | tf_op jit(solution)/shard_map/all_to_all | solution.py:704
  10.9 0.0 copy-done.9
  10.9 0.0 copy-done.8
  10.9 0.0 copy-done.6
  11.0 0.0 copy-done.5
  11.0 2.5 %rotate_keys.1 = (bf16[16,2,32,256]{3,2,1,0:T(8,128)(2,1)}, f32[512,128]{1,0:T(8,128)}, f32[512,128]{1,0:T(8,128)}) custom-call(s32[8]{0:T(128)S(1)} %copy-done.8, f32[1,128]{1,0:T(1,128)S(1)} %copy-done.9, bf16[512,256]{1,0:T(8,128)(2,1)S(1)} %bitcast.5, bf16[512,256]{1,0:T(8,128)(2,1)S(1)} %bitcast.6), custom_call_target="tpu_custom_call" | custom-call | flops 1 | bytes 1 | tf_op jit(solution)/shard_map/rotate_keys/pallas_call | solution.py:128
  13.4 0.0 copy-start.7
  13.4 1.5 %collective-permute-start.1 = (bf16[16,2,32,256]{3,2,1,0:T(8,128)(2,1)}, bf16[16,2,32,256]{3,2,1,0:T(8,128)(2,1)S(1)}, u32[]{:S(2)}, u32[]{:S(2)}) collective-permute-start(bf16[16,2,32,256]{3,2,1,0:T(8,128)(2,1)} %get-tuple-element.22.own_ref.refs_1_), channel_id=1, source_target_pairs={{0,2},{2,0},{1,3},{3,1},{4,6},{6,4},{5,7},{7,5},{8,10},{10,8},{9,1... | collective-permute-start | bytes 1572872 | tf_op jit(solution)/shard_map/ppermute | solution.py:701
  14.9 0.0 collective-permute-start
  14.9 0.0 copy-start.4
  14.9 9.1 %attend_diagonal.1 = (bf16[5,1024,256]{2,1,0:T(8,128)(2,1)}, f32[5,1024,256]{2,1,0:T(8,128)}, f32[5,1024,128]{2,1,0:T(8,128)}, bf16[40,32,256]{2,1,0:T(8,128)(2,1)}, bf16[40,32,256]{2,1,0:T(8,128)(2,1)}) custom-call(bf16[512,2560]{1,0:T(8,128)(2,1)} %bitcast.7, f32[512,128]{1,0:T(8,128)} %get-tuple-element.20.cos_in, f32[512,128]{1,0:T(8,128)} %get-tuple-element.21.sin_in, ...), custom_call_target="tpu_custom_call" | custom-call | flops 1 | bytes 1 | tf_op jit(solution)/shard_map/attend_diagonal/pallas_call | solution.py:476
  24.0 1.4 %all-to-all-done = bf16[8,2,2,32,256]{4,3,2,1,0:T(8,128)(2,1)S(1)} async-done(((bf16[8,2,2,32,256]{4,3,2,1,0:T(8,128)(2,1)}), bf16[8,2,2,32,256]{4,3,2,1,0:T(8,128)(2,1)S(1)}, u32[]{:S(2)}, u32[]{:S(2)}) %all-to-all-start) | async-done | bytes 524320 | tf_op jit(solution)/shard_map/all_to_all | solution.py:704
  25.4 0.0 copy-start.10
  25.4 0.8 %copy-done.10 = bf16[8,2,2,32,256]{4,3,2,1,0:T(8,128)(2,1)} copy-done((bf16[8,2,2,32,256]{4,3,2,1,0:T(8,128)(2,1)}, bf16[8,2,2,32,256]{4,3,2,1,0:T(8,128)(2,1)S(1)}, u32[]{:S(2)}) %copy-start.10) | copy-done | bytes 524312
  26.2 0.0 copy-done.7
  26.2 1.6 %sort_old.1.old_ref = bf16[16,2,32,256]{3,2,1,0:T(8,128)(2,1)S(1)} custom-call(s32[8,32]{1,0:T(8,128)S(1)} %copy-done.7, bf16[16,2,32,256]{3,2,1,0:T(8,128)(2,1)} %bitcast.9), custom_call_target="tpu_custom_call" | custom-call | flops 1 | bytes 1 | tf_op jit(solution)/shard_map/sort_old/pallas_call | solution.py:152
  27.9 0.0 copy-start
  27.9 0.0 collective-permute-done.1.refs_3_.far_ref
  27.9 0.0 copy-start.1
  27.9 0.1 collective-permute-start.2
  28.0 1.6 %collective-permute-start.4 = (bf16[16,2,32,256]{3,2,1,0:T(8,128)(2,1)S(1)}, bf16[16,2,32,256]{3,2,1,0:T(8,128)(2,1)S(1)}, u32[]{:S(2)}, u32[]{:S(2)}) collective-permute-start(bf16[16,2,32,256]{3,2,1,0:T(8,128)(2,1)S(1)} %sort_old.1.old_ref), channel_id=1, source_target_pairs={{0,2},{2,0},{1,3},{3,1},{4,6},{6,4},{5,7},{7,5},{8,10},{10,8},{9,1... | collective-permute-start | bytes 1572872 | tf_op jit(solution)/shard_map/ppermute | solution.py:701
  29.6 0.0 collective-permute-done.refs_2_.core_ref
  29.6 0.0 copy-start.2
  29.6 0.3 collective-permute-done.2.refs_4_.far_core_ref
  29.9 0.0 copy-done.4
  29.9 0.0 copy-start.3
  29.9 2.8 %pick_new.1 = (bf16[16,2,32,256]{3,2,1,0:T(8,128)(2,1)}, s32[16]{0:T(128)S(1)}) custom-call(s32[8,32]{1,0:T(8,128)S(1)} %copy-done.7, bf16[16,2,32,256]{3,2,1,0:T(8,128)(2,1)S(1)} %copy-done.4, bf16[16,2,32,256]{3,2,1,0:T(8,128)(2,1)S(1)} %collective-permute-done.refs_2_.core_ref, bf16[16,2,32,256]{3,2,1,0:T(8,128)(2,1)S(1)} %collective-permute-done.1.refs_3_.far_ref, ...), custom_call_target="tpu_custom_call" | custom-call | flops 1 | bytes 1 | tf_op jit(solution)/shard_map/pick_new/pallas_call | solution.py:189
  32.6 4.8 %all-to-all-start.1 = ((bf16[16,2,32,256]{3,2,1,0:T(8,128)(2,1)}), bf16[16,2,32,256]{3,2,1,0:T(8,128)(2,1)S(1)}, u32[]{:S(2)}, u32[]{:S(2)}) async-start(bf16[16,2,32,256]{3,2,1,0:T(8,128)(2,1)} %get-tuple-element.28), calls=%async_computation.1 | async-start | bytes 1048576 | tf_op jit(solution)/shard_map/all_to_all | solution.py:721
  37.4 0.1 collective-permute-start.3
  37.5 4.8 %collective-permute-done.4.old_far_ref = bf16[16,2,32,256]{3,2,1,0:T(8,128)(2,1)S(1)} collective-permute-done((bf16[16,2,32,256]{3,2,1,0:T(8,128)(2,1)S(1)}, bf16[16,2,32,256]{3,2,1,0:T(8,128)(2,1)S(1)}, u32[]{:S(2)}, u32[]{:S(2)}) %collective-permute-start.4) | collective-permute-done | bytes 524320 | tf_op jit(solution)/shard_map/ppermute | solution.py:701
  42.3 0.0 copy-start.11
  42.3 0.0 collective-permute-start.5
  42.3 0.0 collective-permute-done.3.old_core_ref
  42.3 0.0 copy-start.12
  42.3 1.9 %collective-permute-done.5.old_far_core_ref = bf16[16,2,32,256]{3,2,1,0:T(8,128)(2,1)S(1)} collective-permute-done((bf16[16,2,32,256]{3,2,1,0:T(8,128)(2,1)S(1)}, bf16[16,2,32,256]{3,2,1,0:T(8,128)(2,1)S(1)}, u32[]{:S(2)}, u32[]{:S(2)}) %collective-permute-start.5) | collective-permute-done | bytes 524320 | tf_op jit(solution)/shard_map/ppermute | solution.py:698
  44.2 0.0 copy-start.13
  44.2 0.8 %copy-done.13 = bf16[16,2,32,256]{3,2,1,0:T(8,128)(2,1)} copy-done((bf16[16,2,32,256]{3,2,1,0:T(8,128)(2,1)}, bf16[16,2,32,256]{3,2,1,0:T(8,128)(2,1)S(1)}, u32[]{:S(2)}) %copy-start.13) | copy-done | bytes 524312
  45.0 0.0 copy-done
  45.0 0.0 copy-done.1
  45.0 0.0 copy-done.2
  45.0 0.0 copy-done.3
  45.1 0.0 copy-done.11
  45.1 0.0 copy-done.12
  45.1 30.3 %attend_rest.1 = bf16[512,2560]{1,0:T(8,128)(2,1)} custom-call(s32[8]{0:T(128)} %lengths_ref.3, bf16[5,1024,256]{2,1,0:T(8,128)(2,1)} %get-tuple-element.23.roped_in, f32[5,1024,256]{2,1,0:T(8,128)} %get-tuple-element.24.acc_in, f32[5,1024,128]{2,1,0:T(8,128)} %get-tuple-element.25.stat_in, bf16[16,2,32,256]{3,2,1,0:T(8,128)(2,1)} %copy-done.2, ...), custom_call_target="tpu_custom_call" | custom-call | flops 1 | bytes 1 | tf_op jit(solution)/shard_map/attend_rest/pallas_call | solution.py:627
  75.4 0.0 all-to-all-done.1.arrived_ref
  75.4 1.4 %place_new.1 = (bf16[40,32,256]{2,1,0:T(8,128)(2,1)}, bf16[40,32,256]{2,1,0:T(8,128)(2,1)}) custom-call(s32[16]{0:T(128)S(1)} %get-tuple-element.30.targets_ref, bf16[16,2,32,256]{3,2,1,0:T(8,128)(2,1)S(1)} %all-to-all-done.1.arrived_ref, bf16[40,32,256]{2,1,0:T(8,128)(2,1)} %get-tuple-element.31.key_in, ...), custom_call_target="tpu_custom_call", output_to_operand_aliasing={{0}: (2, {}), {1}: (3, {})} | custom-call | flops 1 | bytes 1 | tf_op jit(solution)/shard_map/place_new/pallas_call | solution.py:667
Async XLA Ops:
  0.6 10.3 %copy-start.9 = (f32[1,128]{1,0:T(1,128)S(1)}, f32[1,128]{1,0:T(1,128)}, u32[]{:S(2)}) copy-start(f32[1,128]{1,0:T(1,128)} %constant.2.clone.freq_ref) | copy-start | bytes 1540
  0.6 10.3 %copy-start.8 = (s32[8]{0:T(128)S(1)}, s32[8]{0:T(128)}, u32[]{:S(2)}) copy-start(s32[8]{0:T(128)} %lengths_ref.3) | copy-start | bytes 100
  0.7 10.3 %copy-start.6 = (bf16[1,512,256]{2,1,0:T(8,128)(2,1)S(1)}, bf16[1,512,256]{2,1,0:T(8,128)(2,1)}, u32[]{:S(2)}) copy-start(bf16[1,512,256]{2,1,0:T(8,128)(2,1)} %param.11) | copy-start | bytes 786436
  0.7 10.3 %copy-start.5 = (bf16[1,512,256]{2,1,0:T(8,128)(2,1)S(1)}, bf16[1,512,256]{2,1,0:T(8,128)(2,1)}, u32[]{:S(2)}) copy-start(bf16[1,512,256]{2,1,0:T(8,128)(2,1)} %param.10) | copy-start | bytes 786436
  3.7 21.8 %all-to-all-start = ((bf16[8,2,2,32,256]{4,3,2,1,0:T(8,128)(2,1)}), bf16[8,2,2,32,256]{4,3,2,1,0:T(8,128)(2,1)S(1)}, u32[]{:S(2)}, u32[]{:S(2)}) async-start(bf16[8,2,2,32,256]{4,3,2,1,0:T(8,128)(2,1)} %pick_old.1), calls=%async_computation | async-start | bytes 1048576 | tf_op jit(solution)/shard_map/all_to_all | solution.py:704
  13.4 12.8 %copy-start.7 = (s32[8,32]{1,0:T(8,128)S(1)}, s32[8,32]{1,0:T(8,128)}, u32[]{:S(2)}) copy-start(s32[8,32]{1,0:T(8,128)} %refs_0_.2) | copy-start | bytes 3076
  13.4 14.5 %collective-permute-start.1 = (bf16[16,2,32,256]{3,2,1,0:T(8,128)(2,1)}, bf16[16,2,32,256]{3,2,1,0:T(8,128)(2,1)S(1)}, u32[]{:S(2)}, u32[]{:S(2)}) collective-permute-start(bf16[16,2,32,256]{3,2,1,0:T(8,128)(2,1)} %get-tuple-element.22.own_ref.refs_1_), channel_id=1, source_target_pairs={{0,2},{2,0},{1,3},{3,1},{4,6},{6,4},{5,7},{7,5},{8,10},{10,8},{9,1... | collective-permute-start | bytes 1572872 | tf_op jit(solution)/shard_map/ppermute | solution.py:701
  14.9 14.6 %collective-permute-start = (bf16[16,2,32,256]{3,2,1,0:T(8,128)(2,1)}, bf16[16,2,32,256]{3,2,1,0:T(8,128)(2,1)S(1)}, u32[]{:S(2)}, u32[]{:S(2)}) collective-permute-start(bf16[16,2,32,256]{3,2,1,0:T(8,128)(2,1)} %get-tuple-element.22.own_ref.refs_1_), channel_id=1, source_target_pairs={{0,1},{1,0},{2,3},{3,2},{4,5},{5,4},{6,7},{7,6},{8,9},{9,8},{10,11... | collective-permute-start | bytes 1572872 | tf_op jit(solution)/shard_map/ppermute | solution.py:698
  14.9 14.9 %copy-start.4 = (bf16[16,2,32,256]{3,2,1,0:T(8,128)(2,1)S(1)}, bf16[16,2,32,256]{3,2,1,0:T(8,128)(2,1)}, u32[]{:S(2)}) copy-start(bf16[16,2,32,256]{3,2,1,0:T(8,128)(2,1)} %get-tuple-element.22.own_ref.refs_1_) | copy-start | bytes 1572868
  25.4 0.8 %copy-start.10 = (bf16[8,2,2,32,256]{4,3,2,1,0:T(8,128)(2,1)}, bf16[8,2,2,32,256]{4,3,2,1,0:T(8,128)(2,1)S(1)}, u32[]{:S(2)}) copy-start(bf16[8,2,2,32,256]{4,3,2,1,0:T(8,128)(2,1)S(1)} %all-to-all-done) | copy-start | bytes 1572868
  27.9 17.2 %copy-start = (bf16[16,2,32,256]{3,2,1,0:T(8,128)(2,1)}, bf16[16,2,32,256]{3,2,1,0:T(8,128)(2,1)S(1)}, u32[]{:S(2)}) copy-start(bf16[16,2,32,256]{3,2,1,0:T(8,128)(2,1)S(1)} %sort_old.1.old_ref) | copy-start | bytes 1572868
  27.9 17.2 %copy-start.1 = (bf16[16,2,32,256]{3,2,1,0:T(8,128)(2,1)}, bf16[16,2,32,256]{3,2,1,0:T(8,128)(2,1)S(1)}, u32[]{:S(2)}) copy-start(bf16[16,2,32,256]{3,2,1,0:T(8,128)(2,1)S(1)} %collective-permute-done.1.refs_3_.far_ref) | copy-start | bytes 1572868
  27.9 2.0 %collective-permute-start.2 = (bf16[16,2,32,256]{3,2,1,0:T(8,128)(2,1)S(1)}, bf16[16,2,32,256]{3,2,1,0:T(8,128)(2,1)S(1)}, u32[]{:S(2)}, u32[]{:S(2)}) collective-permute-start(bf16[16,2,32,256]{3,2,1,0:T(8,128)(2,1)S(1)} %collective-permute-done.1.refs_3_.far_ref), channel_id=1, source_target_pairs={{0,1},{1,0},{2,3},{3,2},{4,5},{5,4},{6,7},{7,6},{8,9},{9,8},{10,11... | collective-permute-start | bytes 1572872 | tf_op jit(solution)/shard_map/ppermute | solution.py:698
  28.0 14.3 %collective-permute-start.4 = (bf16[16,2,32,256]{3,2,1,0:T(8,128)(2,1)S(1)}, bf16[16,2,32,256]{3,2,1,0:T(8,128)(2,1)S(1)}, u32[]{:S(2)}, u32[]{:S(2)}) collective-permute-start(bf16[16,2,32,256]{3,2,1,0:T(8,128)(2,1)S(1)} %sort_old.1.old_ref), channel_id=1, source_target_pairs={{0,2},{2,0},{1,3},{3,1},{4,6},{6,4},{5,7},{7,5},{8,10},{10,8},{9,1... | collective-permute-start | bytes 1572872 | tf_op jit(solution)/shard_map/ppermute | solution.py:701
  29.6 15.5 %copy-start.2 = (bf16[16,2,32,256]{3,2,1,0:T(8,128)(2,1)}, bf16[16,2,32,256]{3,2,1,0:T(8,128)(2,1)S(1)}, u32[]{:S(2)}) copy-start(bf16[16,2,32,256]{3,2,1,0:T(8,128)(2,1)S(1)} %collective-permute-done.refs_2_.core_ref) | copy-start | bytes 1572868
  29.9 15.2 %copy-start.3 = (bf16[16,2,32,256]{3,2,1,0:T(8,128)(2,1)}, bf16[16,2,32,256]{3,2,1,0:T(8,128)(2,1)S(1)}, u32[]{:S(2)}) copy-start(bf16[16,2,32,256]{3,2,1,0:T(8,128)(2,1)S(1)} %collective-permute-done.2.refs_4_.far_core_ref) | copy-start | bytes 1572868
  32.6 42.7 %all-to-all-start.1 = ((bf16[16,2,32,256]{3,2,1,0:T(8,128)(2,1)}), bf16[16,2,32,256]{3,2,1,0:T(8,128)(2,1)S(1)}, u32[]{:S(2)}, u32[]{:S(2)}) async-start(bf16[16,2,32,256]{3,2,1,0:T(8,128)(2,1)} %get-tuple-element.28), calls=%async_computation.1 | async-start | bytes 1048576 | tf_op jit(solution)/shard_map/all_to_all | solution.py:721
  37.4 4.9 %collective-permute-start.3 = (bf16[16,2,32,256]{3,2,1,0:T(8,128)(2,1)S(1)}, bf16[16,2,32,256]{3,2,1,0:T(8,128)(2,1)S(1)}, u32[]{:S(2)}, u32[]{:S(2)}) collective-permute-start(bf16[16,2,32,256]{3,2,1,0:T(8,128)(2,1)S(1)} %sort_old.1.old_ref), channel_id=1, source_target_pairs={{0,1},{1,0},{2,3},{3,2},{4,5},{5,4},{6,7},{7,6},{8,9},{9,8},{10,11... | collective-permute-start | bytes 1572872 | tf_op jit(solution)/shard_map/ppermute | solution.py:698
  42.3 2.7 %copy-start.11 = (bf16[16,2,32,256]{3,2,1,0:T(8,128)(2,1)}, bf16[16,2,32,256]{3,2,1,0:T(8,128)(2,1)S(1)}, u32[]{:S(2)}) copy-start(bf16[16,2,32,256]{3,2,1,0:T(8,128)(2,1)S(1)} %collective-permute-done.4.old_far_ref) | copy-start | bytes 1572868
  42.3 1.9 %collective-permute-start.5 = (bf16[16,2,32,256]{3,2,1,0:T(8,128)(2,1)S(1)}, bf16[16,2,32,256]{3,2,1,0:T(8,128)(2,1)S(1)}, u32[]{:S(2)}, u32[]{:S(2)}) collective-permute-start(bf16[16,2,32,256]{3,2,1,0:T(8,128)(2,1)S(1)} %collective-permute-done.4.old_far_ref), channel_id=1, source_target_pairs={{0,1},{1,0},{2,3},{3,2},{4,5},{5,4},{6,7},{7,6},{8,9},{9,8},{10,11... | collective-permute-start | bytes 1572872 | tf_op jit(solution)/shard_map/ppermute | solution.py:698
  42.3 2.7 %copy-start.12 = (bf16[16,2,32,256]{3,2,1,0:T(8,128)(2,1)}, bf16[16,2,32,256]{3,2,1,0:T(8,128)(2,1)S(1)}, u32[]{:S(2)}) copy-start(bf16[16,2,32,256]{3,2,1,0:T(8,128)(2,1)S(1)} %collective-permute-done.3.old_core_ref) | copy-start | bytes 1572868
  44.2 0.8 %copy-start.13 = (bf16[16,2,32,256]{3,2,1,0:T(8,128)(2,1)}, bf16[16,2,32,256]{3,2,1,0:T(8,128)(2,1)S(1)}, u32[]{:S(2)}) copy-start(bf16[16,2,32,256]{3,2,1,0:T(8,128)(2,1)S(1)} %collective-permute-done.5.old_far_core_ref) | copy-start | bytes 1572868
